TPU v7x, 32 devices: a whole 2x2x4 slice. The times are simulated.
32 devices in a mesh: prow: 8 (over z, x), pcol: 4 (over y, core).
Axes of the slice: x: 2, y: 2, z: 4, core: 2. Of those that a mesh axis runs over, the one named last changes fastest.
Arguments:
- b_panels: bfloat16 [3, 8, 4, 128, 512], P(None, 'prow', 'pcol'), may hold values from -6 to 6
- diag_inverse: bfloat16 [3, 8, 4, 128, 128], P(None, 'prow', 'pcol'), as said below
- l_blocks: bfloat16 [2, 8, 4, 4, 5, 128, 128], P(None, 'prow', 'pcol'), may hold values from -0.125 to 0.125
- block_cols: int32 [2, 8, 4, 4, 5], P(None, 'prow', 'pcol'), may hold values from 0 to 63, as said below
- live_counts: int32 [2, 8, 4, 4], P(None, 'prow', 'pcol'), may hold values from 0 to 5, as said below
Outputs:
- solution: bfloat16 [3, 8, 4, 128, 512], P(None, 'prow', 'pcol')
Inputs may be any that keep to these rules, and one draw needn't show every extreme that they name: `block_cols`: for block row (l, r, q) and device column c, entries are l2 * 32 + p * 4 + c with l2 < l and 0 <= p < 8; the first live_counts[l - 1, r, c, q] slots are distinct. `live_counts`: at most min(5, l * 8) at level l; that bound is reached at every level. `diag_inverse`: lower triangular.
All inputs are finite; a program needn't handle non-finite values.
Results may differ from a plain program's by a relative error of at most 0.014.
Values may be sent and summed in bfloat16 or wider, within the bound.
No kernel may reach another device: no remote copies, remote signals or barrier semaphores. Data moves between devices by JAX's collectives and lax.ppermute only.
A program may use at most 128 MiB of HBM per device.

v0:
```python
import jax
import jax.numpy as jnp
from jax import lax
from jax.sharding import PartitionSpec as P


def solve_front(right_cols, diag_inverse, l_blocks, block_cols, live_counts):
    proc_rows = lax.axis_size("prow")
    proc_cols = lax.axis_size("pcol")
    per_level = proc_rows * proc_cols
    levels = right_cols.shape[0]
    block_size = right_cols.shape[1]
    front_width = right_cols.shape[2]
    slot_count = l_blocks.shape[4]
    solved_cols = jnp.zeros((levels * proc_rows, block_size, front_width), jnp.bfloat16)
    solutions = []
    for level_idx in range(levels):
        right_part = right_cols[level_idx].astype(jnp.float32)
        if level_idx > 0:
            blocks = l_blocks[level_idx - 1, 0, 0]
            chosen = block_cols[level_idx - 1, 0, 0]
            currently_active = live_counts[level_idx - 1, 0, 0]
            local_index = chosen // per_level * proc_rows + chosen % per_level // proc_cols
            known = solved_cols

            def row_term(
                first_row,
                row_count,
                blocks=blocks,
                local_index=local_index,
                currently_active=currently_active,
                known=known,
            ):
                slot_mask = jnp.arange(slot_count)[None, :] < currently_active[:, None]
                masked = jnp.where(slot_mask[:, :, None, None], blocks, jnp.zeros((), jnp.bfloat16))
                fetched = known[local_index]
                return jnp.einsum(
                    "jkab,jkbr->jar", masked, fetched, preferred_element_type=jnp.float32
                )

            row_total = lax.psum_scatter(
                row_term(jnp.int32(0), 1 * lax.axis_size("pcol")).astype(jnp.bfloat16),
                "pcol",
                scatter_dimension=0,
                tiled=True,
            ).astype(jnp.float32)
            right_part = right_part - row_total[0]
        resid = right_part.astype(jnp.bfloat16)
        solution = jnp.dot(
            diag_inverse[level_idx, 0, 0], resid, preferred_element_type=jnp.float32
        ).astype(jnp.bfloat16)
        solutions.append(solution)
        if level_idx + 1 < levels:
            segment = lax.all_gather(solution[None], "prow", axis=0, tiled=True)
            solved_cols = lax.dynamic_update_slice_in_dim(
                solved_cols, segment, level_idx * proc_rows, 0
            )
    return jnp.stack(solutions)


def shards(b_panels, diag_inverse, l_blocks, block_cols, live_counts):
    right_cols = b_panels[:, 0, 0]
    result = solve_front(right_cols, diag_inverse, l_blocks, block_cols, live_counts)
    return result[:, None, None]


def solution(mesh):
    return jax.shard_map(
        shards,
        mesh=mesh,
        in_specs=(
            P(None, "prow", "pcol", None, None),
            P(None, "prow", "pcol", None, None),
            P(None, "prow", "pcol", None, None, None, None),
            P(None, "prow", "pcol", None, None),
            P(None, "prow", "pcol", None),
        ),
        out_specs=P(None, "prow", "pcol", None, None),
        check_vma=False,
    )
```

profile of v0, /device:TPU:0, one launch (start us, length us, event | category | flops | bytes accessed | tf_op | source)
XLA Modules:
  0.0 159.0 jit_solution(9074318592173488152)
XLA Ops:
  6.5 0.0 all-gather.5.cloned.1.call-start
  6.5 1.7 %convolution_convert_fusion.2 = bf16[128,512]{1,0:T(8,128)(2,1)} fusion(bf16[3,1,1,128,512]{4,3,2,1,0:T(8,128)(2,1)} %param.5, bf16[3,1,1,128,128]{4,3,2,1,0:T(8,128)(2,1)} %param.6), kind=kOutput, calls=%fused_computation.8 | convolution fusion | flops 16842752 | bytes 294912 | tf_op jit(solution)/shard_map/dot_general | solution.py:49
  8.3 0.0 all-gather.5.cloned.1.call-update
  8.3 0.0 reduce-scatter.3.cloned.1.call-start
  8.4 0.7 compare_select_fusion
  9.1 0.1 reshape.394
  9.2 0.7 slice_bitcast_fusion
  9.9 0.1 iota_compare_fusion.1
  9.9 42.4 %all-gather.5.cloned.1.call-done = bf16[1024,512]{1,0:T(8,128)(2,1)} async-done(((bf16[128,512]{1,0:T(8,128)(2,1)}), bf16[1024,512]{1,0:T(8,128)(2,1)}) %all-gather.5.cloned.1.call-update) | async-done | bytes 1048592 | tf_op jit(solution)/shard_map/all_gather | solution.py:54
  52.4 1.5 dynamic_update_slice.6
  53.9 2.4 %gather_fusion = bf16[20,128,512]{2,1,0:T(8,128)(2,1)} fusion(bf16[24,128,512]{2,1,0:T(8,128)(2,1)S(1)} %dynamic_update_slice.6, s32[1024]{0:T(1024)S(1)} %pad_clamp_fusion.1), kind=kCustom, calls=%fused_computation | custom fusion | bytes 5242960 | tf_op jit(solution)/shard_map/gather | solution.py:36
  56.3 0.0 copy-start.2
  56.3 3.4 %fusion = bf16[4,128,512]{2,1,0:T(8,128)(2,1)} fusion(bf16[4,5,128,512]{3,2,1,0:T(8,128)(2,1)} %bitcast.105, bf16[2,1,1,4,5,128,128]{6,5,4,3,2,1,0:T(8,128)(2,1)} %param.7, pred[4,5]{1,0:T(4,128)(4,1)S(1)} %iota_compare_fusion.1), kind=kOutput, calls=%fused_computation.4 | convolution fusion | flops 336134144 | bytes 3801108 | tf_op jit(solution)/shard_map/jkab,jkbr->jar/dot_general | solution.py:37
  59.7 0.0 reduce-scatter.3.cloned.1.call-update
  59.7 0.0 all-gather.7.cloned.1.call-start
  59.8 20.5 %reduce-scatter.3.cloned.1.call-done = bf16[1,128,512]{2,1,0:T(8,128)(2,1)} async-done(((bf16[4,128,512]{2,1,0:T(8,128)(2,1)}), bf16[1,128,512]{2,1,0:T(8,128)(2,1)}) %reduce-scatter.3.cloned.1.call-update) | async-done | bytes 131088 | tf_op jit(solution)/shard_map/reduce_scatter | solution.py:41
  80.3 0.0 copy-done.2
  80.3 1.8 %convolution_convert_fusion.1 = bf16[512,128]{0,1:T(8,128)(2,1)} fusion(bf16[1,128,512]{2,1,0:T(8,128)(2,1)} %reduce-scatter.3.cloned.1.call-done, bf16[3,1,1,128,512]{4,3,2,1,0:T(8,128)(2,1)S(1)} %copy-done.2, bf16[3,1,1,128,128]{4,3,2,1,0:T(8,128)(2,1)} %param.6), kind=kOutput, calls=%fused_computation.7 | convolution fusion | flops 17104896 | bytes 425984 | tf_op jit(solution)/shard_map/dot_general | solution.py:49
  82.1 0.0 all-gather.7.cloned.1.call-update
  82.1 0.0 reduce-scatter.5.cloned.1.call-start
  82.1 0.1 reshape.402
  82.2 0.1 iota_compare_fusion
  82.3 40.5 %all-gather.7.cloned.1.call-done = bf16[1024,512]{1,0:T(8,128)(2,1)} async-done(((bf16[128,512]{1,0:T(8,128)(2,1)}), bf16[1024,512]{1,0:T(8,128)(2,1)}) %all-gather.7.cloned.1.call-update) | async-done | bytes 1048592 | tf_op jit(solution)/shard_map/all_gather | solution.py:54
  122.8 1.3 constant_dynamic-update-slice_fusion
  124.2 2.4 %gather_fusion.1 = bf16[20,128,512]{2,1,0:T(8,128)(2,1)} fusion(bf16[24,128,512]{2,1,0:T(8,128)(2,1)S(1)} %constant_dynamic-update-slice_fusion, s32[1024]{0:T(1024)S(1)} %pad_clamp_fusion), kind=kCustom, calls=%fused_computation.1 | custom fusion | bytes 5242960 | tf_op jit(solution)/shard_map/gather | solution.py:36
  126.6 0.0 copy-start
  126.6 0.0 copy-start.1
  126.6 3.4 %fusion.1 = bf16[4,128,512]{2,1,0:T(8,128)(2,1)} fusion(bf16[4,5,128,512]{3,2,1,0:T(8,128)(2,1)} %bitcast.104, bf16[2,1,1,4,5,128,128]{6,5,4,3,2,1,0:T(8,128)(2,1)} %param.7, pred[4,5]{1,0:T(4,128)(4,1)S(1)} %iota_compare_fusion), kind=kOutput, calls=%fused_computation.5 | convolution fusion | flops 336134144 | bytes 3801108 | tf_op jit(solution)/shard_map/jkab,jkbr->jar/dot_general | solution.py:37
  130.0 0.0 reduce-scatter.5.cloned.1.call-update
  130.0 20.6 %reduce-scatter.5.cloned.1.call-done = bf16[1,128,512]{2,1,0:T(8,128)(2,1)} async-done(((bf16[4,128,512]{2,1,0:T(8,128)(2,1)}), bf16[1,128,512]{2,1,0:T(8,128)(2,1)}) %reduce-scatter.5.cloned.1.call-update) | async-done | bytes 131088 | tf_op jit(solution)/shard_map/reduce_scatter | solution.py:41
  150.6 1.1 fusion.2
  151.7 0.0 copy-done
  151.7 0.0 copy-done.1
  151.7 0.8 maximum_bitcast_fusion
  (2 shorter events, 0.0 us)
Async XLA Ops:
  6.5 45.8 %all-gather.5.cloned.1.call-start = ((), (), s32[]{:S(2)}) async-start(), calls=%async_computation.4 | async-start | bytes 1179648 | tf_op jit(solution)/shard_map/all_gather | solution.py:54
  8.3 72.0 %reduce-scatter.3.cloned.1.call-start = ((), (), s32[]{:S(2)}) async-start(), calls=%async_computation.2 | async-start | bytes 655360 | tf_op jit(solution)/shard_map/reduce_scatter | solution.py:41
  56.3 24.0 %copy-start.2 = (bf16[3,1,1,128,512]{4,3,2,1,0:T(8,128)(2,1)S(1)}, bf16[3,1,1,128,512]{4,3,2,1,0:T(8,128)(2,1)}, u32[]{:S(2)}) copy-start(bf16[3,1,1,128,512]{4,3,2,1,0:T(8,128)(2,1)} %param.5) | copy-start | bytes 1179652
  59.7 63.1 %all-gather.7.cloned.1.call-start = ((), (), s32[]{:S(2)}) async-start(), calls=%async_computation.5 | async-start | bytes 1179648 | tf_op jit(solution)/shard_map/all_gather | solution.py:54
  82.1 68.5 %reduce-scatter.5.cloned.1.call-start = ((), (), s32[]{:S(2)}) async-start(), calls=%async_computation.3 | async-start | bytes 655360 | tf_op jit(solution)/shard_map/reduce_scatter | solution.py:41
  126.6 25.1 %copy-start = (bf16[128,512]{1,0:T(8,128)(2,1)S(1)}, bf16[128,512]{1,0:T(8,128)(2,1)}, u32[]{:S(2)}) copy-start(bf16[128,512]{1,0:T(8,128)(2,1)} %convolution_convert_fusion.2) | copy-start | bytes 393220
  126.6 25.1 %copy-start.1 = (bf16[512,128]{0,1:T(8,128)(2,1)S(1)}, bf16[512,128]{0,1:T(8,128)(2,1)}, u32[]{:S(2)}) copy-start(bf16[512,128]{0,1:T(8,128)(2,1)} %convolution_convert_fusion.1) | copy-start | bytes 393220
Sparse Core Ops, SparseCore 0:
  9.5 42.8 all-gather.4
  59.8 20.4 reduce-scatter.2
  82.7 40.1 all-gather.6
  130.1 20.4 reduce-scatter.4
where the time goes:
time: 159 us
  waiting for transfers between devices  124 us (78%)
  between operations  13.2 us (8%)
  matrix products  11.4 us (7%)
  local copies, waits for them, and re-layouts  8.47 us (5%)
  other arithmetic  1.68 us (1%)
    all_gather x2, waiting for transfers between devices, solve_front(): segment = lax.all_gather(solution[None], 'prow', axis=0, tiled=True)  83 us
    reduce_scatter x2, waiting for transfers between devices, solve_front(): lax.psum_scatter(row_term(jnp.int32(0), 1 * lax.axis_size('pcol')).astype...  41.1 us
    dot_general x2, matrix products, row_term(): jnp.einsum('jkab,jkbr->jar', masked, fetched, preferred_element_type=jnp....  6.82 us
    gather x2, local copies, waits for them, and re-layouts, row_term(): fetched = known[local_index]  4.77 us
    dot_general x3, matrix products, solve_front(): jnp.dot(diag_inverse[level_idx, 0, 0], resid, preferred_element_type=jnp....  4.61 us
  transfers between devices with their start and end apart: 4, of which 4 were waited for; matrix products, arithmetic and copies ran while one was open for 1% of the time, Pallas kernels for 0%

commit v1 on v0

v1 whole, which is shorter than its diff:
```python
import functools

import jax
import jax.numpy as jnp
from jax import lax
from jax.experimental import pallas as pl
from jax.experimental.pallas import tpu as pltpu
from jax.sharding import PartitionSpec as P

LANES = 128
PAD_ROWS = 16
GATHER_BYTES = 16 * 2**20
VMEM_BYTES = 40 * 2**20


def vmem():
    return pl.BlockSpec(memory_space=pltpu.VMEM)


def smem():
    return pl.BlockSpec(memory_space=pltpu.SMEM)


def struct(shape, dtype=jnp.bfloat16):
    return jax.ShapeDtypeStruct(shape, dtype)


def params():
    return pltpu.CompilerParams(vmem_limit_bytes=VMEM_BYTES)


def solve_scattered(b_panels, diag_inverse, l_blocks, block_cols, live_counts):
    proc_rows = lax.axis_size("prow")
    proc_cols = lax.axis_size("pcol")
    per_level = proc_rows * proc_cols
    right_cols = b_panels[:, 0, 0]
    levels, block_size, front_width = right_cols.shape
    slot_count = l_blocks.shape[4]
    solved_cols = jnp.zeros((levels * proc_rows, block_size, front_width), jnp.bfloat16)
    solutions = []
    for level in range(levels):
        right_part = right_cols[level].astype(jnp.float32)
        if level > 0:
            chosen = block_cols[level - 1, 0, 0]
            active = live_counts[level - 1, 0, 0]
            local_index = chosen // per_level * proc_rows + chosen % per_level // proc_cols
            live = jnp.arange(slot_count)[None, :] < active[:, None]
            masked = jnp.where(live[:, :, None, None], l_blocks[level - 1, 0, 0], jnp.zeros((), jnp.bfloat16))
            partial = jnp.einsum(
                "jkab,jkbr->jar", masked, solved_cols[local_index], preferred_element_type=jnp.float32
            ).astype(jnp.bfloat16)
            row_total = lax.psum_scatter(partial, "pcol", scatter_dimension=0, tiled=True)
            right_part = right_part - row_total[0].astype(jnp.float32)
        resid = right_part.astype(jnp.bfloat16)
        solved = jnp.dot(diag_inverse[level, 0, 0], resid, preferred_element_type=jnp.float32).astype(jnp.bfloat16)
        solutions.append(solved)
        if level + 1 < levels:
            segment = lax.all_gather(solved[None], "prow", axis=0, tiled=True)
            solved_cols = lax.dynamic_update_slice_in_dim(solved_cols, segment, level * proc_rows, 0)
    return jnp.stack(solutions)[:, None, None]


def first_kernel(n, me_ref, b_ref, d_ref, full_ref, *piece_refs):
    me = me_ref[0]
    width = piece_refs[0].shape[1]
    full_ref[...] = jnp.dot(d_ref[...], b_ref[...], preferred_element_type=jnp.float32).astype(jnp.bfloat16)
    for j in range(n):
        start = pl.multiple_of((me ^ j) * width, LANES)
        piece_refs[j][...] = full_ref[:, pl.ds(start, width)]


def pack_kernel(n, me_ref, b_ref, d_ref, row_ref, *out_refs):
    me = me_ref[0]
    width = out_refs[0].shape[1]
    levels, size, _ = b_ref.shape
    for j in range(n):
        start = pl.multiple_of((me ^ j) * width, LANES)
        for level in range(1, levels):
            at = 2 * (level - 1) * size
            out_refs[j][at : at + size, :] = b_ref[level, :, pl.ds(start, width)]
            out_refs[j][at + size : at + 2 * size, :] = d_ref[level]
        out_refs[j][2 * (levels - 1) * size :, :] = row_ref[...]


def level_kernel(n, level, panels, me_ref, index_ref, *refs):
    x_refs = refs[:panels]
    l_refs = refs[panels : panels + n]
    p_refs = refs[panels + n : panels + 2 * n]
    out_ref = refs[panels + 2 * n]
    piece_refs = refs[panels + 2 * n + 1 : -1]
    known = refs[-1]
    me = me_ref[0]
    size, width = out_ref.shape[1:]
    slots = l_refs[0].shape[1]
    for s in range(panels):
        known[s] = x_refs[s][...]
    none = jnp.zeros((size, width), jnp.bfloat16)
    at = 2 * (level - 1) * size
    for jq in range(n):
        q = me ^ jq
        total = jnp.zeros((size, width), jnp.float32)
        for j in range(n):
            blocks, solved = [], []
            for k in range(slots):
                entry = index_ref[((level - 1) * n + j) * n * slots + q * slots + k]
                blocks.append(l_refs[j][q, k])
                solved.append(jnp.where(entry >= 0, known[jnp.maximum(entry, 0), j], none))
            total += jnp.dot(
                jnp.concatenate(blocks, axis=1), jnp.concatenate(solved, axis=0), preferred_element_type=jnp.float32
            )
        right = p_refs[jq][at : at + size, :].astype(jnp.float32)
        resid = (right - total).astype(jnp.bfloat16)
        inverse = p_refs[jq][at + size : at + 2 * size, :]
        value = jnp.dot(inverse, resid, preferred_element_type=jnp.float32).astype(jnp.bfloat16)
        out_ref[jq] = value
        piece_refs[jq][...] = value


def last_kernel(n, me_ref, full_ref, *refs):
    me = me_ref[0]
    out_ref = refs[-1]
    width = refs[0].shape[1]
    out_ref[0] = full_ref[...]
    for level in range(1, out_ref.shape[0]):
        for j in range(n):
            start = pl.multiple_of((me ^ j) * width, LANES)
            out_ref[level, :, pl.ds(start, width)] = refs[(level - 1) * n + j][...]


def swap(values, n):
    return [values[0]] + [lax.ppermute(values[j], "pcol", [(i, i ^ j) for i in range(n)]) for j in range(1, n)]


def ring_gather(value, cycle):
    m = len(cycle)
    to_next = [(cycle[i], cycle[(i + 1) % m]) for i in range(m)]
    to_last = [(b, a) for a, b in to_next]
    found = {0: value}
    behind = ahead = value
    for step in range(1, m // 2 + 1):
        behind = lax.ppermute(behind, "prow", to_next)
        found[m - step] = behind
        if step < m - step:
            ahead = lax.ppermute(ahead, "prow", to_last)
            found[step] = ahead
    return [found[d] for d in range(m)]


def solve_split(cycle, b_panels, diag_inverse, l_blocks, block_cols, live_counts):
    m = lax.axis_size("prow")
    n = lax.axis_size("pcol")
    levels, _, _, size, front = b_panels.shape
    slots = l_blocks.shape[4]
    width = front // n
    b = b_panels[:, 0, 0]
    inverse = diag_inverse[:, 0, 0]
    my_col = lax.axis_index("pcol")
    me = my_col.astype(jnp.int32)[None]

    full, *pieces = pl.pallas_call(
        functools.partial(first_kernel, n),
        out_shape=[struct((size, front))] + [struct((size, width))] * n,
        in_specs=[smem(), vmem(), vmem()],
        out_specs=[vmem()] * (n + 1),
        compiler_params=params(),
    )(me, b[0], inverse[0])
    solved = jnp.stack(swap(pieces, n))

    place = [cycle.index(p) for p in range(m)]
    chosen, counts = block_cols[:, 0, 0], live_counts[:, 0, 0]
    row_of = chosen % (m * n) // n
    place_of = sum(jnp.where(row_of == p, place[p], 0) for p in range(m))
    my_place = sum(jnp.where(lax.axis_index("prow") == p, place[p], 0) for p in range(m))
    entry = chosen // (m * n) * m + (place_of - my_place + m) % m
    live = jnp.arange(slots)[None, None, :] < counts[:, :, None]
    entry = jnp.where(live, entry, -1).reshape(-1).astype(jnp.bfloat16)
    row = jnp.zeros((PAD_ROWS * width,), jnp.bfloat16).at[: entry.size].set(entry).reshape(PAD_ROWS, width)

    packed = pl.pallas_call(
        functools.partial(pack_kernel, n),
        out_shape=[struct((2 * (levels - 1) * size + PAD_ROWS, width))] * n,
        in_specs=[smem(), vmem(), vmem(), vmem()],
        out_specs=[vmem()] * n,
        compiler_params=params(),
    )(me, b, inverse, row)
    packed = swap(packed, n)
    per_device = (levels - 1) * n * slots
    index = jnp.stack([p[-PAD_ROWS:].reshape(-1)[:per_device] for p in packed]).astype(jnp.int32)
    index = index.reshape(n, levels - 1, n * slots).transpose(1, 0, 2).reshape(-1)

    gathered = []
    for level in range(1, levels):
        held = [l_blocks[level - 1, 0, 0]]
        bit = n // 2
        while bit:
            swapped = [lax.ppermute(h, "pcol", [(i, i ^ bit) for i in range(n)]) for h in held]
            held = [v for pair in zip(held, swapped) for v in pair]
            bit //= 2
        gathered.append(held)

    panels, columns = [], []
    for level in range(1, levels):
        panels += ring_gather(solved, cycle)
        solved, *pieces = pl.pallas_call(
            functools.partial(level_kernel, n, level, len(panels)),
            out_shape=[struct((n, size, width))] + [struct((size, width))] * n,
            in_specs=[smem()] * 2 + [vmem()] * (len(panels) + 2 * n),
            out_specs=[vmem()] * (n + 1),
            scratch_shapes=[pltpu.VMEM((len(panels), n, size, width), jnp.bfloat16)],
            compiler_params=params(),
        )(me, index, *panels, *gathered[level - 1], *packed)
        columns += swap(pieces, n)

    out = pl.pallas_call(
        functools.partial(last_kernel, n),
        out_shape=struct((levels, size, front)),
        in_specs=[smem()] + [vmem()] * (1 + len(columns)),
        out_specs=vmem(),
        compiler_params=params(),
    )(me, full, *columns)
    return out[:, None, None]


def cycle_of(mesh):
    m = mesh.shape["prow"]
    names = list(mesh.axis_names)
    devices = mesh.devices.transpose([names.index("prow"), names.index("pcol")])[:, 0]
    spots = [tuple(getattr(d, "coords", None) or (i, 0, 0)) for i, d in enumerate(devices)]

    def near(a, b):
        return sum(abs(u - v) for u, v in zip(spots[a], spots[b])) == 1

    def extend(path):
        if len(path) == m:
            return path if near(path[-1], path[0]) else None
        for p in range(m):
            if p not in path and near(path[-1], p):
                found = extend(path + [p])
                if found:
                    return found
        return None

    return extend([0]) or list(range(m))


def solution(mesh):
    n = mesh.shape["pcol"]
    cycle = cycle_of(mesh)

    def shards(b_panels, diag_inverse, l_blocks, block_cols, live_counts):
        front = b_panels.shape[-1]
        splits = n & (n - 1) == 0 and front % (n * LANES) == 0
        if splits and n * l_blocks.size * l_blocks.dtype.itemsize <= GATHER_BYTES:
            return solve_split(cycle, b_panels, diag_inverse, l_blocks, block_cols, live_counts)
        return solve_scattered(b_panels, diag_inverse, l_blocks, block_cols, live_counts)

    return jax.shard_map(
        shards,
        mesh=mesh,
        in_specs=(
            P(None, "prow", "pcol", None, None),
            P(None, "prow", "pcol", None, None),
            P(None, "prow", "pcol", None, None, None, None),
            P(None, "prow", "pcol", None, None),
            P(None, "prow", "pcol", None),
        ),
        out_specs=P(None, "prow", "pcol", None, None),
        check_vma=False,
    )
```

time: 159 us -> 87.9 us (0.55)
  waiting for transfers between devices: 124 us -> 40.4 us
  starting transfers between devices: 0.13 us -> 30.2 us
  between operations: 13.2 us -> 0.16 us
  matrix products: 11.4 us -> 0 us
  Pallas kernels: 0 us -> 8.28 us
    all_gather x2 -> x0, waiting for transfers between devices: 83 us -> none  [solve_front(): segment = lax.all_gather(solution[None], 'prow', axis=0, tiled=True)]
    reduce_scatter x2 -> x0, waiting for transfers between devices: 41.1 us -> none  [solve_front(): lax.psum_scatter(row_term(jnp.int32(0), 1 * lax.axis_size('pcol')).astype...]
    ppermute x0 -> x32, waiting for transfers between devices: none -> 40.4 us  [the longest x12 19.9 us: swap(): lax.ppermute(values[j], 'pcol', [(i, i ^ j) for i in range(n)])]
    ppermute x0 -> x32, starting transfers between devices: none -> 30.2 us  [the longest x8 13.1 us: ring_gather(): behind = lax.ppermute(behind, 'prow', to_next)]
    dot_general x5 -> x0, matrix products: 11.4 us -> none  [the longest x2 6.82 us: row_term(): jnp.einsum('jkab,jkbr->jar', masked, fetched, preferred_element_type=jnp....]
    pallas_call x0 -> x5, Pallas kernels: none -> 8.28 us  [the longest x2 6.54 us: solve_split(): pl.pallas_call(functools.partial(level_kernel, n, level, len(panels)), ou...]
    gather x2 -> x0, local copies, waits for them, and re-layouts: 4.77 us -> none  [row_term(): fetched = known[local_index]]
    unnamed x6 -> x26, local copies, waits for them, and re-layouts: 0.01 us -> 4.68 us
  transfers between devices with their start and end apart: 4 -> 32, of which waited for: 4 -> 15; matrix products, arithmetic and copies ran while one was open for 1% -> 3% of each run, Pallas kernels for 0% -> 8%
where the time goes in v1:
time: 87.9 us; the launch traced here: 87.6 us
  waiting for transfers between devices  40.4 us (46%)
  starting transfers between devices  30.2 us (34%)
  local copies, waits for them, and re-layouts  8.41 us (10%)
  Pallas kernels  8.28 us (9%)
    ppermute x12, waiting for transfers between devices, swap(): lax.ppermute(values[j], 'pcol', [(i, i ^ j) for i in range(n)])  19.9 us
    ppermute x8, waiting for transfers between devices, ring_gather(): behind = lax.ppermute(behind, 'prow', to_next)  18.8 us
    ppermute x8, starting transfers between devices, ring_gather(): behind = lax.ppermute(behind, 'prow', to_next)  13.1 us
    ppermute x12, starting transfers between devices, swap(): lax.ppermute(values[j], 'pcol', [(i, i ^ j) for i in range(n)])  8.81 us
    pallas_call x2, Pallas kernels, solve_split(): pl.pallas_call(functools.partial(level_kernel, n, level, len(panels)), ou...  6.54 us
    ppermute x6, starting transfers between devices, ring_gather(): ahead = lax.ppermute(ahead, 'prow', to_last)  6.22 us
    unnamed x26, local copies, waits for them, and re-layouts  4.68 us
    ppermute x6, starting transfers between devices, solve_split(): lax.ppermute(h, 'pcol', [(i, i ^ bit) for i in range(n)])  2.15 us
  transfers between devices with their start and end apart: 32, of which 15 were waited for; matrix products, arithmetic and copies ran while one was open for 3% of the time, Pallas kernels for 8%

profile of v1, /device:TPU:0, one launch (start us, length us, event | category | flops | bytes accessed | tf_op | source)
XLA Modules:
  0.0 87.6 jit_solution(7533118576970475028)
XLA Ops:
  0.0 0.9 %slice_bitcast_fusion.2.b_ref = bf16[128,512]{1,0:T(8,128)(2,1)S(1)} fusion(bf16[3,1,1,128,512]{4,3,2,1,0:T(8,128)(2,1)} %param.7), kind=kLoop, calls=%fused_computation.3 | loop fusion | bytes 262144 | tf_op jit(solution)/shard_map/squeeze | solution.py:166
  0.9 0.8 slice_bitcast_fusion.3.d_ref
  1.7 0.2 shard_map.55
  1.9 2.5 %collective-permute-start.5 = (bf16[128,128]{1,0:T(8,128)(2,1)S(1)}, bf16[128,128]{1,0:T(8,128)(2,1)S(1)}, u32[]{:S(2)}, u32[]{:S(2)}) collective-permute-start(bf16[128,128]{1,0:T(8,128)(2,1)S(1)} %get-tuple-element.43), channel_id=1, source_target_pairs={{0,3},{1,2},{2,1},{3,0},{4,7},{5,6},{6,5},{7,4},{8,11},{9,10},{10,... | collective-permute-start | bytes 98312 | tf_op jit(solution)/shard_map/ppermute | solution.py:131
  4.4 0.6 collective-permute-start.4
  5.0 0.1 collective-permute-start.3
  5.1 1.4 %slice_bitcast_fusion = (bf16[4,5,128,128]{3,2,1,0:T(8,128)(2,1)S(1)}, bf16[4,5,128,128]{3,2,1,0:T(8,128)(2,1)S(1)}) fusion(bf16[2,1,1,4,5,128,128]{6,5,4,3,2,1,0:T(8,128)(2,1)} %param.9), kind=kLoop, calls=%fused_computation | loop fusion | bytes 2621440 | tf_op jit(solution)/shard_map/squeeze | solution.py:193
  6.6 1.7 %collective-permute-start.14 = (bf16[4,5,128,128]{3,2,1,0:T(8,128)(2,1)S(1)}, bf16[4,5,128,128]{3,2,1,0:T(8,128)(2,1)S(1)}, u32[]{:S(2)}, u32[]{:S(2)}) collective-permute-start(bf16[4,5,128,128]{3,2,1,0:T(8,128)(2,1)S(1)} %get-tuple-element.54.refs_8_), channel_id=1, source_target_pairs={{0,2},{1,3},{2,0},{3,1},{4,6},{5,7},{6,4},{7,5},{8,10},{9,11},{10,... | collective-permute-start | bytes 1966088 | tf_op jit(solution)/shard_map/ppermute | solution.py:196
  8.3 0.1 iota_compare_fusion
  8.4 0.1 lt.35
  8.5 0.1 squeeze.25
  8.6 0.7 shard_map.56
  9.4 0.1 collective-permute-start.2
  9.5 1.4 %collective-permute-start.1 = (bf16[528,128]{1,0:T(8,128)(2,1)S(1)}, bf16[528,128]{1,0:T(8,128)(2,1)S(1)}, u32[]{:S(2)}, u32[]{:S(2)}) collective-permute-start(bf16[528,128]{1,0:T(8,128)(2,1)S(1)} %get-tuple-element.38), channel_id=1, source_target_pairs={{0,2},{1,3},{2,0},{3,1},{4,6},{5,7},{6,4},{7,5},{8,10},{9,11},{10,... | collective-permute-start | bytes 405512 | tf_op jit(solution)/shard_map/ppermute | solution.py:131
  10.9 0.4 collective-permute-start
  11.3 0.4 collective-permute-start.27
  11.7 14.6 %collective-permute-done.2.refs_15_.refs_23_ = bf16[528,128]{1,0:T(8,128)(2,1)S(1)} collective-permute-done((bf16[528,128]{1,0:T(8,128)(2,1)S(1)}, bf16[528,128]{1,0:T(8,128)(2,1)S(1)}, u32[]{:S(2)}, u32[]{:S(2)}) %collective-permute-start.2) | collective-permute-done | bytes 135200 | tf_op jit(solution)/shard_map/ppermute | solution.py:131
  26.3 1.6 %collective-permute-start.6 = (bf16[4,128,128]{2,1,0:T(8,128)(2,1)S(1)}, bf16[4,128,128]{2,1,0:T(8,128)(2,1)S(1)}, u32[]{:S(2)}, u32[]{:S(2)}) collective-permute-start(bf16[4,128,128]{2,1,0:T(8,128)(2,1)S(1)} %pad_maximum_fusion.refs_0_), channel_id=1, source_target_pairs={{4,0},{12,4},{20,12},{28,20},{24,28},{16,24},{8,16},{0,8},{5,1},{1... | collective-permute-start | bytes 393224 | tf_op jit(solution)/shard_map/ppermute | solution.py:144
  27.9 2.1 %collective-permute-done.1.refs_14_.refs_22_ = bf16[528,128]{1,0:T(8,128)(2,1)S(1)} collective-permute-done((bf16[528,128]{1,0:T(8,128)(2,1)S(1)}, bf16[528,128]{1,0:T(8,128)(2,1)S(1)}, u32[]{:S(2)}, u32[]{:S(2)}) %collective-permute-start.1) | collective-permute-done | bytes 135200 | tf_op jit(solution)/shard_map/ppermute | solution.py:131
  30.0 1.6 %collective-permute-start.9 = (bf16[4,128,128]{2,1,0:T(8,128)(2,1)S(1)}, bf16[4,128,128]{2,1,0:T(8,128)(2,1)}, u32[]{:S(2)}, u32[]{:S(2)}) collective-permute-start(bf16[4,128,128]{2,1,0:T(8,128)(2,1)S(1)} %pad_maximum_fusion.refs_0_), channel_id=1, source_target_pairs={{0,4},{4,12},{12,20},{20,28},{28,24},{24,16},{16,8},{8,0},{1,5},{5... | collective-permute-start | bytes 393224 | tf_op jit(solution)/shard_map/ppermute | solution.py:141
  31.7 0.1 stack.30
  31.8 0.6 collective-permute-done.6.refs_1_
  32.3 1.7 %collective-permute-start.7 = (bf16[4,128,128]{2,1,0:T(8,128)(2,1)S(1)}, bf16[4,128,128]{2,1,0:T(8,128)(2,1)S(1)}, u32[]{:S(2)}, u32[]{:S(2)}) collective-permute-start(bf16[4,128,128]{2,1,0:T(8,128)(2,1)S(1)} %collective-permute-done.6.refs_1_), channel_id=1, source_target_pairs={{4,0},{12,4},{20,12},{28,20},{24,28},{16,24},{8,16},{0,8},{5,1},{1... | collective-permute-start | bytes 393224 | tf_op jit(solution)/shard_map/ppermute | solution.py:144
  34.1 1.0 %collective-permute-done.9.refs_7_ = bf16[4,128,128]{2,1,0:T(8,128)(2,1)} collective-permute-done((bf16[4,128,128]{2,1,0:T(8,128)(2,1)S(1)}, bf16[4,128,128]{2,1,0:T(8,128)(2,1)}, u32[]{:S(2)}, u32[]{:S(2)}) %collective-permute-start.9) | collective-permute-done | bytes 131104 | tf_op jit(solution)/shard_map/ppermute | solution.py:141
  35.1 1.6 %collective-permute-start.10 = (bf16[4,128,128]{2,1,0:T(8,128)(2,1)}, bf16[4,128,128]{2,1,0:T(8,128)(2,1)S(1)}, u32[]{:S(2)}, u32[]{:S(2)}) collective-permute-start(bf16[4,128,128]{2,1,0:T(8,128)(2,1)} %collective-permute-done.9.refs_7_), channel_id=1, source_target_pairs={{0,4},{4,12},{12,20},{20,28},{28,24},{24,16},{16,8},{8,0},{1,5},{5... | collective-permute-start | bytes 393224 | tf_op jit(solution)/shard_map/ppermute | solution.py:141
  36.7 0.9 %collective-permute-done.7.refs_2_ = bf16[4,128,128]{2,1,0:T(8,128)(2,1)S(1)} collective-permute-done((bf16[4,128,128]{2,1,0:T(8,128)(2,1)S(1)}, bf16[4,128,128]{2,1,0:T(8,128)(2,1)S(1)}, u32[]{:S(2)}, u32[]{:S(2)}) %collective-permute-start.7) | collective-permute-done | bytes 131104 | tf_op jit(solution)/shard_map/ppermute | solution.py:144
  37.7 1.7 %collective-permute-start.8 = (bf16[4,128,128]{2,1,0:T(8,128)(2,1)S(1)}, bf16[4,128,128]{2,1,0:T(8,128)(2,1)S(1)}, u32[]{:S(2)}, u32[]{:S(2)}) collective-permute-start(bf16[4,128,128]{2,1,0:T(8,128)(2,1)S(1)} %collective-permute-done.7.refs_2_), channel_id=1, source_target_pairs={{4,0},{12,4},{20,12},{28,20},{24,28},{16,24},{8,16},{0,8},{5,1},{1... | collective-permute-start | bytes 393224 | tf_op jit(solution)/shard_map/ppermute | solution.py:144
  39.4 0.7 copy-done.1
  40.0 0.2 collective-permute-done.10.refs_6_
  40.3 1.6 %collective-permute-start.11 = (bf16[4,128,128]{2,1,0:T(8,128)(2,1)S(1)}, bf16[4,128,128]{2,1,0:T(8,128)(2,1)}, u32[]{:S(2)}, u32[]{:S(2)}) collective-permute-start(bf16[4,128,128]{2,1,0:T(8,128)(2,1)S(1)} %collective-permute-done.10.refs_6_), channel_id=1, source_target_pairs={{0,4},{4,12},{12,20},{20,28},{28,24},{24,16},{16,8},{8,0},{1,5},{5... | collective-permute-start | bytes 393224 | tf_op jit(solution)/shard_map/ppermute | solution.py:141
  41.9 0.6 copy-done.3
  42.5 0.1 collective-permute-done.8.refs_3_
  42.6 0.6 copy-done.5
  43.3 2.1 %collective-permute-done.11.refs_5_ = bf16[4,128,128]{2,1,0:T(8,128)(2,1)} collective-permute-done((bf16[4,128,128]{2,1,0:T(8,128)(2,1)S(1)}, bf16[4,128,128]{2,1,0:T(8,128)(2,1)}, u32[]{:S(2)}, u32[]{:S(2)}) %collective-permute-start.11) | collective-permute-done | bytes 131104 | tf_op jit(solution)/shard_map/ppermute | solution.py:141
  45.3 1.6 %collective-permute-start.12 = (bf16[4,128,128]{2,1,0:T(8,128)(2,1)}, bf16[4,128,128]{2,1,0:T(8,128)(2,1)}, u32[]{:S(2)}, u32[]{:S(2)}) collective-permute-start(bf16[4,128,128]{2,1,0:T(8,128)(2,1)} %collective-permute-done.11.refs_5_), channel_id=1, source_target_pairs={{0,4},{4,12},{12,20},{20,28},{28,24},{24,16},{16,8},{8,0},{1,5},{5... | collective-permute-start | bytes 393224 | tf_op jit(solution)/shard_map/ppermute | solution.py:141
  47.0 0.1 stack.33
  47.1 0.1 stack.32
  47.2 0.1 stack.31
  47.3 0.1 reshape.69.index_ref
  47.4 3.3 %collective-permute-done.12.refs_4_ = bf16[4,128,128]{2,1,0:T(8,128)(2,1)} collective-permute-done((bf16[4,128,128]{2,1,0:T(8,128)(2,1)}, bf16[4,128,128]{2,1,0:T(8,128)(2,1)}, u32[]{:S(2)}, u32[]{:S(2)}) %collective-permute-start.12) | collective-permute-done | bytes 131104 | tf_op jit(solution)/shard_map/ppermute | solution.py:141
  50.6 0.9 %copy-done.2 = bf16[4,128,128]{2,1,0:T(8,128)(2,1)S(1)} copy-done((bf16[4,128,128]{2,1,0:T(8,128)(2,1)S(1)}, bf16[4,128,128]{2,1,0:T(8,128)(2,1)}, u32[]{:S(2)}) %copy-start.2) | copy-done | bytes 131096
  51.5 0.9 %copy-done.4 = bf16[4,128,128]{2,1,0:T(8,128)(2,1)S(1)} copy-done((bf16[4,128,128]{2,1,0:T(8,128)(2,1)S(1)}, bf16[4,128,128]{2,1,0:T(8,128)(2,1)}, u32[]{:S(2)}) %copy-start.4) | copy-done | bytes 131096
  52.5 0.9 %copy-done.6 = bf16[4,128,128]{2,1,0:T(8,128)(2,1)S(1)} copy-done((bf16[4,128,128]{2,1,0:T(8,128)(2,1)S(1)}, bf16[4,128,128]{2,1,0:T(8,128)(2,1)}, u32[]{:S(2)}) %copy-start.6) | copy-done | bytes 131096
  53.4 2.9 %shard_map.57 = (bf16[4,128,128]{2,1,0:T(8,128)(2,1)S(1)}, bf16[128,128]{1,0:T(8,128)(2,1)S(1)}, bf16[128,128]{1,0:T(8,128)(2,1)S(1)}, bf16[128,128]{1,0:T(8,128)(2,1)S(1)}, bf16[128,128]{1,0:T(8,128)(2,1)S(1)}) custom-call(s32[1]{0:T(128)} %bitcast.me_ref, s32[160]{0:T(256)S(1)} %reshape.69.index_ref, bf16[4,128,128]{2,1,0:T(8,128)(2,1)S(1)} %pad_maximum_fusion.refs_0_, ...), custom_call_target="tpu_custom_call" | custom-call | tf_op jit(solution)/shard_map/pallas_call | solution.py:204
  56.3 1.7 %collective-permute-start.22 = (bf16[4,128,128]{2,1,0:T(8,128)(2,1)S(1)}, bf16[4,128,128]{2,1,0:T(8,128)(2,1)S(1)}, u32[]{:S(2)}, u32[]{:S(2)}) collective-permute-start(bf16[4,128,128]{2,1,0:T(8,128)(2,1)S(1)} %get-tuple-element.48.refs_8_), channel_id=1, source_target_pairs={{0,4},{4,12},{12,20},{20,28},{28,24},{24,16},{16,8},{8,0},{1,5},{5... | collective-permute-start | bytes 393224 | tf_op jit(solution)/shard_map/ppermute | solution.py:141
  57.9 0.4 collective-permute-start.19
  58.4 4.2 %collective-permute-done.22.refs_15_ = bf16[4,128,128]{2,1,0:T(8,128)(2,1)S(1)} collective-permute-done((bf16[4,128,128]{2,1,0:T(8,128)(2,1)S(1)}, bf16[4,128,128]{2,1,0:T(8,128)(2,1)S(1)}, u32[]{:S(2)}, u32[]{:S(2)}) %collective-permute-start.22) | collective-permute-done | bytes 131104 | tf_op jit(solution)/shard_map/ppermute | solution.py:141
  62.5 1.6 %collective-permute-start.23 = (bf16[4,128,128]{2,1,0:T(8,128)(2,1)S(1)}, bf16[4,128,128]{2,1,0:T(8,128)(2,1)S(1)}, u32[]{:S(2)}, u32[]{:S(2)}) collective-permute-start(bf16[4,128,128]{2,1,0:T(8,128)(2,1)S(1)} %collective-permute-done.22.refs_15_), channel_id=1, source_target_pairs={{0,4},{4,12},{12,20},{20,28},{28,24},{24,16},{16,8},{8,0},{1,5},{5... | collective-permute-start | bytes 393224 | tf_op jit(solution)/shard_map/ppermute | solution.py:141
  64.2 0.0 collective-permute-done.19.refs_9_
  64.2 0.4 collective-permute-start.20
  64.6 3.6 %collective-permute-done.23.refs_14_ = bf16[4,128,128]{2,1,0:T(8,128)(2,1)S(1)} collective-permute-done((bf16[4,128,128]{2,1,0:T(8,128)(2,1)S(1)}, bf16[4,128,128]{2,1,0:T(8,128)(2,1)S(1)}, u32[]{:S(2)}, u32[]{:S(2)}) %collective-permute-start.23) | collective-permute-done | bytes 131104 | tf_op jit(solution)/shard_map/ppermute | solution.py:141
  68.2 1.6 %collective-permute-start.24 = (bf16[4,128,128]{2,1,0:T(8,128)(2,1)S(1)}, bf16[4,128,128]{2,1,0:T(8,128)(2,1)S(1)}, u32[]{:S(2)}, u32[]{:S(2)}) collective-permute-start(bf16[4,128,128]{2,1,0:T(8,128)(2,1)S(1)} %collective-permute-done.23.refs_14_), channel_id=1, source_target_pairs={{0,4},{4,12},{12,20},{20,28},{28,24},{24,16},{16,8},{8,0},{1,5},{5... | collective-permute-start | bytes 393224 | tf_op jit(solution)/shard_map/ppermute | solution.py:141
  69.8 0.4 collective-permute-start.21
  70.2 2.9 %collective-permute-done.24.refs_13_ = bf16[4,128,128]{2,1,0:T(8,128)(2,1)S(1)} collective-permute-done((bf16[4,128,128]{2,1,0:T(8,128)(2,1)S(1)}, bf16[4,128,128]{2,1,0:T(8,128)(2,1)S(1)}, u32[]{:S(2)}, u32[]{:S(2)}) %collective-permute-start.24) | collective-permute-done | bytes 131104 | tf_op jit(solution)/shard_map/ppermute | solution.py:141
  73.2 1.6 %collective-permute-start.25 = (bf16[4,128,128]{2,1,0:T(8,128)(2,1)S(1)}, bf16[4,128,128]{2,1,0:T(8,128)(2,1)S(1)}, u32[]{:S(2)}, u32[]{:S(2)}) collective-permute-start(bf16[4,128,128]{2,1,0:T(8,128)(2,1)S(1)} %collective-permute-done.24.refs_13_), channel_id=1, source_target_pairs={{0,4},{4,12},{12,20},{20,28},{28,24},{24,16},{16,8},{8,0},{1,5},{5... | collective-permute-start | bytes 393224 | tf_op jit(solution)/shard_map/ppermute | solution.py:141
  74.8 1.5 %collective-permute-start.17 = (bf16[128,128]{1,0:T(8,128)(2,1)S(1)}, bf16[128,128]{1,0:T(8,128)(2,1)S(1)}, u32[]{:S(2)}, u32[]{:S(2)}) collective-permute-start(bf16[128,128]{1,0:T(8,128)(2,1)S(1)} %get-tuple-element.46), channel_id=1, source_target_pairs={{0,2},{1,3},{2,0},{3,1},{4,6},{5,7},{6,4},{7,5},{8,10},{9,11},{10,... | collective-permute-start | bytes 98312 | tf_op jit(solution)/shard_map/ppermute | solution.py:131
  76.4 0.3 collective-permute-start.18
  76.7 1.5 %collective-permute-done.25.refs_12_ = bf16[4,128,128]{2,1,0:T(8,128)(2,1)S(1)} collective-permute-done((bf16[4,128,128]{2,1,0:T(8,128)(2,1)S(1)}, bf16[4,128,128]{2,1,0:T(8,128)(2,1)S(1)}, u32[]{:S(2)}, u32[]{:S(2)}) %collective-permute-start.25) | collective-permute-done | bytes 131104 | tf_op jit(solution)/shard_map/ppermute | solution.py:141
  78.2 3.6 %shard_map.58 = (bf16[4,128,128]{2,1,0:T(8,128)(2,1)}, bf16[128,128]{1,0:T(8,128)(2,1)S(1)}, bf16[128,128]{1,0:T(8,128)(2,1)S(1)}, bf16[128,128]{1,0:T(8,128)(2,1)S(1)}, bf16[128,128]{1,0:T(8,128)(2,1)S(1)}) custom-call(s32[1]{0:T(128)} %bitcast.me_ref, s32[160]{0:T(256)S(1)} %reshape.69.index_ref, bf16[4,128,128]{2,1,0:T(8,128)(2,1)S(1)} %pad_maximum_fusion.refs_0_, ...), custom_call_target="tpu_custom_call" | custom-call | tf_op jit(solution)/shard_map/pallas_call | solution.py:204
  81.8 1.7 %collective-permute-start.30 = (bf16[128,128]{1,0:T(8,128)(2,1)S(1)}, bf16[128,128]{1,0:T(8,128)(2,1)S(1)}, u32[]{:S(2)}, u32[]{:S(2)}) collective-permute-start(bf16[128,128]{1,0:T(8,128)(2,1)S(1)} %get-tuple-element.51), channel_id=1, source_target_pairs={{0,2},{1,3},{2,0},{3,1},{4,6},{5,7},{6,4},{7,5},{8,10},{9,11},{10,... | collective-permute-start | bytes 98312 | tf_op jit(solution)/shard_map/ppermute | solution.py:131
  83.5 0.2 collective-permute-start.31
  83.7 2.0 %collective-permute-done.30.refs_6_ = bf16[128,128]{1,0:T(8,128)(2,1)S(1)} collective-permute-done((bf16[128,128]{1,0:T(8,128)(2,1)S(1)}, bf16[128,128]{1,0:T(8,128)(2,1)S(1)}, u32[]{:S(2)}, u32[]{:S(2)}) %collective-permute-start.30) | collective-permute-done | bytes 32800 | tf_op jit(solution)/shard_map/ppermute | solution.py:131
  85.7 1.1 %collective-permute-done.31.refs_7_ = bf16[128,128]{1,0:T(8,128)(2,1)S(1)} collective-permute-done((bf16[128,128]{1,0:T(8,128)(2,1)S(1)}, bf16[128,128]{1,0:T(8,128)(2,1)S(1)}, u32[]{:S(2)}, u32[]{:S(2)}) %collective-permute-start.31) | collective-permute-done | bytes 32800 | tf_op jit(solution)/shard_map/ppermute | solution.py:131
  86.8 0.8 shard_map.59
  (55 shorter events, 0.2 us)
Async XLA Ops:
  1.9 4.7 %copy-start.9 = (bf16[128,512]{1,0:T(8,128)(2,1)}, bf16[128,512]{1,0:T(8,128)(2,1)S(1)}, u32[]{:S(2)}) copy-start(bf16[128,512]{1,0:T(8,128)(2,1)S(1)} %get-tuple-element.35.full_ref) | copy-start | bytes 393220
  1.9 7.6 %collective-permute-start.5 = (bf16[128,128]{1,0:T(8,128)(2,1)S(1)}, bf16[128,128]{1,0:T(8,128)(2,1)S(1)}, u32[]{:S(2)}, u32[]{:S(2)}) collective-permute-start(bf16[128,128]{1,0:T(8,128)(2,1)S(1)} %get-tuple-element.43), channel_id=1, source_target_pairs={{0,3},{1,2},{2,1},{3,0},{4,7},{5,6},{6,5},{7,4},{8,11},{9,10},{10,... | collective-permute-start | bytes 98312 | tf_op jit(solution)/shard_map/ppermute | solution.py:131
  4.4 6.5 %collective-permute-start.4 = (bf16[128,128]{1,0:T(8,128)(2,1)S(1)}, bf16[128,128]{1,0:T(8,128)(2,1)S(1)}, u32[]{:S(2)}, u32[]{:S(2)}) collective-permute-start(bf16[128,128]{1,0:T(8,128)(2,1)S(1)} %get-tuple-element.42), channel_id=1, source_target_pairs={{0,2},{1,3},{2,0},{3,1},{4,6},{5,7},{6,4},{7,5},{8,10},{9,11},{10,... | collective-permute-start | bytes 98312 | tf_op jit(solution)/shard_map/ppermute | solution.py:131
  5.0 3.3 %copy-start.12 = (s32[2,1,1,4]{3,2,1,0:T(1,128)S(1)}, s32[2,1,1,4]{3,2,1,0:T(1,128)}, u32[]{:S(2)}) copy-start(s32[2,1,1,4]{3,2,1,0:T(1,128)} %param.11) | copy-start | bytes 100
  5.0 3.5 %copy-start.11 = (s32[2,1,1,4,5]{4,3,2,1,0:T(4,128)S(1)}, s32[2,1,1,4,5]{4,3,2,1,0:T(4,128)}, u32[]{:S(2)}) copy-start(s32[2,1,1,4,5]{4,3,2,1,0:T(4,128)} %param.10) | copy-start | bytes 484
  5.0 3.6 %copy-start = (bf16[3,1,1,128,512]{4,3,2,1,0:T(8,128)(2,1)S(1)}, bf16[3,1,1,128,512]{4,3,2,1,0:T(8,128)(2,1)}, u32[]{:S(2)}) copy-start(bf16[3,1,1,128,512]{4,3,2,1,0:T(8,128)(2,1)} %param.7) | copy-start | bytes 1179652
  5.0 3.6 %copy-start.8 = (bf16[3,1,1,128,128]{4,3,2,1,0:T(8,128)(2,1)S(1)}, bf16[3,1,1,128,128]{4,3,2,1,0:T(8,128)(2,1)}, u32[]{:S(2)}) copy-start(bf16[3,1,1,128,128]{4,3,2,1,0:T(8,128)(2,1)} %param.8) | copy-start | bytes 294916
  5.0 6.2 %collective-permute-start.3 = (bf16[128,128]{1,0:T(8,128)(2,1)S(1)}, bf16[128,128]{1,0:T(8,128)(2,1)S(1)}, u32[]{:S(2)}, u32[]{:S(2)}) collective-permute-start(bf16[128,128]{1,0:T(8,128)(2,1)S(1)} %get-tuple-element.41), channel_id=1, source_target_pairs={{0,1},{1,0},{2,3},{3,2},{4,5},{5,4},{6,7},{7,6},{8,9},{9,8},{10,11... | collective-permute-start | bytes 98312 | tf_op jit(solution)/shard_map/ppermute | solution.py:131
  6.6 30.1 %collective-permute-start.14 = (bf16[4,5,128,128]{3,2,1,0:T(8,128)(2,1)S(1)}, bf16[4,5,128,128]{3,2,1,0:T(8,128)(2,1)S(1)}, u32[]{:S(2)}, u32[]{:S(2)}) collective-permute-start(bf16[4,5,128,128]{3,2,1,0:T(8,128)(2,1)S(1)} %get-tuple-element.54.refs_8_), channel_id=1, source_target_pairs={{0,2},{1,3},{2,0},{3,1},{4,6},{5,7},{6,4},{7,5},{8,10},{9,11},{10,... | collective-permute-start | bytes 1966088 | tf_op jit(solution)/shard_map/ppermute | solution.py:196
  9.4 16.9 %collective-permute-start.2 = (bf16[528,128]{1,0:T(8,128)(2,1)S(1)}, bf16[528,128]{1,0:T(8,128)(2,1)S(1)}, u32[]{:S(2)}, u32[]{:S(2)}) collective-permute-start(bf16[528,128]{1,0:T(8,128)(2,1)S(1)} %get-tuple-element.39), channel_id=1, source_target_pairs={{0,3},{1,2},{2,1},{3,0},{4,7},{5,6},{6,5},{7,4},{8,11},{9,10},{10,... | collective-permute-start | bytes 405512 | tf_op jit(solution)/shard_map/ppermute | solution.py:131
  9.5 20.6 %collective-permute-start.1 = (bf16[528,128]{1,0:T(8,128)(2,1)S(1)}, bf16[528,128]{1,0:T(8,128)(2,1)S(1)}, u32[]{:S(2)}, u32[]{:S(2)}) collective-permute-start(bf16[528,128]{1,0:T(8,128)(2,1)S(1)} %get-tuple-element.38), channel_id=1, source_target_pairs={{0,2},{1,3},{2,0},{3,1},{4,6},{5,7},{6,4},{7,5},{8,10},{9,11},{10,... | collective-permute-start | bytes 405512 | tf_op jit(solution)/shard_map/ppermute | solution.py:131
  10.9 20.9 %collective-permute-start = (bf16[528,128]{1,0:T(8,128)(2,1)}, bf16[528,128]{1,0:T(8,128)(2,1)S(1)}, u32[]{:S(2)}, u32[]{:S(2)}) collective-permute-start(bf16[528,128]{1,0:T(8,128)(2,1)} %get-tuple-element.37), channel_id=1, source_target_pairs={{0,1},{1,0},{2,3},{3,2},{4,5},{5,4},{6,7},{7,6},{8,9},{9,8},{10,11... | collective-permute-start | bytes 405512 | tf_op jit(solution)/shard_map/ppermute | solution.py:131
  11.3 35.7 %collective-permute-start.27 = (bf16[4,5,128,128]{3,2,1,0:T(8,128)(2,1)S(1)}, bf16[4,5,128,128]{3,2,1,0:T(8,128)(2,1)S(1)}, u32[]{:S(2)}, u32[]{:S(2)}) collective-permute-start(bf16[4,5,128,128]{3,2,1,0:T(8,128)(2,1)S(1)} %get-tuple-element.53.refs_16_), channel_id=1, source_target_pairs={{0,2},{1,3},{2,0},{3,1},{4,6},{5,7},{6,4},{7,5},{8,10},{9,11},{10,... | collective-permute-start | bytes 1966088 | tf_op jit(solution)/shard_map/ppermute | solution.py:196
  26.3 6.0 %collective-permute-start.6 = (bf16[4,128,128]{2,1,0:T(8,128)(2,1)S(1)}, bf16[4,128,128]{2,1,0:T(8,128)(2,1)S(1)}, u32[]{:S(2)}, u32[]{:S(2)}) collective-permute-start(bf16[4,128,128]{2,1,0:T(8,128)(2,1)S(1)} %pad_maximum_fusion.refs_0_), channel_id=1, source_target_pairs={{4,0},{12,4},{20,12},{28,20},{24,28},{16,24},{8,16},{0,8},{5,1},{1... | collective-permute-start | bytes 393224 | tf_op jit(solution)/shard_map/ppermute | solution.py:144
  30.0 5.1 %collective-permute-start.9 = (bf16[4,128,128]{2,1,0:T(8,128)(2,1)S(1)}, bf16[4,128,128]{2,1,0:T(8,128)(2,1)}, u32[]{:S(2)}, u32[]{:S(2)}) collective-permute-start(bf16[4,128,128]{2,1,0:T(8,128)(2,1)S(1)} %pad_maximum_fusion.refs_0_), channel_id=1, source_target_pairs={{0,4},{4,12},{12,20},{20,28},{28,24},{24,16},{16,8},{8,0},{1,5},{5... | collective-permute-start | bytes 393224 | tf_op jit(solution)/shard_map/ppermute | solution.py:141
  31.7 18.9 %collective-permute-start.13 = (bf16[4,5,128,128]{3,2,1,0:T(8,128)(2,1)S(1)}, bf16[4,5,128,128]{3,2,1,0:T(8,128)(2,1)}, u32[]{:S(2)}, u32[]{:S(2)}) collective-permute-start(bf16[4,5,128,128]{3,2,1,0:T(8,128)(2,1)S(1)} %get-tuple-element.54.refs_8_), channel_id=1, source_target_pairs={{0,1},{1,0},{2,3},{3,2},{4,5},{5,4},{6,7},{7,6},{8,9},{9,8},{10,11... | collective-permute-start | bytes 1966088 | tf_op jit(solution)/shard_map/ppermute | solution.py:196
  32.3 5.3 %collective-permute-start.7 = (bf16[4,128,128]{2,1,0:T(8,128)(2,1)S(1)}, bf16[4,128,128]{2,1,0:T(8,128)(2,1)S(1)}, u32[]{:S(2)}, u32[]{:S(2)}) collective-permute-start(bf16[4,128,128]{2,1,0:T(8,128)(2,1)S(1)} %collective-permute-done.6.refs_1_), channel_id=1, source_target_pairs={{4,0},{12,4},{20,12},{28,20},{24,28},{16,24},{8,16},{0,8},{5,1},{1... | collective-permute-start | bytes 393224 | tf_op jit(solution)/shard_map/ppermute | solution.py:144
  35.1 5.2 %collective-permute-start.10 = (bf16[4,128,128]{2,1,0:T(8,128)(2,1)}, bf16[4,128,128]{2,1,0:T(8,128)(2,1)S(1)}, u32[]{:S(2)}, u32[]{:S(2)}) collective-permute-start(bf16[4,128,128]{2,1,0:T(8,128)(2,1)} %collective-permute-done.9.refs_7_), channel_id=1, source_target_pairs={{0,4},{4,12},{12,20},{20,28},{28,24},{24,16},{16,8},{8,0},{1,5},{5... | collective-permute-start | bytes 393224 | tf_op jit(solution)/shard_map/ppermute | solution.py:141
  36.7 13.9 %collective-permute-start.15 = (bf16[4,5,128,128]{3,2,1,0:T(8,128)(2,1)S(1)}, bf16[4,5,128,128]{3,2,1,0:T(8,128)(2,1)}, u32[]{:S(2)}, u32[]{:S(2)}) collective-permute-start(bf16[4,5,128,128]{3,2,1,0:T(8,128)(2,1)S(1)} %collective-permute-done.14.refs_10_), channel_id=1, source_target_pairs={{0,1},{1,0},{2,3},{3,2},{4,5},{5,4},{6,7},{7,6},{8,9},{9,8},{10,11... | collective-permute-start | bytes 1966088 | tf_op jit(solution)/shard_map/ppermute | solution.py:196
  37.7 5.0 %collective-permute-start.8 = (bf16[4,128,128]{2,1,0:T(8,128)(2,1)S(1)}, bf16[4,128,128]{2,1,0:T(8,128)(2,1)S(1)}, u32[]{:S(2)}, u32[]{:S(2)}) collective-permute-start(bf16[4,128,128]{2,1,0:T(8,128)(2,1)S(1)} %collective-permute-done.7.refs_2_), channel_id=1, source_target_pairs={{4,0},{12,4},{20,12},{28,20},{24,28},{16,24},{8,16},{0,8},{5,1},{1... | collective-permute-start | bytes 393224 | tf_op jit(solution)/shard_map/ppermute | solution.py:144
  39.4 0.7 copy-start.1
  40.3 5.1 %collective-permute-start.11 = (bf16[4,128,128]{2,1,0:T(8,128)(2,1)S(1)}, bf16[4,128,128]{2,1,0:T(8,128)(2,1)}, u32[]{:S(2)}, u32[]{:S(2)}) collective-permute-start(bf16[4,128,128]{2,1,0:T(8,128)(2,1)S(1)} %collective-permute-done.10.refs_6_), channel_id=1, source_target_pairs={{0,4},{4,12},{12,20},{20,28},{28,24},{24,16},{16,8},{8,0},{1,5},{5... | collective-permute-start | bytes 393224 | tf_op jit(solution)/shard_map/ppermute | solution.py:141
  41.9 0.6 copy-start.3
  42.6 0.6 copy-start.5
  43.3 31.5 %collective-permute-start.26 = (bf16[4,5,128,128]{3,2,1,0:T(8,128)(2,1)S(1)}, bf16[4,5,128,128]{3,2,1,0:T(8,128)(2,1)}, u32[]{:S(2)}, u32[]{:S(2)}) collective-permute-start(bf16[4,5,128,128]{3,2,1,0:T(8,128)(2,1)S(1)} %get-tuple-element.53.refs_16_), channel_id=1, source_target_pairs={{0,1},{1,0},{2,3},{3,2},{4,5},{5,4},{6,7},{7,6},{8,9},{9,8},{10,11... | collective-permute-start | bytes 1966088 | tf_op jit(solution)/shard_map/ppermute | solution.py:196
  45.3 5.3 %collective-permute-start.12 = (bf16[4,128,128]{2,1,0:T(8,128)(2,1)}, bf16[4,128,128]{2,1,0:T(8,128)(2,1)}, u32[]{:S(2)}, u32[]{:S(2)}) collective-permute-start(bf16[4,128,128]{2,1,0:T(8,128)(2,1)} %collective-permute-done.11.refs_5_), channel_id=1, source_target_pairs={{0,4},{4,12},{12,20},{20,28},{28,24},{24,16},{16,8},{8,0},{1,5},{5... | collective-permute-start | bytes 393224 | tf_op jit(solution)/shard_map/ppermute | solution.py:141
  47.0 29.4 %collective-permute-start.28 = (bf16[4,5,128,128]{3,2,1,0:T(8,128)(2,1)S(1)}, bf16[4,5,128,128]{3,2,1,0:T(8,128)(2,1)}, u32[]{:S(2)}, u32[]{:S(2)}) collective-permute-start(bf16[4,5,128,128]{3,2,1,0:T(8,128)(2,1)S(1)} %collective-permute-done.27.refs_18_), channel_id=1, source_target_pairs={{0,1},{1,0},{2,3},{3,2},{4,5},{5,4},{6,7},{7,6},{8,9},{9,8},{10,11... | collective-permute-start | bytes 1966088 | tf_op jit(solution)/shard_map/ppermute | solution.py:196
  50.6 0.9 %copy-start.2 = (bf16[4,128,128]{2,1,0:T(8,128)(2,1)S(1)}, bf16[4,128,128]{2,1,0:T(8,128)(2,1)}, u32[]{:S(2)}) copy-start(bf16[4,128,128]{2,1,0:T(8,128)(2,1)} %copy-done.1) | copy-start | bytes 393220
  51.5 0.9 %copy-start.4 = (bf16[4,128,128]{2,1,0:T(8,128)(2,1)S(1)}, bf16[4,128,128]{2,1,0:T(8,128)(2,1)}, u32[]{:S(2)}) copy-start(bf16[4,128,128]{2,1,0:T(8,128)(2,1)} %copy-done.3) | copy-start | bytes 393220
  52.5 0.9 %copy-start.6 = (bf16[4,128,128]{2,1,0:T(8,128)(2,1)S(1)}, bf16[4,128,128]{2,1,0:T(8,128)(2,1)}, u32[]{:S(2)}) copy-start(bf16[4,128,128]{2,1,0:T(8,128)(2,1)} %copy-done.5) | copy-start | bytes 393220
  53.4 24.8 %copy-start.7 = (bf16[4,128,128]{2,1,0:T(8,128)(2,1)S(1)}, bf16[4,128,128]{2,1,0:T(8,128)(2,1)}, u32[]{:S(2)}) copy-start(bf16[4,128,128]{2,1,0:T(8,128)(2,1)} %copy-done.5) | copy-start | bytes 393220
  56.3 6.3 %collective-permute-start.22 = (bf16[4,128,128]{2,1,0:T(8,128)(2,1)S(1)}, bf16[4,128,128]{2,1,0:T(8,128)(2,1)S(1)}, u32[]{:S(2)}, u32[]{:S(2)}) collective-permute-start(bf16[4,128,128]{2,1,0:T(8,128)(2,1)S(1)} %get-tuple-element.48.refs_8_), channel_id=1, source_target_pairs={{0,4},{4,12},{12,20},{20,28},{28,24},{24,16},{16,8},{8,0},{1,5},{5... | collective-permute-start | bytes 393224 | tf_op jit(solution)/shard_map/ppermute | solution.py:141
  57.9 6.2 %collective-permute-start.19 = (bf16[4,128,128]{2,1,0:T(8,128)(2,1)S(1)}, bf16[4,128,128]{2,1,0:T(8,128)(2,1)S(1)}, u32[]{:S(2)}, u32[]{:S(2)}) collective-permute-start(bf16[4,128,128]{2,1,0:T(8,128)(2,1)S(1)} %get-tuple-element.48.refs_8_), channel_id=1, source_target_pairs={{4,0},{12,4},{20,12},{28,20},{24,28},{16,24},{8,16},{0,8},{5,1},{1... | collective-permute-start | bytes 393224 | tf_op jit(solution)/shard_map/ppermute | solution.py:144
  62.5 5.7 %collective-permute-start.23 = (bf16[4,128,128]{2,1,0:T(8,128)(2,1)S(1)}, bf16[4,128,128]{2,1,0:T(8,128)(2,1)S(1)}, u32[]{:S(2)}, u32[]{:S(2)}) collective-permute-start(bf16[4,128,128]{2,1,0:T(8,128)(2,1)S(1)} %collective-permute-done.22.refs_15_), channel_id=1, source_target_pairs={{0,4},{4,12},{12,20},{20,28},{28,24},{24,16},{16,8},{8,0},{1,5},{5... | collective-permute-start | bytes 393224 | tf_op jit(solution)/shard_map/ppermute | solution.py:141
  64.2 5.6 %collective-permute-start.20 = (bf16[4,128,128]{2,1,0:T(8,128)(2,1)S(1)}, bf16[4,128,128]{2,1,0:T(8,128)(2,1)S(1)}, u32[]{:S(2)}, u32[]{:S(2)}) collective-permute-start(bf16[4,128,128]{2,1,0:T(8,128)(2,1)S(1)} %collective-permute-done.19.refs_9_), channel_id=1, source_target_pairs={{4,0},{12,4},{20,12},{28,20},{24,28},{16,24},{8,16},{0,8},{5,1},{1... | collective-permute-start | bytes 393224 | tf_op jit(solution)/shard_map/ppermute | solution.py:144
  68.2 5.0 %collective-permute-start.24 = (bf16[4,128,128]{2,1,0:T(8,128)(2,1)S(1)}, bf16[4,128,128]{2,1,0:T(8,128)(2,1)S(1)}, u32[]{:S(2)}, u32[]{:S(2)}) collective-permute-start(bf16[4,128,128]{2,1,0:T(8,128)(2,1)S(1)} %collective-permute-done.23.refs_14_), channel_id=1, source_target_pairs={{0,4},{4,12},{12,20},{20,28},{28,24},{24,16},{16,8},{8,0},{1,5},{5... | collective-permute-start | bytes 393224 | tf_op jit(solution)/shard_map/ppermute | solution.py:141
  69.8 6.8 %collective-permute-start.21 = (bf16[4,128,128]{2,1,0:T(8,128)(2,1)S(1)}, bf16[4,128,128]{2,1,0:T(8,128)(2,1)S(1)}, u32[]{:S(2)}, u32[]{:S(2)}) collective-permute-start(bf16[4,128,128]{2,1,0:T(8,128)(2,1)S(1)} %collective-permute-done.20.refs_10_), channel_id=1, source_target_pairs={{4,0},{12,4},{20,12},{28,20},{24,28},{16,24},{8,16},{0,8},{5,1},{1... | collective-permute-start | bytes 393224 | tf_op jit(solution)/shard_map/ppermute | solution.py:144
  73.2 5.0 %collective-permute-start.25 = (bf16[4,128,128]{2,1,0:T(8,128)(2,1)S(1)}, bf16[4,128,128]{2,1,0:T(8,128)(2,1)S(1)}, u32[]{:S(2)}, u32[]{:S(2)}) collective-permute-start(bf16[4,128,128]{2,1,0:T(8,128)(2,1)S(1)} %collective-permute-done.24.refs_13_), channel_id=1, source_target_pairs={{0,4},{4,12},{12,20},{20,28},{28,24},{24,16},{16,8},{8,0},{1,5},{5... | collective-permute-start | bytes 393224 | tf_op jit(solution)/shard_map/ppermute | solution.py:141
  74.8 8.7 %collective-permute-start.16 = (bf16[128,128]{1,0:T(8,128)(2,1)S(1)}, bf16[128,128]{1,0:T(8,128)(2,1)S(1)}, u32[]{:S(2)}, u32[]{:S(2)}) collective-permute-start(bf16[128,128]{1,0:T(8,128)(2,1)S(1)} %get-tuple-element.45), channel_id=1, source_target_pairs={{0,1},{1,0},{2,3},{3,2},{4,5},{5,4},{6,7},{7,6},{8,9},{9,8},{10,11... | collective-permute-start | bytes 98312 | tf_op jit(solution)/shard_map/ppermute | solution.py:131
  74.8 8.8 %collective-permute-start.17 = (bf16[128,128]{1,0:T(8,128)(2,1)S(1)}, bf16[128,128]{1,0:T(8,128)(2,1)S(1)}, u32[]{:S(2)}, u32[]{:S(2)}) collective-permute-start(bf16[128,128]{1,0:T(8,128)(2,1)S(1)} %get-tuple-element.46), channel_id=1, source_target_pairs={{0,2},{1,3},{2,0},{3,1},{4,6},{5,7},{6,4},{7,5},{8,10},{9,11},{10,... | collective-permute-start | bytes 98312 | tf_op jit(solution)/shard_map/ppermute | solution.py:131
  76.4 10.5 %copy-start.10 = (bf16[128,512]{1,0:T(8,128)(2,1)S(1)}, bf16[128,512]{1,0:T(8,128)(2,1)}, u32[]{:S(2)}) copy-start(bf16[128,512]{1,0:T(8,128)(2,1)} %copy-done.9) | copy-start | bytes 393220
  76.4 7.3 %collective-permute-start.18 = (bf16[128,128]{1,0:T(8,128)(2,1)S(1)}, bf16[128,128]{1,0:T(8,128)(2,1)S(1)}, u32[]{:S(2)}, u32[]{:S(2)}) collective-permute-start(bf16[128,128]{1,0:T(8,128)(2,1)S(1)} %get-tuple-element.47), channel_id=1, source_target_pairs={{0,3},{1,2},{2,1},{3,0},{4,7},{5,6},{6,5},{7,4},{8,11},{9,10},{10,... | collective-permute-start | bytes 98312 | tf_op jit(solution)/shard_map/ppermute | solution.py:131
  81.8 1.9 %collective-permute-start.29 = (bf16[128,128]{1,0:T(8,128)(2,1)S(1)}, bf16[128,128]{1,0:T(8,128)(2,1)S(1)}, u32[]{:S(2)}, u32[]{:S(2)}) collective-permute-start(bf16[128,128]{1,0:T(8,128)(2,1)S(1)} %get-tuple-element.50), channel_id=1, source_target_pairs={{0,1},{1,0},{2,3},{3,2},{4,5},{5,4},{6,7},{7,6},{8,9},{9,8},{10,11... | collective-permute-start | bytes 98312 | tf_op jit(solution)/shard_map/ppermute | solution.py:131
  81.8 3.9 %collective-permute-start.30 = (bf16[128,128]{1,0:T(8,128)(2,1)S(1)}, bf16[128,128]{1,0:T(8,128)(2,1)S(1)}, u32[]{:S(2)}, u32[]{:S(2)}) collective-permute-start(bf16[128,128]{1,0:T(8,128)(2,1)S(1)} %get-tuple-element.51), channel_id=1, source_target_pairs={{0,2},{1,3},{2,0},{3,1},{4,6},{5,7},{6,4},{7,5},{8,10},{9,11},{10,... | collective-permute-start | bytes 98312 | tf_op jit(solution)/shard_map/ppermute | solution.py:131
  83.5 3.3 %collective-permute-start.31 = (bf16[128,128]{1,0:T(8,128)(2,1)S(1)}, bf16[128,128]{1,0:T(8,128)(2,1)S(1)}, u32[]{:S(2)}, u32[]{:S(2)}) collective-permute-start(bf16[128,128]{1,0:T(8,128)(2,1)S(1)} %get-tuple-element.52), channel_id=1, source_target_pairs={{0,3},{1,2},{2,1},{3,0},{4,7},{5,6},{6,5},{7,4},{8,11},{9,10},{10,... | collective-permute-start | bytes 98312 | tf_op jit(solution)/shard_map/ppermute | solution.py:131

commit v2 on v0

v2 whole, which is shorter than its diff:
```python
import functools

import jax
import jax.numpy as jnp
from jax import lax
from jax.experimental import pallas as pl
from jax.experimental.pallas import tpu as pltpu
from jax.sharding import PartitionSpec as P

LANES = 128
PAIR = 2
BLOCK_BYTES = 4 * 2**20
VMEM_BYTES = 16 * 2**20


def vmem():
    return pl.BlockSpec(memory_space=pltpu.VMEM)


def smem():
    return pl.BlockSpec(memory_space=pltpu.SMEM)


def anywhere():
    return pl.BlockSpec(memory_space=pl.ANY)


def in_hbm(value):
    return pltpu.with_memory_space_constraint(value, pltpu.HBM)


def struct(shape, dtype=jnp.bfloat16):
    return jax.ShapeDtypeStruct(shape, dtype)


def near(shape, dtype=jnp.bfloat16):
    return pltpu.VMEM(shape, dtype)


def params():
    return pltpu.CompilerParams(vmem_limit_bytes=VMEM_BYTES)


def solve_scattered(b_panels, diag_inverse, l_blocks, block_cols, live_counts):
    proc_rows = lax.axis_size("prow")
    proc_cols = lax.axis_size("pcol")
    per_level = proc_rows * proc_cols
    right_cols = b_panels[:, 0, 0]
    levels, block_size, front_width = right_cols.shape
    slot_count = l_blocks.shape[4]
    solved_cols = jnp.zeros((levels * proc_rows, block_size, front_width), jnp.bfloat16)
    solutions = []
    for level in range(levels):
        right_part = right_cols[level].astype(jnp.float32)
        if level > 0:
            chosen = block_cols[level - 1, 0, 0]
            active = live_counts[level - 1, 0, 0]
            local_index = chosen // per_level * proc_rows + chosen % per_level // proc_cols
            live = jnp.arange(slot_count)[None, :] < active[:, None]
            masked = jnp.where(live[:, :, None, None], l_blocks[level - 1, 0, 0], jnp.zeros((), jnp.bfloat16))
            partial = jnp.einsum(
                "jkab,jkbr->jar", masked, solved_cols[local_index], preferred_element_type=jnp.float32
            ).astype(jnp.bfloat16)
            row_total = lax.psum_scatter(partial, "pcol", scatter_dimension=0, tiled=True)
            right_part = right_part - row_total[0].astype(jnp.float32)
        resid = right_part.astype(jnp.bfloat16)
        solved = jnp.dot(diag_inverse[level, 0, 0], resid, preferred_element_type=jnp.float32).astype(jnp.bfloat16)
        solutions.append(solved)
        if level + 1 < levels:
            segment = lax.all_gather(solved[None], "prow", axis=0, tiled=True)
            solved_cols = lax.dynamic_update_slice_in_dim(solved_cols, segment, level * proc_rows, 0)
    return jnp.stack(solutions)[:, None, None]


def first_kernel(me_ref, b_ref, d_ref, full_ref, *refs):
    piece_refs, (b_buf, d_buf, sems) = refs[:PAIR], refs[PAIR:]
    copies = [
        pltpu.make_async_copy(b_ref.at[0, 0, 0], b_buf, sems.at[0]),
        pltpu.make_async_copy(d_ref.at[0, 0, 0], d_buf, sems.at[1]),
    ]
    for copy in copies:
        copy.start()
    for copy in copies:
        copy.wait()
    width = piece_refs[0].shape[1]
    full_ref[...] = jnp.dot(d_buf[...], b_buf[...], preferred_element_type=jnp.float32).astype(jnp.bfloat16)
    for j in range(PAIR):
        piece_refs[j][...] = full_ref[:, my_columns(me_ref[0] ^ j, width)]


def my_columns(me, width):
    return pl.ds(pl.multiple_of((me & 1) * width, LANES), width)


def gather_kernel(n, level, m, early, late, me_ref, index_ref, *refs):
    l_refs, refs = refs[:PAIR], refs[PAIR:]
    old_refs, refs = refs[: level - 1], refs[level - 1 :]
    x_refs, (total_ref, chosen_ref, known, buf, sems) = refs[:-5], refs[-5:]
    copies = [pltpu.make_async_copy(l_refs[j].at[level - 1, 0, 0], buf.at[j], sems.at[j]) for j in range(PAIR)]
    for copy in copies:
        copy.start()
    me = me_ref[0]
    size, width = total_ref.shape[1:]
    slots = buf.shape[2]
    base = (level - 1) * m
    for back in range(level - 1):
        known[back * m : (back + 1) * m] = old_refs[back][...]
    for d, x_ref in zip(early, x_refs):
        known[base + d] = x_ref[...]
    none = jnp.zeros((size, width), jnp.bfloat16)
    no_block = jnp.zeros((size, size), jnp.bfloat16)
    for j in range(PAIR):
        copies[j].wait()
        for jq in range(n):
            q = me ^ jq
            blocks, solved, chosen = [], [], [no_block] * len(late)
            for k in range(slots):
                entry = index_ref[((j * index_ref.shape[0] // (PAIR * n * slots) + level - 1) * n + q) * slots + k]
                use = entry >= 0
                block = buf[j, q, k]
                for i, d in enumerate(late):
                    is_late = entry == base + d
                    use = jnp.logical_and(use, entry != base + d)
                    chosen[i] = jnp.where(is_late, block, chosen[i])
                blocks.append(block)
                solved.append(jnp.where(use, known[jnp.maximum(entry, 0), j], none))
            product = jnp.dot(
                jnp.concatenate(blocks, axis=1), jnp.concatenate(solved, axis=0), preferred_element_type=jnp.float32
            )
            total_ref[jq] = product if j == 0 else total_ref[jq] + product
            for i in range(len(late)):
                at = (i * PAIR + j) * size
                chosen_ref[jq, :, at : at + size] = chosen[i]


def late_kernel(n, m, early, late, total_ref, chosen_ref, *refs):
    x_refs, refs = refs[: len(early)], refs[len(early) :]
    halves, refs = refs[:PAIR], refs[PAIR:]
    late_refs, refs = refs[: len(late) - 1], refs[len(late) - 1 :]
    panels_ref, keep_ref, send_refs = refs[0], refs[1], refs[2:]
    panels = []
    rest = iter(late_refs)
    for d in late:
        if d == m // 2:
            found = [halves[j][...] for j in range(PAIR)]
        else:
            ref = next(rest)
            found = [ref[j] for j in range(PAIR)]
        panels += found
        for j in range(PAIR):
            panels_ref[d, j] = found[j]
    panels = jnp.concatenate(panels, axis=0)
    for jq in reversed(range(n)):
        total = total_ref[jq] + jnp.dot(chosen_ref[jq], panels, preferred_element_type=jnp.float32)
        if jq < PAIR:
            keep_ref[jq] = total
        else:
            send_refs[jq // PAIR - 1][jq % PAIR] = total.astype(jnp.bfloat16)
    for d, x_ref in zip(early, x_refs):
        panels_ref[d] = x_ref[...]


def solve_kernel(level, me_ref, keep_ref, *refs):
    b_refs, d_refs, refs = refs[:PAIR], refs[PAIR : 2 * PAIR], refs[2 * PAIR :]
    other_refs, out_ref, piece_refs = refs[: -PAIR - 1], refs[-PAIR - 1], refs[-PAIR:]
    width = keep_ref.shape[2]
    columns = my_columns(me_ref[0], width)
    for j in range(PAIR):
        total = keep_ref[j]
        for other in other_refs:
            total += other[j].astype(jnp.float32)
        resid = (b_refs[j][level, 0, 0, :, columns].astype(jnp.float32) - total).astype(jnp.bfloat16)
        value = jnp.dot(d_refs[j][level, 0, 0], resid, preferred_element_type=jnp.float32).astype(jnp.bfloat16)
        out_ref[j] = value
        piece_refs[j][...] = value


def last_kernel(me_ref, full_ref, *refs):
    out_ref, sems = refs[-2:]
    width = refs[0].shape[1]
    copies = [pltpu.make_async_copy(full_ref, out_ref.at[0, 0, 0], sems.at[0])]
    for level in range(1, out_ref.shape[0]):
        for j in range(PAIR):
            at = (level - 1) * PAIR + j
            target = out_ref.at[level, 0, 0, :, my_columns(me_ref[0] ^ j, width)]
            copies.append(pltpu.make_async_copy(refs[at], target, sems.at[1 + at]))
    for copy in copies:
        copy.start()
    for copy in copies:
        copy.wait()


def after(value, *others):
    return lax.optimization_barrier((value, others))[0]


class Ring:
    def __init__(self, value, cycle):
        m = len(cycle)
        self.to_next = [(cycle[i], cycle[(i + 1) % m]) for i in range(m)]
        self.to_last = [(b, a) for a, b in self.to_next]
        self.size, self.step = m, 0
        self.found = {0: value}
        self.behind = self.ahead = value

    def advance(self):
        self.step += 1
        final = 2 * self.step == self.size
        if final:
            self.behind, self.ahead = self.behind[0], self.ahead[1]
        self.behind = lax.ppermute(self.behind, "prow", self.to_next)
        self.ahead = lax.ppermute(self.ahead, "prow", self.to_last)
        if not final:
            self.found[self.size - self.step] = self.behind
            self.found[self.step] = self.ahead


def solve_paired(cycle, b_panels, diag_inverse, l_blocks, block_cols, live_counts):
    m = lax.axis_size("prow")
    n = lax.axis_size("pcol")
    levels, _, _, size, front = b_panels.shape
    slots = l_blocks.shape[4]
    width = front // PAIR
    place = [cycle.index(p) for p in range(m)]
    my_place = sum(jnp.where(lax.axis_index("prow") == p, place[p], 0) for p in range(m))
    me = jnp.stack([lax.axis_index("pcol"), my_place]).astype(jnp.int32)

    def send(value, bits):
        return lax.ppermute(value, "pcol", [(i, i ^ bits) for i in range(n)])

    full, *pieces = pl.pallas_call(
        first_kernel,
        out_shape=[near((size, front))] + [near((size, width))] * PAIR,
        in_specs=[smem()] + [anywhere()] * 2,
        out_specs=[vmem()] * (1 + PAIR),
        scratch_shapes=[
            pltpu.VMEM((size, front), jnp.bfloat16),
            pltpu.VMEM((size, size), jnp.bfloat16),
            pltpu.SemaphoreType.DMA((2,)),
        ],
        compiler_params=params(),
    )(me, in_hbm(b_panels), in_hbm(diag_inverse))
    solved = jnp.stack([pieces[0], send(pieces[1], 1)])

    chosen, counts = block_cols[:, 0, 0], live_counts[:, 0, 0]
    row_of = chosen % (m * n) // n
    place_of = sum(jnp.where(row_of == p, place[p], 0) for p in range(m))
    entry = chosen // (m * n) * m + (place_of - my_place + m) % m
    entry = jnp.where(jnp.arange(slots)[None, None, :] < counts[:, :, None], entry, -1).reshape(-1)
    index = jnp.concatenate([entry, send(after(entry, solved), 1)])

    b, inverse, blocks = [[v, send(after(v, solved), 1)] for v in (b_panels, diag_inverse, l_blocks)]
    late = [d for d in range(1, m) if min(d, m - d) >= m // 2 - 1]
    early = [d for d in range(m) if d not in late]
    columns, kept = [], []
    for level in range(1, levels):
        ring = Ring(solved, cycle)
        for step in range(m // 2):
            ring.advance()
        total, chosen = pl.pallas_call(
            functools.partial(gather_kernel, n, level, m, early, late),
            out_shape=[near((n, size, width), jnp.float32), near((n, size, len(late) * PAIR * size))],
            in_specs=[smem()] * 2 + [anywhere()] * PAIR + [vmem()] * (len(kept) + len(early)),
            out_specs=[vmem()] * 2,
            scratch_shapes=[
                pltpu.VMEM((level * m, PAIR, size, width), jnp.bfloat16),
                pltpu.VMEM((PAIR, n, slots, size, size), jnp.bfloat16),
                pltpu.SemaphoreType.DMA((PAIR,)),
            ],
            compiler_params=params(),
        )(me, index, *[in_hbm(v) for v in blocks], *kept, *[ring.found[d] for d in early])
        panels, keep, *away = pl.pallas_call(
            functools.partial(late_kernel, n, m, early, late),
            out_shape=[near((m, PAIR, size, width)), near((PAIR, size, width), jnp.float32)]
            + [near((PAIR, size, width))] * (n // PAIR - 1),
            in_specs=[vmem()] * (2 + len(early) + PAIR + len(late) - 1),
            out_specs=[vmem()] * (1 + n // PAIR),
            compiler_params=params(),
        )(
            total,
            chosen,
            *[ring.found[d] for d in early],
            ring.behind,
            ring.ahead,
            *[ring.found[d] for d in late if d != m // 2],
        )
        kept.append(panels)
        others = [send(v, PAIR * (h + 1)) for h, v in enumerate(away)]
        solved, *pieces = pl.pallas_call(
            functools.partial(solve_kernel, level),
            out_shape=[near((PAIR, size, width))] + [near((size, width))] * PAIR,
            in_specs=[smem()] + [vmem()] * (1 + 2 * PAIR + len(others)),
            out_specs=[vmem()] * (1 + PAIR),
            compiler_params=params(),
        )(me, keep, *b, *inverse, *others)
        columns += [pieces[0], send(pieces[1], 1)]

    return pl.pallas_call(
        last_kernel,
        out_shape=struct(b_panels.shape),
        in_specs=[smem()] + [vmem()] * (1 + len(columns)),
        out_specs=anywhere(),
        scratch_shapes=[pltpu.SemaphoreType.DMA((1 + len(columns),))],
        compiler_params=params(),
    )(me, full, *columns)


def cycle_of(mesh):
    m = mesh.shape["prow"]
    names = list(mesh.axis_names)
    devices = mesh.devices.transpose([names.index("prow"), names.index("pcol")])[:, 0]
    spots = [tuple(getattr(d, "coords", None) or (i, 0, 0)) for i, d in enumerate(devices)]

    def near(a, b):
        return sum(abs(u - v) for u, v in zip(spots[a], spots[b])) == 1

    def extend(path):
        if len(path) == m:
            return path if near(path[-1], path[0]) else None
        for p in range(m):
            if p not in path and near(path[-1], p):
                found = extend(path + [p])
                if found:
                    return found
        return None

    return extend([0]) or list(range(m))


def solution(mesh):
    n = mesh.shape["pcol"]
    cycle = cycle_of(mesh)

    def shards(b_panels, diag_inverse, l_blocks, block_cols, live_counts):
        front = b_panels.shape[-1]
        rows = mesh.shape["prow"]
        paired = n & (n - 1) == 0 and n >= PAIR and rows % 2 == 0 and front % (PAIR * LANES) == 0
        if paired and l_blocks.size * l_blocks.dtype.itemsize <= BLOCK_BYTES:
            return solve_paired(cycle, b_panels, diag_inverse, l_blocks, block_cols, live_counts)
        return solve_scattered(b_panels, diag_inverse, l_blocks, block_cols, live_counts)

    return jax.shard_map(
        shards,
        mesh=mesh,
        in_specs=(
            P(None, "prow", "pcol", None, None),
            P(None, "prow", "pcol", None, None),
            P(None, "prow", "pcol", None, None, None, None),
            P(None, "prow", "pcol", None, None),
            P(None, "prow", "pcol", None),
        ),
        out_specs=P(None, "prow", "pcol", None, None),
        check_vma=False,
    )
```

time: 159 us -> 67.5 us (0.42)
  waiting for transfers between devices: 124 us -> 30.7 us
  starting transfers between devices: 0.13 us -> 21.2 us
  between operations: 13.2 us -> 0.12 us
  Pallas kernels: 0 us -> 12.3 us
  matrix products: 11.4 us -> 0 us
  local copies, waits for them, and re-layouts: 8.47 us -> 1.98 us
    all_gather x2 -> x0, waiting for transfers between devices: 83 us -> none  [solve_front(): segment = lax.all_gather(solution[None], 'prow', axis=0, tiled=True)]
    reduce_scatter x2 -> x0, waiting for transfers between devices: 41.1 us -> none  [solve_front(): lax.psum_scatter(row_term(jnp.int32(0), 1 * lax.axis_size('pcol')).astype...]
    ppermute x0 -> x25, waiting for transfers between devices: none -> 30.7 us  [the longest x8 17 us: advance(): self.behind = lax.ppermute(self.behind, 'prow', self.to_next)]
    ppermute x0 -> x25, starting transfers between devices: none -> 21.2 us  [the longest x8 14.7 us: advance(): self.behind = lax.ppermute(self.behind, 'prow', self.to_next)]
    pallas_call x0 -> x8, Pallas kernels: none -> 12.3 us  [the longest x2 5.46 us: solve_paired(): pl.pallas_call(functools.partial(gather_kernel, n, level, m, early, late)...]
    dot_general x5 -> x0, matrix products: 11.4 us -> none  [the longest x2 6.82 us: row_term(): jnp.einsum('jkab,jkbr->jar', masked, fetched, preferred_element_type=jnp....]
    gather x2 -> x0, local copies, waits for them, and re-layouts: 4.77 us -> none  [row_term(): fetched = known[local_index]]
    dynamic_update_slice x2 -> x0, local copies, waits for them, and re-layouts: 2.85 us -> none  [solve_front(): lax.dynamic_update_slice_in_dim(solved_cols, segment, level_idx * proc_ro...]
  transfers between devices with their start and end apart: 4 -> 25, of which waited for: 4 -> 15; matrix products, arithmetic and copies ran while one was open for 1% -> 3% of each run, Pallas kernels for 0% -> 11%
where the time goes in v2:
time: 67.5 us; the launch traced here: 67.3 us
  waiting for transfers between devices  30.7 us (45%)
  starting transfers between devices  21.2 us (31%)
  Pallas kernels  12.3 us (18%)
  local copies, waits for them, and re-layouts  1.98 us (3%)
  other arithmetic  0.95 us (1%)
    ppermute x8, waiting for transfers between devices, advance(): self.behind = lax.ppermute(self.behind, 'prow', self.to_next)  17 us
    ppermute x8, starting transfers between devices, advance(): self.behind = lax.ppermute(self.behind, 'prow', self.to_next)  14.7 us
    ppermute x9, waiting for transfers between devices, send(): return lax.ppermute(value, 'pcol', [(i, i ^ bits) for i in range(n)])  9.16 us
    pallas_call x2, Pallas kernels, solve_paired(): pl.pallas_call(functools.partial(gather_kernel, n, level, m, early, late)...  5.46 us
    ppermute x8, waiting for transfers between devices, advance(): self.ahead = lax.ppermute(self.ahead, 'prow', self.to_last)  4.52 us
    ppermute x9, starting transfers between devices, send(): return lax.ppermute(value, 'pcol', [(i, i ^ bits) for i in range(n)])  4.5 us
    pallas_call x2, Pallas kernels, solve_paired(): pl.pallas_call(functools.partial(solve_kernel, level), out_shape=[near((P...  2.14 us
    ppermute x8, starting transfers between devices, advance(): self.ahead = lax.ppermute(self.ahead, 'prow', self.to_last)  1.98 us
  transfers between devices with their start and end apart: 25, of which 15 were waited for; matrix products, arithmetic and copies ran while one was open for 3% of the time, Pallas kernels for 11%

profile of v2, /device:TPU:0, one launch (start us, length us, event | category | flops | bytes accessed | tf_op | source)
XLA Modules:
  0.0 67.3 jit_solution(6739207704528513755)
XLA Ops:
  0.0 0.1 pad_add_fusion.me_ref
  0.1 1.7 %shard_map.55 = (bf16[128,512]{1,0:T(8,128)(2,1)S(1)}, bf16[128,256]{1,0:T(8,128)(2,1)S(1)}, bf16[128,256]{1,0:T(8,128)(2,1)S(1)}) custom-call(s32[2]{0:T(128)S(1)} %pad_add_fusion.me_ref, bf16[3,1,1,128,512]{4,3,2,1,0:T(8,128)(2,1)} %refs_0_.7, bf16[3,1,1,128,128]{4,3,2,1,0:T(8,128)(2,1)} %refs_2_.3), custom_call_target="tpu_custom_call" | custom-call | tf_op jit(solution)/shard_map/pallas_call | solution.py:231
  1.8 0.5 collective-permute-start
  2.3 0.9 %collective-permute-done = bf16[128,256]{1,0:T(8,128)(2,1)S(1)} collective-permute-done((bf16[128,256]{1,0:T(8,128)(2,1)S(1)}, bf16[128,256]{1,0:T(8,128)(2,1)S(1)}, u32[]{:S(2)}, u32[]{:S(2)}) %collective-permute-start) | collective-permute-done | bytes 65568 | tf_op jit(solution)/shard_map/ppermute | solution.py:229
  3.2 0.4 collective-permute-start.2
  3.6 2.6 %collective-permute-start.5 = (bf16[2,128,256]{2,1,0:T(8,128)(2,1)S(1)}, bf16[2,128,256]{2,1,0:T(8,128)(2,1)S(1)}, u32[]{:S(2)}, u32[]{:S(2)}) collective-permute-start(bf16[2,128,256]{2,1,0:T(8,128)(2,1)S(1)} %pad_maximum_fusion.refs_2_.refs_0_), channel_id=1, source_target_pairs={{0,4},{4,12},{12,20},{20,28},{28,24},{24,16},{16,8},{8,0},{1,5},{5... | collective-permute-start | bytes 393224 | tf_op jit(solution)/shard_map/ppermute | solution.py:211
  6.3 0.1 collective-permute-start.3
  6.3 4.0 %collective-permute-done.5.refs_6_.refs_4_ = bf16[2,128,256]{2,1,0:T(8,128)(2,1)S(1)} collective-permute-done((bf16[2,128,256]{2,1,0:T(8,128)(2,1)S(1)}, bf16[2,128,256]{2,1,0:T(8,128)(2,1)S(1)}, u32[]{:S(2)}, u32[]{:S(2)}) %collective-permute-start.5) | collective-permute-done | bytes 131104 | tf_op jit(solution)/shard_map/ppermute | solution.py:211
  10.4 1.7 %collective-permute-start.6 = (bf16[2,128,256]{2,1,0:T(8,128)(2,1)S(1)}, bf16[2,128,256]{2,1,0:T(8,128)(2,1)S(1)}, u32[]{:S(2)}, u32[]{:S(2)}) collective-permute-start(bf16[2,128,256]{2,1,0:T(8,128)(2,1)S(1)} %collective-permute-done.5.refs_6_.refs_4_), channel_id=1, source_target_pairs={{0,4},{4,12},{12,20},{20,28},{28,24},{24,16},{16,8},{8,0},{1,5},{5... | collective-permute-start | bytes 393224 | tf_op jit(solution)/shard_map/ppermute | solution.py:211
  12.0 0.8 %iota_compare_fusion = pred[2,4,5]{2,1,0:T(4,128)(4,1)S(1)} fusion(s32[2,4]{1,0:T(2,128)} %bitcast.15), kind=kLoop, calls=%fused_computation.5 | loop fusion | flops 40 | bytes 72 | tf_op jit(solution)/shard_map/lt | solution.py:249
  12.8 0.1 lt.35
  12.8 0.8 %squeeze.15 = s32[40]{0:T(128)S(1)} reshape(s32[2,1,1,4,5]{4,3,2,1,0:T(4,128)} %param.8) | data formatting | bytes 320 | tf_op jit(solution)/shard_map/squeeze | solution.py:245
  13.6 0.0 collective-permute-done.3.refs_3_.refs_1_
  13.6 0.4 collective-permute-start.4
  14.0 1.5 %collective-permute-done.6.refs_5_.refs_3_ = bf16[2,128,256]{2,1,0:T(8,128)(2,1)S(1)} collective-permute-done((bf16[2,128,256]{2,1,0:T(8,128)(2,1)S(1)}, bf16[2,128,256]{2,1,0:T(8,128)(2,1)S(1)}, u32[]{:S(2)}, u32[]{:S(2)}) %collective-permute-start.6) | collective-permute-done | bytes 131104 | tf_op jit(solution)/shard_map/ppermute | solution.py:211
  15.5 1.4 %collective-permute-start.7 = (bf16[2,128,256]{2,1,0:T(8,128)(2,1)S(1)}, bf16[2,128,256]{2,1,0:T(8,128)(2,1)S(1)}, u32[]{:S(2)}, u32[]{:S(2)}) collective-permute-start(bf16[2,128,256]{2,1,0:T(8,128)(2,1)S(1)} %collective-permute-done.6.refs_5_.refs_3_), channel_id=1, source_target_pairs={{0,4},{4,12},{12,20},{20,28},{28,24},{24,16},{16,8},{8,0},{1,5},{5... | collective-permute-start | bytes 393224 | tf_op jit(solution)/shard_map/ppermute | solution.py:211
  17.0 0.1 collective-permute-start.1
  17.1 0.5 collective-permute-start.11
  17.6 1.1 %collective-permute-done.4.refs_4_.refs_2_ = bf16[2,128,256]{2,1,0:T(8,128)(2,1)S(1)} collective-permute-done((bf16[2,128,256]{2,1,0:T(8,128)(2,1)S(1)}, bf16[2,128,256]{2,1,0:T(8,128)(2,1)S(1)}, u32[]{:S(2)}, u32[]{:S(2)}) %collective-permute-start.4) | collective-permute-done | bytes 131104 | tf_op jit(solution)/shard_map/ppermute | solution.py:212
  18.6 0.4 collective-permute-start.9
  19.0 1.5 %collective-permute-done.7.refs_8_ = bf16[2,128,256]{2,1,0:T(8,128)(2,1)S(1)} collective-permute-done((bf16[2,128,256]{2,1,0:T(8,128)(2,1)S(1)}, bf16[2,128,256]{2,1,0:T(8,128)(2,1)S(1)}, u32[]{:S(2)}, u32[]{:S(2)}) %collective-permute-start.7) | collective-permute-done | bytes 131104 | tf_op jit(solution)/shard_map/ppermute | solution.py:211
  20.5 1.4 %collective-permute-start.8 = (bf16[128,256]{1,0:T(8,128)(2,1)S(1)}, bf16[128,256]{1,0:T(8,128)(2,1)S(1)}, u32[]{:S(2)}, u32[]{:S(2)}) collective-permute-start(bf16[128,256]{1,0:T(8,128)(2,1)S(1)} %slice_bitcast_fusion.3), channel_id=1, source_target_pairs={{0,4},{4,12},{12,20},{20,28},{28,24},{24,16},{16,8},{8,0},{1,5},{5... | collective-permute-start | bytes 196616 | tf_op jit(solution)/shard_map/ppermute | solution.py:211
  22.0 1.7 %collective-permute-done.9.refs_7_ = bf16[2,128,256]{2,1,0:T(8,128)(2,1)S(1)} collective-permute-done((bf16[2,128,256]{2,1,0:T(8,128)(2,1)S(1)}, bf16[2,128,256]{2,1,0:T(8,128)(2,1)S(1)}, u32[]{:S(2)}, u32[]{:S(2)}) %collective-permute-start.9) | collective-permute-done | bytes 131104 | tf_op jit(solution)/shard_map/ppermute | solution.py:212
  23.6 0.4 collective-permute-start.10
  24.0 0.0 collective-permute-done.1
  24.0 0.1 pad_add_fusion.1.index_ref
  24.1 0.0 collective-permute-done.2.refs_1_
  24.1 1.1 %copy-done.2 = bf16[2,1,1,4,5,128,128]{6,5,4,3,2,1,0:T(8,128)(2,1)} copy-done((bf16[2,1,1,4,5,128,128]{6,5,4,3,2,1,0:T(8,128)(2,1)}, bf16[2,1,1,4,5,128,128]{6,5,4,3,2,1,0:T(8,128)(2,1)S(1)}, u32[]{:S(2)}) %copy-start.2) | copy-done | bytes 1310744
  25.2 2.7 %shard_map.56 = (f32[4,128,256]{2,1,0:T(8,128)S(1)}, bf16[4,128,768]{2,1,0:T(8,128)(2,1)S(1)}) custom-call(s32[2]{0:T(128)S(1)} %pad_add_fusion.me_ref, s32[80]{0:T(128)S(1)} %pad_add_fusion.1.index_ref, bf16[2,1,1,4,5,128,128]{6,5,4,3,2,1,0:T(8,128)(2,1)} %refs_0_.6, bf16[2,1,1,4,5,128,128]{6,5,4,3,2,1,0:T(8,128)(2,1)} %copy-done.2, ...), custom_call_target="tpu_custom_call" | custom-call | tf_op jit(solution)/shard_map/pallas_call | solution.py:260
  27.9 0.0 copy-start.1
  27.9 0.0 copy-start
  27.9 0.0 collective-permute-done.8.refs_5_
  27.9 0.0 collective-permute-done.10.refs_6_
  27.9 0.4 shard_map.57
  28.3 1.7 %collective-permute-start.13 = (bf16[2,128,256]{2,1,0:T(8,128)(2,1)S(1)}, bf16[2,128,256]{2,1,0:T(8,128)(2,1)S(1)}, u32[]{:S(2)}, u32[]{:S(2)}) collective-permute-start(bf16[2,128,256]{2,1,0:T(8,128)(2,1)S(1)} %get-tuple-element.36), channel_id=1, source_target_pairs={{0,2},{1,3},{2,0},{3,1},{4,6},{5,7},{6,4},{7,5},{8,10},{9,11},{10,... | collective-permute-start | bytes 393224 | tf_op jit(solution)/shard_map/ppermute | solution.py:229
  30.1 0.0 collective-permute-start.12
  30.1 1.3 %collective-permute-done.12.refs_3_ = bf16[3,1,1,128,128]{4,3,2,1,0:T(8,128)(2,1)S(1)} collective-permute-done((bf16[3,1,1,128,128]{4,3,2,1,0:T(8,128)(2,1)S(1)}, bf16[3,1,1,128,128]{4,3,2,1,0:T(8,128)(2,1)S(1)}, u32[]{:S(2)}, u32[]{:S(2)}) %collective-permute-start.12) | collective-permute-done | bytes 98336 | tf_op jit(solution)/shard_map/ppermute | solution.py:229
  31.4 2.0 %collective-permute-done.13.refs_4_ = bf16[2,128,256]{2,1,0:T(8,128)(2,1)S(1)} collective-permute-done((bf16[2,128,256]{2,1,0:T(8,128)(2,1)S(1)}, bf16[2,128,256]{2,1,0:T(8,128)(2,1)S(1)}, u32[]{:S(2)}, u32[]{:S(2)}) %collective-permute-start.13) | collective-permute-done | bytes 131104 | tf_op jit(solution)/shard_map/ppermute | solution.py:229
  33.4 0.7 %shard_map.58 = (bf16[2,128,256]{2,1,0:T(8,128)(2,1)S(1)}, bf16[128,256]{1,0:T(8,128)(2,1)S(1)}, bf16[128,256]{1,0:T(8,128)(2,1)S(1)}) custom-call(s32[2]{0:T(128)S(1)} %pad_add_fusion.me_ref, f32[2,128,256]{2,1,0:T(8,128)S(1)} %get-tuple-element.33.keep_ref, bf16[3,1,1,128,512]{4,3,2,1,0:T(8,128)(2,1)S(1)} %copy-done, ...), custom_call_target="tpu_custom_call" | custom-call | tf_op jit(solution)/shard_map/pallas_call | solution.py:289
  34.1 1.7 %collective-permute-start.17 = (bf16[2,128,256]{2,1,0:T(8,128)(2,1)S(1)}, bf16[2,128,256]{2,1,0:T(8,128)(2,1)S(1)}, u32[]{:S(2)}, u32[]{:S(2)}) collective-permute-start(bf16[2,128,256]{2,1,0:T(8,128)(2,1)S(1)} %get-tuple-element.40.refs_3_.refs_0_), channel_id=1, source_target_pairs={{0,4},{4,12},{12,20},{20,28},{28,24},{24,16},{16,8},{8,0},{1,5},{5... | collective-permute-start | bytes 393224 | tf_op jit(solution)/shard_map/ppermute | solution.py:211
  35.8 0.4 collective-permute-start.15
  36.2 3.3 %collective-permute-done.17.refs_7_.refs_4_ = bf16[2,128,256]{2,1,0:T(8,128)(2,1)S(1)} collective-permute-done((bf16[2,128,256]{2,1,0:T(8,128)(2,1)S(1)}, bf16[2,128,256]{2,1,0:T(8,128)(2,1)S(1)}, u32[]{:S(2)}, u32[]{:S(2)}) %collective-permute-start.17) | collective-permute-done | bytes 131104 | tf_op jit(solution)/shard_map/ppermute | solution.py:211
  39.5 1.8 %collective-permute-start.18 = (bf16[2,128,256]{2,1,0:T(8,128)(2,1)S(1)}, bf16[2,128,256]{2,1,0:T(8,128)(2,1)S(1)}, u32[]{:S(2)}, u32[]{:S(2)}) collective-permute-start(bf16[2,128,256]{2,1,0:T(8,128)(2,1)S(1)} %collective-permute-done.17.refs_7_.refs_4_), channel_id=1, source_target_pairs={{0,4},{4,12},{12,20},{20,28},{28,24},{24,16},{16,8},{8,0},{1,5},{5... | collective-permute-start | bytes 393224 | tf_op jit(solution)/shard_map/ppermute | solution.py:211
  41.4 0.3 collective-permute-done.15.refs_4_.refs_1_
  41.7 0.2 collective-permute-start.16
  41.8 3.9 %collective-permute-done.18.refs_6_.refs_3_ = bf16[2,128,256]{2,1,0:T(8,128)(2,1)S(1)} collective-permute-done((bf16[2,128,256]{2,1,0:T(8,128)(2,1)S(1)}, bf16[2,128,256]{2,1,0:T(8,128)(2,1)S(1)}, u32[]{:S(2)}, u32[]{:S(2)}) %collective-permute-start.18) | collective-permute-done | bytes 131104 | tf_op jit(solution)/shard_map/ppermute | solution.py:211
  45.7 2.0 %collective-permute-start.19 = (bf16[2,128,256]{2,1,0:T(8,128)(2,1)S(1)}, bf16[2,128,256]{2,1,0:T(8,128)(2,1)S(1)}, u32[]{:S(2)}, u32[]{:S(2)}) collective-permute-start(bf16[2,128,256]{2,1,0:T(8,128)(2,1)S(1)} %collective-permute-done.18.refs_6_.refs_3_), channel_id=1, source_target_pairs={{0,4},{4,12},{12,20},{20,28},{28,24},{24,16},{16,8},{8,0},{1,5},{5... | collective-permute-start | bytes 393224 | tf_op jit(solution)/shard_map/ppermute | solution.py:211
  47.7 0.0 collective-permute-done.16.refs_5_.refs_2_
  47.7 0.1 collective-permute-start.21
  47.8 2.9 %collective-permute-done.19.refs_8_ = bf16[2,128,256]{2,1,0:T(8,128)(2,1)S(1)} collective-permute-done((bf16[2,128,256]{2,1,0:T(8,128)(2,1)S(1)}, bf16[2,128,256]{2,1,0:T(8,128)(2,1)S(1)}, u32[]{:S(2)}, u32[]{:S(2)}) %collective-permute-start.19) | collective-permute-done | bytes 131104 | tf_op jit(solution)/shard_map/ppermute | solution.py:211
  50.7 2.0 %collective-permute-start.20 = (bf16[128,256]{1,0:T(8,128)(2,1)S(1)}, bf16[128,256]{1,0:T(8,128)(2,1)S(1)}, u32[]{:S(2)}, u32[]{:S(2)}) collective-permute-start(bf16[128,256]{1,0:T(8,128)(2,1)S(1)} %slice_bitcast_fusion.1), channel_id=1, source_target_pairs={{0,4},{4,12},{12,20},{20,28},{28,24},{24,16},{16,8},{8,0},{1,5},{5... | collective-permute-start | bytes 196616 | tf_op jit(solution)/shard_map/ppermute | solution.py:211
  52.7 0.0 collective-permute-done.21.refs_7_
  52.7 0.1 collective-permute-start.22
  52.8 2.7 %shard_map.59 = (f32[4,128,256]{2,1,0:T(8,128)S(1)}, bf16[4,128,768]{2,1,0:T(8,128)(2,1)S(1)}) custom-call(s32[2]{0:T(128)S(1)} %pad_add_fusion.me_ref, s32[80]{0:T(128)S(1)} %pad_add_fusion.1.index_ref, bf16[2,1,1,4,5,128,128]{6,5,4,3,2,1,0:T(8,128)(2,1)} %refs_0_.6, bf16[2,1,1,4,5,128,128]{6,5,4,3,2,1,0:T(8,128)(2,1)} %copy-done.2, ...), custom_call_target="tpu_custom_call" | custom-call | tf_op jit(solution)/shard_map/pallas_call | solution.py:260
  55.5 0.0 collective-permute-done.20.refs_5_
  55.6 1.5 %collective-permute-done.22.refs_6_ = bf16[128,256]{1,0:T(8,128)(2,1)S(1)} collective-permute-done((bf16[128,256]{1,0:T(8,128)(2,1)S(1)}, bf16[128,256]{1,0:T(8,128)(2,1)S(1)}, u32[]{:S(2)}, u32[]{:S(2)}) %collective-permute-start.22) | collective-permute-done | bytes 65568 | tf_op jit(solution)/shard_map/ppermute | solution.py:212
  57.0 1.3 %shard_map.60 = (bf16[8,2,128,256]{3,2,1,0:T(8,128)(2,1)}, f32[2,128,256]{2,1,0:T(8,128)S(1)}, bf16[2,128,256]{2,1,0:T(8,128)(2,1)S(1)}) custom-call(f32[4,128,256]{2,1,0:T(8,128)S(1)} %get-tuple-element.41.total_ref, bf16[4,128,768]{2,1,0:T(8,128)(2,1)S(1)} %get-tuple-element.42.chosen_ref, bf16[2,128,256]{2,1,0:T(8,128)(2,1)S(1)} %get-tuple-element.40.refs_3_.refs_0_, ...), custom_call_target="tpu_custom_call" | custom-call | tf_op jit(solution)/shard_map/pallas_call | solution.py:272
  58.3 1.2 %collective-permute-start.23 = (bf16[2,128,256]{2,1,0:T(8,128)(2,1)S(1)}, bf16[2,128,256]{2,1,0:T(8,128)(2,1)S(1)}, u32[]{:S(2)}, u32[]{:S(2)}) collective-permute-start(bf16[2,128,256]{2,1,0:T(8,128)(2,1)S(1)} %get-tuple-element.44), channel_id=1, source_target_pairs={{0,2},{1,3},{2,0},{3,1},{4,6},{5,7},{6,4},{7,5},{8,10},{9,11},{10,... | collective-permute-start | bytes 393224 | tf_op jit(solution)/shard_map/ppermute | solution.py:229
  59.6 3.7 %collective-permute-done.23.refs_4_ = bf16[2,128,256]{2,1,0:T(8,128)(2,1)S(1)} collective-permute-done((bf16[2,128,256]{2,1,0:T(8,128)(2,1)S(1)}, bf16[2,128,256]{2,1,0:T(8,128)(2,1)S(1)}, u32[]{:S(2)}, u32[]{:S(2)}) %collective-permute-start.23) | collective-permute-done | bytes 131104 | tf_op jit(solution)/shard_map/ppermute | solution.py:229
  63.3 1.4 %shard_map.61 = (bf16[2,128,256]{2,1,0:T(8,128)(2,1)}, bf16[128,256]{1,0:T(8,128)(2,1)S(1)}, bf16[128,256]{1,0:T(8,128)(2,1)S(1)}) custom-call(s32[2]{0:T(128)S(1)} %pad_add_fusion.me_ref, f32[2,128,256]{2,1,0:T(8,128)S(1)} %get-tuple-element.43.keep_ref, bf16[3,1,1,128,512]{4,3,2,1,0:T(8,128)(2,1)S(1)} %copy-done, ...), custom_call_target="tpu_custom_call" | custom-call | tf_op jit(solution)/shard_map/pallas_call | solution.py:289
  64.7 0.0 collective-permute-start.24
  64.7 0.0 collective-permute-done.14.refs_1_
  64.7 1.2 %collective-permute-done.24.refs_3_ = bf16[128,256]{1,0:T(8,128)(2,1)S(1)} collective-permute-done((bf16[128,256]{1,0:T(8,128)(2,1)S(1)}, bf16[128,256]{1,0:T(8,128)(2,1)S(1)}, u32[]{:S(2)}, u32[]{:S(2)}) %collective-permute-start.24) | collective-permute-done | bytes 65568 | tf_op jit(solution)/shard_map/ppermute | solution.py:229
  65.9 1.3 %shard_map.62 = bf16[3,1,1,128,512]{4,3,2,1,0:T(8,128)(2,1)} custom-call(s32[2]{0:T(128)S(1)} %pad_add_fusion.me_ref, bf16[128,512]{1,0:T(8,128)(2,1)S(1)} %get-tuple-element.26.full_ref, bf16[128,256]{1,0:T(8,128)(2,1)S(1)} %get-tuple-element.37.refs_0_, bf16[128,256]{1,0:T(8,128)(2,1)S(1)} %collective-permute-done.14.refs_1_, ...), custom_call_target="tpu_custom_call" | custom-call | tf_op jit(solution)/shard_map/pallas_call | solution.py:298
  (11 shorter events, 0.1 us)
Async XLA Ops:
  1.8 1.4 %collective-permute-start = (bf16[128,256]{1,0:T(8,128)(2,1)S(1)}, bf16[128,256]{1,0:T(8,128)(2,1)S(1)}, u32[]{:S(2)}, u32[]{:S(2)}) collective-permute-start(bf16[128,256]{1,0:T(8,128)(2,1)S(1)} %get-tuple-element.28), channel_id=1, source_target_pairs={{0,1},{1,0},{2,3},{3,2},{4,5},{5,4},{6,7},{7,6},{8,9},{9,8},{10,11... | collective-permute-start | bytes 196616 | tf_op jit(solution)/shard_map/ppermute | solution.py:229
  3.2 20.9 %collective-permute-start.2 = (bf16[2,1,1,4,5,128,128]{6,5,4,3,2,1,0:T(8,128)(2,1)}, bf16[2,1,1,4,5,128,128]{6,5,4,3,2,1,0:T(8,128)(2,1)S(1)}, u32[]{:S(2)}, u32[]{:S(2)}) collective-permute-start(bf16[2,1,1,4,5,128,128]{6,5,4,3,2,1,0:T(8,128)(2,1)} %refs_0_.6), channel_id=1, source_target_pairs={{0,1},{1,0},{2,3},{3,2},{4,5},{5,4},{6,7},{7,6},{8,9},{9,8},{10,11... | collective-permute-start | bytes 3932168 | tf_op jit(solution)/shard_map/ppermute | solution.py:229
  3.6 6.7 %collective-permute-start.5 = (bf16[2,128,256]{2,1,0:T(8,128)(2,1)S(1)}, bf16[2,128,256]{2,1,0:T(8,128)(2,1)S(1)}, u32[]{:S(2)}, u32[]{:S(2)}) collective-permute-start(bf16[2,128,256]{2,1,0:T(8,128)(2,1)S(1)} %pad_maximum_fusion.refs_2_.refs_0_), channel_id=1, source_target_pairs={{0,4},{4,12},{12,20},{20,28},{28,24},{24,16},{16,8},{8,0},{1,5},{5... | collective-permute-start | bytes 393224 | tf_op jit(solution)/shard_map/ppermute | solution.py:211
  6.3 7.4 %collective-permute-start.3 = (bf16[2,128,256]{2,1,0:T(8,128)(2,1)S(1)}, bf16[2,128,256]{2,1,0:T(8,128)(2,1)S(1)}, u32[]{:S(2)}, u32[]{:S(2)}) collective-permute-start(bf16[2,128,256]{2,1,0:T(8,128)(2,1)S(1)} %pad_maximum_fusion.refs_2_.refs_0_), channel_id=1, source_target_pairs={{4,0},{12,4},{20,12},{28,20},{24,28},{16,24},{8,16},{0,8},{5,1},{1... | collective-permute-start | bytes 393224 | tf_op jit(solution)/shard_map/ppermute | solution.py:212
  10.4 5.2 %collective-permute-start.6 = (bf16[2,128,256]{2,1,0:T(8,128)(2,1)S(1)}, bf16[2,128,256]{2,1,0:T(8,128)(2,1)S(1)}, u32[]{:S(2)}, u32[]{:S(2)}) collective-permute-start(bf16[2,128,256]{2,1,0:T(8,128)(2,1)S(1)} %collective-permute-done.5.refs_6_.refs_4_), channel_id=1, source_target_pairs={{0,4},{4,12},{12,20},{20,28},{28,24},{24,16},{16,8},{8,0},{1,5},{5... | collective-permute-start | bytes 393224 | tf_op jit(solution)/shard_map/ppermute | solution.py:211
  13.6 5.0 %collective-permute-start.4 = (bf16[2,128,256]{2,1,0:T(8,128)(2,1)S(1)}, bf16[2,128,256]{2,1,0:T(8,128)(2,1)S(1)}, u32[]{:S(2)}, u32[]{:S(2)}) collective-permute-start(bf16[2,128,256]{2,1,0:T(8,128)(2,1)S(1)} %collective-permute-done.3.refs_3_.refs_1_), channel_id=1, source_target_pairs={{4,0},{12,4},{20,12},{28,20},{24,28},{16,24},{8,16},{0,8},{5,1},{1... | collective-permute-start | bytes 393224 | tf_op jit(solution)/shard_map/ppermute | solution.py:212
  15.5 5.0 %collective-permute-start.7 = (bf16[2,128,256]{2,1,0:T(8,128)(2,1)S(1)}, bf16[2,128,256]{2,1,0:T(8,128)(2,1)S(1)}, u32[]{:S(2)}, u32[]{:S(2)}) collective-permute-start(bf16[2,128,256]{2,1,0:T(8,128)(2,1)S(1)} %collective-permute-done.6.refs_5_.refs_3_), channel_id=1, source_target_pairs={{0,4},{4,12},{12,20},{20,28},{28,24},{24,16},{16,8},{8,0},{1,5},{5... | collective-permute-start | bytes 393224 | tf_op jit(solution)/shard_map/ppermute | solution.py:211
  17.0 7.0 %collective-permute-start.1 = (s32[40]{0:T(128)S(1)}, s32[40]{0:T(128)S(1)}, u32[]{:S(2)}, u32[]{:S(2)}) collective-permute-start(s32[40]{0:T(128)S(1)} %fusion.1), channel_id=1, source_target_pairs={{0,1},{1,0},{2,3},{3,2},{4,5},{5,4},{6,7},{7,6},{8,9},{9,8},{10,11... | collective-permute-start | bytes 488 | tf_op jit(solution)/shard_map/ppermute | solution.py:229
  17.1 14.3 %collective-permute-start.11 = (bf16[3,1,1,128,512]{4,3,2,1,0:T(8,128)(2,1)}, bf16[3,1,1,128,512]{4,3,2,1,0:T(8,128)(2,1)S(1)}, u32[]{:S(2)}, u32[]{:S(2)}) collective-permute-start(bf16[3,1,1,128,512]{4,3,2,1,0:T(8,128)(2,1)} %refs_0_.7), channel_id=1, source_target_pairs={{0,1},{1,0},{2,3},{3,2},{4,5},{5,4},{6,7},{7,6},{8,9},{9,8},{10,11... | collective-permute-start | bytes 1179656 | tf_op jit(solution)/shard_map/ppermute | solution.py:229
  18.6 5.0 %collective-permute-start.9 = (bf16[2,128,256]{2,1,0:T(8,128)(2,1)S(1)}, bf16[2,128,256]{2,1,0:T(8,128)(2,1)S(1)}, u32[]{:S(2)}, u32[]{:S(2)}) collective-permute-start(bf16[2,128,256]{2,1,0:T(8,128)(2,1)S(1)} %collective-permute-done.4.refs_4_.refs_2_), channel_id=1, source_target_pairs={{4,0},{12,4},{20,12},{28,20},{24,28},{16,24},{8,16},{0,8},{5,1},{1... | collective-permute-start | bytes 393224 | tf_op jit(solution)/shard_map/ppermute | solution.py:212
  20.5 7.4 %collective-permute-start.8 = (bf16[128,256]{1,0:T(8,128)(2,1)S(1)}, bf16[128,256]{1,0:T(8,128)(2,1)S(1)}, u32[]{:S(2)}, u32[]{:S(2)}) collective-permute-start(bf16[128,256]{1,0:T(8,128)(2,1)S(1)} %slice_bitcast_fusion.3), channel_id=1, source_target_pairs={{0,4},{4,12},{12,20},{20,28},{28,24},{24,16},{16,8},{8,0},{1,5},{5... | collective-permute-start | bytes 196616 | tf_op jit(solution)/shard_map/ppermute | solution.py:211
  23.6 4.3 %collective-permute-start.10 = (bf16[128,256]{1,0:T(8,128)(2,1)S(1)}, bf16[128,256]{1,0:T(8,128)(2,1)S(1)}, u32[]{:S(2)}, u32[]{:S(2)}) collective-permute-start(bf16[128,256]{1,0:T(8,128)(2,1)S(1)} %slice_bitcast_fusion.2), channel_id=1, source_target_pairs={{4,0},{12,4},{20,12},{28,20},{24,28},{16,24},{8,16},{0,8},{5,1},{1... | collective-permute-start | bytes 196616 | tf_op jit(solution)/shard_map/ppermute | solution.py:212
  24.1 1.1 %copy-start.2 = (bf16[2,1,1,4,5,128,128]{6,5,4,3,2,1,0:T(8,128)(2,1)}, bf16[2,1,1,4,5,128,128]{6,5,4,3,2,1,0:T(8,128)(2,1)S(1)}, u32[]{:S(2)}) copy-start(bf16[2,1,1,4,5,128,128]{6,5,4,3,2,1,0:T(8,128)(2,1)S(1)} %collective-permute-done.2.refs_1_) | copy-start | bytes 3932164
  27.9 2.2 %copy-start.1 = (bf16[3,1,1,128,128]{4,3,2,1,0:T(8,128)(2,1)S(1)}, bf16[3,1,1,128,128]{4,3,2,1,0:T(8,128)(2,1)}, u32[]{:S(2)}) copy-start(bf16[3,1,1,128,128]{4,3,2,1,0:T(8,128)(2,1)} %refs_2_.3) | copy-start | bytes 294916
  27.9 5.5 %copy-start = (bf16[3,1,1,128,512]{4,3,2,1,0:T(8,128)(2,1)S(1)}, bf16[3,1,1,128,512]{4,3,2,1,0:T(8,128)(2,1)}, u32[]{:S(2)}) copy-start(bf16[3,1,1,128,512]{4,3,2,1,0:T(8,128)(2,1)} %refs_0_.7) | copy-start | bytes 1179652
  28.3 5.0 %collective-permute-start.13 = (bf16[2,128,256]{2,1,0:T(8,128)(2,1)S(1)}, bf16[2,128,256]{2,1,0:T(8,128)(2,1)S(1)}, u32[]{:S(2)}, u32[]{:S(2)}) collective-permute-start(bf16[2,128,256]{2,1,0:T(8,128)(2,1)S(1)} %get-tuple-element.36), channel_id=1, source_target_pairs={{0,2},{1,3},{2,0},{3,1},{4,6},{5,7},{6,4},{7,5},{8,10},{9,11},{10,... | collective-permute-start | bytes 393224 | tf_op jit(solution)/shard_map/ppermute | solution.py:229
  30.1 1.3 %collective-permute-start.12 = (bf16[3,1,1,128,128]{4,3,2,1,0:T(8,128)(2,1)S(1)}, bf16[3,1,1,128,128]{4,3,2,1,0:T(8,128)(2,1)S(1)}, u32[]{:S(2)}, u32[]{:S(2)}) collective-permute-start(bf16[3,1,1,128,128]{4,3,2,1,0:T(8,128)(2,1)S(1)} %copy-done.1), channel_id=1, source_target_pairs={{0,1},{1,0},{2,3},{3,2},{4,5},{5,4},{6,7},{7,6},{8,9},{9,8},{10,11... | collective-permute-start | bytes 294920 | tf_op jit(solution)/shard_map/ppermute | solution.py:229
  34.1 5.4 %collective-permute-start.17 = (bf16[2,128,256]{2,1,0:T(8,128)(2,1)S(1)}, bf16[2,128,256]{2,1,0:T(8,128)(2,1)S(1)}, u32[]{:S(2)}, u32[]{:S(2)}) collective-permute-start(bf16[2,128,256]{2,1,0:T(8,128)(2,1)S(1)} %get-tuple-element.40.refs_3_.refs_0_), channel_id=1, source_target_pairs={{0,4},{4,12},{12,20},{20,28},{28,24},{24,16},{16,8},{8,0},{1,5},{5... | collective-permute-start | bytes 393224 | tf_op jit(solution)/shard_map/ppermute | solution.py:211
  35.8 5.8 %collective-permute-start.15 = (bf16[2,128,256]{2,1,0:T(8,128)(2,1)S(1)}, bf16[2,128,256]{2,1,0:T(8,128)(2,1)S(1)}, u32[]{:S(2)}, u32[]{:S(2)}) collective-permute-start(bf16[2,128,256]{2,1,0:T(8,128)(2,1)S(1)} %get-tuple-element.40.refs_3_.refs_0_), channel_id=1, source_target_pairs={{4,0},{12,4},{20,12},{28,20},{24,28},{16,24},{8,16},{0,8},{5,1},{1... | collective-permute-start | bytes 393224 | tf_op jit(solution)/shard_map/ppermute | solution.py:212
  39.5 6.2 %collective-permute-start.18 = (bf16[2,128,256]{2,1,0:T(8,128)(2,1)S(1)}, bf16[2,128,256]{2,1,0:T(8,128)(2,1)S(1)}, u32[]{:S(2)}, u32[]{:S(2)}) collective-permute-start(bf16[2,128,256]{2,1,0:T(8,128)(2,1)S(1)} %collective-permute-done.17.refs_7_.refs_4_), channel_id=1, source_target_pairs={{0,4},{4,12},{12,20},{20,28},{28,24},{24,16},{16,8},{8,0},{1,5},{5... | collective-permute-start | bytes 393224 | tf_op jit(solution)/shard_map/ppermute | solution.py:211
  41.7 6.0 %collective-permute-start.16 = (bf16[2,128,256]{2,1,0:T(8,128)(2,1)S(1)}, bf16[2,128,256]{2,1,0:T(8,128)(2,1)S(1)}, u32[]{:S(2)}, u32[]{:S(2)}) collective-permute-start(bf16[2,128,256]{2,1,0:T(8,128)(2,1)S(1)} %collective-permute-done.15.refs_4_.refs_1_), channel_id=1, source_target_pairs={{4,0},{12,4},{20,12},{28,20},{24,28},{16,24},{8,16},{0,8},{5,1},{1... | collective-permute-start | bytes 393224 | tf_op jit(solution)/shard_map/ppermute | solution.py:212
  45.7 5.0 %collective-permute-start.19 = (bf16[2,128,256]{2,1,0:T(8,128)(2,1)S(1)}, bf16[2,128,256]{2,1,0:T(8,128)(2,1)S(1)}, u32[]{:S(2)}, u32[]{:S(2)}) collective-permute-start(bf16[2,128,256]{2,1,0:T(8,128)(2,1)S(1)} %collective-permute-done.18.refs_6_.refs_3_), channel_id=1, source_target_pairs={{0,4},{4,12},{12,20},{20,28},{28,24},{24,16},{16,8},{8,0},{1,5},{5... | collective-permute-start | bytes 393224 | tf_op jit(solution)/shard_map/ppermute | solution.py:211
  47.7 5.0 %collective-permute-start.21 = (bf16[2,128,256]{2,1,0:T(8,128)(2,1)S(1)}, bf16[2,128,256]{2,1,0:T(8,128)(2,1)S(1)}, u32[]{:S(2)}, u32[]{:S(2)}) collective-permute-start(bf16[2,128,256]{2,1,0:T(8,128)(2,1)S(1)} %collective-permute-done.16.refs_5_.refs_2_), channel_id=1, source_target_pairs={{4,0},{12,4},{20,12},{28,20},{24,28},{16,24},{8,16},{0,8},{5,1},{1... | collective-permute-start | bytes 393224 | tf_op jit(solution)/shard_map/ppermute | solution.py:212
  50.7 4.8 %collective-permute-start.20 = (bf16[128,256]{1,0:T(8,128)(2,1)S(1)}, bf16[128,256]{1,0:T(8,128)(2,1)S(1)}, u32[]{:S(2)}, u32[]{:S(2)}) collective-permute-start(bf16[128,256]{1,0:T(8,128)(2,1)S(1)} %slice_bitcast_fusion.1), channel_id=1, source_target_pairs={{0,4},{4,12},{12,20},{20,28},{28,24},{24,16},{16,8},{8,0},{1,5},{5... | collective-permute-start | bytes 196616 | tf_op jit(solution)/shard_map/ppermute | solution.py:211
  52.7 4.3 %collective-permute-start.22 = (bf16[128,256]{1,0:T(8,128)(2,1)S(1)}, bf16[128,256]{1,0:T(8,128)(2,1)S(1)}, u32[]{:S(2)}, u32[]{:S(2)}) collective-permute-start(bf16[128,256]{1,0:T(8,128)(2,1)S(1)} %slice_bitcast_fusion), channel_id=1, source_target_pairs={{4,0},{12,4},{20,12},{28,20},{24,28},{16,24},{8,16},{0,8},{5,1},{1... | collective-permute-start | bytes 196616 | tf_op jit(solution)/shard_map/ppermute | solution.py:212
  58.3 5.0 %collective-permute-start.23 = (bf16[2,128,256]{2,1,0:T(8,128)(2,1)S(1)}, bf16[2,128,256]{2,1,0:T(8,128)(2,1)S(1)}, u32[]{:S(2)}, u32[]{:S(2)}) collective-permute-start(bf16[2,128,256]{2,1,0:T(8,128)(2,1)S(1)} %get-tuple-element.44), channel_id=1, source_target_pairs={{0,2},{1,3},{2,0},{3,1},{4,6},{5,7},{6,4},{7,5},{8,10},{9,11},{10,... | collective-permute-start | bytes 393224 | tf_op jit(solution)/shard_map/ppermute | solution.py:229
  59.6 5.1 %collective-permute-start.14 = (bf16[128,256]{1,0:T(8,128)(2,1)S(1)}, bf16[128,256]{1,0:T(8,128)(2,1)S(1)}, u32[]{:S(2)}, u32[]{:S(2)}) collective-permute-start(bf16[128,256]{1,0:T(8,128)(2,1)S(1)} %get-tuple-element.38), channel_id=1, source_target_pairs={{0,1},{1,0},{2,3},{3,2},{4,5},{5,4},{6,7},{7,6},{8,9},{9,8},{10,11... | collective-permute-start | bytes 196616 | tf_op jit(solution)/shard_map/ppermute | solution.py:229
  64.7 1.3 %collective-permute-start.24 = (bf16[128,256]{1,0:T(8,128)(2,1)S(1)}, bf16[128,256]{1,0:T(8,128)(2,1)S(1)}, u32[]{:S(2)}, u32[]{:S(2)}) collective-permute-start(bf16[128,256]{1,0:T(8,128)(2,1)S(1)} %get-tuple-element.46), channel_id=1, source_target_pairs={{0,1},{1,0},{2,3},{3,2},{4,5},{5,4},{6,7},{7,6},{8,9},{9,8},{10,11... | collective-permute-start | bytes 196616 | tf_op jit(solution)/shard_map/ppermute | solution.py:229

commit v3 on v2

--- a/solution.py
+++ b/solution.py
@@ -72,36 +72,59 @@
     return jnp.stack(solutions)[:, None, None]
 
 
-def first_kernel(me_ref, b_ref, d_ref, full_ref, *refs):
-    piece_refs, (b_buf, d_buf, sems) = refs[:PAIR], refs[PAIR:]
+def first_kernel(n, m, place, me_ref, counts_ref, cols_ref, b_ref, d_ref, full_ref, index_ref, *refs):
+    piece_refs, (b_buf, d_buf, count_ref, col_ref, sems) = refs[:PAIR], refs[PAIR:]
     copies = [
-        pltpu.make_async_copy(b_ref.at[0, 0, 0], b_buf, sems.at[0]),
-        pltpu.make_async_copy(d_ref.at[0, 0, 0], d_buf, sems.at[1]),
+        pltpu.make_async_copy(counts_ref, count_ref, sems.at[0]),
+        pltpu.make_async_copy(cols_ref, col_ref, sems.at[1]),
+        pltpu.make_async_copy(b_ref.at[0, 0, 0], b_buf, sems.at[2]),
+        pltpu.make_async_copy(d_ref.at[0, 0, 0], d_buf, sems.at[3]),
     ]
     for copy in copies:
         copy.start()
-    for copy in copies:
+    for copy in copies[2:]:
         copy.wait()
+    me, my_place = me_ref[0], me_ref[1]
     width = piece_refs[0].shape[1]
     full_ref[...] = jnp.dot(d_buf[...], b_buf[...], preferred_element_type=jnp.float32).astype(jnp.bfloat16)
     for j in range(PAIR):
-        piece_refs[j][...] = full_ref[:, my_columns(me_ref[0] ^ j, width)]
+        piece_refs[j][...] = full_ref[:, my_columns(me ^ j, width)]
+    for copy in copies[:2]:
+        copy.wait()
+    levels, slots = col_ref.shape[0] + 1, col_ref.shape[-1]
+    row_at = lax.broadcasted_iota(jnp.int32, (n, slots), 0)
+    slot_at = lax.broadcasted_iota(jnp.int32, (n, slots), 1)
+    index_ref[...] = jnp.zeros_like(index_ref)
+    for level in range(1, levels):
+        rest = col_ref[level - 1, 0, 0]
+        first = jnp.zeros_like(rest)
+        for _ in range(1, level):
+            past = rest >= m * n
+            first += jnp.where(past, m, 0)
+            rest -= jnp.where(past, m * n, 0)
+        ahead = place[0] - my_place + jnp.zeros_like(rest)
+        for p in range(1, m):
+            ahead += jnp.where(rest >= p * n, place[p] - place[p - 1], 0)
+        entry = first + jnp.where(ahead < 0, ahead + m, ahead)
+        count = jnp.zeros_like(rest)
+        for q in range(n):
+            count = jnp.where(row_at == q, count_ref[level - 1, 0, 0, q], count)
+        index_ref[(level - 1) * n : level * n, :slots] = jnp.where(slot_at < count, entry, -1)
 
 
 def my_columns(me, width):
     return pl.ds(pl.multiple_of((me & 1) * width, LANES), width)
 
 
-def gather_kernel(n, level, m, early, late, me_ref, index_ref, *refs):
-    l_refs, refs = refs[:PAIR], refs[PAIR:]
+def gather_kernel(n, level, m, early, late, me_ref, *refs):
+    index_refs, l_refs, refs = refs[:PAIR], refs[PAIR : 2 * PAIR], refs[2 * PAIR :]
     old_refs, refs = refs[: level - 1], refs[level - 1 :]
-    x_refs, (total_ref, chosen_ref, known, buf, sems) = refs[:-5], refs[-5:]
-    copies = [pltpu.make_async_copy(l_refs[j].at[level - 1, 0, 0], buf.at[j], sems.at[j]) for j in range(PAIR)]
-    for copy in copies:
-        copy.start()
+    x_refs, (total_ref, chosen_ref, known, own, sem) = refs[:-5], refs[-5:]
+    copy = pltpu.make_async_copy(l_refs[0].at[level - 1, 0, 0], own, sem)
+    copy.start()
     me = me_ref[0]
     size, width = total_ref.shape[1:]
-    slots = buf.shape[2]
+    slots = l_refs[0].shape[4]
     base = (level - 1) * m
     for back in range(level - 1):
         known[back * m : (back + 1) * m] = old_refs[back][...]
@@ -109,15 +132,16 @@
         known[base + d] = x_ref[...]
     none = jnp.zeros((size, width), jnp.bfloat16)
     no_block = jnp.zeros((size, size), jnp.bfloat16)
-    for j in range(PAIR):
-        copies[j].wait()
+    for j in reversed(range(PAIR)):
+        if j == 0:
+            copy.wait()
         for jq in range(n):
             q = me ^ jq
             blocks, solved, chosen = [], [], [no_block] * len(late)
             for k in range(slots):
-                entry = index_ref[((j * index_ref.shape[0] // (PAIR * n * slots) + level - 1) * n + q) * slots + k]
+                entry = index_refs[j][(level - 1) * n + q, k]
                 use = entry >= 0
-                block = buf[j, q, k]
+                block = l_refs[j][level - 1, 0, 0, q, k] if j else own[q, k]
                 for i, d in enumerate(late):
                     is_late = entry == base + d
                     use = jnp.logical_and(use, entry != base + d)
@@ -127,37 +151,31 @@
             product = jnp.dot(
                 jnp.concatenate(blocks, axis=1), jnp.concatenate(solved, axis=0), preferred_element_type=jnp.float32
             )
-            total_ref[jq] = product if j == 0 else total_ref[jq] + product
+            total_ref[jq] = product if j == PAIR - 1 else total_ref[jq] + product
             for i in range(len(late)):
                 at = (i * PAIR + j) * size
                 chosen_ref[jq, :, at : at + size] = chosen[i]
 
 
-def late_kernel(n, m, early, late, total_ref, chosen_ref, *refs):
+def late_kernel(n, early, late, final, total_ref, chosen_ref, *refs):
     x_refs, refs = refs[: len(early)], refs[len(early) :]
-    halves, refs = refs[:PAIR], refs[PAIR:]
-    late_refs, refs = refs[: len(late) - 1], refs[len(late) - 1 :]
-    panels_ref, keep_ref, send_refs = refs[0], refs[1], refs[2:]
-    panels = []
-    rest = iter(late_refs)
-    for d in late:
-        if d == m // 2:
-            found = [halves[j][...] for j in range(PAIR)]
-        else:
-            ref = next(rest)
-            found = [ref[j] for j in range(PAIR)]
-        panels += found
-        for j in range(PAIR):
-            panels_ref[d, j] = found[j]
-    panels = jnp.concatenate(panels, axis=0)
+    late_refs, refs = refs[: len(late)], refs[len(late) :]
+    if not final:
+        panels_ref, refs = refs[0], refs[1:]
+    keep_ref, send_refs = refs[0], refs[1:]
+    for d, x_ref in zip(late if not final else (), late_refs):
+        panels_ref[d] = x_ref[...]
+    panels = jnp.concatenate([x_ref[j] for x_ref in late_refs for j in range(PAIR)], axis=0)
+    rows = 1 if final else PAIR
     for jq in reversed(range(n)):
         total = total_ref[jq] + jnp.dot(chosen_ref[jq], panels, preferred_element_type=jnp.float32)
-        if jq < PAIR:
+        if jq < rows:
             keep_ref[jq] = total
         else:
-            send_refs[jq // PAIR - 1][jq % PAIR] = total.astype(jnp.bfloat16)
-    for d, x_ref in zip(early, x_refs):
-        panels_ref[d] = x_ref[...]
+            send_refs[jq // rows - 1][jq % rows] = total.astype(jnp.bfloat16)
+    if not final:
+        for d, x_ref in zip(early, x_refs):
+            panels_ref[d] = x_ref[...]
 
 
 def solve_kernel(level, me_ref, keep_ref, *refs):
@@ -175,17 +193,31 @@
         piece_refs[j][...] = value
 
 
-def last_kernel(me_ref, full_ref, *refs):
-    out_ref, sems = refs[-2:]
-    width = refs[0].shape[1]
+def last_kernel(n, me_ref, b_ref, d_ref, keep_ref, *refs):
+    other_refs, refs = refs[: n - 1], refs[n - 1 :]
+    full_ref, refs = refs[0], refs[1:]
+    piece_refs, (out_ref, buf, sems) = refs[:-3], refs[-3:]
+    me = me_ref[0]
+    width = keep_ref.shape[2]
+    levels = out_ref.shape[0]
     copies = [pltpu.make_async_copy(full_ref, out_ref.at[0, 0, 0], sems.at[0])]
-    for level in range(1, out_ref.shape[0]):
-        for j in range(PAIR):
-            at = (level - 1) * PAIR + j
-            target = out_ref.at[level, 0, 0, :, my_columns(me_ref[0] ^ j, width)]
-            copies.append(pltpu.make_async_copy(refs[at], target, sems.at[1 + at]))
+    for i, ref in enumerate(piece_refs):
+        target = out_ref.at[1 + i // PAIR, 0, 0, :, my_columns(me ^ (i % PAIR), width)]
+        copies.append(pltpu.make_async_copy(ref, target, sems.at[1 + i]))
     for copy in copies:
         copy.start()
+    for j in range(PAIR):
+        total = keep_ref[0] if j == 0 else jnp.zeros_like(keep_ref[0])
+        for jq in range(1, n):
+            if jq % PAIR == j:
+                total += other_refs[jq - 1][0].astype(jnp.float32)
+        columns = my_columns(me ^ j, width)
+        resid = (b_ref[levels - 1, 0, 0, :, columns].astype(jnp.float32) - total).astype(jnp.bfloat16)
+        value = jnp.dot(d_ref[levels - 1, 0, 0], resid, preferred_element_type=jnp.float32)
+        buf[:, columns] = value.astype(jnp.bfloat16)
+        target = out_ref.at[levels - 1, 0, 0, :, columns]
+        copies.append(pltpu.make_async_copy(buf.at[:, columns], target, sems.at[1 + len(piece_refs) + j]))
+        copies[-1].start()
     for copy in copies:
         copy.wait()
 
@@ -205,13 +237,10 @@
 
     def advance(self):
         self.step += 1
-        final = 2 * self.step == self.size
-        if final:
-            self.behind, self.ahead = self.behind[0], self.ahead[1]
         self.behind = lax.ppermute(self.behind, "prow", self.to_next)
-        self.ahead = lax.ppermute(self.ahead, "prow", self.to_last)
-        if not final:
-            self.found[self.size - self.step] = self.behind
+        self.found[self.size - self.step] = self.behind
+        if self.step < self.size - self.step:
+            self.ahead = lax.ppermute(self.ahead, "prow", self.to_last)
             self.found[self.step] = self.ahead
 
 
@@ -228,64 +257,70 @@
     def send(value, bits):
         return lax.ppermute(value, "pcol", [(i, i ^ bits) for i in range(n)])
 
-    full, *pieces = pl.pallas_call(
-        first_kernel,
-        out_shape=[near((size, front))] + [near((size, width))] * PAIR,
-        in_specs=[smem()] + [anywhere()] * 2,
-        out_specs=[vmem()] * (1 + PAIR),
+    index_shape = (-(-(levels - 1) * n // 8) * 8, LANES)
+
+    full, index, *pieces = pl.pallas_call(
+        functools.partial(first_kernel, n, m, place),
+        out_shape=[near((size, front)), near(index_shape, jnp.int32)] + [near((size, width))] * PAIR,
+        in_specs=[smem()] + [anywhere()] * 4,
+        out_specs=[vmem()] * (2 + PAIR),
         scratch_shapes=[
             pltpu.VMEM((size, front), jnp.bfloat16),
             pltpu.VMEM((size, size), jnp.bfloat16),
-            pltpu.SemaphoreType.DMA((2,)),
+            pltpu.SMEM(live_counts.shape, jnp.int32),
+            pltpu.VMEM(block_cols.shape, jnp.int32),
+            pltpu.SemaphoreType.DMA((4,)),
         ],
         compiler_params=params(),
-    )(me, in_hbm(b_panels), in_hbm(diag_inverse))
-    solved = jnp.stack([pieces[0], send(pieces[1], 1)])
-
-    chosen, counts = block_cols[:, 0, 0], live_counts[:, 0, 0]
-    row_of = chosen % (m * n) // n
-    place_of = sum(jnp.where(row_of == p, place[p], 0) for p in range(m))
-    entry = chosen // (m * n) * m + (place_of - my_place + m) % m
-    entry = jnp.where(jnp.arange(slots)[None, None, :] < counts[:, :, None], entry, -1).reshape(-1)
-    index = jnp.concatenate([entry, send(after(entry, solved), 1)])
-
+    )(me, *[in_hbm(v) for v in (live_counts, block_cols, b_panels, diag_inverse)])
+    index = [index, send(index, 1)]
+    solved = after(jnp.stack([pieces[0], send(pieces[1], 1)]), index[1])
     b, inverse, blocks = [[v, send(after(v, solved), 1)] for v in (b_panels, diag_inverse, l_blocks)]
+    blocks[0] = in_hbm(l_blocks)
+
     late = [d for d in range(1, m) if min(d, m - d) >= m // 2 - 1]
     early = [d for d in range(m) if d not in late]
     columns, kept = [], []
     for level in range(1, levels):
+        final = level == levels - 1
         ring = Ring(solved, cycle)
-        for step in range(m // 2):
+        for _ in range(m // 2):
             ring.advance()
         total, chosen = pl.pallas_call(
             functools.partial(gather_kernel, n, level, m, early, late),
             out_shape=[near((n, size, width), jnp.float32), near((n, size, len(late) * PAIR * size))],
-            in_specs=[smem()] * 2 + [anywhere()] * PAIR + [vmem()] * (len(kept) + len(early)),
+            in_specs=[smem()] * (1 + PAIR) + [anywhere()] + [vmem()] * (PAIR - 1 + len(kept) + len(early)),
             out_specs=[vmem()] * 2,
             scratch_shapes=[
                 pltpu.VMEM((level * m, PAIR, size, width), jnp.bfloat16),
-                pltpu.VMEM((PAIR, n, slots, size, size), jnp.bfloat16),
-                pltpu.SemaphoreType.DMA((PAIR,)),
+                pltpu.VMEM(l_blocks.shape[3:], jnp.bfloat16),
+                pltpu.SemaphoreType.DMA,
             ],
             compiler_params=params(),
-        )(me, index, *[in_hbm(v) for v in blocks], *kept, *[ring.found[d] for d in early])
-        panels, keep, *away = pl.pallas_call(
-            functools.partial(late_kernel, n, m, early, late),
-            out_shape=[near((m, PAIR, size, width)), near((PAIR, size, width), jnp.float32)]
-            + [near((PAIR, size, width))] * (n // PAIR - 1),
-            in_specs=[vmem()] * (2 + len(early) + PAIR + len(late) - 1),
-            out_specs=[vmem()] * (1 + n // PAIR),
+        )(me, *index, *blocks, *kept, *[ring.found[d] for d in early])
+        rows = 1 if final else PAIR
+        out_shape = [near((rows, size, width), jnp.float32)] + [near((rows, size, width))] * (n // rows - 1)
+        if not final:
+            out_shape = [near((m, PAIR, size, width))] + out_shape
+        found = pl.pallas_call(
+            functools.partial(late_kernel, n, early, late, final),
+            out_shape=out_shape,
+            in_specs=[vmem()] * (2 + m),
+            out_specs=[vmem()] * len(out_shape),
             compiler_params=params(),
         )(
             total,
             chosen,
-            *[ring.found[d] for d in early],
-            ring.behind,
-            ring.ahead,
-            *[ring.found[d] for d in late if d != m // 2],
+            *[ring.found[d] for d in early + late],
         )
-        kept.append(panels)
-        others = [send(v, PAIR * (h + 1)) for h, v in enumerate(away)]
+        if not final:
+            panels, *found = found
+            kept.append(panels)
+        keep, *away = found
+        others = [send(v, rows * (h + 1)) for h, v in enumerate(away)]
+        if final:
+            columns = [send(after(v, keep), 1) if i % PAIR else v for i, v in enumerate(columns)]
+            break
         solved, *pieces = pl.pallas_call(
             functools.partial(solve_kernel, level),
             out_shape=[near((PAIR, size, width))] + [near((size, width))] * PAIR,
@@ -293,16 +328,19 @@
             out_specs=[vmem()] * (1 + PAIR),
             compiler_params=params(),
         )(me, keep, *b, *inverse, *others)
-        columns += [pieces[0], send(pieces[1], 1)]
+        columns += pieces
 
     return pl.pallas_call(
-        last_kernel,
+        functools.partial(last_kernel, n),
         out_shape=struct(b_panels.shape),
-        in_specs=[smem()] + [vmem()] * (1 + len(columns)),
+        in_specs=[smem()] + [vmem()] * (4 + len(others) + len(columns)),
         out_specs=anywhere(),
-        scratch_shapes=[pltpu.SemaphoreType.DMA((1 + len(columns),))],
+        scratch_shapes=[
+            pltpu.VMEM((size, front), jnp.bfloat16),
+            pltpu.SemaphoreType.DMA((1 + PAIR + len(columns),)),
+        ],
         compiler_params=params(),
-    )(me, full, *columns)
+    )(me, b_panels, diag_inverse, keep, *others, full, *columns)
 
 
 def cycle_of(mesh):
@@ -334,7 +372,8 @@
     def shards(b_panels, diag_inverse, l_blocks, block_cols, live_counts):
         front = b_panels.shape[-1]
         rows = mesh.shape["prow"]
-        paired = n & (n - 1) == 0 and n >= PAIR and rows % 2 == 0 and front % (PAIR * LANES) == 0
+        paired = n & (n - 1) == 0 and n >= PAIR and rows % 2 == 0 and rows > 2 and front % (PAIR * LANES) == 0
+        paired = paired and b_panels.shape[0] > 1
         if paired and l_blocks.size * l_blocks.dtype.itemsize <= BLOCK_BYTES:
             return solve_paired(cycle, b_panels, diag_inverse, l_blocks, block_cols, live_counts)
         return solve_scattered(b_panels, diag_inverse, l_blocks, block_cols, live_counts)

time: 67.5 us -> 61.7 us (0.914)
  local copies, waits for them, and re-layouts: 1.98 us -> 0.01 us
  Pallas kernels: 12.3 us -> 10.4 us
  other arithmetic: 0.95 us -> 0.09 us
  waiting for transfers between devices: 30.7 us -> 30 us
    ppermute x8, waiting for transfers between devices: 17 us -> 21.5 us  [advance(): self.behind = lax.ppermute(self.behind, 'prow', self.to_next)]
    ppermute x8 -> x6, waiting for transfers between devices: 4.52 us -> 0.33 us  [advance(): self.ahead = lax.ppermute(self.ahead, 'prow', self.to_last)]
    pallas_call x2 -> x1, Pallas kernels: 2.14 us -> 0.74 us  [solve_paired(): pl.pallas_call(functools.partial(solve_kernel, level), out_shape=[near((P...]
    unnamed x6 -> x4, local copies, waits for them, and re-layouts: 1.09 us -> 0.01 us
    ppermute x9 -> x10, waiting for transfers between devices: 9.16 us -> 8.11 us  [send(): return lax.ppermute(value, 'pcol', [(i, i ^ bits) for i in range(n)])]
    squeeze x5 -> x0, local copies, waits for them, and re-layouts: 0.79 us -> none  [the longest x1 0.77 us: solve_paired(): chosen, counts = (block_cols[:, 0, 0], live_counts[:, 0, 0])]
    lt x1 -> x0, other arithmetic: 0.75 us -> none  [solve_paired(): jnp.arange(slots)[None, None, :] < counts[:, :, None]]
    pallas_call x4, Pallas kernels: 4.68 us -> 3.93 us  [the longest x1 1.73 us: solve_paired(): pl.pallas_call(functools.partial(first_kernel, n, m, place), out_shape=[n...]
  transfers between devices with their start and end apart: 25 -> 24, of which waited for: 15 -> 15; matrix products, arithmetic and copies ran while one was open for 3% -> 0% of each run, Pallas kernels for 11% -> 10%
where the time goes in v3:
time: 61.7 us; the launch traced here: 61.5 us
  waiting for transfers between devices  30 us (49%)
  starting transfers between devices  20.9 us (34%)
  Pallas kernels  10.4 us (17%)
    ppermute x8, waiting for transfers between devices, advance(): self.behind = lax.ppermute(self.behind, 'prow', self.to_next)  21.5 us
    ppermute x8, starting transfers between devices, advance(): self.behind = lax.ppermute(self.behind, 'prow', self.to_next)  14.6 us
    ppermute x10, waiting for transfers between devices, send(): return lax.ppermute(value, 'pcol', [(i, i ^ bits) for i in range(n)])  8.11 us
    pallas_call x2, Pallas kernels, solve_paired(): pl.pallas_call(functools.partial(gather_kernel, n, level, m, early, late)...  5.69 us
    ppermute x10, starting transfers between devices, send(): return lax.ppermute(value, 'pcol', [(i, i ^ bits) for i in range(n)])  4.49 us
    ppermute x6, starting transfers between devices, advance(): self.ahead = lax.ppermute(self.ahead, 'prow', self.to_last)  1.79 us
    pallas_call x1, Pallas kernels, solve_paired(): pl.pallas_call(functools.partial(first_kernel, n, m, place), out_shape=[n...  1.73 us
    pallas_call x1, Pallas kernels, solve_paired(): pl.pallas_call(functools.partial(last_kernel, n), out_shape=struct(b_pane...  1.44 us
  transfers between devices with their start and end apart: 24, of which 15 were waited for; matrix products, arithmetic and copies ran while one was open for 0% of the time, Pallas kernels for 10%

profile of v3, /device:TPU:0, one launch (start us, length us, event | category | flops | bytes accessed | tf_op | source)
XLA Modules:
  0.0 61.5 jit_solution(15291648568559731788)
XLA Ops:
  0.0 0.1 pad_add_fusion.me_ref
  0.1 1.7 %shard_map.55 = (bf16[128,512]{1,0:T(8,128)(2,1)S(1)}, s32[8,128]{1,0:T(8,128)S(1)}, bf16[128,256]{1,0:T(8,128)(2,1)S(1)}, bf16[128,256]{1,0:T(8,128)(2,1)S(1)}) custom-call(s32[2]{0:T(128)S(1)} %pad_add_fusion.me_ref, s32[2,1,1,4]{3,2,1,0:T(1,128)} %counts_ref.1, s32[2,1,1,4,5]{4,3,2,1,0:T(4,128)} %cols_ref.1, bf16[3,1,1,128,512]{4,3,2,1,0:T(8,128)(2,1)} %b_ref.3, ...), custom_call_target="tpu_custom_call" | custom-call | tf_op jit(solution)/shard_map/pallas_call | solution.py:262
  1.8 0.5 collective-permute-start.1
  2.3 0.1 collective-permute-start
  2.4 0.8 %collective-permute-done.1 = bf16[128,256]{1,0:T(8,128)(2,1)S(1)} collective-permute-done((bf16[128,256]{1,0:T(8,128)(2,1)S(1)}, bf16[128,256]{1,0:T(8,128)(2,1)S(1)}, u32[]{:S(2)}, u32[]{:S(2)}) %collective-permute-start.1) | collective-permute-done | bytes 65568 | tf_op jit(solution)/shard_map/ppermute | solution.py:258
  3.3 0.2 collective-permute-done.refs_1_
  3.5 0.2 collective-permute-start.2
  3.7 2.8 %collective-permute-start.5 = (bf16[2,128,256]{2,1,0:T(8,128)(2,1)S(1)}, bf16[2,128,256]{2,1,0:T(8,128)(2,1)S(1)}, u32[]{:S(2)}, u32[]{:S(2)}) collective-permute-start(bf16[2,128,256]{2,1,0:T(8,128)(2,1)S(1)} %pad_maximum_fusion.refs_4_.refs_0_), channel_id=1, source_target_pairs={{0,4},{4,12},{12,20},{20,28},{28,24},{24,16},{16,8},{8,0},{1,5},{5... | collective-permute-start | bytes 393224 | tf_op jit(solution)/shard_map/ppermute | solution.py:240
  6.5 0.1 collective-permute-start.3
  6.6 3.8 %collective-permute-done.5.refs_8_.refs_4_ = bf16[2,128,256]{2,1,0:T(8,128)(2,1)S(1)} collective-permute-done((bf16[2,128,256]{2,1,0:T(8,128)(2,1)S(1)}, bf16[2,128,256]{2,1,0:T(8,128)(2,1)S(1)}, u32[]{:S(2)}, u32[]{:S(2)}) %collective-permute-start.5) | collective-permute-done | bytes 131104 | tf_op jit(solution)/shard_map/ppermute | solution.py:240
  10.4 1.7 %collective-permute-start.6 = (bf16[2,128,256]{2,1,0:T(8,128)(2,1)S(1)}, bf16[2,128,256]{2,1,0:T(8,128)(2,1)S(1)}, u32[]{:S(2)}, u32[]{:S(2)}) collective-permute-start(bf16[2,128,256]{2,1,0:T(8,128)(2,1)S(1)} %collective-permute-done.5.refs_8_.refs_4_), channel_id=1, source_target_pairs={{0,4},{4,12},{12,20},{20,28},{28,24},{24,16},{16,8},{8,0},{1,5},{5... | collective-permute-start | bytes 393224 | tf_op jit(solution)/shard_map/ppermute | solution.py:240
  12.1 0.0 collective-permute-done.3.refs_5_.refs_1_
  12.1 0.4 collective-permute-start.4
  12.5 3.0 %collective-permute-done.6.refs_7_.refs_3_ = bf16[2,128,256]{2,1,0:T(8,128)(2,1)S(1)} collective-permute-done((bf16[2,128,256]{2,1,0:T(8,128)(2,1)S(1)}, bf16[2,128,256]{2,1,0:T(8,128)(2,1)S(1)}, u32[]{:S(2)}, u32[]{:S(2)}) %collective-permute-start.6) | collective-permute-done | bytes 131104 | tf_op jit(solution)/shard_map/ppermute | solution.py:240
  15.5 1.5 %collective-permute-start.8 = (bf16[2,128,256]{2,1,0:T(8,128)(2,1)S(1)}, bf16[2,128,256]{2,1,0:T(8,128)(2,1)S(1)}, u32[]{:S(2)}, u32[]{:S(2)}) collective-permute-start(bf16[2,128,256]{2,1,0:T(8,128)(2,1)S(1)} %collective-permute-done.6.refs_7_.refs_3_), channel_id=1, source_target_pairs={{0,4},{4,12},{12,20},{20,28},{28,24},{24,16},{16,8},{8,0},{1,5},{5... | collective-permute-start | bytes 393224 | tf_op jit(solution)/shard_map/ppermute | solution.py:240
  17.0 0.0 collective-permute-start.10
  17.1 0.0 collective-permute-done.4.refs_6_.refs_2_
  17.1 0.5 collective-permute-start.7
  17.5 2.9 %collective-permute-done.8.refs_7_ = bf16[2,128,256]{2,1,0:T(8,128)(2,1)S(1)} collective-permute-done((bf16[2,128,256]{2,1,0:T(8,128)(2,1)S(1)}, bf16[2,128,256]{2,1,0:T(8,128)(2,1)S(1)}, u32[]{:S(2)}, u32[]{:S(2)}) %collective-permute-start.8) | collective-permute-done | bytes 131104 | tf_op jit(solution)/shard_map/ppermute | solution.py:240
  20.5 1.6 %collective-permute-start.9 = (bf16[2,128,256]{2,1,0:T(8,128)(2,1)S(1)}, bf16[2,128,256]{2,1,0:T(8,128)(2,1)S(1)}, u32[]{:S(2)}, u32[]{:S(2)}) collective-permute-start(bf16[2,128,256]{2,1,0:T(8,128)(2,1)S(1)} %collective-permute-done.8.refs_7_), channel_id=1, source_target_pairs={{0,4},{4,12},{12,20},{20,28},{28,24},{24,16},{16,8},{8,0},{1,5},{5... | collective-permute-start | bytes 393224 | tf_op jit(solution)/shard_map/ppermute | solution.py:240
  22.1 0.0 collective-permute-done.2.refs_3_
  22.1 2.8 %shard_map.56 = (f32[4,128,256]{2,1,0:T(8,128)S(1)}, bf16[4,128,768]{2,1,0:T(8,128)(2,1)S(1)}) custom-call(s32[2]{0:T(128)S(1)} %pad_add_fusion.me_ref, s32[8,128]{1,0:T(8,128)S(1)} %get-tuple-element.28.refs_0_, s32[8,128]{1,0:T(8,128)S(1)} %collective-permute-done.refs_1_, bf16[2,1,1,4,5,128,128]{6,5,4,3,2,1,0:T(8,128)(2,1)} %refs_2_.5, ...), custom_call_target="tpu_custom_call" | custom-call | tf_op jit(solution)/shard_map/pallas_call | solution.py:289
  24.9 0.0 copy-start.1
  24.9 0.0 copy-start
  24.9 0.0 collective-permute-done.7.refs_5_
  24.9 0.5 collective-permute-done.9.refs_6_
  25.4 0.4 shard_map.57
  25.8 1.7 %collective-permute-start.12 = (bf16[2,128,256]{2,1,0:T(8,128)(2,1)S(1)}, bf16[2,128,256]{2,1,0:T(8,128)(2,1)S(1)}, u32[]{:S(2)}, u32[]{:S(2)}) collective-permute-start(bf16[2,128,256]{2,1,0:T(8,128)(2,1)S(1)} %get-tuple-element.39), channel_id=1, source_target_pairs={{0,2},{1,3},{2,0},{3,1},{4,6},{5,7},{6,4},{7,5},{8,10},{9,11},{10,... | collective-permute-start | bytes 393224 | tf_op jit(solution)/shard_map/ppermute | solution.py:258
  27.5 0.0 copy-done.1
  27.5 0.0 collective-permute-start.11
  27.5 1.3 %collective-permute-done.11.refs_3_ = bf16[3,1,1,128,128]{4,3,2,1,0:T(8,128)(2,1)S(1)} collective-permute-done((bf16[3,1,1,128,128]{4,3,2,1,0:T(8,128)(2,1)S(1)}, bf16[3,1,1,128,128]{4,3,2,1,0:T(8,128)(2,1)S(1)}, u32[]{:S(2)}, u32[]{:S(2)}) %collective-permute-start.11) | collective-permute-done | bytes 98336 | tf_op jit(solution)/shard_map/ppermute | solution.py:258
  28.8 0.0 collective-permute-done.10.refs_1_
  28.8 2.0 %collective-permute-done.12.refs_4_ = bf16[2,128,256]{2,1,0:T(8,128)(2,1)S(1)} collective-permute-done((bf16[2,128,256]{2,1,0:T(8,128)(2,1)S(1)}, bf16[2,128,256]{2,1,0:T(8,128)(2,1)S(1)}, u32[]{:S(2)}, u32[]{:S(2)}) %collective-permute-start.12) | collective-permute-done | bytes 131104 | tf_op jit(solution)/shard_map/ppermute | solution.py:258
  30.9 0.0 copy-done
  30.9 0.7 %shard_map.58 = (bf16[2,128,256]{2,1,0:T(8,128)(2,1)S(1)}, bf16[128,256]{1,0:T(8,128)(2,1)S(1)}, bf16[128,256]{1,0:T(8,128)(2,1)S(1)}) custom-call(s32[2]{0:T(128)S(1)} %pad_add_fusion.me_ref, f32[2,128,256]{2,1,0:T(8,128)S(1)} %get-tuple-element.36.keep_ref, bf16[3,1,1,128,512]{4,3,2,1,0:T(8,128)(2,1)S(1)} %copy-done, ...), custom_call_target="tpu_custom_call" | custom-call | tf_op jit(solution)/shard_map/pallas_call | solution.py:324
  31.6 1.7 %collective-permute-start.15 = (bf16[2,128,256]{2,1,0:T(8,128)(2,1)S(1)}, bf16[2,128,256]{2,1,0:T(8,128)(2,1)S(1)}, u32[]{:S(2)}, u32[]{:S(2)}) collective-permute-start(bf16[2,128,256]{2,1,0:T(8,128)(2,1)S(1)} %get-tuple-element.40.refs_5_.refs_0_), channel_id=1, source_target_pairs={{0,4},{4,12},{12,20},{20,28},{28,24},{24,16},{16,8},{8,0},{1,5},{5... | collective-permute-start | bytes 393224 | tf_op jit(solution)/shard_map/ppermute | solution.py:240
  33.3 0.4 collective-permute-start.13
  33.7 3.4 %collective-permute-done.15.refs_9_.refs_4_ = bf16[2,128,256]{2,1,0:T(8,128)(2,1)S(1)} collective-permute-done((bf16[2,128,256]{2,1,0:T(8,128)(2,1)S(1)}, bf16[2,128,256]{2,1,0:T(8,128)(2,1)S(1)}, u32[]{:S(2)}, u32[]{:S(2)}) %collective-permute-start.15) | collective-permute-done | bytes 131104 | tf_op jit(solution)/shard_map/ppermute | solution.py:240
  37.1 1.7 %collective-permute-start.16 = (bf16[2,128,256]{2,1,0:T(8,128)(2,1)S(1)}, bf16[2,128,256]{2,1,0:T(8,128)(2,1)S(1)}, u32[]{:S(2)}, u32[]{:S(2)}) collective-permute-start(bf16[2,128,256]{2,1,0:T(8,128)(2,1)S(1)} %collective-permute-done.15.refs_9_.refs_4_), channel_id=1, source_target_pairs={{0,4},{4,12},{12,20},{20,28},{28,24},{24,16},{16,8},{8,0},{1,5},{5... | collective-permute-start | bytes 393224 | tf_op jit(solution)/shard_map/ppermute | solution.py:240
  38.8 0.3 collective-permute-done.13.refs_6_.refs_1_
  39.1 0.3 collective-permute-start.14
  39.4 3.9 %collective-permute-done.16.refs_8_.refs_3_ = bf16[2,128,256]{2,1,0:T(8,128)(2,1)S(1)} collective-permute-done((bf16[2,128,256]{2,1,0:T(8,128)(2,1)S(1)}, bf16[2,128,256]{2,1,0:T(8,128)(2,1)S(1)}, u32[]{:S(2)}, u32[]{:S(2)}) %collective-permute-start.16) | collective-permute-done | bytes 131104 | tf_op jit(solution)/shard_map/ppermute | solution.py:240
  43.3 1.9 %collective-permute-start.18 = (bf16[2,128,256]{2,1,0:T(8,128)(2,1)S(1)}, bf16[2,128,256]{2,1,0:T(8,128)(2,1)S(1)}, u32[]{:S(2)}, u32[]{:S(2)}) collective-permute-start(bf16[2,128,256]{2,1,0:T(8,128)(2,1)S(1)} %collective-permute-done.16.refs_8_.refs_3_), channel_id=1, source_target_pairs={{0,4},{4,12},{12,20},{20,28},{28,24},{24,16},{16,8},{8,0},{1,5},{5... | collective-permute-start | bytes 393224 | tf_op jit(solution)/shard_map/ppermute | solution.py:240
  45.2 0.0 collective-permute-done.14.refs_7_.refs_2_
  45.2 0.2 collective-permute-start.17
  45.3 3.6 %collective-permute-done.18.refs_7_ = bf16[2,128,256]{2,1,0:T(8,128)(2,1)S(1)} collective-permute-done((bf16[2,128,256]{2,1,0:T(8,128)(2,1)S(1)}, bf16[2,128,256]{2,1,0:T(8,128)(2,1)S(1)}, u32[]{:S(2)}, u32[]{:S(2)}) %collective-permute-start.18) | collective-permute-done | bytes 131104 | tf_op jit(solution)/shard_map/ppermute | solution.py:240
  48.9 1.7 %collective-permute-start.19 = (bf16[2,128,256]{2,1,0:T(8,128)(2,1)S(1)}, bf16[2,128,256]{2,1,0:T(8,128)(2,1)S(1)}, u32[]{:S(2)}, u32[]{:S(2)}) collective-permute-start(bf16[2,128,256]{2,1,0:T(8,128)(2,1)S(1)} %collective-permute-done.18.refs_7_), channel_id=1, source_target_pairs={{0,4},{4,12},{12,20},{20,28},{28,24},{24,16},{16,8},{8,0},{1,5},{5... | collective-permute-start | bytes 393224 | tf_op jit(solution)/shard_map/ppermute | solution.py:240
  50.7 2.9 %shard_map.59 = (f32[4,128,256]{2,1,0:T(8,128)S(1)}, bf16[4,128,768]{2,1,0:T(8,128)(2,1)S(1)}) custom-call(s32[2]{0:T(128)S(1)} %pad_add_fusion.me_ref, s32[8,128]{1,0:T(8,128)S(1)} %get-tuple-element.28.refs_0_, s32[8,128]{1,0:T(8,128)S(1)} %collective-permute-done.refs_1_, bf16[2,1,1,4,5,128,128]{6,5,4,3,2,1,0:T(8,128)(2,1)} %refs_2_.5, ...), custom_call_target="tpu_custom_call" | custom-call | tf_op jit(solution)/shard_map/pallas_call | solution.py:289
  53.6 0.0 collective-permute-done.17.refs_5_
  53.6 0.3 collective-permute-done.19.refs_6_
  53.9 0.4 shard_map.60
  54.3 0.1 collective-permute-start.23
  54.4 0.5 collective-permute-start.20
  54.9 0.8 %collective-permute-start.21 = (bf16[1,128,256]{2,1,0:T(8,128)(2,1)S(1)}, bf16[1,128,256]{2,1,0:T(8,128)(2,1)S(1)}, u32[]{:S(2)}, u32[]{:S(2)}) collective-permute-start(bf16[1,128,256]{2,1,0:T(8,128)(2,1)S(1)} %get-tuple-element.45), channel_id=1, source_target_pairs={{0,2},{1,3},{2,0},{3,1},{4,6},{5,7},{6,4},{7,5},{8,10},{9,11},{10,... | collective-permute-start | bytes 196616 | tf_op jit(solution)/shard_map/ppermute | solution.py:258
  55.6 0.7 %collective-permute-start.22 = (bf16[1,128,256]{2,1,0:T(8,128)(2,1)S(1)}, bf16[1,128,256]{2,1,0:T(8,128)(2,1)S(1)}, u32[]{:S(2)}, u32[]{:S(2)}) collective-permute-start(bf16[1,128,256]{2,1,0:T(8,128)(2,1)S(1)} %get-tuple-element.46), channel_id=1, source_target_pairs={{0,3},{1,2},{2,1},{3,0},{4,7},{5,6},{6,5},{7,4},{8,11},{9,10},{10,... | collective-permute-start | bytes 196616 | tf_op jit(solution)/shard_map/ppermute | solution.py:258
  56.3 0.0 collective-permute-done.23.refs_5_
  56.3 0.0 collective-permute-done.20.refs_0_
  56.3 3.3 %collective-permute-done.21.refs_1_ = bf16[1,128,256]{2,1,0:T(8,128)(2,1)S(1)} collective-permute-done((bf16[1,128,256]{2,1,0:T(8,128)(2,1)S(1)}, bf16[1,128,256]{2,1,0:T(8,128)(2,1)S(1)}, u32[]{:S(2)}, u32[]{:S(2)}) %collective-permute-start.21) | collective-permute-done | bytes 65568 | tf_op jit(solution)/shard_map/ppermute | solution.py:258
  59.7 0.4 collective-permute-done.22.refs_2_
  60.0 1.4 %shard_map.61 = bf16[3,1,1,128,512]{4,3,2,1,0:T(8,128)(2,1)} custom-call(s32[2]{0:T(128)S(1)} %pad_add_fusion.me_ref, bf16[3,1,1,128,512]{4,3,2,1,0:T(8,128)(2,1)S(1)} %copy-done, bf16[3,1,1,128,128]{4,3,2,1,0:T(8,128)(2,1)S(1)} %copy-done.1, f32[1,128,256]{2,1,0:T(8,128)S(1)} %get-tuple-element.43.keep_ref, ...), custom_call_target="tpu_custom_call" | custom-call | tf_op jit(solution)/shard_map/pallas_call | solution.py:333
  (1 shorter events, 0.0 us)
Async XLA Ops:
  1.8 1.4 %collective-permute-start.1 = (bf16[128,256]{1,0:T(8,128)(2,1)S(1)}, bf16[128,256]{1,0:T(8,128)(2,1)S(1)}, u32[]{:S(2)}, u32[]{:S(2)}) collective-permute-start(bf16[128,256]{1,0:T(8,128)(2,1)S(1)} %get-tuple-element.30), channel_id=1, source_target_pairs={{0,1},{1,0},{2,3},{3,2},{4,5},{5,4},{6,7},{7,6},{8,9},{9,8},{10,11... | collective-permute-start | bytes 196616 | tf_op jit(solution)/shard_map/ppermute | solution.py:258
  2.3 1.2 %collective-permute-start = (s32[8,128]{1,0:T(8,128)S(1)}, s32[8,128]{1,0:T(8,128)S(1)}, u32[]{:S(2)}, u32[]{:S(2)}) collective-permute-start(s32[8,128]{1,0:T(8,128)S(1)} %get-tuple-element.28.refs_0_), channel_id=1, source_target_pairs={{0,1},{1,0},{2,3},{3,2},{4,5},{5,4},{6,7},{7,6},{8,9},{9,8},{10,11... | collective-permute-start | bytes 12296 | tf_op jit(solution)/shard_map/ppermute | solution.py:258
  3.5 18.6 %collective-permute-start.2 = (bf16[2,1,1,4,5,128,128]{6,5,4,3,2,1,0:T(8,128)(2,1)}, bf16[2,1,1,4,5,128,128]{6,5,4,3,2,1,0:T(8,128)(2,1)S(1)}, u32[]{:S(2)}, u32[]{:S(2)}) collective-permute-start(bf16[2,1,1,4,5,128,128]{6,5,4,3,2,1,0:T(8,128)(2,1)} %refs_2_.5), channel_id=1, source_target_pairs={{0,1},{1,0},{2,3},{3,2},{4,5},{5,4},{6,7},{7,6},{8,9},{9,8},{10,11... | collective-permute-start | bytes 3932168 | tf_op jit(solution)/shard_map/ppermute | solution.py:258
  3.7 6.7 %collective-permute-start.5 = (bf16[2,128,256]{2,1,0:T(8,128)(2,1)S(1)}, bf16[2,128,256]{2,1,0:T(8,128)(2,1)S(1)}, u32[]{:S(2)}, u32[]{:S(2)}) collective-permute-start(bf16[2,128,256]{2,1,0:T(8,128)(2,1)S(1)} %pad_maximum_fusion.refs_4_.refs_0_), channel_id=1, source_target_pairs={{0,4},{4,12},{12,20},{20,28},{28,24},{24,16},{16,8},{8,0},{1,5},{5... | collective-permute-start | bytes 393224 | tf_op jit(solution)/shard_map/ppermute | solution.py:240
  6.5 5.6 %collective-permute-start.3 = (bf16[2,128,256]{2,1,0:T(8,128)(2,1)S(1)}, bf16[2,128,256]{2,1,0:T(8,128)(2,1)S(1)}, u32[]{:S(2)}, u32[]{:S(2)}) collective-permute-start(bf16[2,128,256]{2,1,0:T(8,128)(2,1)S(1)} %pad_maximum_fusion.refs_4_.refs_0_), channel_id=1, source_target_pairs={{4,0},{12,4},{20,12},{28,20},{24,28},{16,24},{8,16},{0,8},{5,1},{1... | collective-permute-start | bytes 393224 | tf_op jit(solution)/shard_map/ppermute | solution.py:243
  10.4 5.1 %collective-permute-start.6 = (bf16[2,128,256]{2,1,0:T(8,128)(2,1)S(1)}, bf16[2,128,256]{2,1,0:T(8,128)(2,1)S(1)}, u32[]{:S(2)}, u32[]{:S(2)}) collective-permute-start(bf16[2,128,256]{2,1,0:T(8,128)(2,1)S(1)} %collective-permute-done.5.refs_8_.refs_4_), channel_id=1, source_target_pairs={{0,4},{4,12},{12,20},{20,28},{28,24},{24,16},{16,8},{8,0},{1,5},{5... | collective-permute-start | bytes 393224 | tf_op jit(solution)/shard_map/ppermute | solution.py:240
  12.1 5.0 %collective-permute-start.4 = (bf16[2,128,256]{2,1,0:T(8,128)(2,1)S(1)}, bf16[2,128,256]{2,1,0:T(8,128)(2,1)S(1)}, u32[]{:S(2)}, u32[]{:S(2)}) collective-permute-start(bf16[2,128,256]{2,1,0:T(8,128)(2,1)S(1)} %collective-permute-done.3.refs_5_.refs_1_), channel_id=1, source_target_pairs={{4,0},{12,4},{20,12},{28,20},{24,28},{16,24},{8,16},{0,8},{5,1},{1... | collective-permute-start | bytes 393224 | tf_op jit(solution)/shard_map/ppermute | solution.py:243
  15.5 5.0 %collective-permute-start.8 = (bf16[2,128,256]{2,1,0:T(8,128)(2,1)S(1)}, bf16[2,128,256]{2,1,0:T(8,128)(2,1)S(1)}, u32[]{:S(2)}, u32[]{:S(2)}) collective-permute-start(bf16[2,128,256]{2,1,0:T(8,128)(2,1)S(1)} %collective-permute-done.6.refs_7_.refs_3_), channel_id=1, source_target_pairs={{0,4},{4,12},{12,20},{20,28},{28,24},{24,16},{16,8},{8,0},{1,5},{5... | collective-permute-start | bytes 393224 | tf_op jit(solution)/shard_map/ppermute | solution.py:240
  17.0 11.8 %collective-permute-start.10 = (bf16[3,1,1,128,512]{4,3,2,1,0:T(8,128)(2,1)}, bf16[3,1,1,128,512]{4,3,2,1,0:T(8,128)(2,1)S(1)}, u32[]{:S(2)}, u32[]{:S(2)}) collective-permute-start(bf16[3,1,1,128,512]{4,3,2,1,0:T(8,128)(2,1)} %b_ref.3), channel_id=1, source_target_pairs={{0,1},{1,0},{2,3},{3,2},{4,5},{5,4},{6,7},{7,6},{8,9},{9,8},{10,11... | collective-permute-start | bytes 1179656 | tf_op jit(solution)/shard_map/ppermute | solution.py:258
  17.1 7.9 %collective-permute-start.7 = (bf16[2,128,256]{2,1,0:T(8,128)(2,1)S(1)}, bf16[2,128,256]{2,1,0:T(8,128)(2,1)S(1)}, u32[]{:S(2)}, u32[]{:S(2)}) collective-permute-start(bf16[2,128,256]{2,1,0:T(8,128)(2,1)S(1)} %collective-permute-done.4.refs_6_.refs_2_), channel_id=1, source_target_pairs={{4,0},{12,4},{20,12},{28,20},{24,28},{16,24},{8,16},{0,8},{5,1},{1... | collective-permute-start | bytes 393224 | tf_op jit(solution)/shard_map/ppermute | solution.py:243
  20.5 5.0 %collective-permute-start.9 = (bf16[2,128,256]{2,1,0:T(8,128)(2,1)S(1)}, bf16[2,128,256]{2,1,0:T(8,128)(2,1)S(1)}, u32[]{:S(2)}, u32[]{:S(2)}) collective-permute-start(bf16[2,128,256]{2,1,0:T(8,128)(2,1)S(1)} %collective-permute-done.8.refs_7_), channel_id=1, source_target_pairs={{0,4},{4,12},{12,20},{20,28},{28,24},{24,16},{16,8},{8,0},{1,5},{5... | collective-permute-start | bytes 393224 | tf_op jit(solution)/shard_map/ppermute | solution.py:240
  24.9 2.6 %copy-start.1 = (bf16[3,1,1,128,128]{4,3,2,1,0:T(8,128)(2,1)S(1)}, bf16[3,1,1,128,128]{4,3,2,1,0:T(8,128)(2,1)}, u32[]{:S(2)}) copy-start(bf16[3,1,1,128,128]{4,3,2,1,0:T(8,128)(2,1)} %d_ref.3) | copy-start | bytes 294916
  24.9 5.9 %copy-start = (bf16[3,1,1,128,512]{4,3,2,1,0:T(8,128)(2,1)S(1)}, bf16[3,1,1,128,512]{4,3,2,1,0:T(8,128)(2,1)}, u32[]{:S(2)}) copy-start(bf16[3,1,1,128,512]{4,3,2,1,0:T(8,128)(2,1)} %b_ref.3) | copy-start | bytes 1179652
  25.8 5.0 %collective-permute-start.12 = (bf16[2,128,256]{2,1,0:T(8,128)(2,1)S(1)}, bf16[2,128,256]{2,1,0:T(8,128)(2,1)S(1)}, u32[]{:S(2)}, u32[]{:S(2)}) collective-permute-start(bf16[2,128,256]{2,1,0:T(8,128)(2,1)S(1)} %get-tuple-element.39), channel_id=1, source_target_pairs={{0,2},{1,3},{2,0},{3,1},{4,6},{5,7},{6,4},{7,5},{8,10},{9,11},{10,... | collective-permute-start | bytes 393224 | tf_op jit(solution)/shard_map/ppermute | solution.py:258
  27.5 1.3 %collective-permute-start.11 = (bf16[3,1,1,128,128]{4,3,2,1,0:T(8,128)(2,1)S(1)}, bf16[3,1,1,128,128]{4,3,2,1,0:T(8,128)(2,1)S(1)}, u32[]{:S(2)}, u32[]{:S(2)}) collective-permute-start(bf16[3,1,1,128,128]{4,3,2,1,0:T(8,128)(2,1)S(1)} %copy-done.1), channel_id=1, source_target_pairs={{0,1},{1,0},{2,3},{3,2},{4,5},{5,4},{6,7},{7,6},{8,9},{9,8},{10,11... | collective-permute-start | bytes 294920 | tf_op jit(solution)/shard_map/ppermute | solution.py:258
  31.6 5.4 %collective-permute-start.15 = (bf16[2,128,256]{2,1,0:T(8,128)(2,1)S(1)}, bf16[2,128,256]{2,1,0:T(8,128)(2,1)S(1)}, u32[]{:S(2)}, u32[]{:S(2)}) collective-permute-start(bf16[2,128,256]{2,1,0:T(8,128)(2,1)S(1)} %get-tuple-element.40.refs_5_.refs_0_), channel_id=1, source_target_pairs={{0,4},{4,12},{12,20},{20,28},{28,24},{24,16},{16,8},{8,0},{1,5},{5... | collective-permute-start | bytes 393224 | tf_op jit(solution)/shard_map/ppermute | solution.py:240
  33.3 5.8 %collective-permute-start.13 = (bf16[2,128,256]{2,1,0:T(8,128)(2,1)S(1)}, bf16[2,128,256]{2,1,0:T(8,128)(2,1)S(1)}, u32[]{:S(2)}, u32[]{:S(2)}) collective-permute-start(bf16[2,128,256]{2,1,0:T(8,128)(2,1)S(1)} %get-tuple-element.40.refs_5_.refs_0_), channel_id=1, source_target_pairs={{4,0},{12,4},{20,12},{28,20},{24,28},{16,24},{8,16},{0,8},{5,1},{1... | collective-permute-start | bytes 393224 | tf_op jit(solution)/shard_map/ppermute | solution.py:243
  37.1 6.2 %collective-permute-start.16 = (bf16[2,128,256]{2,1,0:T(8,128)(2,1)S(1)}, bf16[2,128,256]{2,1,0:T(8,128)(2,1)S(1)}, u32[]{:S(2)}, u32[]{:S(2)}) collective-permute-start(bf16[2,128,256]{2,1,0:T(8,128)(2,1)S(1)} %collective-permute-done.15.refs_9_.refs_4_), channel_id=1, source_target_pairs={{0,4},{4,12},{12,20},{20,28},{28,24},{24,16},{16,8},{8,0},{1,5},{5... | collective-permute-start | bytes 393224 | tf_op jit(solution)/shard_map/ppermute | solution.py:240
  39.1 6.1 %collective-permute-start.14 = (bf16[2,128,256]{2,1,0:T(8,128)(2,1)S(1)}, bf16[2,128,256]{2,1,0:T(8,128)(2,1)S(1)}, u32[]{:S(2)}, u32[]{:S(2)}) collective-permute-start(bf16[2,128,256]{2,1,0:T(8,128)(2,1)S(1)} %collective-permute-done.13.refs_6_.refs_1_), channel_id=1, source_target_pairs={{4,0},{12,4},{20,12},{28,20},{24,28},{16,24},{8,16},{0,8},{5,1},{1... | collective-permute-start | bytes 393224 | tf_op jit(solution)/shard_map/ppermute | solution.py:243
  43.3 5.7 %collective-permute-start.18 = (bf16[2,128,256]{2,1,0:T(8,128)(2,1)S(1)}, bf16[2,128,256]{2,1,0:T(8,128)(2,1)S(1)}, u32[]{:S(2)}, u32[]{:S(2)}) collective-permute-start(bf16[2,128,256]{2,1,0:T(8,128)(2,1)S(1)} %collective-permute-done.16.refs_8_.refs_3_), channel_id=1, source_target_pairs={{0,4},{4,12},{12,20},{20,28},{28,24},{24,16},{16,8},{8,0},{1,5},{5... | collective-permute-start | bytes 393224 | tf_op jit(solution)/shard_map/ppermute | solution.py:240
  45.2 8.4 %collective-permute-start.17 = (bf16[2,128,256]{2,1,0:T(8,128)(2,1)S(1)}, bf16[2,128,256]{2,1,0:T(8,128)(2,1)S(1)}, u32[]{:S(2)}, u32[]{:S(2)}) collective-permute-start(bf16[2,128,256]{2,1,0:T(8,128)(2,1)S(1)} %collective-permute-done.14.refs_7_.refs_2_), channel_id=1, source_target_pairs={{4,0},{12,4},{20,12},{28,20},{24,28},{16,24},{8,16},{0,8},{5,1},{1... | collective-permute-start | bytes 393224 | tf_op jit(solution)/shard_map/ppermute | solution.py:243
  48.9 5.0 %collective-permute-start.19 = (bf16[2,128,256]{2,1,0:T(8,128)(2,1)S(1)}, bf16[2,128,256]{2,1,0:T(8,128)(2,1)S(1)}, u32[]{:S(2)}, u32[]{:S(2)}) collective-permute-start(bf16[2,128,256]{2,1,0:T(8,128)(2,1)S(1)} %collective-permute-done.18.refs_7_), channel_id=1, source_target_pairs={{0,4},{4,12},{12,20},{20,28},{28,24},{24,16},{16,8},{8,0},{1,5},{5... | collective-permute-start | bytes 393224 | tf_op jit(solution)/shard_map/ppermute | solution.py:240
  54.3 2.0 %collective-permute-start.23 = (bf16[128,256]{1,0:T(8,128)(2,1)S(1)}, bf16[128,256]{1,0:T(8,128)(2,1)S(1)}, u32[]{:S(2)}, u32[]{:S(2)}) collective-permute-start(bf16[128,256]{1,0:T(8,128)(2,1)S(1)} %get-tuple-element.50), channel_id=1, source_target_pairs={{0,1},{1,0},{2,3},{3,2},{4,5},{5,4},{6,7},{7,6},{8,9},{9,8},{10,11... | collective-permute-start | bytes 196616 | tf_op jit(solution)/shard_map/ppermute | solution.py:258
  54.4 1.9 %collective-permute-start.20 = (bf16[1,128,256]{2,1,0:T(8,128)(2,1)S(1)}, bf16[1,128,256]{2,1,0:T(8,128)(2,1)S(1)}, u32[]{:S(2)}, u32[]{:S(2)}) collective-permute-start(bf16[1,128,256]{2,1,0:T(8,128)(2,1)S(1)} %get-tuple-element.44), channel_id=1, source_target_pairs={{0,1},{1,0},{2,3},{3,2},{4,5},{5,4},{6,7},{7,6},{8,9},{9,8},{10,11... | collective-permute-start | bytes 196616 | tf_op jit(solution)/shard_map/ppermute | solution.py:258
  54.9 4.8 %collective-permute-start.21 = (bf16[1,128,256]{2,1,0:T(8,128)(2,1)S(1)}, bf16[1,128,256]{2,1,0:T(8,128)(2,1)S(1)}, u32[]{:S(2)}, u32[]{:S(2)}) collective-permute-start(bf16[1,128,256]{2,1,0:T(8,128)(2,1)S(1)} %get-tuple-element.45), channel_id=1, source_target_pairs={{0,2},{1,3},{2,0},{3,1},{4,6},{5,7},{6,4},{7,5},{8,10},{9,11},{10,... | collective-permute-start | bytes 196616 | tf_op jit(solution)/shard_map/ppermute | solution.py:258
  55.6 4.4 %collective-permute-start.22 = (bf16[1,128,256]{2,1,0:T(8,128)(2,1)S(1)}, bf16[1,128,256]{2,1,0:T(8,128)(2,1)S(1)}, u32[]{:S(2)}, u32[]{:S(2)}) collective-permute-start(bf16[1,128,256]{2,1,0:T(8,128)(2,1)S(1)} %get-tuple-element.46), channel_id=1, source_target_pairs={{0,3},{1,2},{2,1},{3,0},{4,7},{5,6},{6,5},{7,4},{8,11},{9,10},{10,... | collective-permute-start | bytes 196616 | tf_op jit(solution)/shard_map/ppermute | solution.py:258

commit v4 on v3

--- a/solution.py
+++ b/solution.py
@@ -72,23 +72,29 @@
     return jnp.stack(solutions)[:, None, None]
 
 
-def first_kernel(n, m, place, me_ref, counts_ref, cols_ref, b_ref, d_ref, full_ref, index_ref, *refs):
-    piece_refs, (b_buf, d_buf, count_ref, col_ref, sems) = refs[:PAIR], refs[PAIR:]
+def first_kernel(n, m, place, me_ref, counts_ref, cols_ref, b_ref, d_ref, full_ref, index_ref, own_ref, away_ref, *refs):
+    b_buf, d_buf, count_ref, col_ref, sems = refs
+    middle = b_buf.shape[0]
     copies = [
         pltpu.make_async_copy(counts_ref, count_ref, sems.at[0]),
         pltpu.make_async_copy(cols_ref, col_ref, sems.at[1]),
-        pltpu.make_async_copy(b_ref.at[0, 0, 0], b_buf, sems.at[2]),
-        pltpu.make_async_copy(d_ref.at[0, 0, 0], d_buf, sems.at[3]),
+        pltpu.make_async_copy(d_ref.at[pl.ds(0, middle), 0, 0], d_buf, sems.at[2]),
+        pltpu.make_async_copy(b_ref.at[pl.ds(0, middle), 0, 0], b_buf, sems.at[3]),
     ]
     for copy in copies:
         copy.start()
+    me, my_place = me_ref[0], me_ref[1]
+    size, width = own_ref.shape
     for copy in copies[2:]:
         copy.wait()
-    me, my_place = me_ref[0], me_ref[1]
-    width = piece_refs[0].shape[1]
-    full_ref[...] = jnp.dot(d_buf[...], b_buf[...], preferred_element_type=jnp.float32).astype(jnp.bfloat16)
-    for j in range(PAIR):
-        piece_refs[j][...] = full_ref[:, my_columns(me ^ j, width)]
+    full_ref[...] = jnp.dot(d_buf[0], b_buf[0], preferred_element_type=jnp.float32).astype(jnp.bfloat16)
+    own_ref[...] = full_ref[:, my_columns(me, width)]
+    away_ref[:size, :] = full_ref[:, my_columns(me ^ 1, width)]
+    for level in range(1, middle):
+        at = (2 * level - 1) * size
+        away_ref[at : at + size, :] = b_buf[level, :, my_columns(me ^ 1, width)]
+        away_ref[at + size : at + 2 * size, :size] = d_buf[level]
+        away_ref[at + size : at + 2 * size, size:] = jnp.zeros((size, width - size), jnp.bfloat16)
     for copy in copies[:2]:
         copy.wait()
     levels, slots = col_ref.shape[0] + 1, col_ref.shape[-1]
@@ -178,34 +184,40 @@
             panels_ref[d] = x_ref[...]
 
 
-def solve_kernel(level, me_ref, keep_ref, *refs):
-    b_refs, d_refs, refs = refs[:PAIR], refs[PAIR : 2 * PAIR], refs[2 * PAIR :]
+def solve_kernel(level, me_ref, keep_ref, b_ref, d_ref, away_ref, *refs):
     other_refs, out_ref, piece_refs = refs[: -PAIR - 1], refs[-PAIR - 1], refs[-PAIR:]
-    width = keep_ref.shape[2]
-    columns = my_columns(me_ref[0], width)
+    size, width = keep_ref.shape[1:]
+    at = (2 * level - 1) * size
     for j in range(PAIR):
         total = keep_ref[j]
         for other in other_refs:
             total += other[j].astype(jnp.float32)
-        resid = (b_refs[j][level, 0, 0, :, columns].astype(jnp.float32) - total).astype(jnp.bfloat16)
-        value = jnp.dot(d_refs[j][level, 0, 0], resid, preferred_element_type=jnp.float32).astype(jnp.bfloat16)
+        right = away_ref[at : at + size, :] if j else b_ref[level, 0, 0, :, my_columns(me_ref[0], width)]
+        inverse = away_ref[at + size : at + 2 * size, :size] if j else d_ref[level, 0, 0]
+        resid = (right.astype(jnp.float32) - total).astype(jnp.bfloat16)
+        value = jnp.dot(inverse, resid, preferred_element_type=jnp.float32).astype(jnp.bfloat16)
         out_ref[j] = value
         piece_refs[j][...] = value
 
 
+def write_kernel(me_ref, full_ref, *refs):
+    piece_refs, (out_ref, sems) = refs[:-2], refs[-2:]
+    width = piece_refs[0].shape[1]
+    copies = [pltpu.make_async_copy(full_ref, out_ref.at[0, 0, 0], sems.at[0])]
+    for i, ref in enumerate(piece_refs):
+        target = out_ref.at[1 + i // PAIR, 0, 0, :, my_columns(me_ref[0] ^ (i % PAIR), width)]
+        copies.append(pltpu.make_async_copy(ref, target, sems.at[1 + i]))
+    for copy in copies:
+        copy.start()
+    for copy in copies:
+        copy.wait()
+
+
 def last_kernel(n, me_ref, b_ref, d_ref, keep_ref, *refs):
-    other_refs, refs = refs[: n - 1], refs[n - 1 :]
-    full_ref, refs = refs[0], refs[1:]
-    piece_refs, (out_ref, buf, sems) = refs[:-3], refs[-3:]
+    other_refs, (_, out_ref, buf, sem) = refs[: n - 1], refs[n - 1 :]
     me = me_ref[0]
     width = keep_ref.shape[2]
     levels = out_ref.shape[0]
-    copies = [pltpu.make_async_copy(full_ref, out_ref.at[0, 0, 0], sems.at[0])]
-    for i, ref in enumerate(piece_refs):
-        target = out_ref.at[1 + i // PAIR, 0, 0, :, my_columns(me ^ (i % PAIR), width)]
-        copies.append(pltpu.make_async_copy(ref, target, sems.at[1 + i]))
-    for copy in copies:
-        copy.start()
     for j in range(PAIR):
         total = keep_ref[0] if j == 0 else jnp.zeros_like(keep_ref[0])
         for jq in range(1, n):
@@ -215,11 +227,9 @@
         resid = (b_ref[levels - 1, 0, 0, :, columns].astype(jnp.float32) - total).astype(jnp.bfloat16)
         value = jnp.dot(d_ref[levels - 1, 0, 0], resid, preferred_element_type=jnp.float32)
         buf[:, columns] = value.astype(jnp.bfloat16)
-        target = out_ref.at[levels - 1, 0, 0, :, columns]
-        copies.append(pltpu.make_async_copy(buf.at[:, columns], target, sems.at[1 + len(piece_refs) + j]))
-        copies[-1].start()
-    for copy in copies:
-        copy.wait()
+    copy = pltpu.make_async_copy(buf, out_ref.at[levels - 1, 0, 0], sem)
+    copy.start()
+    copy.wait()
 
 
 def after(value, *others):
@@ -259,24 +269,30 @@
 
     index_shape = (-(-(levels - 1) * n // 8) * 8, LANES)
 
-    full, index, *pieces = pl.pallas_call(
+    middle = levels - 1
+
+    full, index, own, away = pl.pallas_call(
         functools.partial(first_kernel, n, m, place),
-        out_shape=[near((size, front)), near(index_shape, jnp.int32)] + [near((size, width))] * PAIR,
+        out_shape=[
+            near((size, front)),
+            near(index_shape, jnp.int32),
+            near((size, width)),
+            near(((2 * middle - 1) * size, width)),
+        ],
         in_specs=[smem()] + [anywhere()] * 4,
-        out_specs=[vmem()] * (2 + PAIR),
+        out_specs=[vmem()] * 4,
         scratch_shapes=[
-            pltpu.VMEM((size, front), jnp.bfloat16),
-            pltpu.VMEM((size, size), jnp.bfloat16),
+            pltpu.VMEM((middle, size, front), jnp.bfloat16),
+            pltpu.VMEM((middle, size, size), jnp.bfloat16),
             pltpu.SMEM(live_counts.shape, jnp.int32),
             pltpu.VMEM(block_cols.shape, jnp.int32),
             pltpu.SemaphoreType.DMA((4,)),
         ],
         compiler_params=params(),
     )(me, *[in_hbm(v) for v in (live_counts, block_cols, b_panels, diag_inverse)])
-    index = [index, send(index, 1)]
-    solved = after(jnp.stack([pieces[0], send(pieces[1], 1)]), index[1])
-    b, inverse, blocks = [[v, send(after(v, solved), 1)] for v in (b_panels, diag_inverse, l_blocks)]
-    blocks[0] = in_hbm(l_blocks)
+    away, index = send(away, 1), [index, send(index, 1)]
+    solved = after(jnp.stack([own, away[:size]]), index[1])
+    blocks = [in_hbm(l_blocks), send(after(l_blocks, solved), 1)]
 
     late = [d for d in range(1, m) if min(d, m - d) >= m // 2 - 1]
     early = [d for d in range(m) if d not in late]
@@ -316,31 +332,37 @@
         if not final:
             panels, *found = found
             kept.append(panels)
-        keep, *away = found
-        others = [send(v, rows * (h + 1)) for h, v in enumerate(away)]
+        keep, *partial = found
+        others = [send(v, rows * (h + 1)) for h, v in enumerate(partial)]
         if final:
             columns = [send(after(v, keep), 1) if i % PAIR else v for i, v in enumerate(columns)]
             break
         solved, *pieces = pl.pallas_call(
             functools.partial(solve_kernel, level),
             out_shape=[near((PAIR, size, width))] + [near((size, width))] * PAIR,
-            in_specs=[smem()] + [vmem()] * (1 + 2 * PAIR + len(others)),
+            in_specs=[smem()] + [vmem()] * (4 + len(others)),
             out_specs=[vmem()] * (1 + PAIR),
             compiler_params=params(),
-        )(me, keep, *b, *inverse, *others)
+        )(me, keep, b_panels, diag_inverse, away, *others)
         columns += pieces
 
+    result = pl.pallas_call(
+        write_kernel,
+        out_shape=struct(b_panels.shape),
+        in_specs=[smem()] + [vmem()] * (1 + len(columns)),
+        out_specs=anywhere(),
+        scratch_shapes=[pltpu.SemaphoreType.DMA((1 + len(columns),))],
+        compiler_params=params(),
+    )(me, full, *columns)
     return pl.pallas_call(
         functools.partial(last_kernel, n),
         out_shape=struct(b_panels.shape),
-        in_specs=[smem()] + [vmem()] * (4 + len(others) + len(columns)),
+        in_specs=[smem()] + [vmem()] * (3 + len(others)) + [anywhere()],
         out_specs=anywhere(),
-        scratch_shapes=[
-            pltpu.VMEM((size, front), jnp.bfloat16),
-            pltpu.SemaphoreType.DMA((1 + PAIR + len(columns),)),
-        ],
+        scratch_shapes=[pltpu.VMEM((size, front), jnp.bfloat16), pltpu.SemaphoreType.DMA],
+        input_output_aliases={4 + len(others): 0},
         compiler_params=params(),
-    )(me, b_panels, diag_inverse, keep, *others, full, *columns)
+    )(me, b_panels, diag_inverse, keep, *others, result)
 
 
 def cycle_of(mesh):
@@ -373,7 +395,7 @@
         front = b_panels.shape[-1]
         rows = mesh.shape["prow"]
         paired = n & (n - 1) == 0 and n >= PAIR and rows % 2 == 0 and rows > 2 and front % (PAIR * LANES) == 0
-        paired = paired and b_panels.shape[0] > 1
+        paired = paired and b_panels.shape[0] > 1 and front >= PAIR * b_panels.shape[-2]
         if paired and l_blocks.size * l_blocks.dtype.itemsize <= BLOCK_BYTES:
             return solve_paired(cycle, b_panels, diag_inverse, l_blocks, block_cols, live_counts)
         return solve_scattered(b_panels, diag_inverse, l_blocks, block_cols, live_counts)

time: 61.7 us -> 60.9 us (0.987)
  waiting for transfers between devices: 30 us -> 28 us
  Pallas kernels: 10.4 us -> 11.7 us
    pallas_call x0 -> x1, Pallas kernels: none -> 1.26 us  [solve_paired(): pl.pallas_call(write_kernel, out_shape=struct(b_panels.shape), in_specs=[...]
    ppermute x8, starting transfers between devices: 14.6 us -> 13.5 us  [advance(): self.behind = lax.ppermute(self.behind, 'prow', self.to_next)]
    ppermute x8, waiting for transfers between devices: 21.5 us -> 20.4 us  [advance(): self.behind = lax.ppermute(self.behind, 'prow', self.to_next)]
    ppermute x6, starting transfers between devices: 1.79 us -> 2.48 us  [advance(): self.ahead = lax.ppermute(self.ahead, 'prow', self.to_last)]
    ppermute x10 -> x8, waiting for transfers between devices: 8.11 us -> 7.55 us  [send(): return lax.ppermute(value, 'pcol', [(i, i ^ bits) for i in range(n)])]
    ppermute x10 -> x8, starting transfers between devices: 4.49 us -> 4.75 us  [send(): return lax.ppermute(value, 'pcol', [(i, i ^ bits) for i in range(n)])]
  transfers between devices with their start and end apart: 24 -> 22, of which waited for: 15 -> 13; matrix products, arithmetic and copies ran while one was open for 0% -> 0% of each run, Pallas kernels for 10% -> 11%
where the time goes in v4:
time: 60.9 us; the launch traced here: 60.7 us
  waiting for transfers between devices  28 us (46%)
  starting transfers between devices  20.8 us (34%)
  Pallas kernels  11.7 us (19%)
    ppermute x8, waiting for transfers between devices, advance(): self.behind = lax.ppermute(self.behind, 'prow', self.to_next)  20.4 us
    ppermute x8, starting transfers between devices, advance(): self.behind = lax.ppermute(self.behind, 'prow', self.to_next)  13.5 us
    ppermute x8, waiting for transfers between devices, send(): return lax.ppermute(value, 'pcol', [(i, i ^ bits) for i in range(n)])  7.55 us
    pallas_call x2, Pallas kernels, solve_paired(): pl.pallas_call(functools.partial(gather_kernel, n, level, m, early, late)...  5.68 us
    ppermute x8, starting transfers between devices, send(): return lax.ppermute(value, 'pcol', [(i, i ^ bits) for i in range(n)])  4.75 us
    ppermute x6, starting transfers between devices, advance(): self.ahead = lax.ppermute(self.ahead, 'prow', self.to_last)  2.48 us
    pallas_call x1, Pallas kernels, solve_paired(): pl.pallas_call(functools.partial(first_kernel, n, m, place), out_shape=[n...  1.82 us
    pallas_call x1, Pallas kernels, solve_paired(): pl.pallas_call(functools.partial(last_kernel, n), out_shape=struct(b_pane...  1.41 us
  transfers between devices with their start and end apart: 22, of which 13 were waited for; matrix products, arithmetic and copies ran while one was open for 0% of the time, Pallas kernels for 11%

profile of v4, /device:TPU:0, one launch (start us, length us, event | category | flops | bytes accessed | tf_op | source)
XLA Modules:
  0.0 60.7 jit_solution(11118660083700649643)
XLA Ops:
  0.0 0.1 pad_add_fusion.me_ref
  0.1 1.8 %shard_map.55 = (bf16[128,512]{1,0:T(8,128)(2,1)S(1)}, s32[8,128]{1,0:T(8,128)S(1)}, bf16[128,256]{1,0:T(8,128)(2,1)S(1)}, bf16[384,256]{1,0:T(8,128)(2,1)S(1)}) custom-call(s32[2]{0:T(128)S(1)} %pad_add_fusion.me_ref, s32[2,1,1,4]{3,2,1,0:T(1,128)} %counts_ref.1, s32[2,1,1,4,5]{4,3,2,1,0:T(4,128)} %cols_ref.1, bf16[3,1,1,128,512]{4,3,2,1,0:T(8,128)(2,1)} %b_ref.5, ...), custom_call_target="tpu_custom_call" | custom-call | tf_op jit(solution)/shard_map/pallas_call | solution.py:274
  1.9 0.5 collective-permute-start.1
  2.4 0.1 collective-permute-start
  2.5 1.0 %collective-permute-done.1.away_ref = bf16[384,256]{1,0:T(8,128)(2,1)S(1)} collective-permute-done((bf16[384,256]{1,0:T(8,128)(2,1)S(1)}, bf16[384,256]{1,0:T(8,128)(2,1)S(1)}, u32[]{:S(2)}, u32[]{:S(2)}) %collective-permute-start.1) | collective-permute-done | bytes 196640 | tf_op jit(solution)/shard_map/ppermute | solution.py:268
  3.5 0.1 collective-permute-done.refs_1_
  3.6 0.4 collective-permute-start.2
  4.0 2.6 %collective-permute-start.5 = (bf16[2,128,256]{2,1,0:T(8,128)(2,1)S(1)}, bf16[2,128,256]{2,1,0:T(8,128)(2,1)S(1)}, u32[]{:S(2)}, u32[]{:S(2)}) collective-permute-start(bf16[2,128,256]{2,1,0:T(8,128)(2,1)S(1)} %pad_maximum_fusion.refs_4_.refs_0_), channel_id=1, source_target_pairs={{0,4},{4,12},{12,20},{20,28},{28,24},{24,16},{16,8},{8,0},{1,5},{5... | collective-permute-start | bytes 393224 | tf_op jit(solution)/shard_map/ppermute | solution.py:250
  6.6 0.1 collective-permute-start.3
  6.7 4.0 %collective-permute-done.5.refs_8_.refs_4_ = bf16[2,128,256]{2,1,0:T(8,128)(2,1)S(1)} collective-permute-done((bf16[2,128,256]{2,1,0:T(8,128)(2,1)S(1)}, bf16[2,128,256]{2,1,0:T(8,128)(2,1)S(1)}, u32[]{:S(2)}, u32[]{:S(2)}) %collective-permute-start.5) | collective-permute-done | bytes 131104 | tf_op jit(solution)/shard_map/ppermute | solution.py:250
  10.7 1.7 %collective-permute-start.6 = (bf16[2,128,256]{2,1,0:T(8,128)(2,1)S(1)}, bf16[2,128,256]{2,1,0:T(8,128)(2,1)S(1)}, u32[]{:S(2)}, u32[]{:S(2)}) collective-permute-start(bf16[2,128,256]{2,1,0:T(8,128)(2,1)S(1)} %collective-permute-done.5.refs_8_.refs_4_), channel_id=1, source_target_pairs={{0,4},{4,12},{12,20},{20,28},{28,24},{24,16},{16,8},{8,0},{1,5},{5... | collective-permute-start | bytes 393224 | tf_op jit(solution)/shard_map/ppermute | solution.py:250
  12.4 0.0 collective-permute-done.3.refs_5_.refs_1_
  12.4 0.4 collective-permute-start.4
  12.7 3.2 %collective-permute-done.6.refs_7_.refs_3_ = bf16[2,128,256]{2,1,0:T(8,128)(2,1)S(1)} collective-permute-done((bf16[2,128,256]{2,1,0:T(8,128)(2,1)S(1)}, bf16[2,128,256]{2,1,0:T(8,128)(2,1)S(1)}, u32[]{:S(2)}, u32[]{:S(2)}) %collective-permute-start.6) | collective-permute-done | bytes 131104 | tf_op jit(solution)/shard_map/ppermute | solution.py:250
  15.9 1.4 %collective-permute-start.8 = (bf16[2,128,256]{2,1,0:T(8,128)(2,1)S(1)}, bf16[2,128,256]{2,1,0:T(8,128)(2,1)S(1)}, u32[]{:S(2)}, u32[]{:S(2)}) collective-permute-start(bf16[2,128,256]{2,1,0:T(8,128)(2,1)S(1)} %collective-permute-done.6.refs_7_.refs_3_), channel_id=1, source_target_pairs={{0,4},{4,12},{12,20},{20,28},{28,24},{24,16},{16,8},{8,0},{1,5},{5... | collective-permute-start | bytes 393224 | tf_op jit(solution)/shard_map/ppermute | solution.py:250
  17.3 0.0 collective-permute-done.4.refs_6_.refs_2_
  17.3 0.6 collective-permute-start.7
  17.9 2.9 %collective-permute-done.8.refs_7_ = bf16[2,128,256]{2,1,0:T(8,128)(2,1)S(1)} collective-permute-done((bf16[2,128,256]{2,1,0:T(8,128)(2,1)S(1)}, bf16[2,128,256]{2,1,0:T(8,128)(2,1)S(1)}, u32[]{:S(2)}, u32[]{:S(2)}) %collective-permute-start.8) | collective-permute-done | bytes 131104 | tf_op jit(solution)/shard_map/ppermute | solution.py:250
  20.9 1.6 %collective-permute-start.9 = (bf16[2,128,256]{2,1,0:T(8,128)(2,1)S(1)}, bf16[2,128,256]{2,1,0:T(8,128)(2,1)S(1)}, u32[]{:S(2)}, u32[]{:S(2)}) collective-permute-start(bf16[2,128,256]{2,1,0:T(8,128)(2,1)S(1)} %collective-permute-done.8.refs_7_), channel_id=1, source_target_pairs={{0,4},{4,12},{12,20},{20,28},{28,24},{24,16},{16,8},{8,0},{1,5},{5... | collective-permute-start | bytes 393224 | tf_op jit(solution)/shard_map/ppermute | solution.py:250
  22.4 0.0 collective-permute-done.2.refs_3_
  22.4 2.8 %shard_map.56 = (f32[4,128,256]{2,1,0:T(8,128)S(1)}, bf16[4,128,768]{2,1,0:T(8,128)(2,1)S(1)}) custom-call(s32[2]{0:T(128)S(1)} %pad_add_fusion.me_ref, s32[8,128]{1,0:T(8,128)S(1)} %get-tuple-element.26.refs_0_, s32[8,128]{1,0:T(8,128)S(1)} %collective-permute-done.refs_1_, bf16[2,1,1,4,5,128,128]{6,5,4,3,2,1,0:T(8,128)(2,1)} %refs_2_.3, ...), custom_call_target="tpu_custom_call" | custom-call | tf_op jit(solution)/shard_map/pallas_call | solution.py:305
  25.2 0.0 copy-start
  25.3 0.0 copy-start.1
  25.3 0.0 collective-permute-done.7.refs_5_
  25.3 0.6 collective-permute-done.9.refs_6_
  25.8 0.4 shard_map.57
  26.2 1.6 %collective-permute-start.10 = (bf16[2,128,256]{2,1,0:T(8,128)(2,1)S(1)}, bf16[2,128,256]{2,1,0:T(8,128)(2,1)S(1)}, u32[]{:S(2)}, u32[]{:S(2)}) collective-permute-start(bf16[2,128,256]{2,1,0:T(8,128)(2,1)S(1)} %get-tuple-element.35), channel_id=1, source_target_pairs={{0,2},{1,3},{2,0},{3,1},{4,6},{5,7},{6,4},{7,5},{8,10},{9,11},{10,... | collective-permute-start | bytes 393224 | tf_op jit(solution)/shard_map/ppermute | solution.py:268
  27.9 3.4 %collective-permute-done.10.refs_0_ = bf16[2,128,256]{2,1,0:T(8,128)(2,1)S(1)} collective-permute-done((bf16[2,128,256]{2,1,0:T(8,128)(2,1)S(1)}, bf16[2,128,256]{2,1,0:T(8,128)(2,1)S(1)}, u32[]{:S(2)}, u32[]{:S(2)}) %collective-permute-start.10) | collective-permute-done | bytes 131104 | tf_op jit(solution)/shard_map/ppermute | solution.py:268
  31.3 0.0 copy-done
  31.3 0.0 copy-done.1
  31.3 0.7 %shard_map.58 = (bf16[2,128,256]{2,1,0:T(8,128)(2,1)S(1)}, bf16[128,256]{1,0:T(8,128)(2,1)S(1)}, bf16[128,256]{1,0:T(8,128)(2,1)S(1)}) custom-call(s32[2]{0:T(128)S(1)} %pad_add_fusion.me_ref, f32[2,128,256]{2,1,0:T(8,128)S(1)} %get-tuple-element.34.keep_ref, bf16[3,1,1,128,512]{4,3,2,1,0:T(8,128)(2,1)S(1)} %copy-done, ...), custom_call_target="tpu_custom_call" | custom-call | tf_op jit(solution)/shard_map/pallas_call | solution.py:340
  32.0 1.6 %collective-permute-start.13 = (bf16[2,128,256]{2,1,0:T(8,128)(2,1)S(1)}, bf16[2,128,256]{2,1,0:T(8,128)(2,1)S(1)}, u32[]{:S(2)}, u32[]{:S(2)}) collective-permute-start(bf16[2,128,256]{2,1,0:T(8,128)(2,1)S(1)} %get-tuple-element.36.refs_5_.refs_0_), channel_id=1, source_target_pairs={{0,4},{4,12},{12,20},{20,28},{28,24},{24,16},{16,8},{8,0},{1,5},{5... | collective-permute-start | bytes 393224 | tf_op jit(solution)/shard_map/ppermute | solution.py:250
  33.6 0.5 collective-permute-start.11
  34.1 2.9 %collective-permute-done.13.refs_9_.refs_4_ = bf16[2,128,256]{2,1,0:T(8,128)(2,1)S(1)} collective-permute-done((bf16[2,128,256]{2,1,0:T(8,128)(2,1)S(1)}, bf16[2,128,256]{2,1,0:T(8,128)(2,1)S(1)}, u32[]{:S(2)}, u32[]{:S(2)}) %collective-permute-start.13) | collective-permute-done | bytes 131104 | tf_op jit(solution)/shard_map/ppermute | solution.py:250
  37.0 1.5 %collective-permute-start.14 = (bf16[2,128,256]{2,1,0:T(8,128)(2,1)S(1)}, bf16[2,128,256]{2,1,0:T(8,128)(2,1)S(1)}, u32[]{:S(2)}, u32[]{:S(2)}) collective-permute-start(bf16[2,128,256]{2,1,0:T(8,128)(2,1)S(1)} %collective-permute-done.13.refs_9_.refs_4_), channel_id=1, source_target_pairs={{0,4},{4,12},{12,20},{20,28},{28,24},{24,16},{16,8},{8,0},{1,5},{5... | collective-permute-start | bytes 393224 | tf_op jit(solution)/shard_map/ppermute | solution.py:250
  38.6 0.0 collective-permute-done.11.refs_6_.refs_1_
  38.6 0.5 collective-permute-start.12
  39.1 3.3 %collective-permute-done.14.refs_8_.refs_3_ = bf16[2,128,256]{2,1,0:T(8,128)(2,1)S(1)} collective-permute-done((bf16[2,128,256]{2,1,0:T(8,128)(2,1)S(1)}, bf16[2,128,256]{2,1,0:T(8,128)(2,1)S(1)}, u32[]{:S(2)}, u32[]{:S(2)}) %collective-permute-start.14) | collective-permute-done | bytes 131104 | tf_op jit(solution)/shard_map/ppermute | solution.py:250
  42.4 1.5 %collective-permute-start.16 = (bf16[2,128,256]{2,1,0:T(8,128)(2,1)S(1)}, bf16[2,128,256]{2,1,0:T(8,128)(2,1)S(1)}, u32[]{:S(2)}, u32[]{:S(2)}) collective-permute-start(bf16[2,128,256]{2,1,0:T(8,128)(2,1)S(1)} %collective-permute-done.14.refs_8_.refs_3_), channel_id=1, source_target_pairs={{0,4},{4,12},{12,20},{20,28},{28,24},{24,16},{16,8},{8,0},{1,5},{5... | collective-permute-start | bytes 393224 | tf_op jit(solution)/shard_map/ppermute | solution.py:250
  43.9 0.0 collective-permute-done.12.refs_7_.refs_2_
  43.9 0.5 collective-permute-start.15
  44.4 2.9 %collective-permute-done.16.refs_7_ = bf16[2,128,256]{2,1,0:T(8,128)(2,1)S(1)} collective-permute-done((bf16[2,128,256]{2,1,0:T(8,128)(2,1)S(1)}, bf16[2,128,256]{2,1,0:T(8,128)(2,1)S(1)}, u32[]{:S(2)}, u32[]{:S(2)}) %collective-permute-start.16) | collective-permute-done | bytes 131104 | tf_op jit(solution)/shard_map/ppermute | solution.py:250
  47.4 1.5 %collective-permute-start.17 = (bf16[2,128,256]{2,1,0:T(8,128)(2,1)S(1)}, bf16[2,128,256]{2,1,0:T(8,128)(2,1)S(1)}, u32[]{:S(2)}, u32[]{:S(2)}) collective-permute-start(bf16[2,128,256]{2,1,0:T(8,128)(2,1)S(1)} %collective-permute-done.16.refs_7_), channel_id=1, source_target_pairs={{0,4},{4,12},{12,20},{20,28},{28,24},{24,16},{16,8},{8,0},{1,5},{5... | collective-permute-start | bytes 393224 | tf_op jit(solution)/shard_map/ppermute | solution.py:250
  48.9 2.9 %shard_map.59 = (f32[4,128,256]{2,1,0:T(8,128)S(1)}, bf16[4,128,768]{2,1,0:T(8,128)(2,1)S(1)}) custom-call(s32[2]{0:T(128)S(1)} %pad_add_fusion.me_ref, s32[8,128]{1,0:T(8,128)S(1)} %get-tuple-element.26.refs_0_, s32[8,128]{1,0:T(8,128)S(1)} %collective-permute-done.refs_1_, bf16[2,1,1,4,5,128,128]{6,5,4,3,2,1,0:T(8,128)(2,1)} %refs_2_.3, ...), custom_call_target="tpu_custom_call" | custom-call | tf_op jit(solution)/shard_map/pallas_call | solution.py:305
  51.8 0.0 collective-permute-done.15.refs_5_
  51.8 0.5 collective-permute-done.17.refs_6_
  52.3 0.4 shard_map.60
  52.7 0.1 collective-permute-start.21
  52.8 0.5 collective-permute-start.18
  53.3 1.6 %collective-permute-start.19 = (bf16[1,128,256]{2,1,0:T(8,128)(2,1)S(1)}, bf16[1,128,256]{2,1,0:T(8,128)(2,1)S(1)}, u32[]{:S(2)}, u32[]{:S(2)}) collective-permute-start(bf16[1,128,256]{2,1,0:T(8,128)(2,1)S(1)} %get-tuple-element.41), channel_id=1, source_target_pairs={{0,2},{1,3},{2,0},{3,1},{4,6},{5,7},{6,4},{7,5},{8,10},{9,11},{10,... | collective-permute-start | bytes 196616 | tf_op jit(solution)/shard_map/ppermute | solution.py:268
  54.9 0.0 collective-permute-start.20
  54.9 0.0 collective-permute-done.21.refs_1_
  54.9 1.3 %shard_map.61.refs_3_ = bf16[3,1,1,128,512]{4,3,2,1,0:T(8,128)(2,1)} custom-call(s32[2]{0:T(128)S(1)} %pad_add_fusion.me_ref, bf16[128,512]{1,0:T(8,128)(2,1)S(1)} %get-tuple-element.43.full_ref, bf16[128,256]{1,0:T(8,128)(2,1)S(1)} %get-tuple-element.44.refs_0_, bf16[128,256]{1,0:T(8,128)(2,1)S(1)} %collective-permute-done.21.refs_1_), custom_call_target="tpu_custom_call" | custom-call | tf_op jit(solution)/shard_map/pallas_call | solution.py:349
  56.1 0.0 collective-permute-done.18.refs_0_
  56.2 1.4 %collective-permute-done.19.refs_1_ = bf16[1,128,256]{2,1,0:T(8,128)(2,1)S(1)} collective-permute-done((bf16[1,128,256]{2,1,0:T(8,128)(2,1)S(1)}, bf16[1,128,256]{2,1,0:T(8,128)(2,1)S(1)}, u32[]{:S(2)}, u32[]{:S(2)}) %collective-permute-start.19) | collective-permute-done | bytes 65568 | tf_op jit(solution)/shard_map/ppermute | solution.py:268
  57.6 1.7 %collective-permute-done.20.refs_2_ = bf16[1,128,256]{2,1,0:T(8,128)(2,1)S(1)} collective-permute-done((bf16[1,128,256]{2,1,0:T(8,128)(2,1)S(1)}, bf16[1,128,256]{2,1,0:T(8,128)(2,1)S(1)}, u32[]{:S(2)}, u32[]{:S(2)}) %collective-permute-start.20) | collective-permute-done | bytes 65568 | tf_op jit(solution)/shard_map/ppermute | solution.py:268
  59.2 1.4 %shard_map.62 = bf16[3,1,1,128,512]{4,3,2,1,0:T(8,128)(2,1)} custom-call(s32[2]{0:T(128)S(1)} %pad_add_fusion.me_ref, bf16[3,1,1,128,512]{4,3,2,1,0:T(8,128)(2,1)S(1)} %copy-done, bf16[3,1,1,128,128]{4,3,2,1,0:T(8,128)(2,1)S(1)} %copy-done.1, f32[1,128,256]{2,1,0:T(8,128)S(1)} %get-tuple-element.39.keep_ref, ...), custom_call_target="tpu_custom_call", output_to_operand_aliasing={{}: (7, {})} | custom-call | tf_op jit(solution)/shard_map/pallas_call | solution.py:357
  (2 shorter events, 0.0 us)
Async XLA Ops:
  1.9 1.6 %collective-permute-start.1 = (bf16[384,256]{1,0:T(8,128)(2,1)S(1)}, bf16[384,256]{1,0:T(8,128)(2,1)S(1)}, u32[]{:S(2)}, u32[]{:S(2)}) collective-permute-start(bf16[384,256]{1,0:T(8,128)(2,1)S(1)} %get-tuple-element.28), channel_id=1, source_target_pairs={{0,1},{1,0},{2,3},{3,2},{4,5},{5,4},{6,7},{7,6},{8,9},{9,8},{10,11... | collective-permute-start | bytes 589832 | tf_op jit(solution)/shard_map/ppermute | solution.py:268
  2.4 1.2 %collective-permute-start = (s32[8,128]{1,0:T(8,128)S(1)}, s32[8,128]{1,0:T(8,128)S(1)}, u32[]{:S(2)}, u32[]{:S(2)}) collective-permute-start(s32[8,128]{1,0:T(8,128)S(1)} %get-tuple-element.26.refs_0_), channel_id=1, source_target_pairs={{0,1},{1,0},{2,3},{3,2},{4,5},{5,4},{6,7},{7,6},{8,9},{9,8},{10,11... | collective-permute-start | bytes 12296 | tf_op jit(solution)/shard_map/ppermute | solution.py:268
  3.6 18.8 %collective-permute-start.2 = (bf16[2,1,1,4,5,128,128]{6,5,4,3,2,1,0:T(8,128)(2,1)}, bf16[2,1,1,4,5,128,128]{6,5,4,3,2,1,0:T(8,128)(2,1)S(1)}, u32[]{:S(2)}, u32[]{:S(2)}) collective-permute-start(bf16[2,1,1,4,5,128,128]{6,5,4,3,2,1,0:T(8,128)(2,1)} %refs_2_.3), channel_id=1, source_target_pairs={{0,1},{1,0},{2,3},{3,2},{4,5},{5,4},{6,7},{7,6},{8,9},{9,8},{10,11... | collective-permute-start | bytes 3932168 | tf_op jit(solution)/shard_map/ppermute | solution.py:268
  4.0 6.7 %collective-permute-start.5 = (bf16[2,128,256]{2,1,0:T(8,128)(2,1)S(1)}, bf16[2,128,256]{2,1,0:T(8,128)(2,1)S(1)}, u32[]{:S(2)}, u32[]{:S(2)}) collective-permute-start(bf16[2,128,256]{2,1,0:T(8,128)(2,1)S(1)} %pad_maximum_fusion.refs_4_.refs_0_), channel_id=1, source_target_pairs={{0,4},{4,12},{12,20},{20,28},{28,24},{24,16},{16,8},{8,0},{1,5},{5... | collective-permute-start | bytes 393224 | tf_op jit(solution)/shard_map/ppermute | solution.py:250
  6.6 5.8 %collective-permute-start.3 = (bf16[2,128,256]{2,1,0:T(8,128)(2,1)S(1)}, bf16[2,128,256]{2,1,0:T(8,128)(2,1)S(1)}, u32[]{:S(2)}, u32[]{:S(2)}) collective-permute-start(bf16[2,128,256]{2,1,0:T(8,128)(2,1)S(1)} %pad_maximum_fusion.refs_4_.refs_0_), channel_id=1, source_target_pairs={{4,0},{12,4},{20,12},{28,20},{24,28},{16,24},{8,16},{0,8},{5,1},{1... | collective-permute-start | bytes 393224 | tf_op jit(solution)/shard_map/ppermute | solution.py:253
  10.7 5.2 %collective-permute-start.6 = (bf16[2,128,256]{2,1,0:T(8,128)(2,1)S(1)}, bf16[2,128,256]{2,1,0:T(8,128)(2,1)S(1)}, u32[]{:S(2)}, u32[]{:S(2)}) collective-permute-start(bf16[2,128,256]{2,1,0:T(8,128)(2,1)S(1)} %collective-permute-done.5.refs_8_.refs_4_), channel_id=1, source_target_pairs={{0,4},{4,12},{12,20},{20,28},{28,24},{24,16},{16,8},{8,0},{1,5},{5... | collective-permute-start | bytes 393224 | tf_op jit(solution)/shard_map/ppermute | solution.py:250
  12.4 5.0 %collective-permute-start.4 = (bf16[2,128,256]{2,1,0:T(8,128)(2,1)S(1)}, bf16[2,128,256]{2,1,0:T(8,128)(2,1)S(1)}, u32[]{:S(2)}, u32[]{:S(2)}) collective-permute-start(bf16[2,128,256]{2,1,0:T(8,128)(2,1)S(1)} %collective-permute-done.3.refs_5_.refs_1_), channel_id=1, source_target_pairs={{4,0},{12,4},{20,12},{28,20},{24,28},{16,24},{8,16},{0,8},{5,1},{1... | collective-permute-start | bytes 393224 | tf_op jit(solution)/shard_map/ppermute | solution.py:253
  15.9 5.0 %collective-permute-start.8 = (bf16[2,128,256]{2,1,0:T(8,128)(2,1)S(1)}, bf16[2,128,256]{2,1,0:T(8,128)(2,1)S(1)}, u32[]{:S(2)}, u32[]{:S(2)}) collective-permute-start(bf16[2,128,256]{2,1,0:T(8,128)(2,1)S(1)} %collective-permute-done.6.refs_7_.refs_3_), channel_id=1, source_target_pairs={{0,4},{4,12},{12,20},{20,28},{28,24},{24,16},{16,8},{8,0},{1,5},{5... | collective-permute-start | bytes 393224 | tf_op jit(solution)/shard_map/ppermute | solution.py:250
  17.3 7.9 %collective-permute-start.7 = (bf16[2,128,256]{2,1,0:T(8,128)(2,1)S(1)}, bf16[2,128,256]{2,1,0:T(8,128)(2,1)S(1)}, u32[]{:S(2)}, u32[]{:S(2)}) collective-permute-start(bf16[2,128,256]{2,1,0:T(8,128)(2,1)S(1)} %collective-permute-done.4.refs_6_.refs_2_), channel_id=1, source_target_pairs={{4,0},{12,4},{20,12},{28,20},{24,28},{16,24},{8,16},{0,8},{5,1},{1... | collective-permute-start | bytes 393224 | tf_op jit(solution)/shard_map/ppermute | solution.py:253
  20.9 5.0 %collective-permute-start.9 = (bf16[2,128,256]{2,1,0:T(8,128)(2,1)S(1)}, bf16[2,128,256]{2,1,0:T(8,128)(2,1)S(1)}, u32[]{:S(2)}, u32[]{:S(2)}) collective-permute-start(bf16[2,128,256]{2,1,0:T(8,128)(2,1)S(1)} %collective-permute-done.8.refs_7_), channel_id=1, source_target_pairs={{0,4},{4,12},{12,20},{20,28},{28,24},{24,16},{16,8},{8,0},{1,5},{5... | collective-permute-start | bytes 393224 | tf_op jit(solution)/shard_map/ppermute | solution.py:250
  25.2 6.0 %copy-start = (bf16[3,1,1,128,512]{4,3,2,1,0:T(8,128)(2,1)S(1)}, bf16[3,1,1,128,512]{4,3,2,1,0:T(8,128)(2,1)}, u32[]{:S(2)}) copy-start(bf16[3,1,1,128,512]{4,3,2,1,0:T(8,128)(2,1)} %b_ref.5) | copy-start | bytes 1179652
  25.3 6.0 %copy-start.1 = (bf16[3,1,1,128,128]{4,3,2,1,0:T(8,128)(2,1)S(1)}, bf16[3,1,1,128,128]{4,3,2,1,0:T(8,128)(2,1)}, u32[]{:S(2)}) copy-start(bf16[3,1,1,128,128]{4,3,2,1,0:T(8,128)(2,1)} %d_ref.5) | copy-start | bytes 294916
  26.2 5.0 %collective-permute-start.10 = (bf16[2,128,256]{2,1,0:T(8,128)(2,1)S(1)}, bf16[2,128,256]{2,1,0:T(8,128)(2,1)S(1)}, u32[]{:S(2)}, u32[]{:S(2)}) collective-permute-start(bf16[2,128,256]{2,1,0:T(8,128)(2,1)S(1)} %get-tuple-element.35), channel_id=1, source_target_pairs={{0,2},{1,3},{2,0},{3,1},{4,6},{5,7},{6,4},{7,5},{8,10},{9,11},{10,... | collective-permute-start | bytes 393224 | tf_op jit(solution)/shard_map/ppermute | solution.py:268
  32.0 5.0 %collective-permute-start.13 = (bf16[2,128,256]{2,1,0:T(8,128)(2,1)S(1)}, bf16[2,128,256]{2,1,0:T(8,128)(2,1)S(1)}, u32[]{:S(2)}, u32[]{:S(2)}) collective-permute-start(bf16[2,128,256]{2,1,0:T(8,128)(2,1)S(1)} %get-tuple-element.36.refs_5_.refs_0_), channel_id=1, source_target_pairs={{0,4},{4,12},{12,20},{20,28},{28,24},{24,16},{16,8},{8,0},{1,5},{5... | collective-permute-start | bytes 393224 | tf_op jit(solution)/shard_map/ppermute | solution.py:250
  33.6 5.0 %collective-permute-start.11 = (bf16[2,128,256]{2,1,0:T(8,128)(2,1)S(1)}, bf16[2,128,256]{2,1,0:T(8,128)(2,1)S(1)}, u32[]{:S(2)}, u32[]{:S(2)}) collective-permute-start(bf16[2,128,256]{2,1,0:T(8,128)(2,1)S(1)} %get-tuple-element.36.refs_5_.refs_0_), channel_id=1, source_target_pairs={{4,0},{12,4},{20,12},{28,20},{24,28},{16,24},{8,16},{0,8},{5,1},{1... | collective-permute-start | bytes 393224 | tf_op jit(solution)/shard_map/ppermute | solution.py:253
  37.0 5.4 %collective-permute-start.14 = (bf16[2,128,256]{2,1,0:T(8,128)(2,1)S(1)}, bf16[2,128,256]{2,1,0:T(8,128)(2,1)S(1)}, u32[]{:S(2)}, u32[]{:S(2)}) collective-permute-start(bf16[2,128,256]{2,1,0:T(8,128)(2,1)S(1)} %collective-permute-done.13.refs_9_.refs_4_), channel_id=1, source_target_pairs={{0,4},{4,12},{12,20},{20,28},{28,24},{24,16},{16,8},{8,0},{1,5},{5... | collective-permute-start | bytes 393224 | tf_op jit(solution)/shard_map/ppermute | solution.py:250
  38.6 5.4 %collective-permute-start.12 = (bf16[2,128,256]{2,1,0:T(8,128)(2,1)S(1)}, bf16[2,128,256]{2,1,0:T(8,128)(2,1)S(1)}, u32[]{:S(2)}, u32[]{:S(2)}) collective-permute-start(bf16[2,128,256]{2,1,0:T(8,128)(2,1)S(1)} %collective-permute-done.11.refs_6_.refs_1_), channel_id=1, source_target_pairs={{4,0},{12,4},{20,12},{28,20},{24,28},{16,24},{8,16},{0,8},{5,1},{1... | collective-permute-start | bytes 393224 | tf_op jit(solution)/shard_map/ppermute | solution.py:253
  42.4 5.0 %collective-permute-start.16 = (bf16[2,128,256]{2,1,0:T(8,128)(2,1)S(1)}, bf16[2,128,256]{2,1,0:T(8,128)(2,1)S(1)}, u32[]{:S(2)}, u32[]{:S(2)}) collective-permute-start(bf16[2,128,256]{2,1,0:T(8,128)(2,1)S(1)} %collective-permute-done.14.refs_8_.refs_3_), channel_id=1, source_target_pairs={{0,4},{4,12},{12,20},{20,28},{28,24},{24,16},{16,8},{8,0},{1,5},{5... | collective-permute-start | bytes 393224 | tf_op jit(solution)/shard_map/ppermute | solution.py:250
  43.9 7.8 %collective-permute-start.15 = (bf16[2,128,256]{2,1,0:T(8,128)(2,1)S(1)}, bf16[2,128,256]{2,1,0:T(8,128)(2,1)S(1)}, u32[]{:S(2)}, u32[]{:S(2)}) collective-permute-start(bf16[2,128,256]{2,1,0:T(8,128)(2,1)S(1)} %collective-permute-done.12.refs_7_.refs_2_), channel_id=1, source_target_pairs={{4,0},{12,4},{20,12},{28,20},{24,28},{16,24},{8,16},{0,8},{5,1},{1... | collective-permute-start | bytes 393224 | tf_op jit(solution)/shard_map/ppermute | solution.py:253
  47.4 5.0 %collective-permute-start.17 = (bf16[2,128,256]{2,1,0:T(8,128)(2,1)S(1)}, bf16[2,128,256]{2,1,0:T(8,128)(2,1)S(1)}, u32[]{:S(2)}, u32[]{:S(2)}) collective-permute-start(bf16[2,128,256]{2,1,0:T(8,128)(2,1)S(1)} %collective-permute-done.16.refs_7_), channel_id=1, source_target_pairs={{0,4},{4,12},{12,20},{20,28},{28,24},{24,16},{16,8},{8,0},{1,5},{5... | collective-permute-start | bytes 393224 | tf_op jit(solution)/shard_map/ppermute | solution.py:250
  52.7 2.2 %collective-permute-start.21 = (bf16[128,256]{1,0:T(8,128)(2,1)S(1)}, bf16[128,256]{1,0:T(8,128)(2,1)S(1)}, u32[]{:S(2)}, u32[]{:S(2)}) collective-permute-start(bf16[128,256]{1,0:T(8,128)(2,1)S(1)} %get-tuple-element.46), channel_id=1, source_target_pairs={{0,1},{1,0},{2,3},{3,2},{4,5},{5,4},{6,7},{7,6},{8,9},{9,8},{10,11... | collective-permute-start | bytes 196616 | tf_op jit(solution)/shard_map/ppermute | solution.py:268
  52.8 3.3 %collective-permute-start.18 = (bf16[1,128,256]{2,1,0:T(8,128)(2,1)S(1)}, bf16[1,128,256]{2,1,0:T(8,128)(2,1)S(1)}, u32[]{:S(2)}, u32[]{:S(2)}) collective-permute-start(bf16[1,128,256]{2,1,0:T(8,128)(2,1)S(1)} %get-tuple-element.40), channel_id=1, source_target_pairs={{0,1},{1,0},{2,3},{3,2},{4,5},{5,4},{6,7},{7,6},{8,9},{9,8},{10,11... | collective-permute-start | bytes 196616 | tf_op jit(solution)/shard_map/ppermute | solution.py:268
  53.3 4.3 %collective-permute-start.19 = (bf16[1,128,256]{2,1,0:T(8,128)(2,1)S(1)}, bf16[1,128,256]{2,1,0:T(8,128)(2,1)S(1)}, u32[]{:S(2)}, u32[]{:S(2)}) collective-permute-start(bf16[1,128,256]{2,1,0:T(8,128)(2,1)S(1)} %get-tuple-element.41), channel_id=1, source_target_pairs={{0,2},{1,3},{2,0},{3,1},{4,6},{5,7},{6,4},{7,5},{8,10},{9,11},{10,... | collective-permute-start | bytes 196616 | tf_op jit(solution)/shard_map/ppermute | solution.py:268
  54.9 4.4 %collective-permute-start.20 = (bf16[1,128,256]{2,1,0:T(8,128)(2,1)S(1)}, bf16[1,128,256]{2,1,0:T(8,128)(2,1)S(1)}, u32[]{:S(2)}, u32[]{:S(2)}) collective-permute-start(bf16[1,128,256]{2,1,0:T(8,128)(2,1)S(1)} %get-tuple-element.42), channel_id=1, source_target_pairs={{0,3},{1,2},{2,1},{3,0},{4,7},{5,6},{6,5},{7,4},{8,11},{9,10},{10,... | collective-permute-start | bytes 196616 | tf_op jit(solution)/shard_map/ppermute | solution.py:268

commit v5 on v4

--- a/solution.py
+++ b/solution.py
@@ -163,70 +163,81 @@
                 chosen_ref[jq, :, at : at + size] = chosen[i]
 
 
-def late_kernel(n, early, late, final, total_ref, chosen_ref, *refs):
-    x_refs, refs = refs[: len(early)], refs[len(early) :]
-    late_refs, refs = refs[: len(late)], refs[len(late) :]
-    if not final:
-        panels_ref, refs = refs[0], refs[1:]
-    keep_ref, send_refs = refs[0], refs[1:]
-    for d, x_ref in zip(late if not final else (), late_refs):
-        panels_ref[d] = x_ref[...]
-    panels = jnp.concatenate([x_ref[j] for x_ref in late_refs for j in range(PAIR)], axis=0)
-    rows = 1 if final else PAIR
-    for jq in reversed(range(n)):
-        total = total_ref[jq] + jnp.dot(chosen_ref[jq], panels, preferred_element_type=jnp.float32)
-        if jq < rows:
-            keep_ref[jq] = total
-        else:
-            send_refs[jq // rows - 1][jq % rows] = total.astype(jnp.bfloat16)
-    if not final:
-        for d, x_ref in zip(early, x_refs):
-            panels_ref[d] = x_ref[...]
-
-
-def solve_kernel(level, me_ref, keep_ref, b_ref, d_ref, away_ref, *refs):
-    other_refs, out_ref, piece_refs = refs[: -PAIR - 1], refs[-PAIR - 1], refs[-PAIR:]
-    size, width = keep_ref.shape[1:]
+def late_total(jq, total_ref, chosen_ref, panels):
+    return total_ref[jq] + jnp.dot(chosen_ref[jq], panels, preferred_element_type=jnp.float32)
+
+
+def late_panels(x_refs):
+    return jnp.concatenate([x_ref[j] for x_ref in x_refs for j in range(PAIR)], axis=0)
+
+
+def away_kernel(late, total_ref, chosen_ref, *refs):
+    panels, out_refs = late_panels(refs[:late]), refs[late:]
+    rows = out_refs[0].shape[0]
+    for i, out_ref in enumerate(out_refs):
+        for row in range(rows):
+            out_ref[row] = late_total(PAIR + i * rows + row, total_ref, chosen_ref, panels).astype(jnp.bfloat16)
+
+
+def stay_kernel(level, late, early, me_ref, b_ref, d_ref, away_ref, total_ref, chosen_ref, *refs):
+    x_refs, (right_ref, inverse_ref, panels_ref) = refs[: len(late) + len(early)], refs[len(late) + len(early) :]
+    panels = late_panels(x_refs[: len(late)])
+    size, width = right_ref.shape[1:]
     at = (2 * level - 1) * size
     for j in range(PAIR):
-        total = keep_ref[j]
+        total = late_total(j, total_ref, chosen_ref, panels)
+        right = away_ref[at : at + size, :] if j else b_ref[level, 0, 0, :, my_columns(me_ref[0], width)]
+        right_ref[j] = right.astype(jnp.float32) - total
+        inverse_ref[j] = away_ref[at + size : at + 2 * size, :size] if j else d_ref[level, 0, 0]
+    for d, x_ref in zip(late + early, x_refs):
+        panels_ref[d] = x_ref[...]
+
+
+def last_stay_kernel(late, me_ref, b_ref, total_ref, chosen_ref, *refs):
+    x_refs, (right_ref, send_ref) = refs[:late], refs[late:]
+    panels = late_panels(x_refs)
+    level, width = b_ref.shape[0] - 1, right_ref.shape[2]
+    send_ref[...] = late_total(1, total_ref, chosen_ref, panels).astype(jnp.bfloat16)
+    for j in range(PAIR):
+        right_ref[j] = b_ref[level, 0, 0, :, my_columns(me_ref[0] ^ j, width)].astype(jnp.float32)
+    right_ref[0] = right_ref[0] - late_total(0, total_ref, chosen_ref, panels)
+
+
+def solve_kernel(right_ref, inverse_ref, *refs):
+    other_refs, out_ref = refs[:-1], refs[-1]
+    for j in range(PAIR):
+        resid = right_ref[j]
         for other in other_refs:
-            total += other[j].astype(jnp.float32)
-        right = away_ref[at : at + size, :] if j else b_ref[level, 0, 0, :, my_columns(me_ref[0], width)]
-        inverse = away_ref[at + size : at + 2 * size, :size] if j else d_ref[level, 0, 0]
-        resid = (right.astype(jnp.float32) - total).astype(jnp.bfloat16)
-        value = jnp.dot(inverse, resid, preferred_element_type=jnp.float32).astype(jnp.bfloat16)
-        out_ref[j] = value
-        piece_refs[j][...] = value
+            resid -= other[j].astype(jnp.float32)
+        value = jnp.dot(inverse_ref[j], resid.astype(jnp.bfloat16), preferred_element_type=jnp.float32)
+        out_ref[j] = value.astype(jnp.bfloat16)
 
 
 def write_kernel(me_ref, full_ref, *refs):
-    piece_refs, (out_ref, sems) = refs[:-2], refs[-2:]
-    width = piece_refs[0].shape[1]
+    level_refs, (out_ref, sems) = refs[:-2], refs[-2:]
+    width = level_refs[0].shape[2]
     copies = [pltpu.make_async_copy(full_ref, out_ref.at[0, 0, 0], sems.at[0])]
-    for i, ref in enumerate(piece_refs):
+    for i, ref in enumerate(level_refs):
         target = out_ref.at[1 + i // PAIR, 0, 0, :, my_columns(me_ref[0] ^ (i % PAIR), width)]
-        copies.append(pltpu.make_async_copy(ref, target, sems.at[1 + i]))
+        copies.append(pltpu.make_async_copy(ref if i % PAIR else ref.at[0], target, sems.at[1 + i]))
     for copy in copies:
         copy.start()
     for copy in copies:
         copy.wait()
 
 
-def last_kernel(n, me_ref, b_ref, d_ref, keep_ref, *refs):
-    other_refs, (_, out_ref, buf, sem) = refs[: n - 1], refs[n - 1 :]
-    me = me_ref[0]
-    width = keep_ref.shape[2]
+def last_kernel(me_ref, d_ref, right_ref, mate_ref, *refs):
+    other_refs, (_, out_ref, buf, sem) = refs[:-4], refs[-4:]
+    width = right_ref.shape[2]
     levels = out_ref.shape[0]
     for j in range(PAIR):
-        total = keep_ref[0] if j == 0 else jnp.zeros_like(keep_ref[0])
-        for jq in range(1, n):
-            if jq % PAIR == j:
-                total += other_refs[jq - 1][0].astype(jnp.float32)
-        columns = my_columns(me ^ j, width)
-        resid = (b_ref[levels - 1, 0, 0, :, columns].astype(jnp.float32) - total).astype(jnp.bfloat16)
-        value = jnp.dot(d_ref[levels - 1, 0, 0], resid, preferred_element_type=jnp.float32)
-        buf[:, columns] = value.astype(jnp.bfloat16)
+        resid = right_ref[j]
+        if j:
+            resid -= mate_ref[...].astype(jnp.float32)
+        for other in other_refs[j::PAIR]:
+            resid -= other[0].astype(jnp.float32)
+        value = jnp.dot(d_ref[levels - 1, 0, 0], resid.astype(jnp.bfloat16), preferred_element_type=jnp.float32)
+        buf[:, my_columns(me_ref[0] ^ j, width)] = value.astype(jnp.bfloat16)
     copy = pltpu.make_async_copy(buf, out_ref.at[levels - 1, 0, 0], sem)
     copy.start()
     copy.wait()
@@ -315,37 +326,49 @@
             compiler_params=params(),
         )(me, *index, *blocks, *kept, *[ring.found[d] for d in early])
         rows = 1 if final else PAIR
-        out_shape = [near((rows, size, width), jnp.float32)] + [near((rows, size, width))] * (n // rows - 1)
-        if not final:
-            out_shape = [near((m, PAIR, size, width))] + out_shape
-        found = pl.pallas_call(
-            functools.partial(late_kernel, n, early, late, final),
-            out_shape=out_shape,
-            in_specs=[vmem()] * (2 + m),
-            out_specs=[vmem()] * len(out_shape),
+        late_x, early_x = [ring.found[d] for d in late], [ring.found[d] for d in early]
+        partial = pl.pallas_call(
+            functools.partial(away_kernel, len(late)),
+            out_shape=[near((rows, size, width))] * ((n - PAIR) // rows),
+            in_specs=[vmem()] * (2 + len(late)),
+            out_specs=[vmem()] * ((n - PAIR) // rows),
             compiler_params=params(),
-        )(
-            total,
-            chosen,
-            *[ring.found[d] for d in early + late],
-        )
-        if not final:
-            panels, *found = found
-            kept.append(panels)
-        keep, *partial = found
-        others = [send(v, rows * (h + 1)) for h, v in enumerate(partial)]
+        )(total, chosen, *late_x)
+        others = [send(v, PAIR + rows * i) for i, v in enumerate(partial)]
         if final:
-            columns = [send(after(v, keep), 1) if i % PAIR else v for i, v in enumerate(columns)]
+            columns = [v for solved in columns for v in (solved, send(after(solved, total)[1], 1))]
+        total = after(total, partial)
+        if final:
             break
-        solved, *pieces = pl.pallas_call(
-            functools.partial(solve_kernel, level),
-            out_shape=[near((PAIR, size, width))] + [near((size, width))] * PAIR,
-            in_specs=[smem()] + [vmem()] * (4 + len(others)),
-            out_specs=[vmem()] * (1 + PAIR),
+        right, inverse, panels = pl.pallas_call(
+            functools.partial(stay_kernel, level, late, early),
+            out_shape=[
+                near((PAIR, size, width), jnp.float32),
+                near((PAIR, size, size)),
+                near((m, PAIR, size, width)),
+            ],
+            in_specs=[smem()] + [vmem()] * (5 + m),
+            out_specs=[vmem()] * 3,
             compiler_params=params(),
-        )(me, keep, b_panels, diag_inverse, away, *others)
-        columns += pieces
-
+        )(me, b_panels, diag_inverse, away, total, chosen, *late_x, *early_x)
+        kept.append(panels)
+        solved = pl.pallas_call(
+            solve_kernel,
+            out_shape=near((PAIR, size, width)),
+            in_specs=[vmem()] * (2 + len(others)),
+            out_specs=vmem(),
+            compiler_params=params(),
+        )(right, inverse, *others)
+        columns.append(solved)
+
+    right, mate = pl.pallas_call(
+        functools.partial(last_stay_kernel, len(late)),
+        out_shape=[near((PAIR, size, width), jnp.float32), near((size, width))],
+        in_specs=[smem()] + [vmem()] * (3 + len(late)),
+        out_specs=[vmem()] * 2,
+        compiler_params=params(),
+    )(me, b_panels, total, chosen, *late_x)
+    mate = send(after(mate, others[0]), 1)
     result = pl.pallas_call(
         write_kernel,
         out_shape=struct(b_panels.shape),
@@ -355,14 +378,14 @@
         compiler_params=params(),
     )(me, full, *columns)
     return pl.pallas_call(
-        functools.partial(last_kernel, n),
+        last_kernel,
         out_shape=struct(b_panels.shape),
         in_specs=[smem()] + [vmem()] * (3 + len(others)) + [anywhere()],
         out_specs=anywhere(),
         scratch_shapes=[pltpu.VMEM((size, front), jnp.bfloat16), pltpu.SemaphoreType.DMA],
         input_output_aliases={4 + len(others): 0},
         compiler_params=params(),
-    )(me, b_panels, diag_inverse, keep, *others, result)
+    )(me, diag_inverse, right, mate, *others, result)
 
 
 def cycle_of(mesh):
@@ -395,7 +418,7 @@
         front = b_panels.shape[-1]
         rows = mesh.shape["prow"]
         paired = n & (n - 1) == 0 and n >= PAIR and rows % 2 == 0 and rows > 2 and front % (PAIR * LANES) == 0
-        paired = paired and b_panels.shape[0] > 1 and front >= PAIR * b_panels.shape[-2]
+        paired = paired and n > PAIR and b_panels.shape[0] > 2 and front >= PAIR * b_panels.shape[-2]
         if paired and l_blocks.size * l_blocks.dtype.itemsize <= BLOCK_BYTES:
             return solve_paired(cycle, b_panels, diag_inverse, l_blocks, block_cols, live_counts)
         return solve_scattered(b_panels, diag_inverse, l_blocks, block_cols, live_counts)

time: 60.9 us -> 59.4 us (0.975)
  waiting for transfers between devices: 28 us -> 25 us
  Pallas kernels: 11.7 us -> 12.5 us
    ppermute x8, waiting for transfers between devices: 7.55 us -> 4.92 us  [send(): return lax.ppermute(value, 'pcol', [(i, i ^ bits) for i in range(n)])]
    pallas_call x4 -> x6, Pallas kernels: 2.93 us -> 3.77 us  [the longest x1 1.4 us: solve_paired(): pl.pallas_call(last_kernel, out_shape=struct(b_panels.shape), in_specs=[s...]
  transfers between devices with their start and end apart: 22 -> 22, of which waited for: 13 -> 12; matrix products, arithmetic and copies ran while one was open for 0% -> 0% of each run, Pallas kernels for 11% -> 15%
where the time goes in v5:
time: 59.4 us; the launch traced here: 58.8 us
  waiting for transfers between devices  25 us (42%)
  starting transfers between devices  21 us (35%)
  Pallas kernels  12.5 us (21%)
    ppermute x8, waiting for transfers between devices, advance(): self.behind = lax.ppermute(self.behind, 'prow', self.to_next)  20.1 us
    ppermute x8, starting transfers between devices, advance(): self.behind = lax.ppermute(self.behind, 'prow', self.to_next)  13.8 us
    pallas_call x2, Pallas kernels, solve_paired(): pl.pallas_call(functools.partial(gather_kernel, n, level, m, early, late)...  5.69 us
    ppermute x8, waiting for transfers between devices, send(): return lax.ppermute(value, 'pcol', [(i, i ^ bits) for i in range(n)])  4.92 us
    ppermute x8, starting transfers between devices, send(): return lax.ppermute(value, 'pcol', [(i, i ^ bits) for i in range(n)])  4.82 us
    ppermute x6, starting transfers between devices, advance(): self.ahead = lax.ppermute(self.ahead, 'prow', self.to_last)  2.4 us
    pallas_call x1, Pallas kernels, solve_paired(): pl.pallas_call(functools.partial(first_kernel, n, m, place), out_shape=[n...  1.82 us
    pallas_call x1, Pallas kernels, solve_paired(): pl.pallas_call(last_kernel, out_shape=struct(b_panels.shape), in_specs=[s...  1.4 us
  transfers between devices with their start and end apart: 22, of which 12 were waited for; matrix products, arithmetic and copies ran while one was open for 0% of the time, Pallas kernels for 15%

profile of v5, /device:TPU:0, one launch (start us, length us, event | category | flops | bytes accessed | tf_op | source)
XLA Modules:
  0.0 58.8 jit_solution(11330052480330149537)
XLA Ops:
  0.0 0.1 pad_add_fusion.me_ref
  0.1 1.8 %shard_map.55 = (bf16[128,512]{1,0:T(8,128)(2,1)S(1)}, s32[8,128]{1,0:T(8,128)S(1)}, bf16[128,256]{1,0:T(8,128)(2,1)S(1)}, bf16[384,256]{1,0:T(8,128)(2,1)S(1)}) custom-call(s32[2]{0:T(128)S(1)} %pad_add_fusion.me_ref, s32[2,1,1,4]{3,2,1,0:T(1,128)} %counts_ref.1, s32[2,1,1,4,5]{4,3,2,1,0:T(4,128)} %cols_ref.1, bf16[3,1,1,128,512]{4,3,2,1,0:T(8,128)(2,1)} %b_ref.5, ...), custom_call_target="tpu_custom_call" | custom-call | tf_op jit(solution)/shard_map/pallas_call | solution.py:285
  1.9 0.5 collective-permute-start.1
  2.4 0.1 collective-permute-start
  2.5 1.0 %collective-permute-done.1.away_ref = bf16[384,256]{1,0:T(8,128)(2,1)S(1)} collective-permute-done((bf16[384,256]{1,0:T(8,128)(2,1)S(1)}, bf16[384,256]{1,0:T(8,128)(2,1)S(1)}, u32[]{:S(2)}, u32[]{:S(2)}) %collective-permute-start.1) | collective-permute-done | bytes 196640 | tf_op jit(solution)/shard_map/ppermute | solution.py:279
  3.5 0.1 collective-permute-done.refs_1_
  3.6 0.4 collective-permute-start.2
  4.0 2.6 %collective-permute-start.5 = (bf16[2,128,256]{2,1,0:T(8,128)(2,1)S(1)}, bf16[2,128,256]{2,1,0:T(8,128)(2,1)S(1)}, u32[]{:S(2)}, u32[]{:S(2)}) collective-permute-start(bf16[2,128,256]{2,1,0:T(8,128)(2,1)S(1)} %pad_maximum_fusion.refs_4_.refs_3_), channel_id=1, source_target_pairs={{0,4},{4,12},{12,20},{20,28},{28,24},{24,16},{16,8},{8,0},{1,5},{5... | collective-permute-start | bytes 393224 | tf_op jit(solution)/shard_map/ppermute | solution.py:261
  6.6 0.1 collective-permute-start.3
  6.7 4.0 %collective-permute-done.5.refs_8_.refs_7_ = bf16[2,128,256]{2,1,0:T(8,128)(2,1)S(1)} collective-permute-done((bf16[2,128,256]{2,1,0:T(8,128)(2,1)S(1)}, bf16[2,128,256]{2,1,0:T(8,128)(2,1)S(1)}, u32[]{:S(2)}, u32[]{:S(2)}) %collective-permute-start.5) | collective-permute-done | bytes 131104 | tf_op jit(solution)/shard_map/ppermute | solution.py:261
  10.7 1.7 %collective-permute-start.6 = (bf16[2,128,256]{2,1,0:T(8,128)(2,1)S(1)}, bf16[2,128,256]{2,1,0:T(8,128)(2,1)S(1)}, u32[]{:S(2)}, u32[]{:S(2)}) collective-permute-start(bf16[2,128,256]{2,1,0:T(8,128)(2,1)S(1)} %collective-permute-done.5.refs_8_.refs_7_), channel_id=1, source_target_pairs={{0,4},{4,12},{12,20},{20,28},{28,24},{24,16},{16,8},{8,0},{1,5},{5... | collective-permute-start | bytes 393224 | tf_op jit(solution)/shard_map/ppermute | solution.py:261
  12.4 0.0 collective-permute-done.3.refs_5_.refs_4_
  12.4 0.4 collective-permute-start.4
  12.7 3.2 %collective-permute-done.6.refs_7_.refs_6_ = bf16[2,128,256]{2,1,0:T(8,128)(2,1)S(1)} collective-permute-done((bf16[2,128,256]{2,1,0:T(8,128)(2,1)S(1)}, bf16[2,128,256]{2,1,0:T(8,128)(2,1)S(1)}, u32[]{:S(2)}, u32[]{:S(2)}) %collective-permute-start.6) | collective-permute-done | bytes 131104 | tf_op jit(solution)/shard_map/ppermute | solution.py:261
  15.9 1.4 %collective-permute-start.8 = (bf16[2,128,256]{2,1,0:T(8,128)(2,1)S(1)}, bf16[2,128,256]{2,1,0:T(8,128)(2,1)S(1)}, u32[]{:S(2)}, u32[]{:S(2)}) collective-permute-start(bf16[2,128,256]{2,1,0:T(8,128)(2,1)S(1)} %collective-permute-done.6.refs_7_.refs_6_), channel_id=1, source_target_pairs={{0,4},{4,12},{12,20},{20,28},{28,24},{24,16},{16,8},{8,0},{1,5},{5... | collective-permute-start | bytes 393224 | tf_op jit(solution)/shard_map/ppermute | solution.py:261
  17.3 0.0 collective-permute-done.4.refs_6_.refs_5_
  17.3 0.6 %collective-permute-start.7 = (bf16[2,128,256]{2,1,0:T(8,128)(2,1)S(1)}, bf16[2,128,256]{2,1,0:T(8,128)(2,1)S(1)}, u32[]{:S(2)}, u32[]{:S(2)}) collective-permute-start(bf16[2,128,256]{2,1,0:T(8,128)(2,1)S(1)} %collective-permute-done.4.refs_6_.refs_5_), channel_id=1, source_target_pairs={{4,0},{12,4},{20,12},{28,20},{24,28},{16,24},{8,16},{0,8},{5,1},{1... | collective-permute-start | bytes 393224 | tf_op jit(solution)/shard_map/ppermute | solution.py:264
  17.9 2.9 %collective-permute-done.8.refs_2_ = bf16[2,128,256]{2,1,0:T(8,128)(2,1)S(1)} collective-permute-done((bf16[2,128,256]{2,1,0:T(8,128)(2,1)S(1)}, bf16[2,128,256]{2,1,0:T(8,128)(2,1)S(1)}, u32[]{:S(2)}, u32[]{:S(2)}) %collective-permute-start.8) | collective-permute-done | bytes 131104 | tf_op jit(solution)/shard_map/ppermute | solution.py:261
  20.9 1.6 %collective-permute-start.9 = (bf16[2,128,256]{2,1,0:T(8,128)(2,1)S(1)}, bf16[2,128,256]{2,1,0:T(8,128)(2,1)S(1)}, u32[]{:S(2)}, u32[]{:S(2)}) collective-permute-start(bf16[2,128,256]{2,1,0:T(8,128)(2,1)S(1)} %collective-permute-done.8.refs_2_), channel_id=1, source_target_pairs={{0,4},{4,12},{12,20},{20,28},{28,24},{24,16},{16,8},{8,0},{1,5},{5... | collective-permute-start | bytes 393224 | tf_op jit(solution)/shard_map/ppermute | solution.py:261
  22.4 0.0 collective-permute-done.2.refs_3_
  22.4 2.8 %shard_map.56 = (f32[4,128,256]{2,1,0:T(8,128)S(1)}, bf16[4,128,768]{2,1,0:T(8,128)(2,1)S(1)}) custom-call(s32[2]{0:T(128)S(1)} %pad_add_fusion.me_ref, s32[8,128]{1,0:T(8,128)S(1)} %get-tuple-element.26.refs_0_, s32[8,128]{1,0:T(8,128)S(1)} %collective-permute-done.refs_1_, bf16[2,1,1,4,5,128,128]{6,5,4,3,2,1,0:T(8,128)(2,1)} %refs_2_.3, ...), custom_call_target="tpu_custom_call" | custom-call | tf_op jit(solution)/shard_map/pallas_call | solution.py:316
  25.2 0.0 copy-start
  25.3 0.0 copy-start.1
  25.3 0.0 collective-permute-done.7.refs_0_
  25.3 0.5 collective-permute-done.9.refs_1_
  25.8 0.3 shard_map.57
  26.1 1.6 %collective-permute-start.10 = (bf16[2,128,256]{2,1,0:T(8,128)(2,1)S(1)}, bf16[2,128,256]{2,1,0:T(8,128)(2,1)S(1)}, u32[]{:S(2)}, u32[]{:S(2)}) collective-permute-start(bf16[2,128,256]{2,1,0:T(8,128)(2,1)S(1)} %shard_map.57), channel_id=1, source_target_pairs={{0,2},{1,3},{2,0},{3,1},{4,6},{5,7},{6,4},{7,5},{8,10},{9,11},{10,... | collective-permute-start | bytes 393224 | tf_op jit(solution)/shard_map/ppermute | solution.py:279
  27.8 0.0 copy-done
  27.8 0.0 copy-done.1
  27.8 0.8 %shard_map.58 = (f32[2,128,256]{2,1,0:T(8,128)S(1)}, bf16[2,128,128]{2,1,0:T(8,128)(2,1)S(1)}, bf16[8,2,128,256]{3,2,1,0:T(8,128)(2,1)S(1)}) custom-call(s32[2]{0:T(128)S(1)} %pad_add_fusion.me_ref, bf16[3,1,1,128,512]{4,3,2,1,0:T(8,128)(2,1)S(1)} %copy-done, bf16[3,1,1,128,128]{4,3,2,1,0:T(8,128)(2,1)S(1)} %copy-done.1, ...), custom_call_target="tpu_custom_call" | custom-call | tf_op jit(solution)/shard_map/pallas_call | solution.py:343
  28.6 2.5 %collective-permute-done.10.refs_0_ = bf16[2,128,256]{2,1,0:T(8,128)(2,1)S(1)} collective-permute-done((bf16[2,128,256]{2,1,0:T(8,128)(2,1)S(1)}, bf16[2,128,256]{2,1,0:T(8,128)(2,1)S(1)}, u32[]{:S(2)}, u32[]{:S(2)}) %collective-permute-start.10) | collective-permute-done | bytes 131104 | tf_op jit(solution)/shard_map/ppermute | solution.py:279
  31.1 0.2 shard_map.59.refs_5_.refs_0_
  31.3 1.6 %collective-permute-start.13 = (bf16[2,128,256]{2,1,0:T(8,128)(2,1)S(1)}, bf16[2,128,256]{2,1,0:T(8,128)(2,1)S(1)}, u32[]{:S(2)}, u32[]{:S(2)}) collective-permute-start(bf16[2,128,256]{2,1,0:T(8,128)(2,1)S(1)} %shard_map.59.refs_5_.refs_0_), channel_id=1, source_target_pairs={{0,4},{4,12},{12,20},{20,28},{28,24},{24,16},{16,8},{8,0},{1,5},{5... | collective-permute-start | bytes 393224 | tf_op jit(solution)/shard_map/ppermute | solution.py:261
  32.9 0.5 collective-permute-start.11
  33.4 3.0 %collective-permute-done.13.refs_9_ = bf16[2,128,256]{2,1,0:T(8,128)(2,1)S(1)} collective-permute-done((bf16[2,128,256]{2,1,0:T(8,128)(2,1)S(1)}, bf16[2,128,256]{2,1,0:T(8,128)(2,1)S(1)}, u32[]{:S(2)}, u32[]{:S(2)}) %collective-permute-start.13) | collective-permute-done | bytes 131104 | tf_op jit(solution)/shard_map/ppermute | solution.py:261
  36.4 1.5 %collective-permute-start.14 = (bf16[2,128,256]{2,1,0:T(8,128)(2,1)S(1)}, bf16[2,128,256]{2,1,0:T(8,128)(2,1)S(1)}, u32[]{:S(2)}, u32[]{:S(2)}) collective-permute-start(bf16[2,128,256]{2,1,0:T(8,128)(2,1)S(1)} %collective-permute-done.13.refs_9_), channel_id=1, source_target_pairs={{0,4},{4,12},{12,20},{20,28},{28,24},{24,16},{16,8},{8,0},{1,5},{5... | collective-permute-start | bytes 393224 | tf_op jit(solution)/shard_map/ppermute | solution.py:261
  37.9 0.0 collective-permute-done.11.refs_6_
  37.9 0.5 collective-permute-start.12
  38.4 3.0 %collective-permute-done.14.refs_8_ = bf16[2,128,256]{2,1,0:T(8,128)(2,1)S(1)} collective-permute-done((bf16[2,128,256]{2,1,0:T(8,128)(2,1)S(1)}, bf16[2,128,256]{2,1,0:T(8,128)(2,1)S(1)}, u32[]{:S(2)}, u32[]{:S(2)}) %collective-permute-start.14) | collective-permute-done | bytes 131104 | tf_op jit(solution)/shard_map/ppermute | solution.py:261
  41.4 1.7 %collective-permute-start.16 = (bf16[2,128,256]{2,1,0:T(8,128)(2,1)S(1)}, bf16[2,128,256]{2,1,0:T(8,128)(2,1)S(1)}, u32[]{:S(2)}, u32[]{:S(2)}) collective-permute-start(bf16[2,128,256]{2,1,0:T(8,128)(2,1)S(1)} %collective-permute-done.14.refs_8_), channel_id=1, source_target_pairs={{0,4},{4,12},{12,20},{20,28},{28,24},{24,16},{16,8},{8,0},{1,5},{5... | collective-permute-start | bytes 393224 | tf_op jit(solution)/shard_map/ppermute | solution.py:261
  43.2 0.0 collective-permute-done.12.refs_7_
  43.2 0.4 collective-permute-start.15
  43.6 2.9 %collective-permute-done.16.refs_2_ = bf16[2,128,256]{2,1,0:T(8,128)(2,1)S(1)} collective-permute-done((bf16[2,128,256]{2,1,0:T(8,128)(2,1)S(1)}, bf16[2,128,256]{2,1,0:T(8,128)(2,1)S(1)}, u32[]{:S(2)}, u32[]{:S(2)}) %collective-permute-start.16) | collective-permute-done | bytes 131104 | tf_op jit(solution)/shard_map/ppermute | solution.py:261
  46.5 1.6 %collective-permute-start.17 = (bf16[2,128,256]{2,1,0:T(8,128)(2,1)S(1)}, bf16[2,128,256]{2,1,0:T(8,128)(2,1)S(1)}, u32[]{:S(2)}, u32[]{:S(2)}) collective-permute-start(bf16[2,128,256]{2,1,0:T(8,128)(2,1)S(1)} %collective-permute-done.16.refs_2_), channel_id=1, source_target_pairs={{0,4},{4,12},{12,20},{20,28},{28,24},{24,16},{16,8},{8,0},{1,5},{5... | collective-permute-start | bytes 393224 | tf_op jit(solution)/shard_map/ppermute | solution.py:261
  48.1 2.9 %shard_map.60 = (f32[4,128,256]{2,1,0:T(8,128)S(1)}, bf16[4,128,768]{2,1,0:T(8,128)(2,1)S(1)}) custom-call(s32[2]{0:T(128)S(1)} %pad_add_fusion.me_ref, s32[8,128]{1,0:T(8,128)S(1)} %get-tuple-element.26.refs_0_, s32[8,128]{1,0:T(8,128)S(1)} %collective-permute-done.refs_1_, bf16[2,1,1,4,5,128,128]{6,5,4,3,2,1,0:T(8,128)(2,1)} %refs_2_.3, ...), custom_call_target="tpu_custom_call" | custom-call | tf_op jit(solution)/shard_map/pallas_call | solution.py:316
  51.0 0.0 collective-permute-done.15.refs_0_
  51.0 0.5 collective-permute-done.17.refs_1_
  51.5 0.3 shard_map.61
  51.8 1.7 %collective-permute-start.18 = (bf16[1,128,256]{2,1,0:T(8,128)(2,1)S(1)}, bf16[1,128,256]{2,1,0:T(8,128)(2,1)S(1)}, u32[]{:S(2)}, u32[]{:S(2)}) collective-permute-start(bf16[1,128,256]{2,1,0:T(8,128)(2,1)S(1)} %get-tuple-element.39), channel_id=1, source_target_pairs={{0,2},{1,3},{2,0},{3,1},{4,6},{5,7},{6,4},{7,5},{8,10},{9,11},{10,... | collective-permute-start | bytes 196616 | tf_op jit(solution)/shard_map/ppermute | solution.py:279
  53.5 0.0 collective-permute-start.21
  53.5 0.5 collective-permute-start.20
  54.0 0.8 %shard_map.62 = (f32[2,128,256]{2,1,0:T(8,128)S(1)}, bf16[128,256]{1,0:T(8,128)(2,1)S(1)}) custom-call(s32[2]{0:T(128)S(1)} %pad_add_fusion.me_ref, bf16[3,1,1,128,512]{4,3,2,1,0:T(8,128)(2,1)S(1)} %copy-done, f32[4,128,256]{2,1,0:T(8,128)S(1)} %get-tuple-element.41.total_ref, bf16[4,128,768]{2,1,0:T(8,128)(2,1)S(1)} %get-tuple-element.38.chosen_ref, ...), custom_call_target="tpu_custom_call" | custom-call | tf_op jit(solution)/shard_map/pallas_call | solution.py:364
  54.8 1.3 %collective-permute-done.18.refs_0_ = bf16[1,128,256]{2,1,0:T(8,128)(2,1)S(1)} collective-permute-done((bf16[1,128,256]{2,1,0:T(8,128)(2,1)S(1)}, bf16[1,128,256]{2,1,0:T(8,128)(2,1)S(1)}, u32[]{:S(2)}, u32[]{:S(2)}) %collective-permute-start.18) | collective-permute-done | bytes 65568 | tf_op jit(solution)/shard_map/ppermute | solution.py:279
  56.1 0.0 collective-permute-start.19
  56.1 0.0 collective-permute-done.21.refs_1_
  56.1 1.3 %shard_map.63.refs_2_ = bf16[3,1,1,128,512]{4,3,2,1,0:T(8,128)(2,1)} custom-call(s32[2]{0:T(128)S(1)} %pad_add_fusion.me_ref, bf16[128,512]{1,0:T(8,128)(2,1)S(1)} %get-tuple-element.45.full_ref, bf16[2,128,256]{2,1,0:T(8,128)(2,1)S(1)} %shard_map.59.refs_5_.refs_0_, bf16[128,256]{1,0:T(8,128)(2,1)S(1)} %collective-permute-done.21.refs_1_), custom_call_target="tpu_custom_call" | custom-call | tf_op jit(solution)/shard_map/pallas_call | solution.py:372
  57.4 0.0 collective-permute-done.20.refs_1_
  57.4 0.0 collective-permute-done.19.mate_ref
  57.4 1.4 %shard_map.64 = bf16[3,1,1,128,512]{4,3,2,1,0:T(8,128)(2,1)} custom-call(s32[2]{0:T(128)S(1)} %pad_add_fusion.me_ref, bf16[3,1,1,128,128]{4,3,2,1,0:T(8,128)(2,1)S(1)} %copy-done.1, f32[2,128,256]{2,1,0:T(8,128)S(1)} %get-tuple-element.42.right_ref, bf16[128,256]{1,0:T(8,128)(2,1)S(1)} %collective-permute-done.19.mate_ref, ...), custom_call_target="tpu_custom_call", output_to_operand_aliasing={{}: (6, {})} | custom-call | tf_op jit(solution)/shard_map/pallas_call | solution.py:380
  (3 shorter events, 0.0 us)
Async XLA Ops:
  1.9 1.6 %collective-permute-start.1 = (bf16[384,256]{1,0:T(8,128)(2,1)S(1)}, bf16[384,256]{1,0:T(8,128)(2,1)S(1)}, u32[]{:S(2)}, u32[]{:S(2)}) collective-permute-start(bf16[384,256]{1,0:T(8,128)(2,1)S(1)} %get-tuple-element.28), channel_id=1, source_target_pairs={{0,1},{1,0},{2,3},{3,2},{4,5},{5,4},{6,7},{7,6},{8,9},{9,8},{10,11... | collective-permute-start | bytes 589832 | tf_op jit(solution)/shard_map/ppermute | solution.py:279
  2.4 1.2 %collective-permute-start = (s32[8,128]{1,0:T(8,128)S(1)}, s32[8,128]{1,0:T(8,128)S(1)}, u32[]{:S(2)}, u32[]{:S(2)}) collective-permute-start(s32[8,128]{1,0:T(8,128)S(1)} %get-tuple-element.26.refs_0_), channel_id=1, source_target_pairs={{0,1},{1,0},{2,3},{3,2},{4,5},{5,4},{6,7},{7,6},{8,9},{9,8},{10,11... | collective-permute-start | bytes 12296 | tf_op jit(solution)/shard_map/ppermute | solution.py:279
  3.6 18.8 %collective-permute-start.2 = (bf16[2,1,1,4,5,128,128]{6,5,4,3,2,1,0:T(8,128)(2,1)}, bf16[2,1,1,4,5,128,128]{6,5,4,3,2,1,0:T(8,128)(2,1)S(1)}, u32[]{:S(2)}, u32[]{:S(2)}) collective-permute-start(bf16[2,1,1,4,5,128,128]{6,5,4,3,2,1,0:T(8,128)(2,1)} %refs_2_.3), channel_id=1, source_target_pairs={{0,1},{1,0},{2,3},{3,2},{4,5},{5,4},{6,7},{7,6},{8,9},{9,8},{10,11... | collective-permute-start | bytes 3932168 | tf_op jit(solution)/shard_map/ppermute | solution.py:279
  4.0 6.7 %collective-permute-start.5 = (bf16[2,128,256]{2,1,0:T(8,128)(2,1)S(1)}, bf16[2,128,256]{2,1,0:T(8,128)(2,1)S(1)}, u32[]{:S(2)}, u32[]{:S(2)}) collective-permute-start(bf16[2,128,256]{2,1,0:T(8,128)(2,1)S(1)} %pad_maximum_fusion.refs_4_.refs_3_), channel_id=1, source_target_pairs={{0,4},{4,12},{12,20},{20,28},{28,24},{24,16},{16,8},{8,0},{1,5},{5... | collective-permute-start | bytes 393224 | tf_op jit(solution)/shard_map/ppermute | solution.py:261
  6.6 5.8 %collective-permute-start.3 = (bf16[2,128,256]{2,1,0:T(8,128)(2,1)S(1)}, bf16[2,128,256]{2,1,0:T(8,128)(2,1)S(1)}, u32[]{:S(2)}, u32[]{:S(2)}) collective-permute-start(bf16[2,128,256]{2,1,0:T(8,128)(2,1)S(1)} %pad_maximum_fusion.refs_4_.refs_3_), channel_id=1, source_target_pairs={{4,0},{12,4},{20,12},{28,20},{24,28},{16,24},{8,16},{0,8},{5,1},{1... | collective-permute-start | bytes 393224 | tf_op jit(solution)/shard_map/ppermute | solution.py:264
  10.7 5.2 %collective-permute-start.6 = (bf16[2,128,256]{2,1,0:T(8,128)(2,1)S(1)}, bf16[2,128,256]{2,1,0:T(8,128)(2,1)S(1)}, u32[]{:S(2)}, u32[]{:S(2)}) collective-permute-start(bf16[2,128,256]{2,1,0:T(8,128)(2,1)S(1)} %collective-permute-done.5.refs_8_.refs_7_), channel_id=1, source_target_pairs={{0,4},{4,12},{12,20},{20,28},{28,24},{24,16},{16,8},{8,0},{1,5},{5... | collective-permute-start | bytes 393224 | tf_op jit(solution)/shard_map/ppermute | solution.py:261
  12.4 5.0 %collective-permute-start.4 = (bf16[2,128,256]{2,1,0:T(8,128)(2,1)S(1)}, bf16[2,128,256]{2,1,0:T(8,128)(2,1)S(1)}, u32[]{:S(2)}, u32[]{:S(2)}) collective-permute-start(bf16[2,128,256]{2,1,0:T(8,128)(2,1)S(1)} %collective-permute-done.3.refs_5_.refs_4_), channel_id=1, source_target_pairs={{4,0},{12,4},{20,12},{28,20},{24,28},{16,24},{8,16},{0,8},{5,1},{1... | collective-permute-start | bytes 393224 | tf_op jit(solution)/shard_map/ppermute | solution.py:264
  15.9 5.0 %collective-permute-start.8 = (bf16[2,128,256]{2,1,0:T(8,128)(2,1)S(1)}, bf16[2,128,256]{2,1,0:T(8,128)(2,1)S(1)}, u32[]{:S(2)}, u32[]{:S(2)}) collective-permute-start(bf16[2,128,256]{2,1,0:T(8,128)(2,1)S(1)} %collective-permute-done.6.refs_7_.refs_6_), channel_id=1, source_target_pairs={{0,4},{4,12},{12,20},{20,28},{28,24},{24,16},{16,8},{8,0},{1,5},{5... | collective-permute-start | bytes 393224 | tf_op jit(solution)/shard_map/ppermute | solution.py:261
  17.3 7.9 %collective-permute-start.7 = (bf16[2,128,256]{2,1,0:T(8,128)(2,1)S(1)}, bf16[2,128,256]{2,1,0:T(8,128)(2,1)S(1)}, u32[]{:S(2)}, u32[]{:S(2)}) collective-permute-start(bf16[2,128,256]{2,1,0:T(8,128)(2,1)S(1)} %collective-permute-done.4.refs_6_.refs_5_), channel_id=1, source_target_pairs={{4,0},{12,4},{20,12},{28,20},{24,28},{16,24},{8,16},{0,8},{5,1},{1... | collective-permute-start | bytes 393224 | tf_op jit(solution)/shard_map/ppermute | solution.py:264
  20.9 5.0 %collective-permute-start.9 = (bf16[2,128,256]{2,1,0:T(8,128)(2,1)S(1)}, bf16[2,128,256]{2,1,0:T(8,128)(2,1)S(1)}, u32[]{:S(2)}, u32[]{:S(2)}) collective-permute-start(bf16[2,128,256]{2,1,0:T(8,128)(2,1)S(1)} %collective-permute-done.8.refs_2_), channel_id=1, source_target_pairs={{0,4},{4,12},{12,20},{20,28},{28,24},{24,16},{16,8},{8,0},{1,5},{5... | collective-permute-start | bytes 393224 | tf_op jit(solution)/shard_map/ppermute | solution.py:261
  25.2 2.5 %copy-start = (bf16[3,1,1,128,512]{4,3,2,1,0:T(8,128)(2,1)S(1)}, bf16[3,1,1,128,512]{4,3,2,1,0:T(8,128)(2,1)}, u32[]{:S(2)}) copy-start(bf16[3,1,1,128,512]{4,3,2,1,0:T(8,128)(2,1)} %b_ref.5) | copy-start | bytes 1179652
  25.3 2.5 %copy-start.1 = (bf16[3,1,1,128,128]{4,3,2,1,0:T(8,128)(2,1)S(1)}, bf16[3,1,1,128,128]{4,3,2,1,0:T(8,128)(2,1)}, u32[]{:S(2)}) copy-start(bf16[3,1,1,128,128]{4,3,2,1,0:T(8,128)(2,1)} %d_ref.5) | copy-start | bytes 294916
  26.1 5.0 %collective-permute-start.10 = (bf16[2,128,256]{2,1,0:T(8,128)(2,1)S(1)}, bf16[2,128,256]{2,1,0:T(8,128)(2,1)S(1)}, u32[]{:S(2)}, u32[]{:S(2)}) collective-permute-start(bf16[2,128,256]{2,1,0:T(8,128)(2,1)S(1)} %shard_map.57), channel_id=1, source_target_pairs={{0,2},{1,3},{2,0},{3,1},{4,6},{5,7},{6,4},{7,5},{8,10},{9,11},{10,... | collective-permute-start | bytes 393224 | tf_op jit(solution)/shard_map/ppermute | solution.py:279
  31.3 5.0 %collective-permute-start.13 = (bf16[2,128,256]{2,1,0:T(8,128)(2,1)S(1)}, bf16[2,128,256]{2,1,0:T(8,128)(2,1)S(1)}, u32[]{:S(2)}, u32[]{:S(2)}) collective-permute-start(bf16[2,128,256]{2,1,0:T(8,128)(2,1)S(1)} %shard_map.59.refs_5_.refs_0_), channel_id=1, source_target_pairs={{0,4},{4,12},{12,20},{20,28},{28,24},{24,16},{16,8},{8,0},{1,5},{5... | collective-permute-start | bytes 393224 | tf_op jit(solution)/shard_map/ppermute | solution.py:261
  32.9 5.0 %collective-permute-start.11 = (bf16[2,128,256]{2,1,0:T(8,128)(2,1)S(1)}, bf16[2,128,256]{2,1,0:T(8,128)(2,1)S(1)}, u32[]{:S(2)}, u32[]{:S(2)}) collective-permute-start(bf16[2,128,256]{2,1,0:T(8,128)(2,1)S(1)} %shard_map.59.refs_5_.refs_0_), channel_id=1, source_target_pairs={{4,0},{12,4},{20,12},{28,20},{24,28},{16,24},{8,16},{0,8},{5,1},{1... | collective-permute-start | bytes 393224 | tf_op jit(solution)/shard_map/ppermute | solution.py:264
  36.4 5.1 %collective-permute-start.14 = (bf16[2,128,256]{2,1,0:T(8,128)(2,1)S(1)}, bf16[2,128,256]{2,1,0:T(8,128)(2,1)S(1)}, u32[]{:S(2)}, u32[]{:S(2)}) collective-permute-start(bf16[2,128,256]{2,1,0:T(8,128)(2,1)S(1)} %collective-permute-done.13.refs_9_), channel_id=1, source_target_pairs={{0,4},{4,12},{12,20},{20,28},{28,24},{24,16},{16,8},{8,0},{1,5},{5... | collective-permute-start | bytes 393224 | tf_op jit(solution)/shard_map/ppermute | solution.py:261
  37.9 5.3 %collective-permute-start.12 = (bf16[2,128,256]{2,1,0:T(8,128)(2,1)S(1)}, bf16[2,128,256]{2,1,0:T(8,128)(2,1)S(1)}, u32[]{:S(2)}, u32[]{:S(2)}) collective-permute-start(bf16[2,128,256]{2,1,0:T(8,128)(2,1)S(1)} %collective-permute-done.11.refs_6_), channel_id=1, source_target_pairs={{4,0},{12,4},{20,12},{28,20},{24,28},{16,24},{8,16},{0,8},{5,1},{1... | collective-permute-start | bytes 393224 | tf_op jit(solution)/shard_map/ppermute | solution.py:264
  41.4 5.1 %collective-permute-start.16 = (bf16[2,128,256]{2,1,0:T(8,128)(2,1)S(1)}, bf16[2,128,256]{2,1,0:T(8,128)(2,1)S(1)}, u32[]{:S(2)}, u32[]{:S(2)}) collective-permute-start(bf16[2,128,256]{2,1,0:T(8,128)(2,1)S(1)} %collective-permute-done.14.refs_8_), channel_id=1, source_target_pairs={{0,4},{4,12},{12,20},{20,28},{28,24},{24,16},{16,8},{8,0},{1,5},{5... | collective-permute-start | bytes 393224 | tf_op jit(solution)/shard_map/ppermute | solution.py:261
  43.2 7.8 %collective-permute-start.15 = (bf16[2,128,256]{2,1,0:T(8,128)(2,1)S(1)}, bf16[2,128,256]{2,1,0:T(8,128)(2,1)S(1)}, u32[]{:S(2)}, u32[]{:S(2)}) collective-permute-start(bf16[2,128,256]{2,1,0:T(8,128)(2,1)S(1)} %collective-permute-done.12.refs_7_), channel_id=1, source_target_pairs={{4,0},{12,4},{20,12},{28,20},{24,28},{16,24},{8,16},{0,8},{5,1},{1... | collective-permute-start | bytes 393224 | tf_op jit(solution)/shard_map/ppermute | solution.py:264
  46.5 5.0 %collective-permute-start.17 = (bf16[2,128,256]{2,1,0:T(8,128)(2,1)S(1)}, bf16[2,128,256]{2,1,0:T(8,128)(2,1)S(1)}, u32[]{:S(2)}, u32[]{:S(2)}) collective-permute-start(bf16[2,128,256]{2,1,0:T(8,128)(2,1)S(1)} %collective-permute-done.16.refs_2_), channel_id=1, source_target_pairs={{0,4},{4,12},{12,20},{20,28},{28,24},{24,16},{16,8},{8,0},{1,5},{5... | collective-permute-start | bytes 393224 | tf_op jit(solution)/shard_map/ppermute | solution.py:261
  51.8 4.3 %collective-permute-start.18 = (bf16[1,128,256]{2,1,0:T(8,128)(2,1)S(1)}, bf16[1,128,256]{2,1,0:T(8,128)(2,1)S(1)}, u32[]{:S(2)}, u32[]{:S(2)}) collective-permute-start(bf16[1,128,256]{2,1,0:T(8,128)(2,1)S(1)} %get-tuple-element.39), channel_id=1, source_target_pairs={{0,2},{1,3},{2,0},{3,1},{4,6},{5,7},{6,4},{7,5},{8,10},{9,11},{10,... | collective-permute-start | bytes 196616 | tf_op jit(solution)/shard_map/ppermute | solution.py:279
  53.5 2.6 %collective-permute-start.21 = (bf16[128,256]{1,0:T(8,128)(2,1)S(1)}, bf16[128,256]{1,0:T(8,128)(2,1)S(1)}, u32[]{:S(2)}, u32[]{:S(2)}) collective-permute-start(bf16[128,256]{1,0:T(8,128)(2,1)S(1)} %slice_bitcast_fusion.1), channel_id=1, source_target_pairs={{0,1},{1,0},{2,3},{3,2},{4,5},{5,4},{6,7},{7,6},{8,9},{9,8},{10,11... | collective-permute-start | bytes 196616 | tf_op jit(solution)/shard_map/ppermute | solution.py:279
  53.5 3.9 %collective-permute-start.20 = (bf16[1,128,256]{2,1,0:T(8,128)(2,1)S(1)}, bf16[1,128,256]{2,1,0:T(8,128)(2,1)S(1)}, u32[]{:S(2)}, u32[]{:S(2)}) collective-permute-start(bf16[1,128,256]{2,1,0:T(8,128)(2,1)S(1)} %get-tuple-element.40), channel_id=1, source_target_pairs={{0,3},{1,2},{2,1},{3,0},{4,7},{5,6},{6,5},{7,4},{8,11},{9,10},{10,... | collective-permute-start | bytes 196616 | tf_op jit(solution)/shard_map/ppermute | solution.py:279
  56.1 1.3 %collective-permute-start.19 = (bf16[128,256]{1,0:T(8,128)(2,1)S(1)}, bf16[128,256]{1,0:T(8,128)(2,1)S(1)}, u32[]{:S(2)}, u32[]{:S(2)}) collective-permute-start(bf16[128,256]{1,0:T(8,128)(2,1)S(1)} %get-tuple-element.44), channel_id=1, source_target_pairs={{0,1},{1,0},{2,3},{3,2},{4,5},{5,4},{6,7},{7,6},{8,9},{9,8},{10,11... | collective-permute-start | bytes 196616 | tf_op jit(solution)/shard_map/ppermute | solution.py:279

commit v6 on v5

--- a/solution.py
+++ b/solution.py
@@ -72,7 +72,7 @@
     return jnp.stack(solutions)[:, None, None]
 
 
-def first_kernel(n, m, place, me_ref, counts_ref, cols_ref, b_ref, d_ref, full_ref, index_ref, own_ref, away_ref, *refs):
+def first_kernel(n, m, place, me_ref, counts_ref, cols_ref, b_ref, d_ref, full_ref, index_ref, own_ref, other_ref, away_ref, *refs):
     b_buf, d_buf, count_ref, col_ref, sems = refs
     middle = b_buf.shape[0]
     copies = [
@@ -89,9 +89,9 @@
         copy.wait()
     full_ref[...] = jnp.dot(d_buf[0], b_buf[0], preferred_element_type=jnp.float32).astype(jnp.bfloat16)
     own_ref[...] = full_ref[:, my_columns(me, width)]
-    away_ref[:size, :] = full_ref[:, my_columns(me ^ 1, width)]
+    other_ref[...] = full_ref[:, my_columns(me ^ 1, width)]
     for level in range(1, middle):
-        at = (2 * level - 1) * size
+        at = (2 * level - 2) * size
         away_ref[at : at + size, :] = b_buf[level, :, my_columns(me ^ 1, width)]
         away_ref[at + size : at + 2 * size, :size] = d_buf[level]
         away_ref[at + size : at + 2 * size, size:] = jnp.zeros((size, width - size), jnp.bfloat16)
@@ -183,7 +183,7 @@
     x_refs, (right_ref, inverse_ref, panels_ref) = refs[: len(late) + len(early)], refs[len(late) + len(early) :]
     panels = late_panels(x_refs[: len(late)])
     size, width = right_ref.shape[1:]
-    at = (2 * level - 1) * size
+    at = (2 * level - 2) * size
     for j in range(PAIR):
         total = late_total(j, total_ref, chosen_ref, panels)
         right = away_ref[at : at + size, :] if j else b_ref[level, 0, 0, :, my_columns(me_ref[0], width)]
@@ -282,16 +282,17 @@
 
     middle = levels - 1
 
-    full, index, own, away = pl.pallas_call(
+    full, index, own, other, away = pl.pallas_call(
         functools.partial(first_kernel, n, m, place),
         out_shape=[
             near((size, front)),
             near(index_shape, jnp.int32),
             near((size, width)),
-            near(((2 * middle - 1) * size, width)),
+            near((size, width)),
+            near(((2 * middle - 2) * size, width)),
         ],
         in_specs=[smem()] + [anywhere()] * 4,
-        out_specs=[vmem()] * 4,
+        out_specs=[vmem()] * 5,
         scratch_shapes=[
             pltpu.VMEM((middle, size, front), jnp.bfloat16),
             pltpu.VMEM((middle, size, size), jnp.bfloat16),
@@ -301,8 +302,8 @@
         ],
         compiler_params=params(),
     )(me, *[in_hbm(v) for v in (live_counts, block_cols, b_panels, diag_inverse)])
-    away, index = send(away, 1), [index, send(index, 1)]
-    solved = after(jnp.stack([own, away[:size]]), index[1])
+    other, away, index = send(other, 1), send(away, 1), [index, send(index, 1)]
+    solved = after(jnp.stack([own, other]), index[1])
     blocks = [in_hbm(l_blocks), send(after(l_blocks, solved), 1)]
 
     late = [d for d in range(1, m) if min(d, m - d) >= m // 2 - 1]
@@ -311,7 +312,9 @@
     for level in range(1, levels):
         final = level == levels - 1
         ring = Ring(solved, cycle)
-        for _ in range(m // 2):
+        for step in range(m // 2):
+            if level == 1 and step == 2:
+                ring.ahead = after(ring.ahead, away)
             ring.advance()
         total, chosen = pl.pallas_call(
             functools.partial(gather_kernel, n, level, m, early, late),

time: 59.4 us -> 58.7 us (0.988)
    ppermute x6, waiting for transfers between devices: 0.02 us -> 0.96 us  [advance(): self.ahead = lax.ppermute(self.ahead, 'prow', self.to_last)]
    ppermute x8, waiting for transfers between devices: 20.1 us -> 19.2 us  [advance(): self.behind = lax.ppermute(self.behind, 'prow', self.to_next)]
    ppermute x8 -> x9, starting transfers between devices: 4.82 us -> 4.63 us  [send(): return lax.ppermute(value, 'pcol', [(i, i ^ bits) for i in range(n)])]
    ppermute x8 -> x9, waiting for transfers between devices: 4.92 us -> 4.93 us  [send(): return lax.ppermute(value, 'pcol', [(i, i ^ bits) for i in range(n)])]
  transfers between devices with their start and end apart: 22 -> 23, of which waited for: 12 -> 13; matrix products, arithmetic and copies ran while one was open for 0% -> 0% of each run, Pallas kernels for 15% -> 15%
where the time goes in v6:
time: 58.7 us; the launch traced here: 58.4 us
  waiting for transfers between devices  25.1 us (43%)
  starting transfers between devices  20.6 us (35%)
  Pallas kernels  12.5 us (21%)
    ppermute x8, waiting for transfers between devices, advance(): self.behind = lax.ppermute(self.behind, 'prow', self.to_next)  19.2 us
    ppermute x8, starting transfers between devices, advance(): self.behind = lax.ppermute(self.behind, 'prow', self.to_next)  13.5 us
    pallas_call x2, Pallas kernels, solve_paired(): pl.pallas_call(functools.partial(gather_kernel, n, level, m, early, late)...  5.7 us
    ppermute x9, waiting for transfers between devices, send(): return lax.ppermute(value, 'pcol', [(i, i ^ bits) for i in range(n)])  4.93 us
    ppermute x9, starting transfers between devices, send(): return lax.ppermute(value, 'pcol', [(i, i ^ bits) for i in range(n)])  4.63 us
    ppermute x6, starting transfers between devices, advance(): self.ahead = lax.ppermute(self.ahead, 'prow', self.to_last)  2.49 us
    pallas_call x1, Pallas kernels, solve_paired(): pl.pallas_call(functools.partial(first_kernel, n, m, place), out_shape=[n...  1.82 us
    pallas_call x1, Pallas kernels, solve_paired(): pl.pallas_call(last_kernel, out_shape=struct(b_panels.shape), in_specs=[s...  1.4 us
  transfers between devices with their start and end apart: 23, of which 13 were waited for; matrix products, arithmetic and copies ran while one was open for 0% of the time, Pallas kernels for 15%

profile of v6, /device:TPU:0, one launch (start us, length us, event | category | flops | bytes accessed | tf_op | source)
XLA Modules:
  0.0 58.4 jit_solution(5041722772542198175)
XLA Ops:
  0.0 0.1 pad_add_fusion.me_ref
  0.1 1.8 %shard_map.55 = (bf16[128,512]{1,0:T(8,128)(2,1)S(1)}, s32[8,128]{1,0:T(8,128)S(1)}, bf16[128,256]{1,0:T(8,128)(2,1)S(1)}, bf16[128,256]{1,0:T(8,128)(2,1)S(1)}, bf16[256,256]{1,0:T(8,128)(2,1)S(1)}) custom-call(s32[2]{0:T(128)S(1)} %pad_add_fusion.me_ref, s32[2,1,1,4]{3,2,1,0:T(1,128)} %counts_ref.1, s32[2,1,1,4,5]{4,3,2,1,0:T(4,128)} %cols_ref.1, ...), custom_call_target="tpu_custom_call" | custom-call | tf_op jit(solution)/shard_map/pallas_call | solution.py:285
  1.9 0.5 collective-permute-start.1
  2.4 0.1 collective-permute-start
  2.5 0.8 %collective-permute-done.1 = bf16[128,256]{1,0:T(8,128)(2,1)S(1)} collective-permute-done((bf16[128,256]{1,0:T(8,128)(2,1)S(1)}, bf16[128,256]{1,0:T(8,128)(2,1)S(1)}, u32[]{:S(2)}, u32[]{:S(2)}) %collective-permute-start.1) | collective-permute-done | bytes 65568 | tf_op jit(solution)/shard_map/ppermute | solution.py:279
  3.3 0.2 collective-permute-done.refs_1_
  3.6 0.2 collective-permute-start.2
  3.8 2.8 %collective-permute-start.6 = (bf16[2,128,256]{2,1,0:T(8,128)(2,1)S(1)}, bf16[2,128,256]{2,1,0:T(8,128)(2,1)S(1)}, u32[]{:S(2)}, u32[]{:S(2)}) collective-permute-start(bf16[2,128,256]{2,1,0:T(8,128)(2,1)S(1)} %pad_maximum_fusion.refs_4_.refs_3_), channel_id=1, source_target_pairs={{0,4},{4,12},{12,20},{20,28},{28,24},{24,16},{16,8},{8,0},{1,5},{5... | collective-permute-start | bytes 393224 | tf_op jit(solution)/shard_map/ppermute | solution.py:261
  6.6 0.1 collective-permute-start.4
  6.7 3.8 %collective-permute-done.6.refs_8_.refs_7_ = bf16[2,128,256]{2,1,0:T(8,128)(2,1)S(1)} collective-permute-done((bf16[2,128,256]{2,1,0:T(8,128)(2,1)S(1)}, bf16[2,128,256]{2,1,0:T(8,128)(2,1)S(1)}, u32[]{:S(2)}, u32[]{:S(2)}) %collective-permute-start.6) | collective-permute-done | bytes 131104 | tf_op jit(solution)/shard_map/ppermute | solution.py:261
  10.5 1.7 %collective-permute-start.7 = (bf16[2,128,256]{2,1,0:T(8,128)(2,1)S(1)}, bf16[2,128,256]{2,1,0:T(8,128)(2,1)S(1)}, u32[]{:S(2)}, u32[]{:S(2)}) collective-permute-start(bf16[2,128,256]{2,1,0:T(8,128)(2,1)S(1)} %collective-permute-done.6.refs_8_.refs_7_), channel_id=1, source_target_pairs={{0,4},{4,12},{12,20},{20,28},{28,24},{24,16},{16,8},{8,0},{1,5},{5... | collective-permute-start | bytes 393224 | tf_op jit(solution)/shard_map/ppermute | solution.py:261
  12.2 0.0 collective-permute-start.3
  12.2 0.0 collective-permute-done.4.refs_5_.refs_4_
  12.2 0.4 collective-permute-start.5
  12.5 3.0 %collective-permute-done.7.refs_7_.refs_6_ = bf16[2,128,256]{2,1,0:T(8,128)(2,1)S(1)} collective-permute-done((bf16[2,128,256]{2,1,0:T(8,128)(2,1)S(1)}, bf16[2,128,256]{2,1,0:T(8,128)(2,1)S(1)}, u32[]{:S(2)}, u32[]{:S(2)}) %collective-permute-start.7) | collective-permute-done | bytes 131104 | tf_op jit(solution)/shard_map/ppermute | solution.py:261
  15.6 1.6 %collective-permute-start.9 = (bf16[2,128,256]{2,1,0:T(8,128)(2,1)S(1)}, bf16[2,128,256]{2,1,0:T(8,128)(2,1)S(1)}, u32[]{:S(2)}, u32[]{:S(2)}) collective-permute-start(bf16[2,128,256]{2,1,0:T(8,128)(2,1)S(1)} %collective-permute-done.7.refs_7_.refs_6_), channel_id=1, source_target_pairs={{0,4},{4,12},{12,20},{20,28},{28,24},{24,16},{16,8},{8,0},{1,5},{5... | collective-permute-start | bytes 393224 | tf_op jit(solution)/shard_map/ppermute | solution.py:261
  17.1 0.0 collective-permute-done.3.away_ref
  17.1 0.9 %collective-permute-done.5.refs_6_.refs_5_ = bf16[2,128,256]{2,1,0:T(8,128)(2,1)S(1)} collective-permute-done((bf16[2,128,256]{2,1,0:T(8,128)(2,1)S(1)}, bf16[2,128,256]{2,1,0:T(8,128)(2,1)S(1)}, u32[]{:S(2)}, u32[]{:S(2)}) %collective-permute-start.5) | collective-permute-done | bytes 131104 | tf_op jit(solution)/shard_map/ppermute | solution.py:264
  18.1 0.4 collective-permute-start.8
  18.5 2.1 %collective-permute-done.9.refs_2_ = bf16[2,128,256]{2,1,0:T(8,128)(2,1)S(1)} collective-permute-done((bf16[2,128,256]{2,1,0:T(8,128)(2,1)S(1)}, bf16[2,128,256]{2,1,0:T(8,128)(2,1)S(1)}, u32[]{:S(2)}, u32[]{:S(2)}) %collective-permute-start.9) | collective-permute-done | bytes 131104 | tf_op jit(solution)/shard_map/ppermute | solution.py:261
  20.6 1.6 %collective-permute-start.10 = (bf16[2,128,256]{2,1,0:T(8,128)(2,1)S(1)}, bf16[2,128,256]{2,1,0:T(8,128)(2,1)S(1)}, u32[]{:S(2)}, u32[]{:S(2)}) collective-permute-start(bf16[2,128,256]{2,1,0:T(8,128)(2,1)S(1)} %collective-permute-done.9.refs_2_), channel_id=1, source_target_pairs={{0,4},{4,12},{12,20},{20,28},{28,24},{24,16},{16,8},{8,0},{1,5},{5... | collective-permute-start | bytes 393224 | tf_op jit(solution)/shard_map/ppermute | solution.py:261
  22.1 0.0 collective-permute-done.2.refs_3_
  22.1 2.8 %shard_map.56 = (f32[4,128,256]{2,1,0:T(8,128)S(1)}, bf16[4,128,768]{2,1,0:T(8,128)(2,1)S(1)}) custom-call(s32[2]{0:T(128)S(1)} %pad_add_fusion.me_ref, s32[8,128]{1,0:T(8,128)S(1)} %get-tuple-element.28.refs_0_, s32[8,128]{1,0:T(8,128)S(1)} %collective-permute-done.refs_1_, bf16[2,1,1,4,5,128,128]{6,5,4,3,2,1,0:T(8,128)(2,1)} %refs_2_.3, ...), custom_call_target="tpu_custom_call" | custom-call | tf_op jit(solution)/shard_map/pallas_call | solution.py:319
  24.9 0.0 copy-start
  25.0 0.0 copy-start.1
  25.0 0.0 collective-permute-done.8.refs_0_
  25.0 0.5 collective-permute-done.10.refs_1_
  25.5 0.3 shard_map.57
  25.8 1.6 %collective-permute-start.11 = (bf16[2,128,256]{2,1,0:T(8,128)(2,1)S(1)}, bf16[2,128,256]{2,1,0:T(8,128)(2,1)S(1)}, u32[]{:S(2)}, u32[]{:S(2)}) collective-permute-start(bf16[2,128,256]{2,1,0:T(8,128)(2,1)S(1)} %shard_map.57), channel_id=1, source_target_pairs={{0,2},{1,3},{2,0},{3,1},{4,6},{5,7},{6,4},{7,5},{8,10},{9,11},{10,... | collective-permute-start | bytes 393224 | tf_op jit(solution)/shard_map/ppermute | solution.py:279
  27.4 0.0 copy-done
  27.4 0.0 copy-done.1
  27.5 0.8 %shard_map.58 = (f32[2,128,256]{2,1,0:T(8,128)S(1)}, bf16[2,128,128]{2,1,0:T(8,128)(2,1)S(1)}, bf16[8,2,128,256]{3,2,1,0:T(8,128)(2,1)S(1)}) custom-call(s32[2]{0:T(128)S(1)} %pad_add_fusion.me_ref, bf16[3,1,1,128,512]{4,3,2,1,0:T(8,128)(2,1)S(1)} %copy-done, bf16[3,1,1,128,128]{4,3,2,1,0:T(8,128)(2,1)S(1)} %copy-done.1, ...), custom_call_target="tpu_custom_call" | custom-call | tf_op jit(solution)/shard_map/pallas_call | solution.py:346
  28.3 2.6 %collective-permute-done.11.refs_0_ = bf16[2,128,256]{2,1,0:T(8,128)(2,1)S(1)} collective-permute-done((bf16[2,128,256]{2,1,0:T(8,128)(2,1)S(1)}, bf16[2,128,256]{2,1,0:T(8,128)(2,1)S(1)}, u32[]{:S(2)}, u32[]{:S(2)}) %collective-permute-start.11) | collective-permute-done | bytes 131104 | tf_op jit(solution)/shard_map/ppermute | solution.py:279
  30.8 0.2 shard_map.59.refs_5_.refs_0_
  31.0 1.6 %collective-permute-start.14 = (bf16[2,128,256]{2,1,0:T(8,128)(2,1)S(1)}, bf16[2,128,256]{2,1,0:T(8,128)(2,1)S(1)}, u32[]{:S(2)}, u32[]{:S(2)}) collective-permute-start(bf16[2,128,256]{2,1,0:T(8,128)(2,1)S(1)} %shard_map.59.refs_5_.refs_0_), channel_id=1, source_target_pairs={{0,4},{4,12},{12,20},{20,28},{28,24},{24,16},{16,8},{8,0},{1,5},{5... | collective-permute-start | bytes 393224 | tf_op jit(solution)/shard_map/ppermute | solution.py:261
  32.6 0.5 collective-permute-start.12
  33.1 3.1 %collective-permute-done.14.refs_9_ = bf16[2,128,256]{2,1,0:T(8,128)(2,1)S(1)} collective-permute-done((bf16[2,128,256]{2,1,0:T(8,128)(2,1)S(1)}, bf16[2,128,256]{2,1,0:T(8,128)(2,1)S(1)}, u32[]{:S(2)}, u32[]{:S(2)}) %collective-permute-start.14) | collective-permute-done | bytes 131104 | tf_op jit(solution)/shard_map/ppermute | solution.py:261
  36.2 1.4 %collective-permute-start.15 = (bf16[2,128,256]{2,1,0:T(8,128)(2,1)S(1)}, bf16[2,128,256]{2,1,0:T(8,128)(2,1)S(1)}, u32[]{:S(2)}, u32[]{:S(2)}) collective-permute-start(bf16[2,128,256]{2,1,0:T(8,128)(2,1)S(1)} %collective-permute-done.14.refs_9_), channel_id=1, source_target_pairs={{0,4},{4,12},{12,20},{20,28},{28,24},{24,16},{16,8},{8,0},{1,5},{5... | collective-permute-start | bytes 393224 | tf_op jit(solution)/shard_map/ppermute | solution.py:261
  37.7 0.0 collective-permute-done.12.refs_6_
  37.7 0.6 %collective-permute-start.13 = (bf16[2,128,256]{2,1,0:T(8,128)(2,1)S(1)}, bf16[2,128,256]{2,1,0:T(8,128)(2,1)S(1)}, u32[]{:S(2)}, u32[]{:S(2)}) collective-permute-start(bf16[2,128,256]{2,1,0:T(8,128)(2,1)S(1)} %collective-permute-done.12.refs_6_), channel_id=1, source_target_pairs={{4,0},{12,4},{20,12},{28,20},{24,28},{16,24},{8,16},{0,8},{5,1},{1... | collective-permute-start | bytes 393224 | tf_op jit(solution)/shard_map/ppermute | solution.py:264
  38.3 2.9 %collective-permute-done.15.refs_8_ = bf16[2,128,256]{2,1,0:T(8,128)(2,1)S(1)} collective-permute-done((bf16[2,128,256]{2,1,0:T(8,128)(2,1)S(1)}, bf16[2,128,256]{2,1,0:T(8,128)(2,1)S(1)}, u32[]{:S(2)}, u32[]{:S(2)}) %collective-permute-start.15) | collective-permute-done | bytes 131104 | tf_op jit(solution)/shard_map/ppermute | solution.py:261
  41.2 1.4 %collective-permute-start.17 = (bf16[2,128,256]{2,1,0:T(8,128)(2,1)S(1)}, bf16[2,128,256]{2,1,0:T(8,128)(2,1)S(1)}, u32[]{:S(2)}, u32[]{:S(2)}) collective-permute-start(bf16[2,128,256]{2,1,0:T(8,128)(2,1)S(1)} %collective-permute-done.15.refs_8_), channel_id=1, source_target_pairs={{0,4},{4,12},{12,20},{20,28},{28,24},{24,16},{16,8},{8,0},{1,5},{5... | collective-permute-start | bytes 393224 | tf_op jit(solution)/shard_map/ppermute | solution.py:261
  42.6 0.0 collective-permute-done.13.refs_7_
  42.6 0.6 %collective-permute-start.16 = (bf16[2,128,256]{2,1,0:T(8,128)(2,1)S(1)}, bf16[2,128,256]{2,1,0:T(8,128)(2,1)S(1)}, u32[]{:S(2)}, u32[]{:S(2)}) collective-permute-start(bf16[2,128,256]{2,1,0:T(8,128)(2,1)S(1)} %collective-permute-done.13.refs_7_), channel_id=1, source_target_pairs={{4,0},{12,4},{20,12},{28,20},{24,28},{16,24},{8,16},{0,8},{5,1},{1... | collective-permute-start | bytes 393224 | tf_op jit(solution)/shard_map/ppermute | solution.py:264
  43.2 2.9 %collective-permute-done.17.refs_2_ = bf16[2,128,256]{2,1,0:T(8,128)(2,1)S(1)} collective-permute-done((bf16[2,128,256]{2,1,0:T(8,128)(2,1)S(1)}, bf16[2,128,256]{2,1,0:T(8,128)(2,1)S(1)}, u32[]{:S(2)}, u32[]{:S(2)}) %collective-permute-start.17) | collective-permute-done | bytes 131104 | tf_op jit(solution)/shard_map/ppermute | solution.py:261
  46.2 1.4 %collective-permute-start.18 = (bf16[2,128,256]{2,1,0:T(8,128)(2,1)S(1)}, bf16[2,128,256]{2,1,0:T(8,128)(2,1)S(1)}, u32[]{:S(2)}, u32[]{:S(2)}) collective-permute-start(bf16[2,128,256]{2,1,0:T(8,128)(2,1)S(1)} %collective-permute-done.17.refs_2_), channel_id=1, source_target_pairs={{0,4},{4,12},{12,20},{20,28},{28,24},{24,16},{16,8},{8,0},{1,5},{5... | collective-permute-start | bytes 393224 | tf_op jit(solution)/shard_map/ppermute | solution.py:261
  47.6 2.9 %shard_map.60 = (f32[4,128,256]{2,1,0:T(8,128)S(1)}, bf16[4,128,768]{2,1,0:T(8,128)(2,1)S(1)}) custom-call(s32[2]{0:T(128)S(1)} %pad_add_fusion.me_ref, s32[8,128]{1,0:T(8,128)S(1)} %get-tuple-element.28.refs_0_, s32[8,128]{1,0:T(8,128)S(1)} %collective-permute-done.refs_1_, bf16[2,1,1,4,5,128,128]{6,5,4,3,2,1,0:T(8,128)(2,1)} %refs_2_.3, ...), custom_call_target="tpu_custom_call" | custom-call | tf_op jit(solution)/shard_map/pallas_call | solution.py:319
  50.5 0.0 collective-permute-done.16.refs_0_
  50.5 0.6 %collective-permute-done.18.refs_1_ = bf16[2,128,256]{2,1,0:T(8,128)(2,1)S(1)} collective-permute-done((bf16[2,128,256]{2,1,0:T(8,128)(2,1)S(1)}, bf16[2,128,256]{2,1,0:T(8,128)(2,1)S(1)}, u32[]{:S(2)}, u32[]{:S(2)}) %collective-permute-start.18) | collective-permute-done | bytes 131104 | tf_op jit(solution)/shard_map/ppermute | solution.py:261
  51.1 0.3 shard_map.61
  51.4 1.6 %collective-permute-start.19 = (bf16[1,128,256]{2,1,0:T(8,128)(2,1)S(1)}, bf16[1,128,256]{2,1,0:T(8,128)(2,1)S(1)}, u32[]{:S(2)}, u32[]{:S(2)}) collective-permute-start(bf16[1,128,256]{2,1,0:T(8,128)(2,1)S(1)} %get-tuple-element.43), channel_id=1, source_target_pairs={{0,2},{1,3},{2,0},{3,1},{4,6},{5,7},{6,4},{7,5},{8,10},{9,11},{10,... | collective-permute-start | bytes 196616 | tf_op jit(solution)/shard_map/ppermute | solution.py:279
  53.0 0.0 collective-permute-start.22
  53.0 0.6 %collective-permute-start.21 = (bf16[1,128,256]{2,1,0:T(8,128)(2,1)S(1)}, bf16[1,128,256]{2,1,0:T(8,128)(2,1)S(1)}, u32[]{:S(2)}, u32[]{:S(2)}) collective-permute-start(bf16[1,128,256]{2,1,0:T(8,128)(2,1)S(1)} %get-tuple-element.44), channel_id=1, source_target_pairs={{0,3},{1,2},{2,1},{3,0},{4,7},{5,6},{6,5},{7,4},{8,11},{9,10},{10,... | collective-permute-start | bytes 196616 | tf_op jit(solution)/shard_map/ppermute | solution.py:279
  53.6 0.8 %shard_map.62 = (f32[2,128,256]{2,1,0:T(8,128)S(1)}, bf16[128,256]{1,0:T(8,128)(2,1)S(1)}) custom-call(s32[2]{0:T(128)S(1)} %pad_add_fusion.me_ref, bf16[3,1,1,128,512]{4,3,2,1,0:T(8,128)(2,1)S(1)} %copy-done, f32[4,128,256]{2,1,0:T(8,128)S(1)} %get-tuple-element.45.total_ref, bf16[4,128,768]{2,1,0:T(8,128)(2,1)S(1)} %get-tuple-element.42.chosen_ref, ...), custom_call_target="tpu_custom_call" | custom-call | tf_op jit(solution)/shard_map/pallas_call | solution.py:367
  54.4 1.3 %collective-permute-done.19.refs_0_ = bf16[1,128,256]{2,1,0:T(8,128)(2,1)S(1)} collective-permute-done((bf16[1,128,256]{2,1,0:T(8,128)(2,1)S(1)}, bf16[1,128,256]{2,1,0:T(8,128)(2,1)S(1)}, u32[]{:S(2)}, u32[]{:S(2)}) %collective-permute-start.19) | collective-permute-done | bytes 65568 | tf_op jit(solution)/shard_map/ppermute | solution.py:279
  55.7 0.0 collective-permute-start.20
  55.7 0.0 collective-permute-done.22.refs_1_
  55.8 1.3 %shard_map.63.refs_2_ = bf16[3,1,1,128,512]{4,3,2,1,0:T(8,128)(2,1)} custom-call(s32[2]{0:T(128)S(1)} %pad_add_fusion.me_ref, bf16[128,512]{1,0:T(8,128)(2,1)S(1)} %get-tuple-element.49.full_ref, bf16[2,128,256]{2,1,0:T(8,128)(2,1)S(1)} %shard_map.59.refs_5_.refs_0_, bf16[128,256]{1,0:T(8,128)(2,1)S(1)} %collective-permute-done.22.refs_1_), custom_call_target="tpu_custom_call" | custom-call | tf_op jit(solution)/shard_map/pallas_call | solution.py:375
  57.0 0.0 collective-permute-done.21.refs_1_
  57.0 0.0 collective-permute-done.20.mate_ref
  57.0 1.4 %shard_map.64 = bf16[3,1,1,128,512]{4,3,2,1,0:T(8,128)(2,1)} custom-call(s32[2]{0:T(128)S(1)} %pad_add_fusion.me_ref, bf16[3,1,1,128,128]{4,3,2,1,0:T(8,128)(2,1)S(1)} %copy-done.1, f32[2,128,256]{2,1,0:T(8,128)S(1)} %get-tuple-element.46.right_ref, bf16[128,256]{1,0:T(8,128)(2,1)S(1)} %collective-permute-done.20.mate_ref, ...), custom_call_target="tpu_custom_call", output_to_operand_aliasing={{}: (6, {})} | custom-call | tf_op jit(solution)/shard_map/pallas_call | solution.py:383
  (2 shorter events, 0.0 us)
Async XLA Ops:
  1.9 1.4 %collective-permute-start.1 = (bf16[128,256]{1,0:T(8,128)(2,1)S(1)}, bf16[128,256]{1,0:T(8,128)(2,1)S(1)}, u32[]{:S(2)}, u32[]{:S(2)}) collective-permute-start(bf16[128,256]{1,0:T(8,128)(2,1)S(1)} %get-tuple-element.30), channel_id=1, source_target_pairs={{0,1},{1,0},{2,3},{3,2},{4,5},{5,4},{6,7},{7,6},{8,9},{9,8},{10,11... | collective-permute-start | bytes 196616 | tf_op jit(solution)/shard_map/ppermute | solution.py:279
  2.4 1.2 %collective-permute-start = (s32[8,128]{1,0:T(8,128)S(1)}, s32[8,128]{1,0:T(8,128)S(1)}, u32[]{:S(2)}, u32[]{:S(2)}) collective-permute-start(s32[8,128]{1,0:T(8,128)S(1)} %get-tuple-element.28.refs_0_), channel_id=1, source_target_pairs={{0,1},{1,0},{2,3},{3,2},{4,5},{5,4},{6,7},{7,6},{8,9},{9,8},{10,11... | collective-permute-start | bytes 12296 | tf_op jit(solution)/shard_map/ppermute | solution.py:279
  3.6 18.5 %collective-permute-start.2 = (bf16[2,1,1,4,5,128,128]{6,5,4,3,2,1,0:T(8,128)(2,1)}, bf16[2,1,1,4,5,128,128]{6,5,4,3,2,1,0:T(8,128)(2,1)S(1)}, u32[]{:S(2)}, u32[]{:S(2)}) collective-permute-start(bf16[2,1,1,4,5,128,128]{6,5,4,3,2,1,0:T(8,128)(2,1)} %refs_2_.3), channel_id=1, source_target_pairs={{0,1},{1,0},{2,3},{3,2},{4,5},{5,4},{6,7},{7,6},{8,9},{9,8},{10,11... | collective-permute-start | bytes 3932168 | tf_op jit(solution)/shard_map/ppermute | solution.py:279
  3.8 6.7 %collective-permute-start.6 = (bf16[2,128,256]{2,1,0:T(8,128)(2,1)S(1)}, bf16[2,128,256]{2,1,0:T(8,128)(2,1)S(1)}, u32[]{:S(2)}, u32[]{:S(2)}) collective-permute-start(bf16[2,128,256]{2,1,0:T(8,128)(2,1)S(1)} %pad_maximum_fusion.refs_4_.refs_3_), channel_id=1, source_target_pairs={{0,4},{4,12},{12,20},{20,28},{28,24},{24,16},{16,8},{8,0},{1,5},{5... | collective-permute-start | bytes 393224 | tf_op jit(solution)/shard_map/ppermute | solution.py:261
  6.6 5.6 %collective-permute-start.4 = (bf16[2,128,256]{2,1,0:T(8,128)(2,1)S(1)}, bf16[2,128,256]{2,1,0:T(8,128)(2,1)S(1)}, u32[]{:S(2)}, u32[]{:S(2)}) collective-permute-start(bf16[2,128,256]{2,1,0:T(8,128)(2,1)S(1)} %pad_maximum_fusion.refs_4_.refs_3_), channel_id=1, source_target_pairs={{4,0},{12,4},{20,12},{28,20},{24,28},{16,24},{8,16},{0,8},{5,1},{1... | collective-permute-start | bytes 393224 | tf_op jit(solution)/shard_map/ppermute | solution.py:264
  10.5 5.1 %collective-permute-start.7 = (bf16[2,128,256]{2,1,0:T(8,128)(2,1)S(1)}, bf16[2,128,256]{2,1,0:T(8,128)(2,1)S(1)}, u32[]{:S(2)}, u32[]{:S(2)}) collective-permute-start(bf16[2,128,256]{2,1,0:T(8,128)(2,1)S(1)} %collective-permute-done.6.refs_8_.refs_7_), channel_id=1, source_target_pairs={{0,4},{4,12},{12,20},{20,28},{28,24},{24,16},{16,8},{8,0},{1,5},{5... | collective-permute-start | bytes 393224 | tf_op jit(solution)/shard_map/ppermute | solution.py:261
  12.2 5.0 %collective-permute-start.3 = (bf16[256,256]{1,0:T(8,128)(2,1)S(1)}, bf16[256,256]{1,0:T(8,128)(2,1)S(1)}, u32[]{:S(2)}, u32[]{:S(2)}) collective-permute-start(bf16[256,256]{1,0:T(8,128)(2,1)S(1)} %get-tuple-element.33), channel_id=1, source_target_pairs={{0,1},{1,0},{2,3},{3,2},{4,5},{5,4},{6,7},{7,6},{8,9},{9,8},{10,11... | collective-permute-start | bytes 393224 | tf_op jit(solution)/shard_map/ppermute | solution.py:279
  12.2 5.9 %collective-permute-start.5 = (bf16[2,128,256]{2,1,0:T(8,128)(2,1)S(1)}, bf16[2,128,256]{2,1,0:T(8,128)(2,1)S(1)}, u32[]{:S(2)}, u32[]{:S(2)}) collective-permute-start(bf16[2,128,256]{2,1,0:T(8,128)(2,1)S(1)} %collective-permute-done.4.refs_5_.refs_4_), channel_id=1, source_target_pairs={{4,0},{12,4},{20,12},{28,20},{24,28},{16,24},{8,16},{0,8},{5,1},{1... | collective-permute-start | bytes 393224 | tf_op jit(solution)/shard_map/ppermute | solution.py:264
  15.6 5.0 %collective-permute-start.9 = (bf16[2,128,256]{2,1,0:T(8,128)(2,1)S(1)}, bf16[2,128,256]{2,1,0:T(8,128)(2,1)S(1)}, u32[]{:S(2)}, u32[]{:S(2)}) collective-permute-start(bf16[2,128,256]{2,1,0:T(8,128)(2,1)S(1)} %collective-permute-done.7.refs_7_.refs_6_), channel_id=1, source_target_pairs={{0,4},{4,12},{12,20},{20,28},{28,24},{24,16},{16,8},{8,0},{1,5},{5... | collective-permute-start | bytes 393224 | tf_op jit(solution)/shard_map/ppermute | solution.py:261
  18.1 6.9 %collective-permute-start.8 = (bf16[2,128,256]{2,1,0:T(8,128)(2,1)S(1)}, bf16[2,128,256]{2,1,0:T(8,128)(2,1)S(1)}, u32[]{:S(2)}, u32[]{:S(2)}) collective-permute-start(bf16[2,128,256]{2,1,0:T(8,128)(2,1)S(1)} %collective-permute-done.5.refs_6_.refs_5_), channel_id=1, source_target_pairs={{4,0},{12,4},{20,12},{28,20},{24,28},{16,24},{8,16},{0,8},{5,1},{1... | collective-permute-start | bytes 393224 | tf_op jit(solution)/shard_map/ppermute | solution.py:264
  20.6 5.0 %collective-permute-start.10 = (bf16[2,128,256]{2,1,0:T(8,128)(2,1)S(1)}, bf16[2,128,256]{2,1,0:T(8,128)(2,1)S(1)}, u32[]{:S(2)}, u32[]{:S(2)}) collective-permute-start(bf16[2,128,256]{2,1,0:T(8,128)(2,1)S(1)} %collective-permute-done.9.refs_2_), channel_id=1, source_target_pairs={{0,4},{4,12},{12,20},{20,28},{28,24},{24,16},{16,8},{8,0},{1,5},{5... | collective-permute-start | bytes 393224 | tf_op jit(solution)/shard_map/ppermute | solution.py:261
  24.9 2.5 %copy-start = (bf16[3,1,1,128,512]{4,3,2,1,0:T(8,128)(2,1)S(1)}, bf16[3,1,1,128,512]{4,3,2,1,0:T(8,128)(2,1)}, u32[]{:S(2)}) copy-start(bf16[3,1,1,128,512]{4,3,2,1,0:T(8,128)(2,1)} %b_ref.5) | copy-start | bytes 1179652
  25.0 2.5 %copy-start.1 = (bf16[3,1,1,128,128]{4,3,2,1,0:T(8,128)(2,1)S(1)}, bf16[3,1,1,128,128]{4,3,2,1,0:T(8,128)(2,1)}, u32[]{:S(2)}) copy-start(bf16[3,1,1,128,128]{4,3,2,1,0:T(8,128)(2,1)} %d_ref.5) | copy-start | bytes 294916
  25.8 5.0 %collective-permute-start.11 = (bf16[2,128,256]{2,1,0:T(8,128)(2,1)S(1)}, bf16[2,128,256]{2,1,0:T(8,128)(2,1)S(1)}, u32[]{:S(2)}, u32[]{:S(2)}) collective-permute-start(bf16[2,128,256]{2,1,0:T(8,128)(2,1)S(1)} %shard_map.57), channel_id=1, source_target_pairs={{0,2},{1,3},{2,0},{3,1},{4,6},{5,7},{6,4},{7,5},{8,10},{9,11},{10,... | collective-permute-start | bytes 393224 | tf_op jit(solution)/shard_map/ppermute | solution.py:279
  31.0 5.2 %collective-permute-start.14 = (bf16[2,128,256]{2,1,0:T(8,128)(2,1)S(1)}, bf16[2,128,256]{2,1,0:T(8,128)(2,1)S(1)}, u32[]{:S(2)}, u32[]{:S(2)}) collective-permute-start(bf16[2,128,256]{2,1,0:T(8,128)(2,1)S(1)} %shard_map.59.refs_5_.refs_0_), channel_id=1, source_target_pairs={{0,4},{4,12},{12,20},{20,28},{28,24},{24,16},{16,8},{8,0},{1,5},{5... | collective-permute-start | bytes 393224 | tf_op jit(solution)/shard_map/ppermute | solution.py:261
  32.6 5.0 %collective-permute-start.12 = (bf16[2,128,256]{2,1,0:T(8,128)(2,1)S(1)}, bf16[2,128,256]{2,1,0:T(8,128)(2,1)S(1)}, u32[]{:S(2)}, u32[]{:S(2)}) collective-permute-start(bf16[2,128,256]{2,1,0:T(8,128)(2,1)S(1)} %shard_map.59.refs_5_.refs_0_), channel_id=1, source_target_pairs={{4,0},{12,4},{20,12},{28,20},{24,28},{16,24},{8,16},{0,8},{5,1},{1... | collective-permute-start | bytes 393224 | tf_op jit(solution)/shard_map/ppermute | solution.py:264
  36.2 5.0 %collective-permute-start.15 = (bf16[2,128,256]{2,1,0:T(8,128)(2,1)S(1)}, bf16[2,128,256]{2,1,0:T(8,128)(2,1)S(1)}, u32[]{:S(2)}, u32[]{:S(2)}) collective-permute-start(bf16[2,128,256]{2,1,0:T(8,128)(2,1)S(1)} %collective-permute-done.14.refs_9_), channel_id=1, source_target_pairs={{0,4},{4,12},{12,20},{20,28},{28,24},{24,16},{16,8},{8,0},{1,5},{5... | collective-permute-start | bytes 393224 | tf_op jit(solution)/shard_map/ppermute | solution.py:261
  37.7 5.0 %collective-permute-start.13 = (bf16[2,128,256]{2,1,0:T(8,128)(2,1)S(1)}, bf16[2,128,256]{2,1,0:T(8,128)(2,1)S(1)}, u32[]{:S(2)}, u32[]{:S(2)}) collective-permute-start(bf16[2,128,256]{2,1,0:T(8,128)(2,1)S(1)} %collective-permute-done.12.refs_6_), channel_id=1, source_target_pairs={{4,0},{12,4},{20,12},{28,20},{24,28},{16,24},{8,16},{0,8},{5,1},{1... | collective-permute-start | bytes 393224 | tf_op jit(solution)/shard_map/ppermute | solution.py:264
  41.2 5.0 %collective-permute-start.17 = (bf16[2,128,256]{2,1,0:T(8,128)(2,1)S(1)}, bf16[2,128,256]{2,1,0:T(8,128)(2,1)S(1)}, u32[]{:S(2)}, u32[]{:S(2)}) collective-permute-start(bf16[2,128,256]{2,1,0:T(8,128)(2,1)S(1)} %collective-permute-done.15.refs_8_), channel_id=1, source_target_pairs={{0,4},{4,12},{12,20},{20,28},{28,24},{24,16},{16,8},{8,0},{1,5},{5... | collective-permute-start | bytes 393224 | tf_op jit(solution)/shard_map/ppermute | solution.py:261
  42.6 7.8 %collective-permute-start.16 = (bf16[2,128,256]{2,1,0:T(8,128)(2,1)S(1)}, bf16[2,128,256]{2,1,0:T(8,128)(2,1)S(1)}, u32[]{:S(2)}, u32[]{:S(2)}) collective-permute-start(bf16[2,128,256]{2,1,0:T(8,128)(2,1)S(1)} %collective-permute-done.13.refs_7_), channel_id=1, source_target_pairs={{4,0},{12,4},{20,12},{28,20},{24,28},{16,24},{8,16},{0,8},{5,1},{1... | collective-permute-start | bytes 393224 | tf_op jit(solution)/shard_map/ppermute | solution.py:264
  46.2 5.0 %collective-permute-start.18 = (bf16[2,128,256]{2,1,0:T(8,128)(2,1)S(1)}, bf16[2,128,256]{2,1,0:T(8,128)(2,1)S(1)}, u32[]{:S(2)}, u32[]{:S(2)}) collective-permute-start(bf16[2,128,256]{2,1,0:T(8,128)(2,1)S(1)} %collective-permute-done.17.refs_2_), channel_id=1, source_target_pairs={{0,4},{4,12},{12,20},{20,28},{28,24},{24,16},{16,8},{8,0},{1,5},{5... | collective-permute-start | bytes 393224 | tf_op jit(solution)/shard_map/ppermute | solution.py:261
  51.4 4.3 %collective-permute-start.19 = (bf16[1,128,256]{2,1,0:T(8,128)(2,1)S(1)}, bf16[1,128,256]{2,1,0:T(8,128)(2,1)S(1)}, u32[]{:S(2)}, u32[]{:S(2)}) collective-permute-start(bf16[1,128,256]{2,1,0:T(8,128)(2,1)S(1)} %get-tuple-element.43), channel_id=1, source_target_pairs={{0,2},{1,3},{2,0},{3,1},{4,6},{5,7},{6,4},{7,5},{8,10},{9,11},{10,... | collective-permute-start | bytes 196616 | tf_op jit(solution)/shard_map/ppermute | solution.py:279
  53.0 2.8 %collective-permute-start.22 = (bf16[128,256]{1,0:T(8,128)(2,1)S(1)}, bf16[128,256]{1,0:T(8,128)(2,1)S(1)}, u32[]{:S(2)}, u32[]{:S(2)}) collective-permute-start(bf16[128,256]{1,0:T(8,128)(2,1)S(1)} %slice_bitcast_fusion), channel_id=1, source_target_pairs={{0,1},{1,0},{2,3},{3,2},{4,5},{5,4},{6,7},{7,6},{8,9},{9,8},{10,11... | collective-permute-start | bytes 196616 | tf_op jit(solution)/shard_map/ppermute | solution.py:279
  53.0 4.0 %collective-permute-start.21 = (bf16[1,128,256]{2,1,0:T(8,128)(2,1)S(1)}, bf16[1,128,256]{2,1,0:T(8,128)(2,1)S(1)}, u32[]{:S(2)}, u32[]{:S(2)}) collective-permute-start(bf16[1,128,256]{2,1,0:T(8,128)(2,1)S(1)} %get-tuple-element.44), channel_id=1, source_target_pairs={{0,3},{1,2},{2,1},{3,0},{4,7},{5,6},{6,5},{7,4},{8,11},{9,10},{10,... | collective-permute-start | bytes 196616 | tf_op jit(solution)/shard_map/ppermute | solution.py:279
  55.7 1.3 %collective-permute-start.20 = (bf16[128,256]{1,0:T(8,128)(2,1)S(1)}, bf16[128,256]{1,0:T(8,128)(2,1)S(1)}, u32[]{:S(2)}, u32[]{:S(2)}) collective-permute-start(bf16[128,256]{1,0:T(8,128)(2,1)S(1)} %get-tuple-element.48), channel_id=1, source_target_pairs={{0,1},{1,0},{2,3},{3,2},{4,5},{5,4},{6,7},{7,6},{8,9},{9,8},{10,11... | collective-permute-start | bytes 196616 | tf_op jit(solution)/shard_map/ppermute | solution.py:279

commit v7 on v6

--- a/solution.py
+++ b/solution.py
@@ -72,31 +72,35 @@
     return jnp.stack(solutions)[:, None, None]
 
 
-def first_kernel(n, m, place, me_ref, counts_ref, cols_ref, b_ref, d_ref, full_ref, index_ref, own_ref, other_ref, away_ref, *refs):
+def first_kernel(n, m, place, counts_ref, cols_ref, b_ref, d_ref, full_ref, index_ref, own_ref, other_ref, away_ref, *refs):
     b_buf, d_buf, count_ref, col_ref, sems = refs
     middle = b_buf.shape[0]
     copies = [
-        pltpu.make_async_copy(counts_ref, count_ref, sems.at[0]),
-        pltpu.make_async_copy(cols_ref, col_ref, sems.at[1]),
-        pltpu.make_async_copy(d_ref.at[pl.ds(0, middle), 0, 0], d_buf, sems.at[2]),
-        pltpu.make_async_copy(b_ref.at[pl.ds(0, middle), 0, 0], b_buf, sems.at[3]),
+        pltpu.make_async_copy(b_ref.at[0, 0, 0], b_buf.at[0], sems.at[0]),
+        pltpu.make_async_copy(d_ref.at[0, 0, 0], d_buf.at[0], sems.at[1]),
+        pltpu.make_async_copy(cols_ref, col_ref, sems.at[2]),
+        pltpu.make_async_copy(counts_ref, count_ref, sems.at[3]),
+        pltpu.make_async_copy(d_ref.at[pl.ds(1, middle - 1), 0, 0], d_buf.at[pl.ds(1, middle - 1)], sems.at[4]),
+        pltpu.make_async_copy(b_ref.at[pl.ds(1, middle - 1), 0, 0], b_buf.at[pl.ds(1, middle - 1)], sems.at[5]),
     ]
     for copy in copies:
         copy.start()
-    me, my_place = me_ref[0], me_ref[1]
+    me, my_row, my_place = lax.axis_index("pcol"), lax.axis_index("prow"), place[0]
+    for p in range(1, m):
+        my_place = jnp.where(my_row == p, place[p], my_place)
     size, width = own_ref.shape
-    for copy in copies[2:]:
+    for copy in copies[:2]:
         copy.wait()
     full_ref[...] = jnp.dot(d_buf[0], b_buf[0], preferred_element_type=jnp.float32).astype(jnp.bfloat16)
     own_ref[...] = full_ref[:, my_columns(me, width)]
     other_ref[...] = full_ref[:, my_columns(me ^ 1, width)]
+    for copy in copies[2:]:
+        copy.wait()
     for level in range(1, middle):
         at = (2 * level - 2) * size
         away_ref[at : at + size, :] = b_buf[level, :, my_columns(me ^ 1, width)]
         away_ref[at + size : at + 2 * size, :size] = d_buf[level]
         away_ref[at + size : at + 2 * size, size:] = jnp.zeros((size, width - size), jnp.bfloat16)
-    for copy in copies[:2]:
-        copy.wait()
     levels, slots = col_ref.shape[0] + 1, col_ref.shape[-1]
     row_at = lax.broadcasted_iota(jnp.int32, (n, slots), 0)
     slot_at = lax.broadcasted_iota(jnp.int32, (n, slots), 1)
@@ -122,13 +126,13 @@
     return pl.ds(pl.multiple_of((me & 1) * width, LANES), width)
 
 
-def gather_kernel(n, level, m, early, late, me_ref, *refs):
+def gather_kernel(n, level, m, early, late, *refs):
     index_refs, l_refs, refs = refs[:PAIR], refs[PAIR : 2 * PAIR], refs[2 * PAIR :]
     old_refs, refs = refs[: level - 1], refs[level - 1 :]
     x_refs, (total_ref, chosen_ref, known, own, sem) = refs[:-5], refs[-5:]
     copy = pltpu.make_async_copy(l_refs[0].at[level - 1, 0, 0], own, sem)
     copy.start()
-    me = me_ref[0]
+    me = lax.axis_index("pcol")
     size, width = total_ref.shape[1:]
     slots = l_refs[0].shape[4]
     base = (level - 1) * m
@@ -179,27 +183,27 @@
             out_ref[row] = late_total(PAIR + i * rows + row, total_ref, chosen_ref, panels).astype(jnp.bfloat16)
 
 
-def stay_kernel(level, late, early, me_ref, b_ref, d_ref, away_ref, total_ref, chosen_ref, *refs):
+def stay_kernel(level, late, early, b_ref, d_ref, away_ref, total_ref, chosen_ref, *refs):
     x_refs, (right_ref, inverse_ref, panels_ref) = refs[: len(late) + len(early)], refs[len(late) + len(early) :]
     panels = late_panels(x_refs[: len(late)])
     size, width = right_ref.shape[1:]
     at = (2 * level - 2) * size
     for j in range(PAIR):
         total = late_total(j, total_ref, chosen_ref, panels)
-        right = away_ref[at : at + size, :] if j else b_ref[level, 0, 0, :, my_columns(me_ref[0], width)]
+        right = away_ref[at : at + size, :] if j else b_ref[level, 0, 0, :, my_columns(lax.axis_index("pcol"), width)]
         right_ref[j] = right.astype(jnp.float32) - total
         inverse_ref[j] = away_ref[at + size : at + 2 * size, :size] if j else d_ref[level, 0, 0]
     for d, x_ref in zip(late + early, x_refs):
         panels_ref[d] = x_ref[...]
 
 
-def last_stay_kernel(late, me_ref, b_ref, total_ref, chosen_ref, *refs):
+def last_stay_kernel(late, b_ref, total_ref, chosen_ref, *refs):
     x_refs, (right_ref, send_ref) = refs[:late], refs[late:]
     panels = late_panels(x_refs)
     level, width = b_ref.shape[0] - 1, right_ref.shape[2]
     send_ref[...] = late_total(1, total_ref, chosen_ref, panels).astype(jnp.bfloat16)
     for j in range(PAIR):
-        right_ref[j] = b_ref[level, 0, 0, :, my_columns(me_ref[0] ^ j, width)].astype(jnp.float32)
+        right_ref[j] = b_ref[level, 0, 0, :, my_columns(lax.axis_index("pcol") ^ j, width)].astype(jnp.float32)
     right_ref[0] = right_ref[0] - late_total(0, total_ref, chosen_ref, panels)
 
 
@@ -213,12 +217,12 @@
         out_ref[j] = value.astype(jnp.bfloat16)
 
 
-def write_kernel(me_ref, full_ref, *refs):
+def write_kernel(full_ref, *refs):
     level_refs, (out_ref, sems) = refs[:-2], refs[-2:]
     width = level_refs[0].shape[2]
     copies = [pltpu.make_async_copy(full_ref, out_ref.at[0, 0, 0], sems.at[0])]
     for i, ref in enumerate(level_refs):
-        target = out_ref.at[1 + i // PAIR, 0, 0, :, my_columns(me_ref[0] ^ (i % PAIR), width)]
+        target = out_ref.at[1 + i // PAIR, 0, 0, :, my_columns(lax.axis_index("pcol") ^ (i % PAIR), width)]
         copies.append(pltpu.make_async_copy(ref if i % PAIR else ref.at[0], target, sems.at[1 + i]))
     for copy in copies:
         copy.start()
@@ -226,7 +230,7 @@
         copy.wait()
 
 
-def last_kernel(me_ref, d_ref, right_ref, mate_ref, *refs):
+def last_kernel(d_ref, right_ref, mate_ref, *refs):
     other_refs, (_, out_ref, buf, sem) = refs[:-4], refs[-4:]
     width = right_ref.shape[2]
     levels = out_ref.shape[0]
@@ -237,7 +241,7 @@
         for other in other_refs[j::PAIR]:
             resid -= other[0].astype(jnp.float32)
         value = jnp.dot(d_ref[levels - 1, 0, 0], resid.astype(jnp.bfloat16), preferred_element_type=jnp.float32)
-        buf[:, my_columns(me_ref[0] ^ j, width)] = value.astype(jnp.bfloat16)
+        buf[:, my_columns(lax.axis_index("pcol") ^ j, width)] = value.astype(jnp.bfloat16)
     copy = pltpu.make_async_copy(buf, out_ref.at[levels - 1, 0, 0], sem)
     copy.start()
     copy.wait()
@@ -272,8 +276,6 @@
     slots = l_blocks.shape[4]
     width = front // PAIR
     place = [cycle.index(p) for p in range(m)]
-    my_place = sum(jnp.where(lax.axis_index("prow") == p, place[p], 0) for p in range(m))
-    me = jnp.stack([lax.axis_index("pcol"), my_place]).astype(jnp.int32)
 
     def send(value, bits):
         return lax.ppermute(value, "pcol", [(i, i ^ bits) for i in range(n)])
@@ -291,17 +293,17 @@
             near((size, width)),
             near(((2 * middle - 2) * size, width)),
         ],
-        in_specs=[smem()] + [anywhere()] * 4,
+        in_specs=[anywhere()] * 4,
         out_specs=[vmem()] * 5,
         scratch_shapes=[
             pltpu.VMEM((middle, size, front), jnp.bfloat16),
             pltpu.VMEM((middle, size, size), jnp.bfloat16),
             pltpu.SMEM(live_counts.shape, jnp.int32),
             pltpu.VMEM(block_cols.shape, jnp.int32),
-            pltpu.SemaphoreType.DMA((4,)),
+            pltpu.SemaphoreType.DMA((6,)),
         ],
         compiler_params=params(),
-    )(me, *[in_hbm(v) for v in (live_counts, block_cols, b_panels, diag_inverse)])
+    )(*[in_hbm(v) for v in (live_counts, block_cols, b_panels, diag_inverse)])
     other, away, index = send(other, 1), send(away, 1), [index, send(index, 1)]
     solved = after(jnp.stack([own, other]), index[1])
     blocks = [in_hbm(l_blocks), send(after(l_blocks, solved), 1)]
@@ -319,7 +321,7 @@
         total, chosen = pl.pallas_call(
             functools.partial(gather_kernel, n, level, m, early, late),
             out_shape=[near((n, size, width), jnp.float32), near((n, size, len(late) * PAIR * size))],
-            in_specs=[smem()] * (1 + PAIR) + [anywhere()] + [vmem()] * (PAIR - 1 + len(kept) + len(early)),
+            in_specs=[smem()] * PAIR + [anywhere()] + [vmem()] * (PAIR - 1 + len(kept) + len(early)),
             out_specs=[vmem()] * 2,
             scratch_shapes=[
                 pltpu.VMEM((level * m, PAIR, size, width), jnp.bfloat16),
@@ -327,7 +329,7 @@
                 pltpu.SemaphoreType.DMA,
             ],
             compiler_params=params(),
-        )(me, *index, *blocks, *kept, *[ring.found[d] for d in early])
+        )(*index, *blocks, *kept, *[ring.found[d] for d in early])
         rows = 1 if final else PAIR
         late_x, early_x = [ring.found[d] for d in late], [ring.found[d] for d in early]
         partial = pl.pallas_call(
@@ -350,10 +352,10 @@
                 near((PAIR, size, size)),
                 near((m, PAIR, size, width)),
             ],
-            in_specs=[smem()] + [vmem()] * (5 + m),
+            in_specs=[vmem()] * (5 + m),
             out_specs=[vmem()] * 3,
             compiler_params=params(),
-        )(me, b_panels, diag_inverse, away, total, chosen, *late_x, *early_x)
+        )(b_panels, diag_inverse, away, total, chosen, *late_x, *early_x)
         kept.append(panels)
         solved = pl.pallas_call(
             solve_kernel,
@@ -367,28 +369,28 @@
     right, mate = pl.pallas_call(
         functools.partial(last_stay_kernel, len(late)),
         out_shape=[near((PAIR, size, width), jnp.float32), near((size, width))],
-        in_specs=[smem()] + [vmem()] * (3 + len(late)),
+        in_specs=[vmem()] * (3 + len(late)),
         out_specs=[vmem()] * 2,
         compiler_params=params(),
-    )(me, b_panels, total, chosen, *late_x)
+    )(b_panels, total, chosen, *late_x)
     mate = send(after(mate, others[0]), 1)
     result = pl.pallas_call(
         write_kernel,
         out_shape=struct(b_panels.shape),
-        in_specs=[smem()] + [vmem()] * (1 + len(columns)),
+        in_specs=[vmem()] * (1 + len(columns)),
         out_specs=anywhere(),
         scratch_shapes=[pltpu.SemaphoreType.DMA((1 + len(columns),))],
         compiler_params=params(),
-    )(me, full, *columns)
+    )(full, *columns)
     return pl.pallas_call(
         last_kernel,
         out_shape=struct(b_panels.shape),
-        in_specs=[smem()] + [vmem()] * (3 + len(others)) + [anywhere()],
+        in_specs=[vmem()] * (3 + len(others)) + [anywhere()],
         out_specs=anywhere(),
         scratch_shapes=[pltpu.VMEM((size, front), jnp.bfloat16), pltpu.SemaphoreType.DMA],
-        input_output_aliases={4 + len(others): 0},
+        input_output_aliases={3 + len(others): 0},
         compiler_params=params(),
-    )(me, diag_inverse, right, mate, *others, result)
+    )(diag_inverse, right, mate, *others, result)
 
 
 def cycle_of(mesh):

time: 58.7 us -> 57.4 us (0.978)
  Pallas kernels: 12.5 us -> 9.72 us
  waiting for transfers between devices: 25.1 us -> 26.6 us
    ppermute x9, waiting for transfers between devices: 4.93 us -> 6.53 us  [send(): return lax.ppermute(value, 'pcol', [(i, i ^ bits) for i in range(n)])]
    pallas_call x1, Pallas kernels: 1.82 us -> 1.21 us  [solve_paired(): pl.pallas_call(functools.partial(first_kernel, n, m, place), out_shape=[n...]
  transfers between devices with their start and end apart: 23 -> 23, of which waited for: 13 -> 15; matrix products, arithmetic and copies ran while one was open for 0% -> 0% of each run, Pallas kernels for 15% -> 12%
where the time goes in v7:
time: 57.4 us; the launch traced here: 57.2 us
  waiting for transfers between devices  26.6 us (46%)
  starting transfers between devices  20.7 us (36%)
  Pallas kernels  9.72 us (17%)
    ppermute x8, waiting for transfers between devices, advance(): self.behind = lax.ppermute(self.behind, 'prow', self.to_next)  19.1 us
    ppermute x8, starting transfers between devices, advance(): self.behind = lax.ppermute(self.behind, 'prow', self.to_next)  13.6 us
    ppermute x9, waiting for transfers between devices, send(): return lax.ppermute(value, 'pcol', [(i, i ^ bits) for i in range(n)])  6.53 us
    pallas_call x2, Pallas kernels, solve_paired(): pl.pallas_call(functools.partial(gather_kernel, n, level, m, early, late)...  5.66 us
    ppermute x9, starting transfers between devices, send(): return lax.ppermute(value, 'pcol', [(i, i ^ bits) for i in range(n)])  4.63 us
    ppermute x6, starting transfers between devices, advance(): self.ahead = lax.ppermute(self.ahead, 'prow', self.to_last)  2.45 us
    pallas_call x1, Pallas kernels, solve_paired(): pl.pallas_call(functools.partial(first_kernel, n, m, place), out_shape=[n...  1.21 us
  transfers between devices with their start and end apart: 23, of which 15 were waited for; matrix products, arithmetic and copies ran while one was open for 0% of the time, Pallas kernels for 12%

profile of v7, /device:TPU:0, one launch (start us, length us, event | category | flops | bytes accessed | tf_op | source)
XLA Modules:
  0.0 57.2 jit_solution(14690539982304780028)
XLA Ops:
  0.0 1.2 %shard_map.55 = (bf16[128,512]{1,0:T(8,128)(2,1)S(1)}, s32[8,128]{1,0:T(8,128)S(1)}, bf16[128,256]{1,0:T(8,128)(2,1)S(1)}, bf16[128,256]{1,0:T(8,128)(2,1)S(1)}, bf16[256,256]{1,0:T(8,128)(2,1)S(1)}) custom-call(s32[2,1,1,4]{3,2,1,0:T(1,128)} %counts_ref.1, s32[2,1,1,4,5]{4,3,2,1,0:T(4,128)} %cols_ref.1, bf16[3,1,1,128,512]{4,3,2,1,0:T(8,128)(2,1)} %b_ref.5, ...), custom_call_target="tpu_custom_call" | custom-call | tf_op jit(solution)/shard_map/pallas_call | solution.py:287
  1.2 0.5 collective-permute-start.1
  1.7 0.1 collective-permute-start
  1.8 0.8 %collective-permute-done.1 = bf16[128,256]{1,0:T(8,128)(2,1)S(1)} collective-permute-done((bf16[128,256]{1,0:T(8,128)(2,1)S(1)}, bf16[128,256]{1,0:T(8,128)(2,1)S(1)}, u32[]{:S(2)}, u32[]{:S(2)}) %collective-permute-start.1) | collective-permute-done | bytes 65568 | tf_op jit(solution)/shard_map/ppermute | solution.py:281
  2.7 0.2 collective-permute-done.refs_1_
  2.9 0.2 collective-permute-start.2
  3.1 2.8 %collective-permute-start.6 = (bf16[2,128,256]{2,1,0:T(8,128)(2,1)S(1)}, bf16[2,128,256]{2,1,0:T(8,128)(2,1)S(1)}, u32[]{:S(2)}, u32[]{:S(2)}) collective-permute-start(bf16[2,128,256]{2,1,0:T(8,128)(2,1)S(1)} %pad_maximum_fusion.refs_4_.refs_3_), channel_id=1, source_target_pairs={{0,4},{4,12},{12,20},{20,28},{28,24},{24,16},{16,8},{8,0},{1,5},{5... | collective-permute-start | bytes 393224 | tf_op jit(solution)/shard_map/ppermute | solution.py:265
  5.9 0.1 collective-permute-start.4
  6.0 3.8 %collective-permute-done.6.refs_8_.refs_7_ = bf16[2,128,256]{2,1,0:T(8,128)(2,1)S(1)} collective-permute-done((bf16[2,128,256]{2,1,0:T(8,128)(2,1)S(1)}, bf16[2,128,256]{2,1,0:T(8,128)(2,1)S(1)}, u32[]{:S(2)}, u32[]{:S(2)}) %collective-permute-start.6) | collective-permute-done | bytes 131104 | tf_op jit(solution)/shard_map/ppermute | solution.py:265
  9.8 1.7 %collective-permute-start.7 = (bf16[2,128,256]{2,1,0:T(8,128)(2,1)S(1)}, bf16[2,128,256]{2,1,0:T(8,128)(2,1)S(1)}, u32[]{:S(2)}, u32[]{:S(2)}) collective-permute-start(bf16[2,128,256]{2,1,0:T(8,128)(2,1)S(1)} %collective-permute-done.6.refs_8_.refs_7_), channel_id=1, source_target_pairs={{0,4},{4,12},{12,20},{20,28},{28,24},{24,16},{16,8},{8,0},{1,5},{5... | collective-permute-start | bytes 393224 | tf_op jit(solution)/shard_map/ppermute | solution.py:265
  11.5 0.0 collective-permute-start.3
  11.5 0.0 collective-permute-done.4.refs_5_.refs_4_
  11.5 0.4 collective-permute-start.5
  11.9 3.0 %collective-permute-done.7.refs_7_.refs_6_ = bf16[2,128,256]{2,1,0:T(8,128)(2,1)S(1)} collective-permute-done((bf16[2,128,256]{2,1,0:T(8,128)(2,1)S(1)}, bf16[2,128,256]{2,1,0:T(8,128)(2,1)S(1)}, u32[]{:S(2)}, u32[]{:S(2)}) %collective-permute-start.7) | collective-permute-done | bytes 131104 | tf_op jit(solution)/shard_map/ppermute | solution.py:265
  14.9 1.5 %collective-permute-start.9 = (bf16[2,128,256]{2,1,0:T(8,128)(2,1)S(1)}, bf16[2,128,256]{2,1,0:T(8,128)(2,1)S(1)}, u32[]{:S(2)}, u32[]{:S(2)}) collective-permute-start(bf16[2,128,256]{2,1,0:T(8,128)(2,1)S(1)} %collective-permute-done.7.refs_7_.refs_6_), channel_id=1, source_target_pairs={{0,4},{4,12},{12,20},{20,28},{28,24},{24,16},{16,8},{8,0},{1,5},{5... | collective-permute-start | bytes 393224 | tf_op jit(solution)/shard_map/ppermute | solution.py:265
  16.4 0.0 collective-permute-done.3.away_ref
  16.5 0.9 %collective-permute-done.5.refs_6_.refs_5_ = bf16[2,128,256]{2,1,0:T(8,128)(2,1)S(1)} collective-permute-done((bf16[2,128,256]{2,1,0:T(8,128)(2,1)S(1)}, bf16[2,128,256]{2,1,0:T(8,128)(2,1)S(1)}, u32[]{:S(2)}, u32[]{:S(2)}) %collective-permute-start.5) | collective-permute-done | bytes 131104 | tf_op jit(solution)/shard_map/ppermute | solution.py:268
  17.4 0.4 collective-permute-start.8
  17.8 2.1 %collective-permute-done.9.refs_2_ = bf16[2,128,256]{2,1,0:T(8,128)(2,1)S(1)} collective-permute-done((bf16[2,128,256]{2,1,0:T(8,128)(2,1)S(1)}, bf16[2,128,256]{2,1,0:T(8,128)(2,1)S(1)}, u32[]{:S(2)}, u32[]{:S(2)}) %collective-permute-start.9) | collective-permute-done | bytes 131104 | tf_op jit(solution)/shard_map/ppermute | solution.py:265
  19.9 1.5 %collective-permute-start.10 = (bf16[2,128,256]{2,1,0:T(8,128)(2,1)S(1)}, bf16[2,128,256]{2,1,0:T(8,128)(2,1)S(1)}, u32[]{:S(2)}, u32[]{:S(2)}) collective-permute-start(bf16[2,128,256]{2,1,0:T(8,128)(2,1)S(1)} %collective-permute-done.9.refs_2_), channel_id=1, source_target_pairs={{0,4},{4,12},{12,20},{20,28},{28,24},{24,16},{16,8},{8,0},{1,5},{5... | collective-permute-start | bytes 393224 | tf_op jit(solution)/shard_map/ppermute | solution.py:265
  21.4 0.0 collective-permute-done.2.refs_3_
  21.4 2.8 %shard_map.56 = (f32[4,128,256]{2,1,0:T(8,128)S(1)}, bf16[4,128,768]{2,1,0:T(8,128)(2,1)S(1)}) custom-call(s32[8,128]{1,0:T(8,128)S(1)} %get-tuple-element.28.refs_0_, s32[8,128]{1,0:T(8,128)S(1)} %collective-permute-done.refs_1_, bf16[2,1,1,4,5,128,128]{6,5,4,3,2,1,0:T(8,128)(2,1)} %refs_2_.3, ...), custom_call_target="tpu_custom_call" | custom-call | tf_op jit(solution)/shard_map/pallas_call | solution.py:321
  24.2 0.0 copy-start
  24.2 0.0 copy-start.1
  24.2 0.0 collective-permute-done.8.refs_0_
  24.3 0.6 %collective-permute-done.10.refs_1_ = bf16[2,128,256]{2,1,0:T(8,128)(2,1)S(1)} collective-permute-done((bf16[2,128,256]{2,1,0:T(8,128)(2,1)S(1)}, bf16[2,128,256]{2,1,0:T(8,128)(2,1)S(1)}, u32[]{:S(2)}, u32[]{:S(2)}) %collective-permute-start.10) | collective-permute-done | bytes 131104 | tf_op jit(solution)/shard_map/ppermute | solution.py:265
  24.8 0.3 shard_map.57
  25.1 1.6 %collective-permute-start.11 = (bf16[2,128,256]{2,1,0:T(8,128)(2,1)S(1)}, bf16[2,128,256]{2,1,0:T(8,128)(2,1)S(1)}, u32[]{:S(2)}, u32[]{:S(2)}) collective-permute-start(bf16[2,128,256]{2,1,0:T(8,128)(2,1)S(1)} %shard_map.57), channel_id=1, source_target_pairs={{0,2},{1,3},{2,0},{3,1},{4,6},{5,7},{6,4},{7,5},{8,10},{9,11},{10,... | collective-permute-start | bytes 393224 | tf_op jit(solution)/shard_map/ppermute | solution.py:281
  26.8 0.0 copy-done
  26.8 0.0 copy-done.1
  26.8 0.3 shard_map.58
  27.1 3.1 %collective-permute-done.11.refs_0_ = bf16[2,128,256]{2,1,0:T(8,128)(2,1)S(1)} collective-permute-done((bf16[2,128,256]{2,1,0:T(8,128)(2,1)S(1)}, bf16[2,128,256]{2,1,0:T(8,128)(2,1)S(1)}, u32[]{:S(2)}, u32[]{:S(2)}) %collective-permute-start.11) | collective-permute-done | bytes 131104 | tf_op jit(solution)/shard_map/ppermute | solution.py:281
  30.1 0.2 shard_map.59.refs_5_.refs_0_
  30.3 1.6 %collective-permute-start.14 = (bf16[2,128,256]{2,1,0:T(8,128)(2,1)S(1)}, bf16[2,128,256]{2,1,0:T(8,128)(2,1)S(1)}, u32[]{:S(2)}, u32[]{:S(2)}) collective-permute-start(bf16[2,128,256]{2,1,0:T(8,128)(2,1)S(1)} %shard_map.59.refs_5_.refs_0_), channel_id=1, source_target_pairs={{0,4},{4,12},{12,20},{20,28},{28,24},{24,16},{16,8},{8,0},{1,5},{5... | collective-permute-start | bytes 393224 | tf_op jit(solution)/shard_map/ppermute | solution.py:265
  31.9 0.5 collective-permute-start.12
  32.4 3.1 %collective-permute-done.14.refs_9_ = bf16[2,128,256]{2,1,0:T(8,128)(2,1)S(1)} collective-permute-done((bf16[2,128,256]{2,1,0:T(8,128)(2,1)S(1)}, bf16[2,128,256]{2,1,0:T(8,128)(2,1)S(1)}, u32[]{:S(2)}, u32[]{:S(2)}) %collective-permute-start.14) | collective-permute-done | bytes 131104 | tf_op jit(solution)/shard_map/ppermute | solution.py:265
  35.5 1.4 %collective-permute-start.15 = (bf16[2,128,256]{2,1,0:T(8,128)(2,1)S(1)}, bf16[2,128,256]{2,1,0:T(8,128)(2,1)S(1)}, u32[]{:S(2)}, u32[]{:S(2)}) collective-permute-start(bf16[2,128,256]{2,1,0:T(8,128)(2,1)S(1)} %collective-permute-done.14.refs_9_), channel_id=1, source_target_pairs={{0,4},{4,12},{12,20},{20,28},{28,24},{24,16},{16,8},{8,0},{1,5},{5... | collective-permute-start | bytes 393224 | tf_op jit(solution)/shard_map/ppermute | solution.py:265
  36.9 0.0 collective-permute-done.12.refs_6_
  36.9 0.6 %collective-permute-start.13 = (bf16[2,128,256]{2,1,0:T(8,128)(2,1)S(1)}, bf16[2,128,256]{2,1,0:T(8,128)(2,1)S(1)}, u32[]{:S(2)}, u32[]{:S(2)}) collective-permute-start(bf16[2,128,256]{2,1,0:T(8,128)(2,1)S(1)} %collective-permute-done.12.refs_6_), channel_id=1, source_target_pairs={{4,0},{12,4},{20,12},{28,20},{24,28},{16,24},{8,16},{0,8},{5,1},{1... | collective-permute-start | bytes 393224 | tf_op jit(solution)/shard_map/ppermute | solution.py:268
  37.6 2.9 %collective-permute-done.15.refs_8_ = bf16[2,128,256]{2,1,0:T(8,128)(2,1)S(1)} collective-permute-done((bf16[2,128,256]{2,1,0:T(8,128)(2,1)S(1)}, bf16[2,128,256]{2,1,0:T(8,128)(2,1)S(1)}, u32[]{:S(2)}, u32[]{:S(2)}) %collective-permute-start.15) | collective-permute-done | bytes 131104 | tf_op jit(solution)/shard_map/ppermute | solution.py:265
  40.5 1.5 %collective-permute-start.17 = (bf16[2,128,256]{2,1,0:T(8,128)(2,1)S(1)}, bf16[2,128,256]{2,1,0:T(8,128)(2,1)S(1)}, u32[]{:S(2)}, u32[]{:S(2)}) collective-permute-start(bf16[2,128,256]{2,1,0:T(8,128)(2,1)S(1)} %collective-permute-done.15.refs_8_), channel_id=1, source_target_pairs={{0,4},{4,12},{12,20},{20,28},{28,24},{24,16},{16,8},{8,0},{1,5},{5... | collective-permute-start | bytes 393224 | tf_op jit(solution)/shard_map/ppermute | solution.py:265
  42.0 0.0 collective-permute-done.13.refs_7_
  42.0 0.5 collective-permute-start.16
  42.5 2.9 %collective-permute-done.17.refs_2_ = bf16[2,128,256]{2,1,0:T(8,128)(2,1)S(1)} collective-permute-done((bf16[2,128,256]{2,1,0:T(8,128)(2,1)S(1)}, bf16[2,128,256]{2,1,0:T(8,128)(2,1)S(1)}, u32[]{:S(2)}, u32[]{:S(2)}) %collective-permute-start.17) | collective-permute-done | bytes 131104 | tf_op jit(solution)/shard_map/ppermute | solution.py:265
  45.5 1.5 %collective-permute-start.18 = (bf16[2,128,256]{2,1,0:T(8,128)(2,1)S(1)}, bf16[2,128,256]{2,1,0:T(8,128)(2,1)S(1)}, u32[]{:S(2)}, u32[]{:S(2)}) collective-permute-start(bf16[2,128,256]{2,1,0:T(8,128)(2,1)S(1)} %collective-permute-done.17.refs_2_), channel_id=1, source_target_pairs={{0,4},{4,12},{12,20},{20,28},{28,24},{24,16},{16,8},{8,0},{1,5},{5... | collective-permute-start | bytes 393224 | tf_op jit(solution)/shard_map/ppermute | solution.py:265
  47.0 2.9 %shard_map.60 = (f32[4,128,256]{2,1,0:T(8,128)S(1)}, bf16[4,128,768]{2,1,0:T(8,128)(2,1)S(1)}) custom-call(s32[8,128]{1,0:T(8,128)S(1)} %get-tuple-element.28.refs_0_, s32[8,128]{1,0:T(8,128)S(1)} %collective-permute-done.refs_1_, bf16[2,1,1,4,5,128,128]{6,5,4,3,2,1,0:T(8,128)(2,1)} %refs_2_.3, ...), custom_call_target="tpu_custom_call" | custom-call | tf_op jit(solution)/shard_map/pallas_call | solution.py:321
  49.9 0.0 collective-permute-done.16.refs_0_
  49.9 0.6 %collective-permute-done.18.refs_1_ = bf16[2,128,256]{2,1,0:T(8,128)(2,1)S(1)} collective-permute-done((bf16[2,128,256]{2,1,0:T(8,128)(2,1)S(1)}, bf16[2,128,256]{2,1,0:T(8,128)(2,1)S(1)}, u32[]{:S(2)}, u32[]{:S(2)}) %collective-permute-start.18) | collective-permute-done | bytes 131104 | tf_op jit(solution)/shard_map/ppermute | solution.py:265
  50.4 0.3 shard_map.61
  50.7 1.6 %collective-permute-start.19 = (bf16[1,128,256]{2,1,0:T(8,128)(2,1)S(1)}, bf16[1,128,256]{2,1,0:T(8,128)(2,1)S(1)}, u32[]{:S(2)}, u32[]{:S(2)}) collective-permute-start(bf16[1,128,256]{2,1,0:T(8,128)(2,1)S(1)} %get-tuple-element.43), channel_id=1, source_target_pairs={{0,2},{1,3},{2,0},{3,1},{4,6},{5,7},{6,4},{7,5},{8,10},{9,11},{10,... | collective-permute-start | bytes 196616 | tf_op jit(solution)/shard_map/ppermute | solution.py:281
  52.3 0.0 collective-permute-start.22
  52.3 0.6 %collective-permute-start.21 = (bf16[1,128,256]{2,1,0:T(8,128)(2,1)S(1)}, bf16[1,128,256]{2,1,0:T(8,128)(2,1)S(1)}, u32[]{:S(2)}, u32[]{:S(2)}) collective-permute-start(bf16[1,128,256]{2,1,0:T(8,128)(2,1)S(1)} %get-tuple-element.44), channel_id=1, source_target_pairs={{0,3},{1,2},{2,1},{3,0},{4,7},{5,6},{6,5},{7,4},{8,11},{9,10},{10,... | collective-permute-start | bytes 196616 | tf_op jit(solution)/shard_map/ppermute | solution.py:281
  52.9 0.3 shard_map.62
  53.2 1.8 %collective-permute-done.19.refs_0_ = bf16[1,128,256]{2,1,0:T(8,128)(2,1)S(1)} collective-permute-done((bf16[1,128,256]{2,1,0:T(8,128)(2,1)S(1)}, bf16[1,128,256]{2,1,0:T(8,128)(2,1)S(1)}, u32[]{:S(2)}, u32[]{:S(2)}) %collective-permute-start.19) | collective-permute-done | bytes 65568 | tf_op jit(solution)/shard_map/ppermute | solution.py:281
  55.1 0.0 collective-permute-start.20
  55.1 0.0 collective-permute-done.22.refs_1_
  55.1 0.7 %shard_map.63.refs_2_ = bf16[3,1,1,128,512]{4,3,2,1,0:T(8,128)(2,1)} custom-call(bf16[128,512]{1,0:T(8,128)(2,1)S(1)} %get-tuple-element.49.full_ref, bf16[2,128,256]{2,1,0:T(8,128)(2,1)S(1)} %shard_map.59.refs_5_.refs_0_, bf16[128,256]{1,0:T(8,128)(2,1)S(1)} %collective-permute-done.22.refs_1_), custom_call_target="tpu_custom_call" | custom-call | tf_op jit(solution)/shard_map/pallas_call | solution.py:377
  55.8 0.4 collective-permute-done.21.refs_1_
  56.2 0.1 collective-permute-done.20.mate_ref
  56.3 0.9 %shard_map.64 = bf16[3,1,1,128,512]{4,3,2,1,0:T(8,128)(2,1)} custom-call(bf16[3,1,1,128,128]{4,3,2,1,0:T(8,128)(2,1)S(1)} %copy-done.1, f32[2,128,256]{2,1,0:T(8,128)S(1)} %get-tuple-element.46.right_ref, bf16[128,256]{1,0:T(8,128)(2,1)S(1)} %collective-permute-done.20.mate_ref, ...), custom_call_target="tpu_custom_call", output_to_operand_aliasing={{}: (5, {})} | custom-call | tf_op jit(solution)/shard_map/pallas_call | solution.py:385
  (2 shorter events, 0.0 us)
Async XLA Ops:
  1.2 1.4 %collective-permute-start.1 = (bf16[128,256]{1,0:T(8,128)(2,1)S(1)}, bf16[128,256]{1,0:T(8,128)(2,1)S(1)}, u32[]{:S(2)}, u32[]{:S(2)}) collective-permute-start(bf16[128,256]{1,0:T(8,128)(2,1)S(1)} %get-tuple-element.30), channel_id=1, source_target_pairs={{0,1},{1,0},{2,3},{3,2},{4,5},{5,4},{6,7},{7,6},{8,9},{9,8},{10,11... | collective-permute-start | bytes 196616 | tf_op jit(solution)/shard_map/ppermute | solution.py:281
  1.7 1.2 %collective-permute-start = (s32[8,128]{1,0:T(8,128)S(1)}, s32[8,128]{1,0:T(8,128)S(1)}, u32[]{:S(2)}, u32[]{:S(2)}) collective-permute-start(s32[8,128]{1,0:T(8,128)S(1)} %get-tuple-element.28.refs_0_), channel_id=1, source_target_pairs={{0,1},{1,0},{2,3},{3,2},{4,5},{5,4},{6,7},{7,6},{8,9},{9,8},{10,11... | collective-permute-start | bytes 12296 | tf_op jit(solution)/shard_map/ppermute | solution.py:281
  2.9 18.5 %collective-permute-start.2 = (bf16[2,1,1,4,5,128,128]{6,5,4,3,2,1,0:T(8,128)(2,1)}, bf16[2,1,1,4,5,128,128]{6,5,4,3,2,1,0:T(8,128)(2,1)S(1)}, u32[]{:S(2)}, u32[]{:S(2)}) collective-permute-start(bf16[2,1,1,4,5,128,128]{6,5,4,3,2,1,0:T(8,128)(2,1)} %refs_2_.3), channel_id=1, source_target_pairs={{0,1},{1,0},{2,3},{3,2},{4,5},{5,4},{6,7},{7,6},{8,9},{9,8},{10,11... | collective-permute-start | bytes 3932168 | tf_op jit(solution)/shard_map/ppermute | solution.py:281
  3.1 6.7 %collective-permute-start.6 = (bf16[2,128,256]{2,1,0:T(8,128)(2,1)S(1)}, bf16[2,128,256]{2,1,0:T(8,128)(2,1)S(1)}, u32[]{:S(2)}, u32[]{:S(2)}) collective-permute-start(bf16[2,128,256]{2,1,0:T(8,128)(2,1)S(1)} %pad_maximum_fusion.refs_4_.refs_3_), channel_id=1, source_target_pairs={{0,4},{4,12},{12,20},{20,28},{28,24},{24,16},{16,8},{8,0},{1,5},{5... | collective-permute-start | bytes 393224 | tf_op jit(solution)/shard_map/ppermute | solution.py:265
  5.9 5.6 %collective-permute-start.4 = (bf16[2,128,256]{2,1,0:T(8,128)(2,1)S(1)}, bf16[2,128,256]{2,1,0:T(8,128)(2,1)S(1)}, u32[]{:S(2)}, u32[]{:S(2)}) collective-permute-start(bf16[2,128,256]{2,1,0:T(8,128)(2,1)S(1)} %pad_maximum_fusion.refs_4_.refs_3_), channel_id=1, source_target_pairs={{4,0},{12,4},{20,12},{28,20},{24,28},{16,24},{8,16},{0,8},{5,1},{1... | collective-permute-start | bytes 393224 | tf_op jit(solution)/shard_map/ppermute | solution.py:268
  9.8 5.1 %collective-permute-start.7 = (bf16[2,128,256]{2,1,0:T(8,128)(2,1)S(1)}, bf16[2,128,256]{2,1,0:T(8,128)(2,1)S(1)}, u32[]{:S(2)}, u32[]{:S(2)}) collective-permute-start(bf16[2,128,256]{2,1,0:T(8,128)(2,1)S(1)} %collective-permute-done.6.refs_8_.refs_7_), channel_id=1, source_target_pairs={{0,4},{4,12},{12,20},{20,28},{28,24},{24,16},{16,8},{8,0},{1,5},{5... | collective-permute-start | bytes 393224 | tf_op jit(solution)/shard_map/ppermute | solution.py:265
  11.5 5.0 %collective-permute-start.3 = (bf16[256,256]{1,0:T(8,128)(2,1)S(1)}, bf16[256,256]{1,0:T(8,128)(2,1)S(1)}, u32[]{:S(2)}, u32[]{:S(2)}) collective-permute-start(bf16[256,256]{1,0:T(8,128)(2,1)S(1)} %get-tuple-element.33), channel_id=1, source_target_pairs={{0,1},{1,0},{2,3},{3,2},{4,5},{5,4},{6,7},{7,6},{8,9},{9,8},{10,11... | collective-permute-start | bytes 393224 | tf_op jit(solution)/shard_map/ppermute | solution.py:281
  11.5 5.9 %collective-permute-start.5 = (bf16[2,128,256]{2,1,0:T(8,128)(2,1)S(1)}, bf16[2,128,256]{2,1,0:T(8,128)(2,1)S(1)}, u32[]{:S(2)}, u32[]{:S(2)}) collective-permute-start(bf16[2,128,256]{2,1,0:T(8,128)(2,1)S(1)} %collective-permute-done.4.refs_5_.refs_4_), channel_id=1, source_target_pairs={{4,0},{12,4},{20,12},{28,20},{24,28},{16,24},{8,16},{0,8},{5,1},{1... | collective-permute-start | bytes 393224 | tf_op jit(solution)/shard_map/ppermute | solution.py:268
  14.9 5.0 %collective-permute-start.9 = (bf16[2,128,256]{2,1,0:T(8,128)(2,1)S(1)}, bf16[2,128,256]{2,1,0:T(8,128)(2,1)S(1)}, u32[]{:S(2)}, u32[]{:S(2)}) collective-permute-start(bf16[2,128,256]{2,1,0:T(8,128)(2,1)S(1)} %collective-permute-done.7.refs_7_.refs_6_), channel_id=1, source_target_pairs={{0,4},{4,12},{12,20},{20,28},{28,24},{24,16},{16,8},{8,0},{1,5},{5... | collective-permute-start | bytes 393224 | tf_op jit(solution)/shard_map/ppermute | solution.py:265
  17.4 6.9 %collective-permute-start.8 = (bf16[2,128,256]{2,1,0:T(8,128)(2,1)S(1)}, bf16[2,128,256]{2,1,0:T(8,128)(2,1)S(1)}, u32[]{:S(2)}, u32[]{:S(2)}) collective-permute-start(bf16[2,128,256]{2,1,0:T(8,128)(2,1)S(1)} %collective-permute-done.5.refs_6_.refs_5_), channel_id=1, source_target_pairs={{4,0},{12,4},{20,12},{28,20},{24,28},{16,24},{8,16},{0,8},{5,1},{1... | collective-permute-start | bytes 393224 | tf_op jit(solution)/shard_map/ppermute | solution.py:268
  19.9 5.0 %collective-permute-start.10 = (bf16[2,128,256]{2,1,0:T(8,128)(2,1)S(1)}, bf16[2,128,256]{2,1,0:T(8,128)(2,1)S(1)}, u32[]{:S(2)}, u32[]{:S(2)}) collective-permute-start(bf16[2,128,256]{2,1,0:T(8,128)(2,1)S(1)} %collective-permute-done.9.refs_2_), channel_id=1, source_target_pairs={{0,4},{4,12},{12,20},{20,28},{28,24},{24,16},{16,8},{8,0},{1,5},{5... | collective-permute-start | bytes 393224 | tf_op jit(solution)/shard_map/ppermute | solution.py:265
  24.2 2.5 %copy-start = (bf16[3,1,1,128,512]{4,3,2,1,0:T(8,128)(2,1)S(1)}, bf16[3,1,1,128,512]{4,3,2,1,0:T(8,128)(2,1)}, u32[]{:S(2)}) copy-start(bf16[3,1,1,128,512]{4,3,2,1,0:T(8,128)(2,1)} %b_ref.5) | copy-start | bytes 1179652
  24.2 2.5 %copy-start.1 = (bf16[3,1,1,128,128]{4,3,2,1,0:T(8,128)(2,1)S(1)}, bf16[3,1,1,128,128]{4,3,2,1,0:T(8,128)(2,1)}, u32[]{:S(2)}) copy-start(bf16[3,1,1,128,128]{4,3,2,1,0:T(8,128)(2,1)} %d_ref.5) | copy-start | bytes 294916
  25.1 5.0 %collective-permute-start.11 = (bf16[2,128,256]{2,1,0:T(8,128)(2,1)S(1)}, bf16[2,128,256]{2,1,0:T(8,128)(2,1)S(1)}, u32[]{:S(2)}, u32[]{:S(2)}) collective-permute-start(bf16[2,128,256]{2,1,0:T(8,128)(2,1)S(1)} %shard_map.57), channel_id=1, source_target_pairs={{0,2},{1,3},{2,0},{3,1},{4,6},{5,7},{6,4},{7,5},{8,10},{9,11},{10,... | collective-permute-start | bytes 393224 | tf_op jit(solution)/shard_map/ppermute | solution.py:281
  30.3 5.2 %collective-permute-start.14 = (bf16[2,128,256]{2,1,0:T(8,128)(2,1)S(1)}, bf16[2,128,256]{2,1,0:T(8,128)(2,1)S(1)}, u32[]{:S(2)}, u32[]{:S(2)}) collective-permute-start(bf16[2,128,256]{2,1,0:T(8,128)(2,1)S(1)} %shard_map.59.refs_5_.refs_0_), channel_id=1, source_target_pairs={{0,4},{4,12},{12,20},{20,28},{28,24},{24,16},{16,8},{8,0},{1,5},{5... | collective-permute-start | bytes 393224 | tf_op jit(solution)/shard_map/ppermute | solution.py:265
  31.9 5.0 %collective-permute-start.12 = (bf16[2,128,256]{2,1,0:T(8,128)(2,1)S(1)}, bf16[2,128,256]{2,1,0:T(8,128)(2,1)S(1)}, u32[]{:S(2)}, u32[]{:S(2)}) collective-permute-start(bf16[2,128,256]{2,1,0:T(8,128)(2,1)S(1)} %shard_map.59.refs_5_.refs_0_), channel_id=1, source_target_pairs={{4,0},{12,4},{20,12},{28,20},{24,28},{16,24},{8,16},{0,8},{5,1},{1... | collective-permute-start | bytes 393224 | tf_op jit(solution)/shard_map/ppermute | solution.py:268
  35.5 5.0 %collective-permute-start.15 = (bf16[2,128,256]{2,1,0:T(8,128)(2,1)S(1)}, bf16[2,128,256]{2,1,0:T(8,128)(2,1)S(1)}, u32[]{:S(2)}, u32[]{:S(2)}) collective-permute-start(bf16[2,128,256]{2,1,0:T(8,128)(2,1)S(1)} %collective-permute-done.14.refs_9_), channel_id=1, source_target_pairs={{0,4},{4,12},{12,20},{20,28},{28,24},{24,16},{16,8},{8,0},{1,5},{5... | collective-permute-start | bytes 393224 | tf_op jit(solution)/shard_map/ppermute | solution.py:265
  36.9 5.1 %collective-permute-start.13 = (bf16[2,128,256]{2,1,0:T(8,128)(2,1)S(1)}, bf16[2,128,256]{2,1,0:T(8,128)(2,1)S(1)}, u32[]{:S(2)}, u32[]{:S(2)}) collective-permute-start(bf16[2,128,256]{2,1,0:T(8,128)(2,1)S(1)} %collective-permute-done.12.refs_6_), channel_id=1, source_target_pairs={{4,0},{12,4},{20,12},{28,20},{24,28},{16,24},{8,16},{0,8},{5,1},{1... | collective-permute-start | bytes 393224 | tf_op jit(solution)/shard_map/ppermute | solution.py:268
  40.5 5.0 %collective-permute-start.17 = (bf16[2,128,256]{2,1,0:T(8,128)(2,1)S(1)}, bf16[2,128,256]{2,1,0:T(8,128)(2,1)S(1)}, u32[]{:S(2)}, u32[]{:S(2)}) collective-permute-start(bf16[2,128,256]{2,1,0:T(8,128)(2,1)S(1)} %collective-permute-done.15.refs_8_), channel_id=1, source_target_pairs={{0,4},{4,12},{12,20},{20,28},{28,24},{24,16},{16,8},{8,0},{1,5},{5... | collective-permute-start | bytes 393224 | tf_op jit(solution)/shard_map/ppermute | solution.py:265
  42.0 7.8 %collective-permute-start.16 = (bf16[2,128,256]{2,1,0:T(8,128)(2,1)S(1)}, bf16[2,128,256]{2,1,0:T(8,128)(2,1)S(1)}, u32[]{:S(2)}, u32[]{:S(2)}) collective-permute-start(bf16[2,128,256]{2,1,0:T(8,128)(2,1)S(1)} %collective-permute-done.13.refs_7_), channel_id=1, source_target_pairs={{4,0},{12,4},{20,12},{28,20},{24,28},{16,24},{8,16},{0,8},{5,1},{1... | collective-permute-start | bytes 393224 | tf_op jit(solution)/shard_map/ppermute | solution.py:268
  45.5 5.0 %collective-permute-start.18 = (bf16[2,128,256]{2,1,0:T(8,128)(2,1)S(1)}, bf16[2,128,256]{2,1,0:T(8,128)(2,1)S(1)}, u32[]{:S(2)}, u32[]{:S(2)}) collective-permute-start(bf16[2,128,256]{2,1,0:T(8,128)(2,1)S(1)} %collective-permute-done.17.refs_2_), channel_id=1, source_target_pairs={{0,4},{4,12},{12,20},{20,28},{28,24},{24,16},{16,8},{8,0},{1,5},{5... | collective-permute-start | bytes 393224 | tf_op jit(solution)/shard_map/ppermute | solution.py:265
  50.7 4.3 %collective-permute-start.19 = (bf16[1,128,256]{2,1,0:T(8,128)(2,1)S(1)}, bf16[1,128,256]{2,1,0:T(8,128)(2,1)S(1)}, u32[]{:S(2)}, u32[]{:S(2)}) collective-permute-start(bf16[1,128,256]{2,1,0:T(8,128)(2,1)S(1)} %get-tuple-element.43), channel_id=1, source_target_pairs={{0,2},{1,3},{2,0},{3,1},{4,6},{5,7},{6,4},{7,5},{8,10},{9,11},{10,... | collective-permute-start | bytes 196616 | tf_op jit(solution)/shard_map/ppermute | solution.py:281
  52.3 2.8 %collective-permute-start.22 = (bf16[128,256]{1,0:T(8,128)(2,1)S(1)}, bf16[128,256]{1,0:T(8,128)(2,1)S(1)}, u32[]{:S(2)}, u32[]{:S(2)}) collective-permute-start(bf16[128,256]{1,0:T(8,128)(2,1)S(1)} %slice_bitcast_fusion), channel_id=1, source_target_pairs={{0,1},{1,0},{2,3},{3,2},{4,5},{5,4},{6,7},{7,6},{8,9},{9,8},{10,11... | collective-permute-start | bytes 196616 | tf_op jit(solution)/shard_map/ppermute | solution.py:281
  52.3 3.9 %collective-permute-start.21 = (bf16[1,128,256]{2,1,0:T(8,128)(2,1)S(1)}, bf16[1,128,256]{2,1,0:T(8,128)(2,1)S(1)}, u32[]{:S(2)}, u32[]{:S(2)}) collective-permute-start(bf16[1,128,256]{2,1,0:T(8,128)(2,1)S(1)} %get-tuple-element.44), channel_id=1, source_target_pairs={{0,3},{1,2},{2,1},{3,0},{4,7},{5,6},{6,5},{7,4},{8,11},{9,10},{10,... | collective-permute-start | bytes 196616 | tf_op jit(solution)/shard_map/ppermute | solution.py:281
  55.1 1.3 %collective-permute-start.20 = (bf16[128,256]{1,0:T(8,128)(2,1)S(1)}, bf16[128,256]{1,0:T(8,128)(2,1)S(1)}, u32[]{:S(2)}, u32[]{:S(2)}) collective-permute-start(bf16[128,256]{1,0:T(8,128)(2,1)S(1)} %get-tuple-element.48), channel_id=1, source_target_pairs={{0,1},{1,0},{2,3},{3,2},{4,5},{5,4},{6,7},{7,6},{8,9},{9,8},{10,11... | collective-permute-start | bytes 196616 | tf_op jit(solution)/shard_map/ppermute | solution.py:281

commit v8 on v7

--- a/solution.py
+++ b/solution.py
@@ -308,7 +308,7 @@
     solved = after(jnp.stack([own, other]), index[1])
     blocks = [in_hbm(l_blocks), send(after(l_blocks, solved), 1)]
 
-    late = [d for d in range(1, m) if min(d, m - d) >= m // 2 - 1]
+    late = [m // 2 - 1, m // 2]
     early = [d for d in range(m) if d not in late]
     columns, kept = [], []
     for level in range(1, levels):

time: 57.4 us -> 57.3 us (level)
  no operation moved by 1% of the time
where the time goes in v8:
time: 57.3 us; the launch traced here: 57.1 us
  waiting for transfers between devices  26.9 us (47%)
  starting transfers between devices  20.6 us (36%)
  Pallas kernels  9.41 us (16%)
    ppermute x8, waiting for transfers between devices, advance(): self.behind = lax.ppermute(self.behind, 'prow', self.to_next)  19.3 us
    ppermute x8, starting transfers between devices, advance(): self.behind = lax.ppermute(self.behind, 'prow', self.to_next)  13.5 us
    ppermute x9, waiting for transfers between devices, send(): return lax.ppermute(value, 'pcol', [(i, i ^ bits) for i in range(n)])  6.61 us
    pallas_call x2, Pallas kernels, solve_paired(): pl.pallas_call(functools.partial(gather_kernel, n, level, m, early, late)...  5.52 us
    ppermute x9, starting transfers between devices, send(): return lax.ppermute(value, 'pcol', [(i, i ^ bits) for i in range(n)])  4.63 us
    ppermute x6, starting transfers between devices, advance(): self.ahead = lax.ppermute(self.ahead, 'prow', self.to_last)  2.53 us
    pallas_call x1, Pallas kernels, solve_paired(): pl.pallas_call(functools.partial(first_kernel, n, m, place), out_shape=[n...  1.21 us
  transfers between devices with their start and end apart: 23, of which 15 were waited for; matrix products, arithmetic and copies ran while one was open for 0% of the time, Pallas kernels for 12%

profile of v8, /device:TPU:0, one launch (start us, length us, event | category | flops | bytes accessed | tf_op | source)
XLA Modules:
  0.0 57.1 jit_solution(18372382685563913569)
XLA Ops:
  0.0 1.2 %shard_map.55 = (bf16[128,512]{1,0:T(8,128)(2,1)S(1)}, s32[8,128]{1,0:T(8,128)S(1)}, bf16[128,256]{1,0:T(8,128)(2,1)S(1)}, bf16[128,256]{1,0:T(8,128)(2,1)S(1)}, bf16[256,256]{1,0:T(8,128)(2,1)S(1)}) custom-call(s32[2,1,1,4]{3,2,1,0:T(1,128)} %counts_ref.1, s32[2,1,1,4,5]{4,3,2,1,0:T(4,128)} %cols_ref.1, bf16[3,1,1,128,512]{4,3,2,1,0:T(8,128)(2,1)} %b_ref.5, ...), custom_call_target="tpu_custom_call" | custom-call | tf_op jit(solution)/shard_map/pallas_call | solution.py:287
  1.2 0.5 collective-permute-start.1
  1.7 0.1 collective-permute-start
  1.8 0.8 %collective-permute-done.1 = bf16[128,256]{1,0:T(8,128)(2,1)S(1)} collective-permute-done((bf16[128,256]{1,0:T(8,128)(2,1)S(1)}, bf16[128,256]{1,0:T(8,128)(2,1)S(1)}, u32[]{:S(2)}, u32[]{:S(2)}) %collective-permute-start.1) | collective-permute-done | bytes 65568 | tf_op jit(solution)/shard_map/ppermute | solution.py:281
  2.7 0.2 collective-permute-done.refs_1_
  2.9 0.2 collective-permute-start.2
  3.1 2.8 %collective-permute-start.6 = (bf16[2,128,256]{2,1,0:T(8,128)(2,1)S(1)}, bf16[2,128,256]{2,1,0:T(8,128)(2,1)S(1)}, u32[]{:S(2)}, u32[]{:S(2)}) collective-permute-start(bf16[2,128,256]{2,1,0:T(8,128)(2,1)S(1)} %pad_maximum_fusion.refs_4_.refs_2_), channel_id=1, source_target_pairs={{0,4},{4,12},{12,20},{20,28},{28,24},{24,16},{16,8},{8,0},{1,5},{5... | collective-permute-start | bytes 393224 | tf_op jit(solution)/shard_map/ppermute | solution.py:265
  5.9 0.1 collective-permute-start.4
  6.0 3.8 %collective-permute-done.6.refs_9_.refs_7_ = bf16[2,128,256]{2,1,0:T(8,128)(2,1)S(1)} collective-permute-done((bf16[2,128,256]{2,1,0:T(8,128)(2,1)S(1)}, bf16[2,128,256]{2,1,0:T(8,128)(2,1)S(1)}, u32[]{:S(2)}, u32[]{:S(2)}) %collective-permute-start.6) | collective-permute-done | bytes 131104 | tf_op jit(solution)/shard_map/ppermute | solution.py:265
  9.8 1.7 %collective-permute-start.7 = (bf16[2,128,256]{2,1,0:T(8,128)(2,1)S(1)}, bf16[2,128,256]{2,1,0:T(8,128)(2,1)S(1)}, u32[]{:S(2)}, u32[]{:S(2)}) collective-permute-start(bf16[2,128,256]{2,1,0:T(8,128)(2,1)S(1)} %collective-permute-done.6.refs_9_.refs_7_), channel_id=1, source_target_pairs={{0,4},{4,12},{12,20},{20,28},{28,24},{24,16},{16,8},{8,0},{1,5},{5... | collective-permute-start | bytes 393224 | tf_op jit(solution)/shard_map/ppermute | solution.py:265
  11.5 0.0 collective-permute-start.3
  11.5 0.0 collective-permute-done.4.refs_5_.refs_3_
  11.5 0.4 collective-permute-start.5
  11.9 3.0 %collective-permute-done.7.refs_8_.refs_6_ = bf16[2,128,256]{2,1,0:T(8,128)(2,1)S(1)} collective-permute-done((bf16[2,128,256]{2,1,0:T(8,128)(2,1)S(1)}, bf16[2,128,256]{2,1,0:T(8,128)(2,1)S(1)}, u32[]{:S(2)}, u32[]{:S(2)}) %collective-permute-start.7) | collective-permute-done | bytes 131104 | tf_op jit(solution)/shard_map/ppermute | solution.py:265
  14.9 1.5 %collective-permute-start.8 = (bf16[2,128,256]{2,1,0:T(8,128)(2,1)S(1)}, bf16[2,128,256]{2,1,0:T(8,128)(2,1)S(1)}, u32[]{:S(2)}, u32[]{:S(2)}) collective-permute-start(bf16[2,128,256]{2,1,0:T(8,128)(2,1)S(1)} %collective-permute-done.7.refs_8_.refs_6_), channel_id=1, source_target_pairs={{0,4},{4,12},{12,20},{20,28},{28,24},{24,16},{16,8},{8,0},{1,5},{5... | collective-permute-start | bytes 393224 | tf_op jit(solution)/shard_map/ppermute | solution.py:265
  16.4 0.0 collective-permute-done.3.away_ref
  16.5 0.9 %collective-permute-done.5.refs_6_.refs_4_ = bf16[2,128,256]{2,1,0:T(8,128)(2,1)S(1)} collective-permute-done((bf16[2,128,256]{2,1,0:T(8,128)(2,1)S(1)}, bf16[2,128,256]{2,1,0:T(8,128)(2,1)S(1)}, u32[]{:S(2)}, u32[]{:S(2)}) %collective-permute-start.5) | collective-permute-done | bytes 131104 | tf_op jit(solution)/shard_map/ppermute | solution.py:268
  17.4 0.4 collective-permute-start.9
  17.8 2.1 %collective-permute-done.8.refs_7_.refs_5_ = bf16[2,128,256]{2,1,0:T(8,128)(2,1)S(1)} collective-permute-done((bf16[2,128,256]{2,1,0:T(8,128)(2,1)S(1)}, bf16[2,128,256]{2,1,0:T(8,128)(2,1)S(1)}, u32[]{:S(2)}, u32[]{:S(2)}) %collective-permute-start.8) | collective-permute-done | bytes 131104 | tf_op jit(solution)/shard_map/ppermute | solution.py:265
  19.9 1.5 %collective-permute-start.10 = (bf16[2,128,256]{2,1,0:T(8,128)(2,1)S(1)}, bf16[2,128,256]{2,1,0:T(8,128)(2,1)S(1)}, u32[]{:S(2)}, u32[]{:S(2)}) collective-permute-start(bf16[2,128,256]{2,1,0:T(8,128)(2,1)S(1)} %collective-permute-done.8.refs_7_.refs_5_), channel_id=1, source_target_pairs={{0,4},{4,12},{12,20},{20,28},{28,24},{24,16},{16,8},{8,0},{1,5},{5... | collective-permute-start | bytes 393224 | tf_op jit(solution)/shard_map/ppermute | solution.py:265
  21.4 0.0 collective-permute-done.2.refs_3_
  21.4 2.7 %shard_map.56 = (f32[4,128,256]{2,1,0:T(8,128)S(1)}, bf16[4,128,512]{2,1,0:T(8,128)(2,1)S(1)}) custom-call(s32[8,128]{1,0:T(8,128)S(1)} %get-tuple-element.28.refs_0_, s32[8,128]{1,0:T(8,128)S(1)} %collective-permute-done.refs_1_, bf16[2,1,1,4,5,128,128]{6,5,4,3,2,1,0:T(8,128)(2,1)} %refs_2_.3, ...), custom_call_target="tpu_custom_call" | custom-call | tf_op jit(solution)/shard_map/pallas_call | solution.py:321
  24.2 0.0 copy-start
  24.2 0.0 copy-start.1
  24.2 0.0 collective-permute-done.9.refs_0_
  24.2 0.6 %collective-permute-done.10.refs_1_ = bf16[2,128,256]{2,1,0:T(8,128)(2,1)S(1)} collective-permute-done((bf16[2,128,256]{2,1,0:T(8,128)(2,1)S(1)}, bf16[2,128,256]{2,1,0:T(8,128)(2,1)S(1)}, u32[]{:S(2)}, u32[]{:S(2)}) %collective-permute-start.10) | collective-permute-done | bytes 131104 | tf_op jit(solution)/shard_map/ppermute | solution.py:265
  24.8 0.2 shard_map.57
  25.1 1.6 %collective-permute-start.11 = (bf16[2,128,256]{2,1,0:T(8,128)(2,1)S(1)}, bf16[2,128,256]{2,1,0:T(8,128)(2,1)S(1)}, u32[]{:S(2)}, u32[]{:S(2)}) collective-permute-start(bf16[2,128,256]{2,1,0:T(8,128)(2,1)S(1)} %shard_map.57), channel_id=1, source_target_pairs={{0,2},{1,3},{2,0},{3,1},{4,6},{5,7},{6,4},{7,5},{8,10},{9,11},{10,... | collective-permute-start | bytes 393224 | tf_op jit(solution)/shard_map/ppermute | solution.py:281
  26.7 0.0 copy-done
  26.7 0.0 copy-done.1
  26.7 0.2 shard_map.58
  27.0 3.1 %collective-permute-done.11.refs_0_ = bf16[2,128,256]{2,1,0:T(8,128)(2,1)S(1)} collective-permute-done((bf16[2,128,256]{2,1,0:T(8,128)(2,1)S(1)}, bf16[2,128,256]{2,1,0:T(8,128)(2,1)S(1)}, u32[]{:S(2)}, u32[]{:S(2)}) %collective-permute-start.11) | collective-permute-done | bytes 131104 | tf_op jit(solution)/shard_map/ppermute | solution.py:281
  30.1 0.2 shard_map.59.refs_5_.refs_0_
  30.3 1.6 %collective-permute-start.14 = (bf16[2,128,256]{2,1,0:T(8,128)(2,1)S(1)}, bf16[2,128,256]{2,1,0:T(8,128)(2,1)S(1)}, u32[]{:S(2)}, u32[]{:S(2)}) collective-permute-start(bf16[2,128,256]{2,1,0:T(8,128)(2,1)S(1)} %shard_map.59.refs_5_.refs_0_), channel_id=1, source_target_pairs={{0,4},{4,12},{12,20},{20,28},{28,24},{24,16},{16,8},{8,0},{1,5},{5... | collective-permute-start | bytes 393224 | tf_op jit(solution)/shard_map/ppermute | solution.py:265
  31.9 0.5 collective-permute-start.12
  32.4 3.1 %collective-permute-done.14.refs_10_ = bf16[2,128,256]{2,1,0:T(8,128)(2,1)S(1)} collective-permute-done((bf16[2,128,256]{2,1,0:T(8,128)(2,1)S(1)}, bf16[2,128,256]{2,1,0:T(8,128)(2,1)S(1)}, u32[]{:S(2)}, u32[]{:S(2)}) %collective-permute-start.14) | collective-permute-done | bytes 131104 | tf_op jit(solution)/shard_map/ppermute | solution.py:265
  35.5 1.4 %collective-permute-start.15 = (bf16[2,128,256]{2,1,0:T(8,128)(2,1)S(1)}, bf16[2,128,256]{2,1,0:T(8,128)(2,1)S(1)}, u32[]{:S(2)}, u32[]{:S(2)}) collective-permute-start(bf16[2,128,256]{2,1,0:T(8,128)(2,1)S(1)} %collective-permute-done.14.refs_10_), channel_id=1, source_target_pairs={{0,4},{4,12},{12,20},{20,28},{28,24},{24,16},{16,8},{8,0},{1,5},{5... | collective-permute-start | bytes 393224 | tf_op jit(solution)/shard_map/ppermute | solution.py:265
  36.9 0.0 collective-permute-done.12.refs_6_
  36.9 0.7 %collective-permute-start.13 = (bf16[2,128,256]{2,1,0:T(8,128)(2,1)S(1)}, bf16[2,128,256]{2,1,0:T(8,128)(2,1)S(1)}, u32[]{:S(2)}, u32[]{:S(2)}) collective-permute-start(bf16[2,128,256]{2,1,0:T(8,128)(2,1)S(1)} %collective-permute-done.12.refs_6_), channel_id=1, source_target_pairs={{4,0},{12,4},{20,12},{28,20},{24,28},{16,24},{8,16},{0,8},{5,1},{1... | collective-permute-start | bytes 393224 | tf_op jit(solution)/shard_map/ppermute | solution.py:268
  37.5 2.9 %collective-permute-done.15.refs_9_ = bf16[2,128,256]{2,1,0:T(8,128)(2,1)S(1)} collective-permute-done((bf16[2,128,256]{2,1,0:T(8,128)(2,1)S(1)}, bf16[2,128,256]{2,1,0:T(8,128)(2,1)S(1)}, u32[]{:S(2)}, u32[]{:S(2)}) %collective-permute-start.15) | collective-permute-done | bytes 131104 | tf_op jit(solution)/shard_map/ppermute | solution.py:265
  40.5 1.5 %collective-permute-start.16 = (bf16[2,128,256]{2,1,0:T(8,128)(2,1)S(1)}, bf16[2,128,256]{2,1,0:T(8,128)(2,1)S(1)}, u32[]{:S(2)}, u32[]{:S(2)}) collective-permute-start(bf16[2,128,256]{2,1,0:T(8,128)(2,1)S(1)} %collective-permute-done.15.refs_9_), channel_id=1, source_target_pairs={{0,4},{4,12},{12,20},{20,28},{28,24},{24,16},{16,8},{8,0},{1,5},{5... | collective-permute-start | bytes 393224 | tf_op jit(solution)/shard_map/ppermute | solution.py:265
  41.9 0.0 collective-permute-done.13.refs_7_
  41.9 0.6 collective-permute-start.17
  42.5 2.9 %collective-permute-done.16.refs_8_ = bf16[2,128,256]{2,1,0:T(8,128)(2,1)S(1)} collective-permute-done((bf16[2,128,256]{2,1,0:T(8,128)(2,1)S(1)}, bf16[2,128,256]{2,1,0:T(8,128)(2,1)S(1)}, u32[]{:S(2)}, u32[]{:S(2)}) %collective-permute-start.16) | collective-permute-done | bytes 131104 | tf_op jit(solution)/shard_map/ppermute | solution.py:265
  45.4 1.5 %collective-permute-start.18 = (bf16[2,128,256]{2,1,0:T(8,128)(2,1)S(1)}, bf16[2,128,256]{2,1,0:T(8,128)(2,1)S(1)}, u32[]{:S(2)}, u32[]{:S(2)}) collective-permute-start(bf16[2,128,256]{2,1,0:T(8,128)(2,1)S(1)} %collective-permute-done.16.refs_8_), channel_id=1, source_target_pairs={{0,4},{4,12},{12,20},{20,28},{28,24},{24,16},{16,8},{8,0},{1,5},{5... | collective-permute-start | bytes 393224 | tf_op jit(solution)/shard_map/ppermute | solution.py:265
  46.9 2.8 %shard_map.60 = (f32[4,128,256]{2,1,0:T(8,128)S(1)}, bf16[4,128,512]{2,1,0:T(8,128)(2,1)S(1)}) custom-call(s32[8,128]{1,0:T(8,128)S(1)} %get-tuple-element.28.refs_0_, s32[8,128]{1,0:T(8,128)S(1)} %collective-permute-done.refs_1_, bf16[2,1,1,4,5,128,128]{6,5,4,3,2,1,0:T(8,128)(2,1)} %refs_2_.3, ...), custom_call_target="tpu_custom_call" | custom-call | tf_op jit(solution)/shard_map/pallas_call | solution.py:321
  49.7 0.0 collective-permute-done.17.refs_0_
  49.7 0.7 %collective-permute-done.18.refs_1_ = bf16[2,128,256]{2,1,0:T(8,128)(2,1)S(1)} collective-permute-done((bf16[2,128,256]{2,1,0:T(8,128)(2,1)S(1)}, bf16[2,128,256]{2,1,0:T(8,128)(2,1)S(1)}, u32[]{:S(2)}, u32[]{:S(2)}) %collective-permute-start.18) | collective-permute-done | bytes 131104 | tf_op jit(solution)/shard_map/ppermute | solution.py:265
  50.4 0.2 shard_map.61
  50.6 1.6 %collective-permute-start.19 = (bf16[1,128,256]{2,1,0:T(8,128)(2,1)S(1)}, bf16[1,128,256]{2,1,0:T(8,128)(2,1)S(1)}, u32[]{:S(2)}, u32[]{:S(2)}) collective-permute-start(bf16[1,128,256]{2,1,0:T(8,128)(2,1)S(1)} %get-tuple-element.43), channel_id=1, source_target_pairs={{0,2},{1,3},{2,0},{3,1},{4,6},{5,7},{6,4},{7,5},{8,10},{9,11},{10,... | collective-permute-start | bytes 196616 | tf_op jit(solution)/shard_map/ppermute | solution.py:281
  52.2 0.0 collective-permute-start.22
  52.2 0.6 %collective-permute-start.21 = (bf16[1,128,256]{2,1,0:T(8,128)(2,1)S(1)}, bf16[1,128,256]{2,1,0:T(8,128)(2,1)S(1)}, u32[]{:S(2)}, u32[]{:S(2)}) collective-permute-start(bf16[1,128,256]{2,1,0:T(8,128)(2,1)S(1)} %get-tuple-element.44), channel_id=1, source_target_pairs={{0,3},{1,2},{2,1},{3,0},{4,7},{5,6},{6,5},{7,4},{8,11},{9,10},{10,... | collective-permute-start | bytes 196616 | tf_op jit(solution)/shard_map/ppermute | solution.py:281
  52.9 0.2 shard_map.62
  53.1 1.9 %collective-permute-done.19.refs_0_ = bf16[1,128,256]{2,1,0:T(8,128)(2,1)S(1)} collective-permute-done((bf16[1,128,256]{2,1,0:T(8,128)(2,1)S(1)}, bf16[1,128,256]{2,1,0:T(8,128)(2,1)S(1)}, u32[]{:S(2)}, u32[]{:S(2)}) %collective-permute-start.19) | collective-permute-done | bytes 65568 | tf_op jit(solution)/shard_map/ppermute | solution.py:281
  55.0 0.0 collective-permute-start.20
  55.0 0.0 collective-permute-done.22.refs_1_
  55.0 0.7 %shard_map.63.refs_2_ = bf16[3,1,1,128,512]{4,3,2,1,0:T(8,128)(2,1)} custom-call(bf16[128,512]{1,0:T(8,128)(2,1)S(1)} %get-tuple-element.49.full_ref, bf16[2,128,256]{2,1,0:T(8,128)(2,1)S(1)} %shard_map.59.refs_5_.refs_0_, bf16[128,256]{1,0:T(8,128)(2,1)S(1)} %collective-permute-done.22.refs_1_), custom_call_target="tpu_custom_call" | custom-call | tf_op jit(solution)/shard_map/pallas_call | solution.py:377
  55.7 0.4 collective-permute-done.21.refs_1_
  56.1 0.1 collective-permute-done.20.mate_ref
  56.2 0.9 %shard_map.64 = bf16[3,1,1,128,512]{4,3,2,1,0:T(8,128)(2,1)} custom-call(bf16[3,1,1,128,128]{4,3,2,1,0:T(8,128)(2,1)S(1)} %copy-done.1, f32[2,128,256]{2,1,0:T(8,128)S(1)} %get-tuple-element.46.right_ref, bf16[128,256]{1,0:T(8,128)(2,1)S(1)} %collective-permute-done.20.mate_ref, ...), custom_call_target="tpu_custom_call", output_to_operand_aliasing={{}: (5, {})} | custom-call | tf_op jit(solution)/shard_map/pallas_call | solution.py:385
  (2 shorter events, 0.0 us)
Async XLA Ops:
  1.2 1.4 %collective-permute-start.1 = (bf16[128,256]{1,0:T(8,128)(2,1)S(1)}, bf16[128,256]{1,0:T(8,128)(2,1)S(1)}, u32[]{:S(2)}, u32[]{:S(2)}) collective-permute-start(bf16[128,256]{1,0:T(8,128)(2,1)S(1)} %get-tuple-element.30), channel_id=1, source_target_pairs={{0,1},{1,0},{2,3},{3,2},{4,5},{5,4},{6,7},{7,6},{8,9},{9,8},{10,11... | collective-permute-start | bytes 196616 | tf_op jit(solution)/shard_map/ppermute | solution.py:281
  1.7 1.2 %collective-permute-start = (s32[8,128]{1,0:T(8,128)S(1)}, s32[8,128]{1,0:T(8,128)S(1)}, u32[]{:S(2)}, u32[]{:S(2)}) collective-permute-start(s32[8,128]{1,0:T(8,128)S(1)} %get-tuple-element.28.refs_0_), channel_id=1, source_target_pairs={{0,1},{1,0},{2,3},{3,2},{4,5},{5,4},{6,7},{7,6},{8,9},{9,8},{10,11... | collective-permute-start | bytes 12296 | tf_op jit(solution)/shard_map/ppermute | solution.py:281
  2.9 18.5 %collective-permute-start.2 = (bf16[2,1,1,4,5,128,128]{6,5,4,3,2,1,0:T(8,128)(2,1)}, bf16[2,1,1,4,5,128,128]{6,5,4,3,2,1,0:T(8,128)(2,1)S(1)}, u32[]{:S(2)}, u32[]{:S(2)}) collective-permute-start(bf16[2,1,1,4,5,128,128]{6,5,4,3,2,1,0:T(8,128)(2,1)} %refs_2_.3), channel_id=1, source_target_pairs={{0,1},{1,0},{2,3},{3,2},{4,5},{5,4},{6,7},{7,6},{8,9},{9,8},{10,11... | collective-permute-start | bytes 3932168 | tf_op jit(solution)/shard_map/ppermute | solution.py:281
  3.1 6.7 %collective-permute-start.6 = (bf16[2,128,256]{2,1,0:T(8,128)(2,1)S(1)}, bf16[2,128,256]{2,1,0:T(8,128)(2,1)S(1)}, u32[]{:S(2)}, u32[]{:S(2)}) collective-permute-start(bf16[2,128,256]{2,1,0:T(8,128)(2,1)S(1)} %pad_maximum_fusion.refs_4_.refs_2_), channel_id=1, source_target_pairs={{0,4},{4,12},{12,20},{20,28},{28,24},{24,16},{16,8},{8,0},{1,5},{5... | collective-permute-start | bytes 393224 | tf_op jit(solution)/shard_map/ppermute | solution.py:265
  5.9 5.6 %collective-permute-start.4 = (bf16[2,128,256]{2,1,0:T(8,128)(2,1)S(1)}, bf16[2,128,256]{2,1,0:T(8,128)(2,1)S(1)}, u32[]{:S(2)}, u32[]{:S(2)}) collective-permute-start(bf16[2,128,256]{2,1,0:T(8,128)(2,1)S(1)} %pad_maximum_fusion.refs_4_.refs_2_), channel_id=1, source_target_pairs={{4,0},{12,4},{20,12},{28,20},{24,28},{16,24},{8,16},{0,8},{5,1},{1... | collective-permute-start | bytes 393224 | tf_op jit(solution)/shard_map/ppermute | solution.py:268
  9.8 5.1 %collective-permute-start.7 = (bf16[2,128,256]{2,1,0:T(8,128)(2,1)S(1)}, bf16[2,128,256]{2,1,0:T(8,128)(2,1)S(1)}, u32[]{:S(2)}, u32[]{:S(2)}) collective-permute-start(bf16[2,128,256]{2,1,0:T(8,128)(2,1)S(1)} %collective-permute-done.6.refs_9_.refs_7_), channel_id=1, source_target_pairs={{0,4},{4,12},{12,20},{20,28},{28,24},{24,16},{16,8},{8,0},{1,5},{5... | collective-permute-start | bytes 393224 | tf_op jit(solution)/shard_map/ppermute | solution.py:265
  11.5 5.0 %collective-permute-start.3 = (bf16[256,256]{1,0:T(8,128)(2,1)S(1)}, bf16[256,256]{1,0:T(8,128)(2,1)S(1)}, u32[]{:S(2)}, u32[]{:S(2)}) collective-permute-start(bf16[256,256]{1,0:T(8,128)(2,1)S(1)} %get-tuple-element.33), channel_id=1, source_target_pairs={{0,1},{1,0},{2,3},{3,2},{4,5},{5,4},{6,7},{7,6},{8,9},{9,8},{10,11... | collective-permute-start | bytes 393224 | tf_op jit(solution)/shard_map/ppermute | solution.py:281
  11.5 5.9 %collective-permute-start.5 = (bf16[2,128,256]{2,1,0:T(8,128)(2,1)S(1)}, bf16[2,128,256]{2,1,0:T(8,128)(2,1)S(1)}, u32[]{:S(2)}, u32[]{:S(2)}) collective-permute-start(bf16[2,128,256]{2,1,0:T(8,128)(2,1)S(1)} %collective-permute-done.4.refs_5_.refs_3_), channel_id=1, source_target_pairs={{4,0},{12,4},{20,12},{28,20},{24,28},{16,24},{8,16},{0,8},{5,1},{1... | collective-permute-start | bytes 393224 | tf_op jit(solution)/shard_map/ppermute | solution.py:268
  14.9 5.0 %collective-permute-start.8 = (bf16[2,128,256]{2,1,0:T(8,128)(2,1)S(1)}, bf16[2,128,256]{2,1,0:T(8,128)(2,1)S(1)}, u32[]{:S(2)}, u32[]{:S(2)}) collective-permute-start(bf16[2,128,256]{2,1,0:T(8,128)(2,1)S(1)} %collective-permute-done.7.refs_8_.refs_6_), channel_id=1, source_target_pairs={{0,4},{4,12},{12,20},{20,28},{28,24},{24,16},{16,8},{8,0},{1,5},{5... | collective-permute-start | bytes 393224 | tf_op jit(solution)/shard_map/ppermute | solution.py:265
  17.4 6.8 %collective-permute-start.9 = (bf16[2,128,256]{2,1,0:T(8,128)(2,1)S(1)}, bf16[2,128,256]{2,1,0:T(8,128)(2,1)S(1)}, u32[]{:S(2)}, u32[]{:S(2)}) collective-permute-start(bf16[2,128,256]{2,1,0:T(8,128)(2,1)S(1)} %collective-permute-done.5.refs_6_.refs_4_), channel_id=1, source_target_pairs={{4,0},{12,4},{20,12},{28,20},{24,28},{16,24},{8,16},{0,8},{5,1},{1... | collective-permute-start | bytes 393224 | tf_op jit(solution)/shard_map/ppermute | solution.py:268
  19.9 5.0 %collective-permute-start.10 = (bf16[2,128,256]{2,1,0:T(8,128)(2,1)S(1)}, bf16[2,128,256]{2,1,0:T(8,128)(2,1)S(1)}, u32[]{:S(2)}, u32[]{:S(2)}) collective-permute-start(bf16[2,128,256]{2,1,0:T(8,128)(2,1)S(1)} %collective-permute-done.8.refs_7_.refs_5_), channel_id=1, source_target_pairs={{0,4},{4,12},{12,20},{20,28},{28,24},{24,16},{16,8},{8,0},{1,5},{5... | collective-permute-start | bytes 393224 | tf_op jit(solution)/shard_map/ppermute | solution.py:265
  24.2 2.6 %copy-start = (bf16[3,1,1,128,512]{4,3,2,1,0:T(8,128)(2,1)S(1)}, bf16[3,1,1,128,512]{4,3,2,1,0:T(8,128)(2,1)}, u32[]{:S(2)}) copy-start(bf16[3,1,1,128,512]{4,3,2,1,0:T(8,128)(2,1)} %b_ref.5) | copy-start | bytes 1179652
  24.2 2.5 %copy-start.1 = (bf16[3,1,1,128,128]{4,3,2,1,0:T(8,128)(2,1)S(1)}, bf16[3,1,1,128,128]{4,3,2,1,0:T(8,128)(2,1)}, u32[]{:S(2)}) copy-start(bf16[3,1,1,128,128]{4,3,2,1,0:T(8,128)(2,1)} %d_ref.5) | copy-start | bytes 294916
  25.1 5.0 %collective-permute-start.11 = (bf16[2,128,256]{2,1,0:T(8,128)(2,1)S(1)}, bf16[2,128,256]{2,1,0:T(8,128)(2,1)S(1)}, u32[]{:S(2)}, u32[]{:S(2)}) collective-permute-start(bf16[2,128,256]{2,1,0:T(8,128)(2,1)S(1)} %shard_map.57), channel_id=1, source_target_pairs={{0,2},{1,3},{2,0},{3,1},{4,6},{5,7},{6,4},{7,5},{8,10},{9,11},{10,... | collective-permute-start | bytes 393224 | tf_op jit(solution)/shard_map/ppermute | solution.py:281
  30.3 5.2 %collective-permute-start.14 = (bf16[2,128,256]{2,1,0:T(8,128)(2,1)S(1)}, bf16[2,128,256]{2,1,0:T(8,128)(2,1)S(1)}, u32[]{:S(2)}, u32[]{:S(2)}) collective-permute-start(bf16[2,128,256]{2,1,0:T(8,128)(2,1)S(1)} %shard_map.59.refs_5_.refs_0_), channel_id=1, source_target_pairs={{0,4},{4,12},{12,20},{20,28},{28,24},{24,16},{16,8},{8,0},{1,5},{5... | collective-permute-start | bytes 393224 | tf_op jit(solution)/shard_map/ppermute | solution.py:265
  31.9 5.0 %collective-permute-start.12 = (bf16[2,128,256]{2,1,0:T(8,128)(2,1)S(1)}, bf16[2,128,256]{2,1,0:T(8,128)(2,1)S(1)}, u32[]{:S(2)}, u32[]{:S(2)}) collective-permute-start(bf16[2,128,256]{2,1,0:T(8,128)(2,1)S(1)} %shard_map.59.refs_5_.refs_0_), channel_id=1, source_target_pairs={{4,0},{12,4},{20,12},{28,20},{24,28},{16,24},{8,16},{0,8},{5,1},{1... | collective-permute-start | bytes 393224 | tf_op jit(solution)/shard_map/ppermute | solution.py:268
  35.5 5.0 %collective-permute-start.15 = (bf16[2,128,256]{2,1,0:T(8,128)(2,1)S(1)}, bf16[2,128,256]{2,1,0:T(8,128)(2,1)S(1)}, u32[]{:S(2)}, u32[]{:S(2)}) collective-permute-start(bf16[2,128,256]{2,1,0:T(8,128)(2,1)S(1)} %collective-permute-done.14.refs_10_), channel_id=1, source_target_pairs={{0,4},{4,12},{12,20},{20,28},{28,24},{24,16},{16,8},{8,0},{1,5},{5... | collective-permute-start | bytes 393224 | tf_op jit(solution)/shard_map/ppermute | solution.py:265
  36.9 5.1 %collective-permute-start.13 = (bf16[2,128,256]{2,1,0:T(8,128)(2,1)S(1)}, bf16[2,128,256]{2,1,0:T(8,128)(2,1)S(1)}, u32[]{:S(2)}, u32[]{:S(2)}) collective-permute-start(bf16[2,128,256]{2,1,0:T(8,128)(2,1)S(1)} %collective-permute-done.12.refs_6_), channel_id=1, source_target_pairs={{4,0},{12,4},{20,12},{28,20},{24,28},{16,24},{8,16},{0,8},{5,1},{1... | collective-permute-start | bytes 393224 | tf_op jit(solution)/shard_map/ppermute | solution.py:268
  40.5 5.0 %collective-permute-start.16 = (bf16[2,128,256]{2,1,0:T(8,128)(2,1)S(1)}, bf16[2,128,256]{2,1,0:T(8,128)(2,1)S(1)}, u32[]{:S(2)}, u32[]{:S(2)}) collective-permute-start(bf16[2,128,256]{2,1,0:T(8,128)(2,1)S(1)} %collective-permute-done.15.refs_9_), channel_id=1, source_target_pairs={{0,4},{4,12},{12,20},{20,28},{28,24},{24,16},{16,8},{8,0},{1,5},{5... | collective-permute-start | bytes 393224 | tf_op jit(solution)/shard_map/ppermute | solution.py:265
  41.9 7.8 %collective-permute-start.17 = (bf16[2,128,256]{2,1,0:T(8,128)(2,1)S(1)}, bf16[2,128,256]{2,1,0:T(8,128)(2,1)S(1)}, u32[]{:S(2)}, u32[]{:S(2)}) collective-permute-start(bf16[2,128,256]{2,1,0:T(8,128)(2,1)S(1)} %collective-permute-done.13.refs_7_), channel_id=1, source_target_pairs={{4,0},{12,4},{20,12},{28,20},{24,28},{16,24},{8,16},{0,8},{5,1},{1... | collective-permute-start | bytes 393224 | tf_op jit(solution)/shard_map/ppermute | solution.py:268
  45.4 5.0 %collective-permute-start.18 = (bf16[2,128,256]{2,1,0:T(8,128)(2,1)S(1)}, bf16[2,128,256]{2,1,0:T(8,128)(2,1)S(1)}, u32[]{:S(2)}, u32[]{:S(2)}) collective-permute-start(bf16[2,128,256]{2,1,0:T(8,128)(2,1)S(1)} %collective-permute-done.16.refs_8_), channel_id=1, source_target_pairs={{0,4},{4,12},{12,20},{20,28},{28,24},{24,16},{16,8},{8,0},{1,5},{5... | collective-permute-start | bytes 393224 | tf_op jit(solution)/shard_map/ppermute | solution.py:265
  50.6 4.3 %collective-permute-start.19 = (bf16[1,128,256]{2,1,0:T(8,128)(2,1)S(1)}, bf16[1,128,256]{2,1,0:T(8,128)(2,1)S(1)}, u32[]{:S(2)}, u32[]{:S(2)}) collective-permute-start(bf16[1,128,256]{2,1,0:T(8,128)(2,1)S(1)} %get-tuple-element.43), channel_id=1, source_target_pairs={{0,2},{1,3},{2,0},{3,1},{4,6},{5,7},{6,4},{7,5},{8,10},{9,11},{10,... | collective-permute-start | bytes 196616 | tf_op jit(solution)/shard_map/ppermute | solution.py:281
  52.2 2.8 %collective-permute-start.22 = (bf16[128,256]{1,0:T(8,128)(2,1)S(1)}, bf16[128,256]{1,0:T(8,128)(2,1)S(1)}, u32[]{:S(2)}, u32[]{:S(2)}) collective-permute-start(bf16[128,256]{1,0:T(8,128)(2,1)S(1)} %slice_bitcast_fusion), channel_id=1, source_target_pairs={{0,1},{1,0},{2,3},{3,2},{4,5},{5,4},{6,7},{7,6},{8,9},{9,8},{10,11... | collective-permute-start | bytes 196616 | tf_op jit(solution)/shard_map/ppermute | solution.py:281
  52.2 3.9 %collective-permute-start.21 = (bf16[1,128,256]{2,1,0:T(8,128)(2,1)S(1)}, bf16[1,128,256]{2,1,0:T(8,128)(2,1)S(1)}, u32[]{:S(2)}, u32[]{:S(2)}) collective-permute-start(bf16[1,128,256]{2,1,0:T(8,128)(2,1)S(1)} %get-tuple-element.44), channel_id=1, source_target_pairs={{0,3},{1,2},{2,1},{3,0},{4,7},{5,6},{6,5},{7,4},{8,11},{9,10},{10,... | collective-permute-start | bytes 196616 | tf_op jit(solution)/shard_map/ppermute | solution.py:281
  55.0 1.3 %collective-permute-start.20 = (bf16[128,256]{1,0:T(8,128)(2,1)S(1)}, bf16[128,256]{1,0:T(8,128)(2,1)S(1)}, u32[]{:S(2)}, u32[]{:S(2)}) collective-permute-start(bf16[128,256]{1,0:T(8,128)(2,1)S(1)} %get-tuple-element.48), channel_id=1, source_target_pairs={{0,1},{1,0},{2,3},{3,2},{4,5},{5,4},{6,7},{7,6},{8,9},{9,8},{10,11... | collective-permute-start | bytes 196616 | tf_op jit(solution)/shard_map/ppermute | solution.py:281

commit v9 on v8

--- a/solution.py
+++ b/solution.py
@@ -76,25 +76,29 @@
     b_buf, d_buf, count_ref, col_ref, sems = refs
     middle = b_buf.shape[0]
     copies = [
-        pltpu.make_async_copy(b_ref.at[0, 0, 0], b_buf.at[0], sems.at[0]),
-        pltpu.make_async_copy(d_ref.at[0, 0, 0], d_buf.at[0], sems.at[1]),
-        pltpu.make_async_copy(cols_ref, col_ref, sems.at[2]),
-        pltpu.make_async_copy(counts_ref, count_ref, sems.at[3]),
-        pltpu.make_async_copy(d_ref.at[pl.ds(1, middle - 1), 0, 0], d_buf.at[pl.ds(1, middle - 1)], sems.at[4]),
-        pltpu.make_async_copy(b_ref.at[pl.ds(1, middle - 1), 0, 0], b_buf.at[pl.ds(1, middle - 1)], sems.at[5]),
+        pltpu.make_async_copy(d_ref.at[0, 0, 0], d_buf.at[0], sems.at[4]),
+        pltpu.make_async_copy(cols_ref, col_ref, sems.at[5]),
+        pltpu.make_async_copy(counts_ref, count_ref, sems.at[6]),
+        pltpu.make_async_copy(d_ref.at[pl.ds(1, middle - 1), 0, 0], d_buf.at[pl.ds(1, middle - 1)], sems.at[7]),
+        pltpu.make_async_copy(b_ref.at[pl.ds(1, middle - 1), 0, 0], b_buf.at[pl.ds(1, middle - 1)], sems.at[8]),
     ]
-    for copy in copies:
+    quarter = b_buf.shape[1] // 4
+    first = [
+        pltpu.make_async_copy(b_ref.at[0, 0, 0, pl.ds(i * quarter, quarter)], b_buf.at[0, pl.ds(i * quarter, quarter)], sems.at[i])
+        for i in range(4)
+    ]
+    for copy in first + copies:
         copy.start()
     me, my_row, my_place = lax.axis_index("pcol"), lax.axis_index("prow"), place[0]
     for p in range(1, m):
         my_place = jnp.where(my_row == p, place[p], my_place)
     size, width = own_ref.shape
-    for copy in copies[:2]:
+    for copy in first + copies[:1]:
         copy.wait()
     full_ref[...] = jnp.dot(d_buf[0], b_buf[0], preferred_element_type=jnp.float32).astype(jnp.bfloat16)
     own_ref[...] = full_ref[:, my_columns(me, width)]
     other_ref[...] = full_ref[:, my_columns(me ^ 1, width)]
-    for copy in copies[2:]:
+    for copy in copies[1:]:
         copy.wait()
     for level in range(1, middle):
         at = (2 * level - 2) * size
@@ -300,7 +304,7 @@
             pltpu.VMEM((middle, size, size), jnp.bfloat16),
             pltpu.SMEM(live_counts.shape, jnp.int32),
             pltpu.VMEM(block_cols.shape, jnp.int32),
-            pltpu.SemaphoreType.DMA((6,)),
+            pltpu.SemaphoreType.DMA((9,)),
         ],
         compiler_params=params(),
     )(*[in_hbm(v) for v in (live_counts, block_cols, b_panels, diag_inverse)])
@@ -423,7 +427,7 @@
         front = b_panels.shape[-1]
         rows = mesh.shape["prow"]
         paired = n & (n - 1) == 0 and n >= PAIR and rows % 2 == 0 and rows > 2 and front % (PAIR * LANES) == 0
-        paired = paired and n > PAIR and b_panels.shape[0] > 2 and front >= PAIR * b_panels.shape[-2]
+        paired = paired and b_panels.shape[-2] % 64 == 0 and n > PAIR and b_panels.shape[0] > 2 and front >= PAIR * b_panels.shape[-2]
         if paired and l_blocks.size * l_blocks.dtype.itemsize <= BLOCK_BYTES:
             return solve_paired(cycle, b_panels, diag_inverse, l_blocks, block_cols, live_counts)
         return solve_scattered(b_panels, diag_inverse, l_blocks, block_cols, live_counts)

time: 57.3 us -> 57.2 us (level)
  no operation moved by 1% of the time
where the time goes in v9:
time: 57.2 us; the launch traced here: 57 us
  waiting for transfers between devices  26.9 us (47%)
  starting transfers between devices  20.6 us (36%)
  Pallas kernels  9.35 us (16%)
    ppermute x8, waiting for transfers between devices, advance(): self.behind = lax.ppermute(self.behind, 'prow', self.to_next)  19.3 us
    ppermute x8, starting transfers between devices, advance(): self.behind = lax.ppermute(self.behind, 'prow', self.to_next)  13.5 us
    ppermute x9, waiting for transfers between devices, send(): return lax.ppermute(value, 'pcol', [(i, i ^ bits) for i in range(n)])  6.61 us
    pallas_call x2, Pallas kernels, solve_paired(): pl.pallas_call(functools.partial(gather_kernel, n, level, m, early, late)...  5.51 us
    ppermute x9, starting transfers between devices, send(): return lax.ppermute(value, 'pcol', [(i, i ^ bits) for i in range(n)])  4.63 us
    ppermute x6, starting transfers between devices, advance(): self.ahead = lax.ppermute(self.ahead, 'prow', self.to_last)  2.52 us
    pallas_call x1, Pallas kernels, solve_paired(): pl.pallas_call(functools.partial(first_kernel, n, m, place), out_shape=[n...  1.15 us
  transfers between devices with their start and end apart: 23, of which 15 were waited for; matrix products, arithmetic and copies ran while one was open for 0% of the time, Pallas kernels for 12%

profile of v9, /device:TPU:0, one launch (start us, length us, event | category | flops | bytes accessed | tf_op | source)
XLA Modules:
  0.0 57.0 jit_solution(2667748319010924523)
XLA Ops:
  0.0 1.1 %shard_map.55 = (bf16[128,512]{1,0:T(8,128)(2,1)S(1)}, s32[8,128]{1,0:T(8,128)S(1)}, bf16[128,256]{1,0:T(8,128)(2,1)S(1)}, bf16[128,256]{1,0:T(8,128)(2,1)S(1)}, bf16[256,256]{1,0:T(8,128)(2,1)S(1)}) custom-call(s32[2,1,1,4]{3,2,1,0:T(1,128)} %counts_ref.1, s32[2,1,1,4,5]{4,3,2,1,0:T(4,128)} %cols_ref.1, bf16[3,1,1,128,512]{4,3,2,1,0:T(8,128)(2,1)} %b_ref.5, ...), custom_call_target="tpu_custom_call" | custom-call | tf_op jit(solution)/shard_map/pallas_call | solution.py:291
  1.2 0.5 collective-permute-start.1
  1.7 0.1 collective-permute-start
  1.8 0.8 %collective-permute-done.1 = bf16[128,256]{1,0:T(8,128)(2,1)S(1)} collective-permute-done((bf16[128,256]{1,0:T(8,128)(2,1)S(1)}, bf16[128,256]{1,0:T(8,128)(2,1)S(1)}, u32[]{:S(2)}, u32[]{:S(2)}) %collective-permute-start.1) | collective-permute-done | bytes 65568 | tf_op jit(solution)/shard_map/ppermute | solution.py:285
  2.6 0.2 collective-permute-done.refs_1_
  2.8 0.2 collective-permute-start.2
  3.0 2.8 %collective-permute-start.6 = (bf16[2,128,256]{2,1,0:T(8,128)(2,1)S(1)}, bf16[2,128,256]{2,1,0:T(8,128)(2,1)S(1)}, u32[]{:S(2)}, u32[]{:S(2)}) collective-permute-start(bf16[2,128,256]{2,1,0:T(8,128)(2,1)S(1)} %pad_maximum_fusion.refs_4_.refs_2_), channel_id=1, source_target_pairs={{0,4},{4,12},{12,20},{20,28},{28,24},{24,16},{16,8},{8,0},{1,5},{5... | collective-permute-start | bytes 393224 | tf_op jit(solution)/shard_map/ppermute | solution.py:269
  5.8 0.1 collective-permute-start.4
  5.9 3.8 %collective-permute-done.6.refs_9_.refs_7_ = bf16[2,128,256]{2,1,0:T(8,128)(2,1)S(1)} collective-permute-done((bf16[2,128,256]{2,1,0:T(8,128)(2,1)S(1)}, bf16[2,128,256]{2,1,0:T(8,128)(2,1)S(1)}, u32[]{:S(2)}, u32[]{:S(2)}) %collective-permute-start.6) | collective-permute-done | bytes 131104 | tf_op jit(solution)/shard_map/ppermute | solution.py:269
  9.8 1.7 %collective-permute-start.7 = (bf16[2,128,256]{2,1,0:T(8,128)(2,1)S(1)}, bf16[2,128,256]{2,1,0:T(8,128)(2,1)S(1)}, u32[]{:S(2)}, u32[]{:S(2)}) collective-permute-start(bf16[2,128,256]{2,1,0:T(8,128)(2,1)S(1)} %collective-permute-done.6.refs_9_.refs_7_), channel_id=1, source_target_pairs={{0,4},{4,12},{12,20},{20,28},{28,24},{24,16},{16,8},{8,0},{1,5},{5... | collective-permute-start | bytes 393224 | tf_op jit(solution)/shard_map/ppermute | solution.py:269
  11.4 0.0 collective-permute-start.3
  11.4 0.0 collective-permute-done.4.refs_5_.refs_3_
  11.4 0.4 collective-permute-start.5
  11.8 3.0 %collective-permute-done.7.refs_8_.refs_6_ = bf16[2,128,256]{2,1,0:T(8,128)(2,1)S(1)} collective-permute-done((bf16[2,128,256]{2,1,0:T(8,128)(2,1)S(1)}, bf16[2,128,256]{2,1,0:T(8,128)(2,1)S(1)}, u32[]{:S(2)}, u32[]{:S(2)}) %collective-permute-start.7) | collective-permute-done | bytes 131104 | tf_op jit(solution)/shard_map/ppermute | solution.py:269
  14.8 1.5 %collective-permute-start.8 = (bf16[2,128,256]{2,1,0:T(8,128)(2,1)S(1)}, bf16[2,128,256]{2,1,0:T(8,128)(2,1)S(1)}, u32[]{:S(2)}, u32[]{:S(2)}) collective-permute-start(bf16[2,128,256]{2,1,0:T(8,128)(2,1)S(1)} %collective-permute-done.7.refs_8_.refs_6_), channel_id=1, source_target_pairs={{0,4},{4,12},{12,20},{20,28},{28,24},{24,16},{16,8},{8,0},{1,5},{5... | collective-permute-start | bytes 393224 | tf_op jit(solution)/shard_map/ppermute | solution.py:269
  16.4 0.0 collective-permute-done.3.away_ref
  16.4 0.9 %collective-permute-done.5.refs_6_.refs_4_ = bf16[2,128,256]{2,1,0:T(8,128)(2,1)S(1)} collective-permute-done((bf16[2,128,256]{2,1,0:T(8,128)(2,1)S(1)}, bf16[2,128,256]{2,1,0:T(8,128)(2,1)S(1)}, u32[]{:S(2)}, u32[]{:S(2)}) %collective-permute-start.5) | collective-permute-done | bytes 131104 | tf_op jit(solution)/shard_map/ppermute | solution.py:272
  17.3 0.4 collective-permute-start.9
  17.7 2.1 %collective-permute-done.8.refs_7_.refs_5_ = bf16[2,128,256]{2,1,0:T(8,128)(2,1)S(1)} collective-permute-done((bf16[2,128,256]{2,1,0:T(8,128)(2,1)S(1)}, bf16[2,128,256]{2,1,0:T(8,128)(2,1)S(1)}, u32[]{:S(2)}, u32[]{:S(2)}) %collective-permute-start.8) | collective-permute-done | bytes 131104 | tf_op jit(solution)/shard_map/ppermute | solution.py:269
  19.8 1.5 %collective-permute-start.10 = (bf16[2,128,256]{2,1,0:T(8,128)(2,1)S(1)}, bf16[2,128,256]{2,1,0:T(8,128)(2,1)S(1)}, u32[]{:S(2)}, u32[]{:S(2)}) collective-permute-start(bf16[2,128,256]{2,1,0:T(8,128)(2,1)S(1)} %collective-permute-done.8.refs_7_.refs_5_), channel_id=1, source_target_pairs={{0,4},{4,12},{12,20},{20,28},{28,24},{24,16},{16,8},{8,0},{1,5},{5... | collective-permute-start | bytes 393224 | tf_op jit(solution)/shard_map/ppermute | solution.py:269
  21.4 0.0 collective-permute-done.2.refs_3_
  21.4 2.7 %shard_map.56 = (f32[4,128,256]{2,1,0:T(8,128)S(1)}, bf16[4,128,512]{2,1,0:T(8,128)(2,1)S(1)}) custom-call(s32[8,128]{1,0:T(8,128)S(1)} %get-tuple-element.28.refs_0_, s32[8,128]{1,0:T(8,128)S(1)} %collective-permute-done.refs_1_, bf16[2,1,1,4,5,128,128]{6,5,4,3,2,1,0:T(8,128)(2,1)} %refs_2_.3, ...), custom_call_target="tpu_custom_call" | custom-call | tf_op jit(solution)/shard_map/pallas_call | solution.py:325
  24.1 0.0 copy-start
  24.1 0.0 copy-start.1
  24.1 0.0 collective-permute-done.9.refs_0_
  24.1 0.7 %collective-permute-done.10.refs_1_ = bf16[2,128,256]{2,1,0:T(8,128)(2,1)S(1)} collective-permute-done((bf16[2,128,256]{2,1,0:T(8,128)(2,1)S(1)}, bf16[2,128,256]{2,1,0:T(8,128)(2,1)S(1)}, u32[]{:S(2)}, u32[]{:S(2)}) %collective-permute-start.10) | collective-permute-done | bytes 131104 | tf_op jit(solution)/shard_map/ppermute | solution.py:269
  24.8 0.2 shard_map.57
  25.0 1.6 %collective-permute-start.11 = (bf16[2,128,256]{2,1,0:T(8,128)(2,1)S(1)}, bf16[2,128,256]{2,1,0:T(8,128)(2,1)S(1)}, u32[]{:S(2)}, u32[]{:S(2)}) collective-permute-start(bf16[2,128,256]{2,1,0:T(8,128)(2,1)S(1)} %shard_map.57), channel_id=1, source_target_pairs={{0,2},{1,3},{2,0},{3,1},{4,6},{5,7},{6,4},{7,5},{8,10},{9,11},{10,... | collective-permute-start | bytes 393224 | tf_op jit(solution)/shard_map/ppermute | solution.py:285
  26.7 0.0 copy-done
  26.7 0.0 copy-done.1
  26.7 0.2 shard_map.58
  26.9 3.1 %collective-permute-done.11.refs_0_ = bf16[2,128,256]{2,1,0:T(8,128)(2,1)S(1)} collective-permute-done((bf16[2,128,256]{2,1,0:T(8,128)(2,1)S(1)}, bf16[2,128,256]{2,1,0:T(8,128)(2,1)S(1)}, u32[]{:S(2)}, u32[]{:S(2)}) %collective-permute-start.11) | collective-permute-done | bytes 131104 | tf_op jit(solution)/shard_map/ppermute | solution.py:285
  30.0 0.2 shard_map.59.refs_5_.refs_0_
  30.2 1.6 %collective-permute-start.14 = (bf16[2,128,256]{2,1,0:T(8,128)(2,1)S(1)}, bf16[2,128,256]{2,1,0:T(8,128)(2,1)S(1)}, u32[]{:S(2)}, u32[]{:S(2)}) collective-permute-start(bf16[2,128,256]{2,1,0:T(8,128)(2,1)S(1)} %shard_map.59.refs_5_.refs_0_), channel_id=1, source_target_pairs={{0,4},{4,12},{12,20},{20,28},{28,24},{24,16},{16,8},{8,0},{1,5},{5... | collective-permute-start | bytes 393224 | tf_op jit(solution)/shard_map/ppermute | solution.py:269
  31.8 0.5 collective-permute-start.12
  32.3 3.1 %collective-permute-done.14.refs_10_ = bf16[2,128,256]{2,1,0:T(8,128)(2,1)S(1)} collective-permute-done((bf16[2,128,256]{2,1,0:T(8,128)(2,1)S(1)}, bf16[2,128,256]{2,1,0:T(8,128)(2,1)S(1)}, u32[]{:S(2)}, u32[]{:S(2)}) %collective-permute-start.14) | collective-permute-done | bytes 131104 | tf_op jit(solution)/shard_map/ppermute | solution.py:269
  35.4 1.4 %collective-permute-start.15 = (bf16[2,128,256]{2,1,0:T(8,128)(2,1)S(1)}, bf16[2,128,256]{2,1,0:T(8,128)(2,1)S(1)}, u32[]{:S(2)}, u32[]{:S(2)}) collective-permute-start(bf16[2,128,256]{2,1,0:T(8,128)(2,1)S(1)} %collective-permute-done.14.refs_10_), channel_id=1, source_target_pairs={{0,4},{4,12},{12,20},{20,28},{28,24},{24,16},{16,8},{8,0},{1,5},{5... | collective-permute-start | bytes 393224 | tf_op jit(solution)/shard_map/ppermute | solution.py:269
  36.8 0.0 collective-permute-done.12.refs_6_
  36.8 0.7 %collective-permute-start.13 = (bf16[2,128,256]{2,1,0:T(8,128)(2,1)S(1)}, bf16[2,128,256]{2,1,0:T(8,128)(2,1)S(1)}, u32[]{:S(2)}, u32[]{:S(2)}) collective-permute-start(bf16[2,128,256]{2,1,0:T(8,128)(2,1)S(1)} %collective-permute-done.12.refs_6_), channel_id=1, source_target_pairs={{4,0},{12,4},{20,12},{28,20},{24,28},{16,24},{8,16},{0,8},{5,1},{1... | collective-permute-start | bytes 393224 | tf_op jit(solution)/shard_map/ppermute | solution.py:272
  37.5 2.9 %collective-permute-done.15.refs_9_ = bf16[2,128,256]{2,1,0:T(8,128)(2,1)S(1)} collective-permute-done((bf16[2,128,256]{2,1,0:T(8,128)(2,1)S(1)}, bf16[2,128,256]{2,1,0:T(8,128)(2,1)S(1)}, u32[]{:S(2)}, u32[]{:S(2)}) %collective-permute-start.15) | collective-permute-done | bytes 131104 | tf_op jit(solution)/shard_map/ppermute | solution.py:269
  40.4 1.5 %collective-permute-start.16 = (bf16[2,128,256]{2,1,0:T(8,128)(2,1)S(1)}, bf16[2,128,256]{2,1,0:T(8,128)(2,1)S(1)}, u32[]{:S(2)}, u32[]{:S(2)}) collective-permute-start(bf16[2,128,256]{2,1,0:T(8,128)(2,1)S(1)} %collective-permute-done.15.refs_9_), channel_id=1, source_target_pairs={{0,4},{4,12},{12,20},{20,28},{28,24},{24,16},{16,8},{8,0},{1,5},{5... | collective-permute-start | bytes 393224 | tf_op jit(solution)/shard_map/ppermute | solution.py:269
  41.9 0.0 collective-permute-done.13.refs_7_
  41.9 0.6 collective-permute-start.17
  42.4 2.9 %collective-permute-done.16.refs_8_ = bf16[2,128,256]{2,1,0:T(8,128)(2,1)S(1)} collective-permute-done((bf16[2,128,256]{2,1,0:T(8,128)(2,1)S(1)}, bf16[2,128,256]{2,1,0:T(8,128)(2,1)S(1)}, u32[]{:S(2)}, u32[]{:S(2)}) %collective-permute-start.16) | collective-permute-done | bytes 131104 | tf_op jit(solution)/shard_map/ppermute | solution.py:269
  45.4 1.5 %collective-permute-start.18 = (bf16[2,128,256]{2,1,0:T(8,128)(2,1)S(1)}, bf16[2,128,256]{2,1,0:T(8,128)(2,1)S(1)}, u32[]{:S(2)}, u32[]{:S(2)}) collective-permute-start(bf16[2,128,256]{2,1,0:T(8,128)(2,1)S(1)} %collective-permute-done.16.refs_8_), channel_id=1, source_target_pairs={{0,4},{4,12},{12,20},{20,28},{28,24},{24,16},{16,8},{8,0},{1,5},{5... | collective-permute-start | bytes 393224 | tf_op jit(solution)/shard_map/ppermute | solution.py:269
  46.8 2.8 %shard_map.60 = (f32[4,128,256]{2,1,0:T(8,128)S(1)}, bf16[4,128,512]{2,1,0:T(8,128)(2,1)S(1)}) custom-call(s32[8,128]{1,0:T(8,128)S(1)} %get-tuple-element.28.refs_0_, s32[8,128]{1,0:T(8,128)S(1)} %collective-permute-done.refs_1_, bf16[2,1,1,4,5,128,128]{6,5,4,3,2,1,0:T(8,128)(2,1)} %refs_2_.3, ...), custom_call_target="tpu_custom_call" | custom-call | tf_op jit(solution)/shard_map/pallas_call | solution.py:325
  49.6 0.0 collective-permute-done.17.refs_0_
  49.6 0.7 %collective-permute-done.18.refs_1_ = bf16[2,128,256]{2,1,0:T(8,128)(2,1)S(1)} collective-permute-done((bf16[2,128,256]{2,1,0:T(8,128)(2,1)S(1)}, bf16[2,128,256]{2,1,0:T(8,128)(2,1)S(1)}, u32[]{:S(2)}, u32[]{:S(2)}) %collective-permute-start.18) | collective-permute-done | bytes 131104 | tf_op jit(solution)/shard_map/ppermute | solution.py:269
  50.3 0.2 shard_map.61
  50.6 1.6 %collective-permute-start.19 = (bf16[1,128,256]{2,1,0:T(8,128)(2,1)S(1)}, bf16[1,128,256]{2,1,0:T(8,128)(2,1)S(1)}, u32[]{:S(2)}, u32[]{:S(2)}) collective-permute-start(bf16[1,128,256]{2,1,0:T(8,128)(2,1)S(1)} %get-tuple-element.43), channel_id=1, source_target_pairs={{0,2},{1,3},{2,0},{3,1},{4,6},{5,7},{6,4},{7,5},{8,10},{9,11},{10,... | collective-permute-start | bytes 196616 | tf_op jit(solution)/shard_map/ppermute | solution.py:285
  52.1 0.0 collective-permute-start.22
  52.2 0.6 %collective-permute-start.21 = (bf16[1,128,256]{2,1,0:T(8,128)(2,1)S(1)}, bf16[1,128,256]{2,1,0:T(8,128)(2,1)S(1)}, u32[]{:S(2)}, u32[]{:S(2)}) collective-permute-start(bf16[1,128,256]{2,1,0:T(8,128)(2,1)S(1)} %get-tuple-element.44), channel_id=1, source_target_pairs={{0,3},{1,2},{2,1},{3,0},{4,7},{5,6},{6,5},{7,4},{8,11},{9,10},{10,... | collective-permute-start | bytes 196616 | tf_op jit(solution)/shard_map/ppermute | solution.py:285
  52.8 0.2 shard_map.62
  53.0 1.9 %collective-permute-done.19.refs_0_ = bf16[1,128,256]{2,1,0:T(8,128)(2,1)S(1)} collective-permute-done((bf16[1,128,256]{2,1,0:T(8,128)(2,1)S(1)}, bf16[1,128,256]{2,1,0:T(8,128)(2,1)S(1)}, u32[]{:S(2)}, u32[]{:S(2)}) %collective-permute-start.19) | collective-permute-done | bytes 65568 | tf_op jit(solution)/shard_map/ppermute | solution.py:285
  54.9 0.0 collective-permute-start.20
  54.9 0.0 collective-permute-done.22.refs_1_
  54.9 0.7 %shard_map.63.refs_2_ = bf16[3,1,1,128,512]{4,3,2,1,0:T(8,128)(2,1)} custom-call(bf16[128,512]{1,0:T(8,128)(2,1)S(1)} %get-tuple-element.49.full_ref, bf16[2,128,256]{2,1,0:T(8,128)(2,1)S(1)} %shard_map.59.refs_5_.refs_0_, bf16[128,256]{1,0:T(8,128)(2,1)S(1)} %collective-permute-done.22.refs_1_), custom_call_target="tpu_custom_call" | custom-call | tf_op jit(solution)/shard_map/pallas_call | solution.py:381
  55.6 0.4 collective-permute-done.21.refs_1_
  56.0 0.1 collective-permute-done.20.mate_ref
  56.2 0.9 %shard_map.64 = bf16[3,1,1,128,512]{4,3,2,1,0:T(8,128)(2,1)} custom-call(bf16[3,1,1,128,128]{4,3,2,1,0:T(8,128)(2,1)S(1)} %copy-done.1, f32[2,128,256]{2,1,0:T(8,128)S(1)} %get-tuple-element.46.right_ref, bf16[128,256]{1,0:T(8,128)(2,1)S(1)} %collective-permute-done.20.mate_ref, ...), custom_call_target="tpu_custom_call", output_to_operand_aliasing={{}: (5, {})} | custom-call | tf_op jit(solution)/shard_map/pallas_call | solution.py:389
  (2 shorter events, 0.0 us)
Async XLA Ops:
  1.2 1.4 %collective-permute-start.1 = (bf16[128,256]{1,0:T(8,128)(2,1)S(1)}, bf16[128,256]{1,0:T(8,128)(2,1)S(1)}, u32[]{:S(2)}, u32[]{:S(2)}) collective-permute-start(bf16[128,256]{1,0:T(8,128)(2,1)S(1)} %get-tuple-element.30), channel_id=1, source_target_pairs={{0,1},{1,0},{2,3},{3,2},{4,5},{5,4},{6,7},{7,6},{8,9},{9,8},{10,11... | collective-permute-start | bytes 196616 | tf_op jit(solution)/shard_map/ppermute | solution.py:285
  1.7 1.2 %collective-permute-start = (s32[8,128]{1,0:T(8,128)S(1)}, s32[8,128]{1,0:T(8,128)S(1)}, u32[]{:S(2)}, u32[]{:S(2)}) collective-permute-start(s32[8,128]{1,0:T(8,128)S(1)} %get-tuple-element.28.refs_0_), channel_id=1, source_target_pairs={{0,1},{1,0},{2,3},{3,2},{4,5},{5,4},{6,7},{7,6},{8,9},{9,8},{10,11... | collective-permute-start | bytes 12296 | tf_op jit(solution)/shard_map/ppermute | solution.py:285
  2.8 18.5 %collective-permute-start.2 = (bf16[2,1,1,4,5,128,128]{6,5,4,3,2,1,0:T(8,128)(2,1)}, bf16[2,1,1,4,5,128,128]{6,5,4,3,2,1,0:T(8,128)(2,1)S(1)}, u32[]{:S(2)}, u32[]{:S(2)}) collective-permute-start(bf16[2,1,1,4,5,128,128]{6,5,4,3,2,1,0:T(8,128)(2,1)} %refs_2_.3), channel_id=1, source_target_pairs={{0,1},{1,0},{2,3},{3,2},{4,5},{5,4},{6,7},{7,6},{8,9},{9,8},{10,11... | collective-permute-start | bytes 3932168 | tf_op jit(solution)/shard_map/ppermute | solution.py:285
  3.0 6.7 %collective-permute-start.6 = (bf16[2,128,256]{2,1,0:T(8,128)(2,1)S(1)}, bf16[2,128,256]{2,1,0:T(8,128)(2,1)S(1)}, u32[]{:S(2)}, u32[]{:S(2)}) collective-permute-start(bf16[2,128,256]{2,1,0:T(8,128)(2,1)S(1)} %pad_maximum_fusion.refs_4_.refs_2_), channel_id=1, source_target_pairs={{0,4},{4,12},{12,20},{20,28},{28,24},{24,16},{16,8},{8,0},{1,5},{5... | collective-permute-start | bytes 393224 | tf_op jit(solution)/shard_map/ppermute | solution.py:269
  5.8 5.6 %collective-permute-start.4 = (bf16[2,128,256]{2,1,0:T(8,128)(2,1)S(1)}, bf16[2,128,256]{2,1,0:T(8,128)(2,1)S(1)}, u32[]{:S(2)}, u32[]{:S(2)}) collective-permute-start(bf16[2,128,256]{2,1,0:T(8,128)(2,1)S(1)} %pad_maximum_fusion.refs_4_.refs_2_), channel_id=1, source_target_pairs={{4,0},{12,4},{20,12},{28,20},{24,28},{16,24},{8,16},{0,8},{5,1},{1... | collective-permute-start | bytes 393224 | tf_op jit(solution)/shard_map/ppermute | solution.py:272
  9.8 5.1 %collective-permute-start.7 = (bf16[2,128,256]{2,1,0:T(8,128)(2,1)S(1)}, bf16[2,128,256]{2,1,0:T(8,128)(2,1)S(1)}, u32[]{:S(2)}, u32[]{:S(2)}) collective-permute-start(bf16[2,128,256]{2,1,0:T(8,128)(2,1)S(1)} %collective-permute-done.6.refs_9_.refs_7_), channel_id=1, source_target_pairs={{0,4},{4,12},{12,20},{20,28},{28,24},{24,16},{16,8},{8,0},{1,5},{5... | collective-permute-start | bytes 393224 | tf_op jit(solution)/shard_map/ppermute | solution.py:269
  11.4 5.0 %collective-permute-start.3 = (bf16[256,256]{1,0:T(8,128)(2,1)S(1)}, bf16[256,256]{1,0:T(8,128)(2,1)S(1)}, u32[]{:S(2)}, u32[]{:S(2)}) collective-permute-start(bf16[256,256]{1,0:T(8,128)(2,1)S(1)} %get-tuple-element.33), channel_id=1, source_target_pairs={{0,1},{1,0},{2,3},{3,2},{4,5},{5,4},{6,7},{7,6},{8,9},{9,8},{10,11... | collective-permute-start | bytes 393224 | tf_op jit(solution)/shard_map/ppermute | solution.py:285
  11.4 5.9 %collective-permute-start.5 = (bf16[2,128,256]{2,1,0:T(8,128)(2,1)S(1)}, bf16[2,128,256]{2,1,0:T(8,128)(2,1)S(1)}, u32[]{:S(2)}, u32[]{:S(2)}) collective-permute-start(bf16[2,128,256]{2,1,0:T(8,128)(2,1)S(1)} %collective-permute-done.4.refs_5_.refs_3_), channel_id=1, source_target_pairs={{4,0},{12,4},{20,12},{28,20},{24,28},{16,24},{8,16},{0,8},{5,1},{1... | collective-permute-start | bytes 393224 | tf_op jit(solution)/shard_map/ppermute | solution.py:272
  14.8 5.0 %collective-permute-start.8 = (bf16[2,128,256]{2,1,0:T(8,128)(2,1)S(1)}, bf16[2,128,256]{2,1,0:T(8,128)(2,1)S(1)}, u32[]{:S(2)}, u32[]{:S(2)}) collective-permute-start(bf16[2,128,256]{2,1,0:T(8,128)(2,1)S(1)} %collective-permute-done.7.refs_8_.refs_6_), channel_id=1, source_target_pairs={{0,4},{4,12},{12,20},{20,28},{28,24},{24,16},{16,8},{8,0},{1,5},{5... | collective-permute-start | bytes 393224 | tf_op jit(solution)/shard_map/ppermute | solution.py:269
  17.3 6.8 %collective-permute-start.9 = (bf16[2,128,256]{2,1,0:T(8,128)(2,1)S(1)}, bf16[2,128,256]{2,1,0:T(8,128)(2,1)S(1)}, u32[]{:S(2)}, u32[]{:S(2)}) collective-permute-start(bf16[2,128,256]{2,1,0:T(8,128)(2,1)S(1)} %collective-permute-done.5.refs_6_.refs_4_), channel_id=1, source_target_pairs={{4,0},{12,4},{20,12},{28,20},{24,28},{16,24},{8,16},{0,8},{5,1},{1... | collective-permute-start | bytes 393224 | tf_op jit(solution)/shard_map/ppermute | solution.py:272
  19.8 5.0 %collective-permute-start.10 = (bf16[2,128,256]{2,1,0:T(8,128)(2,1)S(1)}, bf16[2,128,256]{2,1,0:T(8,128)(2,1)S(1)}, u32[]{:S(2)}, u32[]{:S(2)}) collective-permute-start(bf16[2,128,256]{2,1,0:T(8,128)(2,1)S(1)} %collective-permute-done.8.refs_7_.refs_5_), channel_id=1, source_target_pairs={{0,4},{4,12},{12,20},{20,28},{28,24},{24,16},{16,8},{8,0},{1,5},{5... | collective-permute-start | bytes 393224 | tf_op jit(solution)/shard_map/ppermute | solution.py:269
  24.1 2.6 %copy-start = (bf16[3,1,1,128,512]{4,3,2,1,0:T(8,128)(2,1)S(1)}, bf16[3,1,1,128,512]{4,3,2,1,0:T(8,128)(2,1)}, u32[]{:S(2)}) copy-start(bf16[3,1,1,128,512]{4,3,2,1,0:T(8,128)(2,1)} %b_ref.5) | copy-start | bytes 1179652
  24.1 2.6 %copy-start.1 = (bf16[3,1,1,128,128]{4,3,2,1,0:T(8,128)(2,1)S(1)}, bf16[3,1,1,128,128]{4,3,2,1,0:T(8,128)(2,1)}, u32[]{:S(2)}) copy-start(bf16[3,1,1,128,128]{4,3,2,1,0:T(8,128)(2,1)} %d_ref.5) | copy-start | bytes 294916
  25.0 5.0 %collective-permute-start.11 = (bf16[2,128,256]{2,1,0:T(8,128)(2,1)S(1)}, bf16[2,128,256]{2,1,0:T(8,128)(2,1)S(1)}, u32[]{:S(2)}, u32[]{:S(2)}) collective-permute-start(bf16[2,128,256]{2,1,0:T(8,128)(2,1)S(1)} %shard_map.57), channel_id=1, source_target_pairs={{0,2},{1,3},{2,0},{3,1},{4,6},{5,7},{6,4},{7,5},{8,10},{9,11},{10,... | collective-permute-start | bytes 393224 | tf_op jit(solution)/shard_map/ppermute | solution.py:285
  30.2 5.2 %collective-permute-start.14 = (bf16[2,128,256]{2,1,0:T(8,128)(2,1)S(1)}, bf16[2,128,256]{2,1,0:T(8,128)(2,1)S(1)}, u32[]{:S(2)}, u32[]{:S(2)}) collective-permute-start(bf16[2,128,256]{2,1,0:T(8,128)(2,1)S(1)} %shard_map.59.refs_5_.refs_0_), channel_id=1, source_target_pairs={{0,4},{4,12},{12,20},{20,28},{28,24},{24,16},{16,8},{8,0},{1,5},{5... | collective-permute-start | bytes 393224 | tf_op jit(solution)/shard_map/ppermute | solution.py:269
  31.8 5.0 %collective-permute-start.12 = (bf16[2,128,256]{2,1,0:T(8,128)(2,1)S(1)}, bf16[2,128,256]{2,1,0:T(8,128)(2,1)S(1)}, u32[]{:S(2)}, u32[]{:S(2)}) collective-permute-start(bf16[2,128,256]{2,1,0:T(8,128)(2,1)S(1)} %shard_map.59.refs_5_.refs_0_), channel_id=1, source_target_pairs={{4,0},{12,4},{20,12},{28,20},{24,28},{16,24},{8,16},{0,8},{5,1},{1... | collective-permute-start | bytes 393224 | tf_op jit(solution)/shard_map/ppermute | solution.py:272
  35.4 5.0 %collective-permute-start.15 = (bf16[2,128,256]{2,1,0:T(8,128)(2,1)S(1)}, bf16[2,128,256]{2,1,0:T(8,128)(2,1)S(1)}, u32[]{:S(2)}, u32[]{:S(2)}) collective-permute-start(bf16[2,128,256]{2,1,0:T(8,128)(2,1)S(1)} %collective-permute-done.14.refs_10_), channel_id=1, source_target_pairs={{0,4},{4,12},{12,20},{20,28},{28,24},{24,16},{16,8},{8,0},{1,5},{5... | collective-permute-start | bytes 393224 | tf_op jit(solution)/shard_map/ppermute | solution.py:269
  36.8 5.1 %collective-permute-start.13 = (bf16[2,128,256]{2,1,0:T(8,128)(2,1)S(1)}, bf16[2,128,256]{2,1,0:T(8,128)(2,1)S(1)}, u32[]{:S(2)}, u32[]{:S(2)}) collective-permute-start(bf16[2,128,256]{2,1,0:T(8,128)(2,1)S(1)} %collective-permute-done.12.refs_6_), channel_id=1, source_target_pairs={{4,0},{12,4},{20,12},{28,20},{24,28},{16,24},{8,16},{0,8},{5,1},{1... | collective-permute-start | bytes 393224 | tf_op jit(solution)/shard_map/ppermute | solution.py:272
  40.4 5.0 %collective-permute-start.16 = (bf16[2,128,256]{2,1,0:T(8,128)(2,1)S(1)}, bf16[2,128,256]{2,1,0:T(8,128)(2,1)S(1)}, u32[]{:S(2)}, u32[]{:S(2)}) collective-permute-start(bf16[2,128,256]{2,1,0:T(8,128)(2,1)S(1)} %collective-permute-done.15.refs_9_), channel_id=1, source_target_pairs={{0,4},{4,12},{12,20},{20,28},{28,24},{24,16},{16,8},{8,0},{1,5},{5... | collective-permute-start | bytes 393224 | tf_op jit(solution)/shard_map/ppermute | solution.py:269
  41.9 7.8 %collective-permute-start.17 = (bf16[2,128,256]{2,1,0:T(8,128)(2,1)S(1)}, bf16[2,128,256]{2,1,0:T(8,128)(2,1)S(1)}, u32[]{:S(2)}, u32[]{:S(2)}) collective-permute-start(bf16[2,128,256]{2,1,0:T(8,128)(2,1)S(1)} %collective-permute-done.13.refs_7_), channel_id=1, source_target_pairs={{4,0},{12,4},{20,12},{28,20},{24,28},{16,24},{8,16},{0,8},{5,1},{1... | collective-permute-start | bytes 393224 | tf_op jit(solution)/shard_map/ppermute | solution.py:272
  45.4 5.0 %collective-permute-start.18 = (bf16[2,128,256]{2,1,0:T(8,128)(2,1)S(1)}, bf16[2,128,256]{2,1,0:T(8,128)(2,1)S(1)}, u32[]{:S(2)}, u32[]{:S(2)}) collective-permute-start(bf16[2,128,256]{2,1,0:T(8,128)(2,1)S(1)} %collective-permute-done.16.refs_8_), channel_id=1, source_target_pairs={{0,4},{4,12},{12,20},{20,28},{28,24},{24,16},{16,8},{8,0},{1,5},{5... | collective-permute-start | bytes 393224 | tf_op jit(solution)/shard_map/ppermute | solution.py:269
  50.6 4.3 %collective-permute-start.19 = (bf16[1,128,256]{2,1,0:T(8,128)(2,1)S(1)}, bf16[1,128,256]{2,1,0:T(8,128)(2,1)S(1)}, u32[]{:S(2)}, u32[]{:S(2)}) collective-permute-start(bf16[1,128,256]{2,1,0:T(8,128)(2,1)S(1)} %get-tuple-element.43), channel_id=1, source_target_pairs={{0,2},{1,3},{2,0},{3,1},{4,6},{5,7},{6,4},{7,5},{8,10},{9,11},{10,... | collective-permute-start | bytes 196616 | tf_op jit(solution)/shard_map/ppermute | solution.py:285
  52.1 2.8 %collective-permute-start.22 = (bf16[128,256]{1,0:T(8,128)(2,1)S(1)}, bf16[128,256]{1,0:T(8,128)(2,1)S(1)}, u32[]{:S(2)}, u32[]{:S(2)}) collective-permute-start(bf16[128,256]{1,0:T(8,128)(2,1)S(1)} %slice_bitcast_fusion), channel_id=1, source_target_pairs={{0,1},{1,0},{2,3},{3,2},{4,5},{5,4},{6,7},{7,6},{8,9},{9,8},{10,11... | collective-permute-start | bytes 196616 | tf_op jit(solution)/shard_map/ppermute | solution.py:285
  52.2 3.9 %collective-permute-start.21 = (bf16[1,128,256]{2,1,0:T(8,128)(2,1)S(1)}, bf16[1,128,256]{2,1,0:T(8,128)(2,1)S(1)}, u32[]{:S(2)}, u32[]{:S(2)}) collective-permute-start(bf16[1,128,256]{2,1,0:T(8,128)(2,1)S(1)} %get-tuple-element.44), channel_id=1, source_target_pairs={{0,3},{1,2},{2,1},{3,0},{4,7},{5,6},{6,5},{7,4},{8,11},{9,10},{10,... | collective-permute-start | bytes 196616 | tf_op jit(solution)/shard_map/ppermute | solution.py:285
  54.9 1.3 %collective-permute-start.20 = (bf16[128,256]{1,0:T(8,128)(2,1)S(1)}, bf16[128,256]{1,0:T(8,128)(2,1)S(1)}, u32[]{:S(2)}, u32[]{:S(2)}) collective-permute-start(bf16[128,256]{1,0:T(8,128)(2,1)S(1)} %get-tuple-element.48), channel_id=1, source_target_pairs={{0,1},{1,0},{2,3},{3,2},{4,5},{5,4},{6,7},{7,6},{8,9},{9,8},{10,11... | collective-permute-start | bytes 196616 | tf_op jit(solution)/shard_map/ppermute | solution.py:285

commit v10 on v8

--- a/solution.py
+++ b/solution.py
@@ -72,7 +72,7 @@
     return jnp.stack(solutions)[:, None, None]
 
 
-def first_kernel(n, m, place, counts_ref, cols_ref, b_ref, d_ref, full_ref, index_ref, own_ref, other_ref, away_ref, *refs):
+def first_kernel(n, m, place, counts_ref, cols_ref, b_ref, d_ref, index_ref, own_ref, other_ref, away_ref, *refs):
     b_buf, d_buf, count_ref, col_ref, sems = refs
     middle = b_buf.shape[0]
     copies = [
@@ -91,9 +91,9 @@
     size, width = own_ref.shape
     for copy in copies[:2]:
         copy.wait()
-    full_ref[...] = jnp.dot(d_buf[0], b_buf[0], preferred_element_type=jnp.float32).astype(jnp.bfloat16)
-    own_ref[...] = full_ref[:, my_columns(me, width)]
-    other_ref[...] = full_ref[:, my_columns(me ^ 1, width)]
+    for j, out_ref in enumerate((own_ref, other_ref)):
+        value = jnp.dot(d_buf[0], b_buf[0, :, my_columns(me ^ j, width)], preferred_element_type=jnp.float32)
+        out_ref[...] = value.astype(jnp.bfloat16)
     for copy in copies[2:]:
         copy.wait()
     for level in range(1, middle):
@@ -217,13 +217,14 @@
         out_ref[j] = value.astype(jnp.bfloat16)
 
 
-def write_kernel(full_ref, *refs):
-    level_refs, (out_ref, sems) = refs[:-2], refs[-2:]
-    width = level_refs[0].shape[2]
-    copies = [pltpu.make_async_copy(full_ref, out_ref.at[0, 0, 0], sems.at[0])]
-    for i, ref in enumerate(level_refs):
-        target = out_ref.at[1 + i // PAIR, 0, 0, :, my_columns(lax.axis_index("pcol") ^ (i % PAIR), width)]
-        copies.append(pltpu.make_async_copy(ref if i % PAIR else ref.at[0], target, sems.at[1 + i]))
+def write_kernel(*refs):
+    piece_refs, (out_ref, sems) = refs[:-2], refs[-2:]
+    width = piece_refs[0].shape[1]
+    copies = []
+    for i, ref in enumerate(piece_refs):
+        target = out_ref.at[i // PAIR, 0, 0, :, my_columns(lax.axis_index("pcol") ^ (i % PAIR), width)]
+        source = ref.at[0] if len(ref.shape) == 3 else ref
+        copies.append(pltpu.make_async_copy(source, target, sems.at[i]))
     for copy in copies:
         copy.start()
     for copy in copies:
@@ -284,17 +285,16 @@
 
     middle = levels - 1
 
-    full, index, own, other, away = pl.pallas_call(
+    index, own, other, away = pl.pallas_call(
         functools.partial(first_kernel, n, m, place),
         out_shape=[
-            near((size, front)),
             near(index_shape, jnp.int32),
             near((size, width)),
             near((size, width)),
             near(((2 * middle - 2) * size, width)),
         ],
         in_specs=[anywhere()] * 4,
-        out_specs=[vmem()] * 5,
+        out_specs=[vmem()] * 4,
         scratch_shapes=[
             pltpu.VMEM((middle, size, front), jnp.bfloat16),
             pltpu.VMEM((middle, size, size), jnp.bfloat16),
@@ -304,6 +304,7 @@
         ],
         compiler_params=params(),
     )(*[in_hbm(v) for v in (live_counts, block_cols, b_panels, diag_inverse)])
+    first = [own, other]
     other, away, index = send(other, 1), send(away, 1), [index, send(index, 1)]
     solved = after(jnp.stack([own, other]), index[1])
     blocks = [in_hbm(l_blocks), send(after(l_blocks, solved), 1)]
@@ -377,11 +378,11 @@
     result = pl.pallas_call(
         write_kernel,
         out_shape=struct(b_panels.shape),
-        in_specs=[vmem()] * (1 + len(columns)),
+        in_specs=[vmem()] * (PAIR + len(columns)),
         out_specs=anywhere(),
-        scratch_shapes=[pltpu.SemaphoreType.DMA((1 + len(columns),))],
+        scratch_shapes=[pltpu.SemaphoreType.DMA((PAIR + len(columns),))],
         compiler_params=params(),
-    )(full, *columns)
+    )(*first, *columns)
     return pl.pallas_call(
         last_kernel,
         out_shape=struct(b_panels.shape),

time: 57.3 us -> 57.3 us (level)
  no operation moved by 1% of the time
where the time goes in v10:
time: 57.3 us; the launch traced here: 57 us
  waiting for transfers between devices  26.9 us (47%)
  starting transfers between devices  20.6 us (36%)
  Pallas kernels  9.38 us (16%)
    ppermute x8, waiting for transfers between devices, advance(): self.behind = lax.ppermute(self.behind, 'prow', self.to_next)  19.3 us
    ppermute x8, starting transfers between devices, advance(): self.behind = lax.ppermute(self.behind, 'prow', self.to_next)  13.5 us
    ppermute x9, waiting for transfers between devices, send(): return lax.ppermute(value, 'pcol', [(i, i ^ bits) for i in range(n)])  6.61 us
    pallas_call x2, Pallas kernels, solve_paired(): pl.pallas_call(functools.partial(gather_kernel, n, level, m, early, late)...  5.51 us
    ppermute x9, starting transfers between devices, send(): return lax.ppermute(value, 'pcol', [(i, i ^ bits) for i in range(n)])  4.63 us
    ppermute x6, starting transfers between devices, advance(): self.ahead = lax.ppermute(self.ahead, 'prow', self.to_last)  2.53 us
    pallas_call x1, Pallas kernels, solve_paired(): pl.pallas_call(functools.partial(first_kernel, n, m, place), out_shape=[n...  1.17 us
  transfers between devices with their start and end apart: 23, of which 15 were waited for; matrix products, arithmetic and copies ran while one was open for 0% of the time, Pallas kernels for 12%

profile of v10, /device:TPU:0, one launch (start us, length us, event | category | flops | bytes accessed | tf_op | source)
XLA Modules:
  0.0 57.0 jit_solution(1095129177353738603)
XLA Ops:
  0.0 1.2 %shard_map.55 = (s32[8,128]{1,0:T(8,128)S(1)}, bf16[128,256]{1,0:T(8,128)(2,1)S(1)}, bf16[128,256]{1,0:T(8,128)(2,1)S(1)}, bf16[256,256]{1,0:T(8,128)(2,1)S(1)}) custom-call(s32[2,1,1,4]{3,2,1,0:T(1,128)} %counts_ref.1, s32[2,1,1,4,5]{4,3,2,1,0:T(4,128)} %cols_ref.1, bf16[3,1,1,128,512]{4,3,2,1,0:T(8,128)(2,1)} %b_ref.5, bf16[3,1,1,128,128]{4,3,2,1,0:T(8,128)(2,1)} %d_ref.5), custom_call_target="tpu_custom_call" | custom-call | tf_op jit(solution)/shard_map/pallas_call | solution.py:288
  1.2 0.5 collective-permute-start.1
  1.7 0.1 collective-permute-start
  1.8 0.8 %collective-permute-done.1 = bf16[128,256]{1,0:T(8,128)(2,1)S(1)} collective-permute-done((bf16[128,256]{1,0:T(8,128)(2,1)S(1)}, bf16[128,256]{1,0:T(8,128)(2,1)S(1)}, u32[]{:S(2)}, u32[]{:S(2)}) %collective-permute-start.1) | collective-permute-done | bytes 65568 | tf_op jit(solution)/shard_map/ppermute | solution.py:282
  2.6 0.2 collective-permute-done.refs_1_
  2.9 0.2 collective-permute-start.2
  3.0 2.8 %collective-permute-start.6 = (bf16[2,128,256]{2,1,0:T(8,128)(2,1)S(1)}, bf16[2,128,256]{2,1,0:T(8,128)(2,1)S(1)}, u32[]{:S(2)}, u32[]{:S(2)}) collective-permute-start(bf16[2,128,256]{2,1,0:T(8,128)(2,1)S(1)} %pad_maximum_fusion.refs_4_.refs_2_), channel_id=1, source_target_pairs={{0,4},{4,12},{12,20},{20,28},{28,24},{24,16},{16,8},{8,0},{1,5},{5... | collective-permute-start | bytes 393224 | tf_op jit(solution)/shard_map/ppermute | solution.py:266
  5.9 0.1 collective-permute-start.4
  6.0 3.8 %collective-permute-done.6.refs_9_.refs_7_ = bf16[2,128,256]{2,1,0:T(8,128)(2,1)S(1)} collective-permute-done((bf16[2,128,256]{2,1,0:T(8,128)(2,1)S(1)}, bf16[2,128,256]{2,1,0:T(8,128)(2,1)S(1)}, u32[]{:S(2)}, u32[]{:S(2)}) %collective-permute-start.6) | collective-permute-done | bytes 131104 | tf_op jit(solution)/shard_map/ppermute | solution.py:266
  9.8 1.7 %collective-permute-start.7 = (bf16[2,128,256]{2,1,0:T(8,128)(2,1)S(1)}, bf16[2,128,256]{2,1,0:T(8,128)(2,1)S(1)}, u32[]{:S(2)}, u32[]{:S(2)}) collective-permute-start(bf16[2,128,256]{2,1,0:T(8,128)(2,1)S(1)} %collective-permute-done.6.refs_9_.refs_7_), channel_id=1, source_target_pairs={{0,4},{4,12},{12,20},{20,28},{28,24},{24,16},{16,8},{8,0},{1,5},{5... | collective-permute-start | bytes 393224 | tf_op jit(solution)/shard_map/ppermute | solution.py:266
  11.4 0.0 collective-permute-start.3
  11.5 0.0 collective-permute-done.4.refs_5_.refs_3_
  11.5 0.4 collective-permute-start.5
  11.8 3.0 %collective-permute-done.7.refs_8_.refs_6_ = bf16[2,128,256]{2,1,0:T(8,128)(2,1)S(1)} collective-permute-done((bf16[2,128,256]{2,1,0:T(8,128)(2,1)S(1)}, bf16[2,128,256]{2,1,0:T(8,128)(2,1)S(1)}, u32[]{:S(2)}, u32[]{:S(2)}) %collective-permute-start.7) | collective-permute-done | bytes 131104 | tf_op jit(solution)/shard_map/ppermute | solution.py:266
  14.9 1.5 %collective-permute-start.8 = (bf16[2,128,256]{2,1,0:T(8,128)(2,1)S(1)}, bf16[2,128,256]{2,1,0:T(8,128)(2,1)S(1)}, u32[]{:S(2)}, u32[]{:S(2)}) collective-permute-start(bf16[2,128,256]{2,1,0:T(8,128)(2,1)S(1)} %collective-permute-done.7.refs_8_.refs_6_), channel_id=1, source_target_pairs={{0,4},{4,12},{12,20},{20,28},{28,24},{24,16},{16,8},{8,0},{1,5},{5... | collective-permute-start | bytes 393224 | tf_op jit(solution)/shard_map/ppermute | solution.py:266
  16.4 0.0 collective-permute-done.3.away_ref
  16.4 0.9 %collective-permute-done.5.refs_6_.refs_4_ = bf16[2,128,256]{2,1,0:T(8,128)(2,1)S(1)} collective-permute-done((bf16[2,128,256]{2,1,0:T(8,128)(2,1)S(1)}, bf16[2,128,256]{2,1,0:T(8,128)(2,1)S(1)}, u32[]{:S(2)}, u32[]{:S(2)}) %collective-permute-start.5) | collective-permute-done | bytes 131104 | tf_op jit(solution)/shard_map/ppermute | solution.py:269
  17.4 0.4 collective-permute-start.9
  17.7 2.1 %collective-permute-done.8.refs_7_.refs_5_ = bf16[2,128,256]{2,1,0:T(8,128)(2,1)S(1)} collective-permute-done((bf16[2,128,256]{2,1,0:T(8,128)(2,1)S(1)}, bf16[2,128,256]{2,1,0:T(8,128)(2,1)S(1)}, u32[]{:S(2)}, u32[]{:S(2)}) %collective-permute-start.8) | collective-permute-done | bytes 131104 | tf_op jit(solution)/shard_map/ppermute | solution.py:266
  19.8 1.5 %collective-permute-start.10 = (bf16[2,128,256]{2,1,0:T(8,128)(2,1)S(1)}, bf16[2,128,256]{2,1,0:T(8,128)(2,1)S(1)}, u32[]{:S(2)}, u32[]{:S(2)}) collective-permute-start(bf16[2,128,256]{2,1,0:T(8,128)(2,1)S(1)} %collective-permute-done.8.refs_7_.refs_5_), channel_id=1, source_target_pairs={{0,4},{4,12},{12,20},{20,28},{28,24},{24,16},{16,8},{8,0},{1,5},{5... | collective-permute-start | bytes 393224 | tf_op jit(solution)/shard_map/ppermute | solution.py:266
  21.4 0.0 collective-permute-done.2.refs_3_
  21.4 2.7 %shard_map.56 = (f32[4,128,256]{2,1,0:T(8,128)S(1)}, bf16[4,128,512]{2,1,0:T(8,128)(2,1)S(1)}) custom-call(s32[8,128]{1,0:T(8,128)S(1)} %get-tuple-element.27.refs_0_, s32[8,128]{1,0:T(8,128)S(1)} %collective-permute-done.refs_1_, bf16[2,1,1,4,5,128,128]{6,5,4,3,2,1,0:T(8,128)(2,1)} %refs_2_.3, ...), custom_call_target="tpu_custom_call" | custom-call | tf_op jit(solution)/shard_map/pallas_call | solution.py:322
  24.1 0.0 copy-start
  24.1 0.0 copy-start.1
  24.1 0.0 collective-permute-done.9.refs_0_
  24.2 0.6 %collective-permute-done.10.refs_1_ = bf16[2,128,256]{2,1,0:T(8,128)(2,1)S(1)} collective-permute-done((bf16[2,128,256]{2,1,0:T(8,128)(2,1)S(1)}, bf16[2,128,256]{2,1,0:T(8,128)(2,1)S(1)}, u32[]{:S(2)}, u32[]{:S(2)}) %collective-permute-start.10) | collective-permute-done | bytes 131104 | tf_op jit(solution)/shard_map/ppermute | solution.py:266
  24.8 0.2 shard_map.57
  25.0 1.6 %collective-permute-start.11 = (bf16[2,128,256]{2,1,0:T(8,128)(2,1)S(1)}, bf16[2,128,256]{2,1,0:T(8,128)(2,1)S(1)}, u32[]{:S(2)}, u32[]{:S(2)}) collective-permute-start(bf16[2,128,256]{2,1,0:T(8,128)(2,1)S(1)} %shard_map.57), channel_id=1, source_target_pairs={{0,2},{1,3},{2,0},{3,1},{4,6},{5,7},{6,4},{7,5},{8,10},{9,11},{10,... | collective-permute-start | bytes 393224 | tf_op jit(solution)/shard_map/ppermute | solution.py:282
  26.7 0.0 copy-done
  26.7 0.0 copy-done.1
  26.7 0.2 shard_map.58
  26.9 3.1 %collective-permute-done.11.refs_0_ = bf16[2,128,256]{2,1,0:T(8,128)(2,1)S(1)} collective-permute-done((bf16[2,128,256]{2,1,0:T(8,128)(2,1)S(1)}, bf16[2,128,256]{2,1,0:T(8,128)(2,1)S(1)}, u32[]{:S(2)}, u32[]{:S(2)}) %collective-permute-start.11) | collective-permute-done | bytes 131104 | tf_op jit(solution)/shard_map/ppermute | solution.py:282
  30.1 0.2 shard_map.59.refs_5_.refs_2_
  30.3 1.6 %collective-permute-start.14 = (bf16[2,128,256]{2,1,0:T(8,128)(2,1)S(1)}, bf16[2,128,256]{2,1,0:T(8,128)(2,1)S(1)}, u32[]{:S(2)}, u32[]{:S(2)}) collective-permute-start(bf16[2,128,256]{2,1,0:T(8,128)(2,1)S(1)} %shard_map.59.refs_5_.refs_2_), channel_id=1, source_target_pairs={{0,4},{4,12},{12,20},{20,28},{28,24},{24,16},{16,8},{8,0},{1,5},{5... | collective-permute-start | bytes 393224 | tf_op jit(solution)/shard_map/ppermute | solution.py:266
  31.9 0.5 collective-permute-start.12
  32.3 3.1 %collective-permute-done.14.refs_10_ = bf16[2,128,256]{2,1,0:T(8,128)(2,1)S(1)} collective-permute-done((bf16[2,128,256]{2,1,0:T(8,128)(2,1)S(1)}, bf16[2,128,256]{2,1,0:T(8,128)(2,1)S(1)}, u32[]{:S(2)}, u32[]{:S(2)}) %collective-permute-start.14) | collective-permute-done | bytes 131104 | tf_op jit(solution)/shard_map/ppermute | solution.py:266
  35.5 1.4 %collective-permute-start.15 = (bf16[2,128,256]{2,1,0:T(8,128)(2,1)S(1)}, bf16[2,128,256]{2,1,0:T(8,128)(2,1)S(1)}, u32[]{:S(2)}, u32[]{:S(2)}) collective-permute-start(bf16[2,128,256]{2,1,0:T(8,128)(2,1)S(1)} %collective-permute-done.14.refs_10_), channel_id=1, source_target_pairs={{0,4},{4,12},{12,20},{20,28},{28,24},{24,16},{16,8},{8,0},{1,5},{5... | collective-permute-start | bytes 393224 | tf_op jit(solution)/shard_map/ppermute | solution.py:266
  36.8 0.0 collective-permute-done.12.refs_6_
  36.8 0.7 %collective-permute-start.13 = (bf16[2,128,256]{2,1,0:T(8,128)(2,1)S(1)}, bf16[2,128,256]{2,1,0:T(8,128)(2,1)S(1)}, u32[]{:S(2)}, u32[]{:S(2)}) collective-permute-start(bf16[2,128,256]{2,1,0:T(8,128)(2,1)S(1)} %collective-permute-done.12.refs_6_), channel_id=1, source_target_pairs={{4,0},{12,4},{20,12},{28,20},{24,28},{16,24},{8,16},{0,8},{5,1},{1... | collective-permute-start | bytes 393224 | tf_op jit(solution)/shard_map/ppermute | solution.py:269
  37.5 2.9 %collective-permute-done.15.refs_9_ = bf16[2,128,256]{2,1,0:T(8,128)(2,1)S(1)} collective-permute-done((bf16[2,128,256]{2,1,0:T(8,128)(2,1)S(1)}, bf16[2,128,256]{2,1,0:T(8,128)(2,1)S(1)}, u32[]{:S(2)}, u32[]{:S(2)}) %collective-permute-start.15) | collective-permute-done | bytes 131104 | tf_op jit(solution)/shard_map/ppermute | solution.py:266
  40.4 1.5 %collective-permute-start.16 = (bf16[2,128,256]{2,1,0:T(8,128)(2,1)S(1)}, bf16[2,128,256]{2,1,0:T(8,128)(2,1)S(1)}, u32[]{:S(2)}, u32[]{:S(2)}) collective-permute-start(bf16[2,128,256]{2,1,0:T(8,128)(2,1)S(1)} %collective-permute-done.15.refs_9_), channel_id=1, source_target_pairs={{0,4},{4,12},{12,20},{20,28},{28,24},{24,16},{16,8},{8,0},{1,5},{5... | collective-permute-start | bytes 393224 | tf_op jit(solution)/shard_map/ppermute | solution.py:266
  41.9 0.0 collective-permute-done.13.refs_7_
  41.9 0.6 collective-permute-start.17
  42.5 2.9 %collective-permute-done.16.refs_8_ = bf16[2,128,256]{2,1,0:T(8,128)(2,1)S(1)} collective-permute-done((bf16[2,128,256]{2,1,0:T(8,128)(2,1)S(1)}, bf16[2,128,256]{2,1,0:T(8,128)(2,1)S(1)}, u32[]{:S(2)}, u32[]{:S(2)}) %collective-permute-start.16) | collective-permute-done | bytes 131104 | tf_op jit(solution)/shard_map/ppermute | solution.py:266
  45.4 1.5 %collective-permute-start.18 = (bf16[2,128,256]{2,1,0:T(8,128)(2,1)S(1)}, bf16[2,128,256]{2,1,0:T(8,128)(2,1)S(1)}, u32[]{:S(2)}, u32[]{:S(2)}) collective-permute-start(bf16[2,128,256]{2,1,0:T(8,128)(2,1)S(1)} %collective-permute-done.16.refs_8_), channel_id=1, source_target_pairs={{0,4},{4,12},{12,20},{20,28},{28,24},{24,16},{16,8},{8,0},{1,5},{5... | collective-permute-start | bytes 393224 | tf_op jit(solution)/shard_map/ppermute | solution.py:266
  46.9 2.8 %shard_map.60 = (f32[4,128,256]{2,1,0:T(8,128)S(1)}, bf16[4,128,512]{2,1,0:T(8,128)(2,1)S(1)}) custom-call(s32[8,128]{1,0:T(8,128)S(1)} %get-tuple-element.27.refs_0_, s32[8,128]{1,0:T(8,128)S(1)} %collective-permute-done.refs_1_, bf16[2,1,1,4,5,128,128]{6,5,4,3,2,1,0:T(8,128)(2,1)} %refs_2_.3, ...), custom_call_target="tpu_custom_call" | custom-call | tf_op jit(solution)/shard_map/pallas_call | solution.py:322
  49.7 0.0 collective-permute-done.17.refs_0_
  49.7 0.7 %collective-permute-done.18.refs_1_ = bf16[2,128,256]{2,1,0:T(8,128)(2,1)S(1)} collective-permute-done((bf16[2,128,256]{2,1,0:T(8,128)(2,1)S(1)}, bf16[2,128,256]{2,1,0:T(8,128)(2,1)S(1)}, u32[]{:S(2)}, u32[]{:S(2)}) %collective-permute-start.18) | collective-permute-done | bytes 131104 | tf_op jit(solution)/shard_map/ppermute | solution.py:266
  50.4 0.2 shard_map.61
  50.6 1.6 %collective-permute-start.19 = (bf16[1,128,256]{2,1,0:T(8,128)(2,1)S(1)}, bf16[1,128,256]{2,1,0:T(8,128)(2,1)S(1)}, u32[]{:S(2)}, u32[]{:S(2)}) collective-permute-start(bf16[1,128,256]{2,1,0:T(8,128)(2,1)S(1)} %get-tuple-element.42), channel_id=1, source_target_pairs={{0,2},{1,3},{2,0},{3,1},{4,6},{5,7},{6,4},{7,5},{8,10},{9,11},{10,... | collective-permute-start | bytes 196616 | tf_op jit(solution)/shard_map/ppermute | solution.py:282
  52.2 0.0 collective-permute-start.22
  52.2 0.6 %collective-permute-start.21 = (bf16[1,128,256]{2,1,0:T(8,128)(2,1)S(1)}, bf16[1,128,256]{2,1,0:T(8,128)(2,1)S(1)}, u32[]{:S(2)}, u32[]{:S(2)}) collective-permute-start(bf16[1,128,256]{2,1,0:T(8,128)(2,1)S(1)} %get-tuple-element.43), channel_id=1, source_target_pairs={{0,3},{1,2},{2,1},{3,0},{4,7},{5,6},{6,5},{7,4},{8,11},{9,10},{10,... | collective-permute-start | bytes 196616 | tf_op jit(solution)/shard_map/ppermute | solution.py:282
  52.8 0.2 shard_map.62
  53.1 1.9 %collective-permute-done.19.refs_0_ = bf16[1,128,256]{2,1,0:T(8,128)(2,1)S(1)} collective-permute-done((bf16[1,128,256]{2,1,0:T(8,128)(2,1)S(1)}, bf16[1,128,256]{2,1,0:T(8,128)(2,1)S(1)}, u32[]{:S(2)}, u32[]{:S(2)}) %collective-permute-start.19) | collective-permute-done | bytes 65568 | tf_op jit(solution)/shard_map/ppermute | solution.py:282
  54.9 0.0 collective-permute-start.20
  54.9 0.0 collective-permute-done.22.refs_3_
  54.9 0.7 %shard_map.63.refs_2_ = bf16[3,1,1,128,512]{4,3,2,1,0:T(8,128)(2,1)} custom-call(bf16[128,256]{1,0:T(8,128)(2,1)S(1)} %get-tuple-element.28.refs_0_, bf16[128,256]{1,0:T(8,128)(2,1)S(1)} %get-tuple-element.29.refs_1_, bf16[2,128,256]{2,1,0:T(8,128)(2,1)S(1)} %shard_map.59.refs_5_.refs_2_, bf16[128,256]{1,0:T(8,128)(2,1)S(1)} %collective-permute-done.22.refs_3_), custom_call_target="tpu_custom_call" | custom-call | tf_op jit(solution)/shard_map/pallas_call | solution.py:378
  55.7 0.4 collective-permute-done.21.refs_1_
  56.1 0.1 collective-permute-done.20.mate_ref
  56.2 0.9 %shard_map.64 = bf16[3,1,1,128,512]{4,3,2,1,0:T(8,128)(2,1)} custom-call(bf16[3,1,1,128,128]{4,3,2,1,0:T(8,128)(2,1)S(1)} %copy-done.1, f32[2,128,256]{2,1,0:T(8,128)S(1)} %get-tuple-element.45.right_ref, bf16[128,256]{1,0:T(8,128)(2,1)S(1)} %collective-permute-done.20.mate_ref, ...), custom_call_target="tpu_custom_call", output_to_operand_aliasing={{}: (5, {})} | custom-call | tf_op jit(solution)/shard_map/pallas_call | solution.py:386
  (2 shorter events, 0.0 us)
Async XLA Ops:
  1.2 1.4 %collective-permute-start.1 = (bf16[128,256]{1,0:T(8,128)(2,1)S(1)}, bf16[128,256]{1,0:T(8,128)(2,1)S(1)}, u32[]{:S(2)}, u32[]{:S(2)}) collective-permute-start(bf16[128,256]{1,0:T(8,128)(2,1)S(1)} %get-tuple-element.29.refs_1_), channel_id=1, source_target_pairs={{0,1},{1,0},{2,3},{3,2},{4,5},{5,4},{6,7},{7,6},{8,9},{9,8},{10,11... | collective-permute-start | bytes 196616 | tf_op jit(solution)/shard_map/ppermute | solution.py:282
  1.7 1.2 %collective-permute-start = (s32[8,128]{1,0:T(8,128)S(1)}, s32[8,128]{1,0:T(8,128)S(1)}, u32[]{:S(2)}, u32[]{:S(2)}) collective-permute-start(s32[8,128]{1,0:T(8,128)S(1)} %get-tuple-element.27.refs_0_), channel_id=1, source_target_pairs={{0,1},{1,0},{2,3},{3,2},{4,5},{5,4},{6,7},{7,6},{8,9},{9,8},{10,11... | collective-permute-start | bytes 12296 | tf_op jit(solution)/shard_map/ppermute | solution.py:282
  2.9 18.5 %collective-permute-start.2 = (bf16[2,1,1,4,5,128,128]{6,5,4,3,2,1,0:T(8,128)(2,1)}, bf16[2,1,1,4,5,128,128]{6,5,4,3,2,1,0:T(8,128)(2,1)S(1)}, u32[]{:S(2)}, u32[]{:S(2)}) collective-permute-start(bf16[2,1,1,4,5,128,128]{6,5,4,3,2,1,0:T(8,128)(2,1)} %refs_2_.3), channel_id=1, source_target_pairs={{0,1},{1,0},{2,3},{3,2},{4,5},{5,4},{6,7},{7,6},{8,9},{9,8},{10,11... | collective-permute-start | bytes 3932168 | tf_op jit(solution)/shard_map/ppermute | solution.py:282
  3.0 6.7 %collective-permute-start.6 = (bf16[2,128,256]{2,1,0:T(8,128)(2,1)S(1)}, bf16[2,128,256]{2,1,0:T(8,128)(2,1)S(1)}, u32[]{:S(2)}, u32[]{:S(2)}) collective-permute-start(bf16[2,128,256]{2,1,0:T(8,128)(2,1)S(1)} %pad_maximum_fusion.refs_4_.refs_2_), channel_id=1, source_target_pairs={{0,4},{4,12},{12,20},{20,28},{28,24},{24,16},{16,8},{8,0},{1,5},{5... | collective-permute-start | bytes 393224 | tf_op jit(solution)/shard_map/ppermute | solution.py:266
  5.9 5.6 %collective-permute-start.4 = (bf16[2,128,256]{2,1,0:T(8,128)(2,1)S(1)}, bf16[2,128,256]{2,1,0:T(8,128)(2,1)S(1)}, u32[]{:S(2)}, u32[]{:S(2)}) collective-permute-start(bf16[2,128,256]{2,1,0:T(8,128)(2,1)S(1)} %pad_maximum_fusion.refs_4_.refs_2_), channel_id=1, source_target_pairs={{4,0},{12,4},{20,12},{28,20},{24,28},{16,24},{8,16},{0,8},{5,1},{1... | collective-permute-start | bytes 393224 | tf_op jit(solution)/shard_map/ppermute | solution.py:269
  9.8 5.1 %collective-permute-start.7 = (bf16[2,128,256]{2,1,0:T(8,128)(2,1)S(1)}, bf16[2,128,256]{2,1,0:T(8,128)(2,1)S(1)}, u32[]{:S(2)}, u32[]{:S(2)}) collective-permute-start(bf16[2,128,256]{2,1,0:T(8,128)(2,1)S(1)} %collective-permute-done.6.refs_9_.refs_7_), channel_id=1, source_target_pairs={{0,4},{4,12},{12,20},{20,28},{28,24},{24,16},{16,8},{8,0},{1,5},{5... | collective-permute-start | bytes 393224 | tf_op jit(solution)/shard_map/ppermute | solution.py:266
  11.4 5.0 %collective-permute-start.3 = (bf16[256,256]{1,0:T(8,128)(2,1)S(1)}, bf16[256,256]{1,0:T(8,128)(2,1)S(1)}, u32[]{:S(2)}, u32[]{:S(2)}) collective-permute-start(bf16[256,256]{1,0:T(8,128)(2,1)S(1)} %get-tuple-element.32), channel_id=1, source_target_pairs={{0,1},{1,0},{2,3},{3,2},{4,5},{5,4},{6,7},{7,6},{8,9},{9,8},{10,11... | collective-permute-start | bytes 393224 | tf_op jit(solution)/shard_map/ppermute | solution.py:282
  11.5 5.9 %collective-permute-start.5 = (bf16[2,128,256]{2,1,0:T(8,128)(2,1)S(1)}, bf16[2,128,256]{2,1,0:T(8,128)(2,1)S(1)}, u32[]{:S(2)}, u32[]{:S(2)}) collective-permute-start(bf16[2,128,256]{2,1,0:T(8,128)(2,1)S(1)} %collective-permute-done.4.refs_5_.refs_3_), channel_id=1, source_target_pairs={{4,0},{12,4},{20,12},{28,20},{24,28},{16,24},{8,16},{0,8},{5,1},{1... | collective-permute-start | bytes 393224 | tf_op jit(solution)/shard_map/ppermute | solution.py:269
  14.9 5.0 %collective-permute-start.8 = (bf16[2,128,256]{2,1,0:T(8,128)(2,1)S(1)}, bf16[2,128,256]{2,1,0:T(8,128)(2,1)S(1)}, u32[]{:S(2)}, u32[]{:S(2)}) collective-permute-start(bf16[2,128,256]{2,1,0:T(8,128)(2,1)S(1)} %collective-permute-done.7.refs_8_.refs_6_), channel_id=1, source_target_pairs={{0,4},{4,12},{12,20},{20,28},{28,24},{24,16},{16,8},{8,0},{1,5},{5... | collective-permute-start | bytes 393224 | tf_op jit(solution)/shard_map/ppermute | solution.py:266
  17.4 6.8 %collective-permute-start.9 = (bf16[2,128,256]{2,1,0:T(8,128)(2,1)S(1)}, bf16[2,128,256]{2,1,0:T(8,128)(2,1)S(1)}, u32[]{:S(2)}, u32[]{:S(2)}) collective-permute-start(bf16[2,128,256]{2,1,0:T(8,128)(2,1)S(1)} %collective-permute-done.5.refs_6_.refs_4_), channel_id=1, source_target_pairs={{4,0},{12,4},{20,12},{28,20},{24,28},{16,24},{8,16},{0,8},{5,1},{1... | collective-permute-start | bytes 393224 | tf_op jit(solution)/shard_map/ppermute | solution.py:269
  19.8 5.0 %collective-permute-start.10 = (bf16[2,128,256]{2,1,0:T(8,128)(2,1)S(1)}, bf16[2,128,256]{2,1,0:T(8,128)(2,1)S(1)}, u32[]{:S(2)}, u32[]{:S(2)}) collective-permute-start(bf16[2,128,256]{2,1,0:T(8,128)(2,1)S(1)} %collective-permute-done.8.refs_7_.refs_5_), channel_id=1, source_target_pairs={{0,4},{4,12},{12,20},{20,28},{28,24},{24,16},{16,8},{8,0},{1,5},{5... | collective-permute-start | bytes 393224 | tf_op jit(solution)/shard_map/ppermute | solution.py:266
  24.1 2.6 %copy-start = (bf16[3,1,1,128,512]{4,3,2,1,0:T(8,128)(2,1)S(1)}, bf16[3,1,1,128,512]{4,3,2,1,0:T(8,128)(2,1)}, u32[]{:S(2)}) copy-start(bf16[3,1,1,128,512]{4,3,2,1,0:T(8,128)(2,1)} %b_ref.5) | copy-start | bytes 1179652
  24.1 2.5 %copy-start.1 = (bf16[3,1,1,128,128]{4,3,2,1,0:T(8,128)(2,1)S(1)}, bf16[3,1,1,128,128]{4,3,2,1,0:T(8,128)(2,1)}, u32[]{:S(2)}) copy-start(bf16[3,1,1,128,128]{4,3,2,1,0:T(8,128)(2,1)} %d_ref.5) | copy-start | bytes 294916
  25.0 5.0 %collective-permute-start.11 = (bf16[2,128,256]{2,1,0:T(8,128)(2,1)S(1)}, bf16[2,128,256]{2,1,0:T(8,128)(2,1)S(1)}, u32[]{:S(2)}, u32[]{:S(2)}) collective-permute-start(bf16[2,128,256]{2,1,0:T(8,128)(2,1)S(1)} %shard_map.57), channel_id=1, source_target_pairs={{0,2},{1,3},{2,0},{3,1},{4,6},{5,7},{6,4},{7,5},{8,10},{9,11},{10,... | collective-permute-start | bytes 393224 | tf_op jit(solution)/shard_map/ppermute | solution.py:282
  30.3 5.2 %collective-permute-start.14 = (bf16[2,128,256]{2,1,0:T(8,128)(2,1)S(1)}, bf16[2,128,256]{2,1,0:T(8,128)(2,1)S(1)}, u32[]{:S(2)}, u32[]{:S(2)}) collective-permute-start(bf16[2,128,256]{2,1,0:T(8,128)(2,1)S(1)} %shard_map.59.refs_5_.refs_2_), channel_id=1, source_target_pairs={{0,4},{4,12},{12,20},{20,28},{28,24},{24,16},{16,8},{8,0},{1,5},{5... | collective-permute-start | bytes 393224 | tf_op jit(solution)/shard_map/ppermute | solution.py:266
  31.9 5.0 %collective-permute-start.12 = (bf16[2,128,256]{2,1,0:T(8,128)(2,1)S(1)}, bf16[2,128,256]{2,1,0:T(8,128)(2,1)S(1)}, u32[]{:S(2)}, u32[]{:S(2)}) collective-permute-start(bf16[2,128,256]{2,1,0:T(8,128)(2,1)S(1)} %shard_map.59.refs_5_.refs_2_), channel_id=1, source_target_pairs={{4,0},{12,4},{20,12},{28,20},{24,28},{16,24},{8,16},{0,8},{5,1},{1... | collective-permute-start | bytes 393224 | tf_op jit(solution)/shard_map/ppermute | solution.py:269
  35.5 5.0 %collective-permute-start.15 = (bf16[2,128,256]{2,1,0:T(8,128)(2,1)S(1)}, bf16[2,128,256]{2,1,0:T(8,128)(2,1)S(1)}, u32[]{:S(2)}, u32[]{:S(2)}) collective-permute-start(bf16[2,128,256]{2,1,0:T(8,128)(2,1)S(1)} %collective-permute-done.14.refs_10_), channel_id=1, source_target_pairs={{0,4},{4,12},{12,20},{20,28},{28,24},{24,16},{16,8},{8,0},{1,5},{5... | collective-permute-start | bytes 393224 | tf_op jit(solution)/shard_map/ppermute | solution.py:266
  36.8 5.1 %collective-permute-start.13 = (bf16[2,128,256]{2,1,0:T(8,128)(2,1)S(1)}, bf16[2,128,256]{2,1,0:T(8,128)(2,1)S(1)}, u32[]{:S(2)}, u32[]{:S(2)}) collective-permute-start(bf16[2,128,256]{2,1,0:T(8,128)(2,1)S(1)} %collective-permute-done.12.refs_6_), channel_id=1, source_target_pairs={{4,0},{12,4},{20,12},{28,20},{24,28},{16,24},{8,16},{0,8},{5,1},{1... | collective-permute-start | bytes 393224 | tf_op jit(solution)/shard_map/ppermute | solution.py:269
  40.4 5.0 %collective-permute-start.16 = (bf16[2,128,256]{2,1,0:T(8,128)(2,1)S(1)}, bf16[2,128,256]{2,1,0:T(8,128)(2,1)S(1)}, u32[]{:S(2)}, u32[]{:S(2)}) collective-permute-start(bf16[2,128,256]{2,1,0:T(8,128)(2,1)S(1)} %collective-permute-done.15.refs_9_), channel_id=1, source_target_pairs={{0,4},{4,12},{12,20},{20,28},{28,24},{24,16},{16,8},{8,0},{1,5},{5... | collective-permute-start | bytes 393224 | tf_op jit(solution)/shard_map/ppermute | solution.py:266
  41.9 7.8 %collective-permute-start.17 = (bf16[2,128,256]{2,1,0:T(8,128)(2,1)S(1)}, bf16[2,128,256]{2,1,0:T(8,128)(2,1)S(1)}, u32[]{:S(2)}, u32[]{:S(2)}) collective-permute-start(bf16[2,128,256]{2,1,0:T(8,128)(2,1)S(1)} %collective-permute-done.13.refs_7_), channel_id=1, source_target_pairs={{4,0},{12,4},{20,12},{28,20},{24,28},{16,24},{8,16},{0,8},{5,1},{1... | collective-permute-start | bytes 393224 | tf_op jit(solution)/shard_map/ppermute | solution.py:269
  45.4 5.0 %collective-permute-start.18 = (bf16[2,128,256]{2,1,0:T(8,128)(2,1)S(1)}, bf16[2,128,256]{2,1,0:T(8,128)(2,1)S(1)}, u32[]{:S(2)}, u32[]{:S(2)}) collective-permute-start(bf16[2,128,256]{2,1,0:T(8,128)(2,1)S(1)} %collective-permute-done.16.refs_8_), channel_id=1, source_target_pairs={{0,4},{4,12},{12,20},{20,28},{28,24},{24,16},{16,8},{8,0},{1,5},{5... | collective-permute-start | bytes 393224 | tf_op jit(solution)/shard_map/ppermute | solution.py:266
  50.6 4.3 %collective-permute-start.19 = (bf16[1,128,256]{2,1,0:T(8,128)(2,1)S(1)}, bf16[1,128,256]{2,1,0:T(8,128)(2,1)S(1)}, u32[]{:S(2)}, u32[]{:S(2)}) collective-permute-start(bf16[1,128,256]{2,1,0:T(8,128)(2,1)S(1)} %get-tuple-element.42), channel_id=1, source_target_pairs={{0,2},{1,3},{2,0},{3,1},{4,6},{5,7},{6,4},{7,5},{8,10},{9,11},{10,... | collective-permute-start | bytes 196616 | tf_op jit(solution)/shard_map/ppermute | solution.py:282
  52.2 2.8 %collective-permute-start.22 = (bf16[128,256]{1,0:T(8,128)(2,1)S(1)}, bf16[128,256]{1,0:T(8,128)(2,1)S(1)}, u32[]{:S(2)}, u32[]{:S(2)}) collective-permute-start(bf16[128,256]{1,0:T(8,128)(2,1)S(1)} %slice_bitcast_fusion), channel_id=1, source_target_pairs={{0,1},{1,0},{2,3},{3,2},{4,5},{5,4},{6,7},{7,6},{8,9},{9,8},{10,11... | collective-permute-start | bytes 196616 | tf_op jit(solution)/shard_map/ppermute | solution.py:282
  52.2 3.9 %collective-permute-start.21 = (bf16[1,128,256]{2,1,0:T(8,128)(2,1)S(1)}, bf16[1,128,256]{2,1,0:T(8,128)(2,1)S(1)}, u32[]{:S(2)}, u32[]{:S(2)}) collective-permute-start(bf16[1,128,256]{2,1,0:T(8,128)(2,1)S(1)} %get-tuple-element.43), channel_id=1, source_target_pairs={{0,3},{1,2},{2,1},{3,0},{4,7},{5,6},{6,5},{7,4},{8,11},{9,10},{10,... | collective-permute-start | bytes 196616 | tf_op jit(solution)/shard_map/ppermute | solution.py:282
  54.9 1.3 %collective-permute-start.20 = (bf16[128,256]{1,0:T(8,128)(2,1)S(1)}, bf16[128,256]{1,0:T(8,128)(2,1)S(1)}, u32[]{:S(2)}, u32[]{:S(2)}) collective-permute-start(bf16[128,256]{1,0:T(8,128)(2,1)S(1)} %get-tuple-element.47), channel_id=1, source_target_pairs={{0,1},{1,0},{2,3},{3,2},{4,5},{5,4},{6,7},{7,6},{8,9},{9,8},{10,11... | collective-permute-start | bytes 196616 | tf_op jit(solution)/shard_map/ppermute | solution.py:282
